TPU v7x, 32 devices: a whole 2x2x4 slice. The times are simulated.
32 devices in a mesh: tm: 8 (over z, x), batch: 4 (over y, core).
Axes of the slice: x: 2, y: 2, z: 4, core: 2. Of those that a mesh axis runs over, the one named last changes fastest.
Arguments:
- clip_input: bfloat16 [32, 64, 8, 256], P('batch', 'tm'), may hold values from -6 to 6
- frame_counts: int32 [32], replicated, may hold values from 8 to 64, as said below
- clip_order: int32 [4, 8], replicated, may hold values from 0 to 7, each once within a row
- cotangent: float32 [32, 512], P('batch'), may hold values from -6 to 6
- kernel_one: float32 [9, 256, 512], P(None, 'batch', 'tm'), may hold values from -0.125 to 0.125
- kernel_one_mean: float32 [9, 256, 512], P(None, 'batch', 'tm'), may hold values from -0.00018310547 to 0.00018310547
- kernel_one_square: float32 [9, 256, 512], P(None, 'batch', 'tm'), may hold values from 3.5300842e-11 to 5.648135e-10
- kernel_two: float32 [9, 512, 512], P(None, 'batch', 'tm'), may hold values from -0.09375 to 0.09375
- kernel_two_mean: float32 [9, 512, 512], P(None, 'batch', 'tm'), may hold values from -0.00018310547 to 0.00018310547
- kernel_two_square: float32 [9, 512, 512], P(None, 'batch', 'tm'), may hold values from 3.5300842e-11 to 5.648135e-10
- norm_params: float32 [4, 512], P(None, 'tm')
- norm_mean: float32 [4, 512], P(None, 'tm'), may hold values from -0.0007324219 to 0.0007324219
- norm_square: float32 [4, 512], P(None, 'tm'), may hold values from 5.648135e-10 to 9.037016e-09
Outputs:
- pooled: float32 [32, 512], P('batch')
- input_grad: bfloat16 [32, 64, 8, 256], P('batch', 'tm')
- grad_norm: float32 [], replicated
- kernel_one_grad: float32 [9, 256, 512], P(None, 'batch', 'tm')
- kernel_one_mean_new: float32 [9, 256, 512], P(None, 'batch', 'tm')
- kernel_one_square_new: float32 [9, 256, 512], P(None, 'batch', 'tm')
- kernel_one_new: float32 [9, 256, 512], P(None, 'batch', 'tm')
- kernel_one_copy: bfloat16 [9, 256, 512], P(None, 'batch', 'tm')
- kernel_two_grad: float32 [9, 512, 512], P(None, 'batch', 'tm')
- kernel_two_mean_new: float32 [9, 512, 512], P(None, 'batch', 'tm')
- kernel_two_square_new: float32 [9, 512, 512], P(None, 'batch', 'tm')
- kernel_two_new: float32 [9, 512, 512], P(None, 'batch', 'tm')
- kernel_two_copy: bfloat16 [9, 512, 512], P(None, 'batch', 'tm')
- norm_grad: float32 [4, 512], P(None, 'tm')
- norm_mean_new: float32 [4, 512], P(None, 'tm')
- norm_square_new: float32 [4, 512], P(None, 'tm')
- norm_new: float32 [4, 512], P(None, 'tm')
- norm_copy: bfloat16 [4, 512], P(None, 'tm')
Inputs may be any that keep to these rules, and one draw needn't show every extreme that they name: `frame_counts`: in every group of 8 consecutive clips one clip, drawn from the seed, has all 64 frames valid. `clip_order`: each row holds every number below 8 once.
All inputs are finite; a program needn't handle non-finite values.
Results may differ from a plain program's by a relative error of at most 0.012.
Values may be sent and summed in bfloat16 or wider, within the bound.
No kernel may reach another device: no remote copies, remote signals or barrier semaphores. Data moves between devices by JAX's collectives and lax.ppermute only.
A program may use at most 128 MiB of HBM per device.

v0:
```python
import jax
import jax.numpy as jnp
from jax import lax
from jax.sharding import PartitionSpec as P

C1 = 256
C2 = 512
MEL = 8
FR_DEV = 8
CL_MB = 2
MB = 4
STEP = 10


BETA_ONE = 0.9
BETA_TWO = 0.999
ADAM_EPS = 1e-08
NORM_EPS = 1e-05
WEIGHT_DECAY = 0.01
CLIP_NORM = 0.5
GAIN_RATE = 1.0


def extended(block, sides, width):
    for axis, dim in sides:
        count = lax.axis_size(axis)
        forward = [(i, i + 1) for i in range(count - 1)]
        backward = [(target, source) for source, target in forward]
        low = lax.ppermute(
            lax.slice_in_dim(block, block.shape[dim] - width, None, axis=dim), axis, forward
        )
        high = lax.ppermute(lax.slice_in_dim(block, 0, width, axis=dim), axis, backward)
        block = jnp.concatenate([low, block, high], axis=dim)
    return block


def silu_slope(shaped):
    sigmoid_value = jax.nn.sigmoid(shaped)
    return sigmoid_value * (1.0 + shaped * (1.0 - sigmoid_value))


def pad_mel(field_data):
    return jnp.pad(field_data, ((0, 0), (0, 0), (1, 1), (0, 0)))


def frame_rim(field_data):
    return pad_mel(extended(field_data, (("tm", 1),), 1))


def grad_rim(field_data):
    return pad_mel(extended(field_data, (("tm", 1),), 1))


def patches(padded, frame_count, mel_count):
    pieces = [
        padded[:, step_time : step_time + frame_count, step_mel : step_mel + mel_count, :]
        for step_time in range(3)
        for step_mel in range(3)
    ]
    columns = jnp.concatenate(pieces, axis=-1)
    return columns.reshape(-1, columns.shape[-1])


def norm_forward(pre_norm, frame_mask, pixels, gain_row, shift_row):
    masked = pre_norm * frame_mask
    total_sum, square_sum = lax.psum(
        (jnp.sum(masked, axis=(0, 1, 2)), jnp.sum(masked * pre_norm, axis=(0, 1, 2))),
        ("tm", "batch"),
    )
    channel_mean = total_sum / pixels
    variance = square_sum / pixels - channel_mean * channel_mean
    inv_scale = lax.rsqrt(variance + NORM_EPS)
    normed = (pre_norm - channel_mean) * inv_scale
    return (normed, inv_scale, gain_row * normed + shift_row)


def norm_backward(outer_grad, frame_mask, shaped, normed, inv_scale, gain_row, pixels):
    slope_grad = outer_grad * frame_mask * silu_slope(shaped)
    shift_grad, gain_grad = lax.psum(
        (jnp.sum(slope_grad, axis=(0, 1, 2)), jnp.sum(slope_grad * normed, axis=(0, 1, 2))),
        ("tm", "batch"),
    )
    pre_grad = (
        frame_mask
        * inv_scale
        * gain_row
        * (slope_grad - shift_grad / pixels - normed * gain_grad / pixels)
    )
    return (pre_grad.astype(jnp.bfloat16), gain_grad, shift_grad)


def adam_step(weight, moment, square, summed, factor, step_rate, decay_rate):
    clipped = summed * factor
    moment_new = BETA_ONE * moment + (1.0 - BETA_ONE) * clipped
    square_new = BETA_TWO * square + (1.0 - BETA_TWO) * clipped * clipped
    corrected = moment_new / (1.0 - BETA_ONE**STEP)
    scaled = jnp.sqrt(square_new / (1.0 - BETA_TWO**STEP)) + ADAM_EPS
    weight_new = weight - step_rate * (corrected / scaled + decay_rate * weight)
    return (clipped, moment_new, square_new, weight_new, weight_new.astype(jnp.bfloat16))


def contract_rows(columns, grads):
    return lax.dot_general(
        columns, grads, (((0,), (0,)), ((), ())), preferred_element_type=jnp.float32
    )


def body(
    clip_input,
    frame_counts,
    clip_order,
    cotangent,
    kernel_one,
    kernel_one_mean,
    kernel_one_square,
    kernel_two,
    kernel_two_mean,
    kernel_two_square,
    norm_params,
    norm_mean,
    norm_square,
):
    batch_count = lax.axis_size("batch")
    tm_count = lax.axis_size("tm")
    tm_index = lax.axis_index("tm")
    batch_index = lax.axis_index("batch")
    half_frames = FR_DEV // 2
    counts_table = jnp.take_along_axis(frame_counts.reshape(batch_count, -1), clip_order, axis=1)
    valid_pixels = (
        MEL * jnp.sum(counts_table.reshape(batch_count, MB, CL_MB), axis=(0, 2))
    ).astype(jnp.float32)
    local_order = lax.dynamic_index_in_dim(clip_order, batch_index, 0, keepdims=False)
    local_counts = lax.dynamic_index_in_dim(counts_table, batch_index, 0, keepdims=False)
    frame_place = tm_index * FR_DEV + jnp.arange(FR_DEV, dtype=jnp.int32)
    pooled_place = 2 * (tm_index * half_frames + jnp.arange(half_frames, dtype=jnp.int32)) + 1
    low_one = kernel_one.astype(jnp.bfloat16)
    low_two = kernel_two.astype(jnp.bfloat16)
    low_gains = norm_params.astype(jnp.bfloat16)
    shape_out = (CL_MB, FR_DEV, MEL, C2)
    pooled = jnp.zeros((MB * CL_MB, C2), jnp.float32)
    input_grad = jnp.zeros(clip_input.shape, jnp.bfloat16)
    sum_one = jnp.zeros((9 * C1, C2), jnp.float32)
    sum_two = jnp.zeros((9 * C2, C2), jnp.float32)
    norm_sum = jnp.zeros((4, C2), jnp.float32)
    for micro_step in range(MB):
        tm_parts = (
            lax.all_gather(low_one, "tm", axis=2, tiled=True),
            lax.all_gather(low_two, "tm", axis=2, tiled=True),
            lax.all_gather(low_gains, "tm", axis=1, tiled=True),
        )
        full_one, full_two = (
            lax.all_gather(tm_parts[0], "batch", axis=1, tiled=True),
            lax.all_gather(tm_parts[1], "batch", axis=1, tiled=True),
        )
        weights = (full_one, full_two, tm_parts[2])
        gain_table = weights[2].astype(jnp.float32)
        flat_one = weights[0].reshape(9 * C1, C2)
        flat_two = weights[1].reshape(9 * C2, C2)
        slot_ids = local_order[micro_step * CL_MB : (micro_step + 1) * CL_MB]
        clip_counts = local_counts[micro_step * CL_MB : (micro_step + 1) * CL_MB]
        frame_mask = (frame_place[None, :] < clip_counts[:, None]).astype(jnp.float32)[
            :, :, None, None
        ]
        pool_mask = (pooled_place[None, :] < clip_counts[:, None]).astype(jnp.float32)[:, :, None]
        halves = (clip_counts // 2).astype(jnp.float32)[:, None]
        pixels = valid_pixels[micro_step]
        masked_input = jnp.take(clip_input, slot_ids, axis=0) * frame_mask.astype(jnp.bfloat16)
        input_columns = patches(frame_rim(masked_input), FR_DEV, MEL)
        pre_one = jnp.dot(input_columns, flat_one, preferred_element_type=jnp.float32).reshape(
            shape_out
        )
        normed_one, scale_one, shaped_one = norm_forward(
            pre_one, frame_mask, pixels, gain_table[0], gain_table[1]
        )
        hidden = (jax.nn.silu(shaped_one) * frame_mask).astype(jnp.bfloat16)
        hidden_columns = patches(frame_rim(hidden), FR_DEV, MEL)
        pre_two = jnp.dot(hidden_columns, flat_two, preferred_element_type=jnp.float32).reshape(
            shape_out
        )
        normed_two, scale_two, shaped_two = norm_forward(
            pre_two, frame_mask, pixels, gain_table[2], gain_table[3]
        )
        activation = jax.nn.silu(shaped_two) * frame_mask
        summary = jnp.mean(activation.reshape(CL_MB, half_frames, 2, MEL, C2), axis=(2, 3))
        exp_summary = jnp.exp(summary)
        mean_part, exp_part = lax.psum(
            (jnp.sum(summary * pool_mask, axis=1), jnp.sum(exp_summary * pool_mask, axis=1)), "tm"
        )
        pooled = pooled.at[slot_ids].set(mean_part / halves + jnp.log(exp_part / halves))
        cot_rows = jnp.take(cotangent, slot_ids, axis=0)[:, None, :]
        summary_grad = pool_mask * (
            cot_rows / halves[:, :, None] + cot_rows * exp_summary / exp_part[:, None, :]
        )
        activation_grad = jnp.broadcast_to(
            (summary_grad / (2 * MEL))[:, :, None, None, :], (CL_MB, half_frames, 2, MEL, C2)
        ).reshape(shape_out)
        grad_two, gain_two_grad, shift_two_grad = norm_backward(
            activation_grad, frame_mask, shaped_two, normed_two, scale_two, gain_table[2], pixels
        )
        sum_two = sum_two + contract_rows(hidden_columns, grad_two.reshape(-1, C2))
        flip_two = weights[1][::-1].transpose(0, 2, 1).reshape(9 * C2, C2)
        hidden_grad = jnp.dot(
            patches(grad_rim(grad_two), FR_DEV, MEL), flip_two, preferred_element_type=jnp.float32
        ).reshape(shape_out)
        grad_one, gain_one_grad, shift_one_grad = norm_backward(
            hidden_grad, frame_mask, shaped_one, normed_one, scale_one, gain_table[0], pixels
        )
        sum_one = sum_one + contract_rows(input_columns, grad_one.reshape(-1, C2))
        flip_one = weights[0][::-1].transpose(0, 2, 1).reshape(9 * C2, C1)
        rows_grad = jnp.dot(
            patches(grad_rim(grad_one), FR_DEV, MEL), flip_one, preferred_element_type=jnp.float32
        ).reshape(CL_MB, FR_DEV, MEL, C1)
        input_grad = input_grad.at[slot_ids].set((rows_grad * frame_mask).astype(jnp.bfloat16))
        norm_sum = norm_sum + jnp.stack(
            [gain_one_grad, shift_one_grad, gain_two_grad, shift_two_grad]
        )
    batch_parts = (
        lax.psum_scatter(sum_one.reshape(9, C1, C2), "batch", scatter_dimension=1, tiled=True),
        lax.psum_scatter(sum_two.reshape(9, C2, C2), "batch", scatter_dimension=1, tiled=True),
    )
    grad_one_shard, grad_two_shard = (
        lax.psum_scatter(batch_parts[0], "tm", scatter_dimension=2, tiled=True),
        lax.psum_scatter(batch_parts[1], "tm", scatter_dimension=2, tiled=True),
    )
    shard_width = C2 // tm_count
    norm_shard = lax.dynamic_slice_in_dim(norm_sum, tm_index * shard_width, shard_width, 1)
    norm_term = jnp.where(batch_index == 0, jnp.sum(norm_shard * norm_shard), 0.0)
    own_squares = (
        jnp.sum(grad_one_shard * grad_one_shard)
        + jnp.sum(grad_two_shard * grad_two_shard)
        + norm_term
    )
    grad_norm = jnp.sqrt(lax.psum(own_squares, ("tm", "batch")))
    factor = jnp.minimum(1.0, CLIP_NORM / (grad_norm + 1e-06))
    first_update = adam_step(
        kernel_one,
        kernel_one_mean,
        kernel_one_square,
        grad_one_shard,
        factor,
        (9 * C1) ** (-0.5),
        WEIGHT_DECAY,
    )
    second_update = adam_step(
        kernel_two,
        kernel_two_mean,
        kernel_two_square,
        grad_two_shard,
        factor,
        (9 * C2) ** (-0.5),
        WEIGHT_DECAY,
    )
    norm_update = adam_step(norm_params, norm_mean, norm_square, norm_shard, factor, GAIN_RATE, 0.0)
    return (pooled, input_grad, grad_norm) + first_update + second_update + norm_update


def solution(mesh):
    in_specs = (
        P("batch", "tm", None, None),
        P(),
        P(),
        P("batch", None),
        P(None, "batch", "tm"),
        P(None, "batch", "tm"),
        P(None, "batch", "tm"),
        P(None, "batch", "tm"),
        P(None, "batch", "tm"),
        P(None, "batch", "tm"),
        P(None, "tm"),
        P(None, "tm"),
        P(None, "tm"),
    )
    out_specs = (
        P("batch", None),
        P("batch", "tm", None, None),
        P(),
        P(None, "batch", "tm"),
        P(None, "batch", "tm"),
        P(None, "batch", "tm"),
        P(None, "batch", "tm"),
        P(None, "batch", "tm"),
        P(None, "batch", "tm"),
        P(None, "batch", "tm"),
        P(None, "batch", "tm"),
        P(None, "batch", "tm"),
        P(None, "batch", "tm"),
        P(None, "tm"),
        P(None, "tm"),
        P(None, "tm"),
        P(None, "tm"),
        P(None, "tm"),
    )
    return jax.shard_map(body, mesh=mesh, in_specs=in_specs, out_specs=out_specs, check_vma=False)
```

profile of v0, /device:TPU:0, one launch (start us, length us, event | category | flops | bytes accessed | tf_op | source)
XLA Modules:
  0.0 794.8 jit_solution(18166094526058933013)
XLA Ops:
  12.8 4.8 collective-permute-start.12
  19.6 4.5 collective-permute-start.4
  26.2 5.0 collective-permute-start
  31.5 52.6 %all_gather.11 = bf16[9,64,512]{1,0,2:T(8,128)(2,1)S(1)} all-gather(bf16[9,64,64]{1,0,2:T(8,128)(2,1)S(1)} %copy.79), channel_id=1, replica_groups=mesh['tm'=8,'batch'=4] {'tm'}, dimensions={2}, use_global_device_ids=true | all-gather | bytes 663552 | tf_op jit(solution)/shard_map/all_gather | solution.py:147
  90.6 18.1 %all-gather = bf16[8,64,4]{1,2,0:T(4,128)(2,1)S(1)} all-gather(bf16[1,64,4]{1,2,0:T(4,128)(2,1)S(1)} %convert_bitcast_fusion), channel_id=1, replica_groups=mesh['tm'=8,'batch'=4] {'tm'}, dimensions={0}, use_global_device_ids=true | all-gather | bytes 4608 | tf_op jit(solution)/shard_map/all_gather | solution.py:149
  113.0 4.5 collective-permute-start.8
  129.6 38.8 %all-reduce.19 = (f32[512]{0:T(512)S(1)}, f32[512]{0:T(512)S(1)}, f32[512]{0:T(512)S(1)}, f32[512]{0:T(512)S(1)}, f32[512]{0:T(512)S(1)}, /*index=5*/f32[512]{0:T(512)S(1)}, f32[512]{0:T(512)S(1)}, f32[512]{0:T(512)S(1)}) all-reduce(f32[512]{0:T(512)S(1)} %get-tuple-element.31, ...), channel_id=1, replica_groups=mesh['tm'=8,'batch'=4] {'tm','batch'}, use_global_device_ids=true, to_apply=%region_50.52 | all-reduce | flops 4096 | bytes 32768 | tf_op jit(solution)/shard_map/psum | solution.py:66
  177.1 4.6 collective-permute-start.2
  183.1 5.4 collective-permute-start.6
  189.9 5.4 collective-permute-start.14
  210.0 6.7 copy.81
  224.6 41.8 %all-reduce.18 = (f32[512]{0:T(512)S(1)}, f32[512]{0:T(512)S(1)}, f32[512]{0:T(512)S(1)}, f32[512]{0:T(512)S(1)}, f32[512]{0:T(512)S(1)}, /*index=5*/f32[512]{0:T(512)S(1)}, f32[512]{0:T(512)S(1)}, f32[512]{0:T(512)S(1)}) all-reduce(f32[512]{0:T(512)S(1)} %get-tuple-element.29, ...), channel_id=1, replica_groups=mesh['tm'=8,'batch'=4] {'tm','batch'}, use_global_device_ids=true, to_apply=%region_54.56 | all-reduce | flops 4096 | bytes 32768 | tf_op jit(solution)/shard_map/psum | solution.py:66
  268.4 20.4 %psum.292 = f32[2,512]{1,0:T(2,128)S(1)} all-reduce(f32[2,512]{1,0:T(2,128)S(1)} %get-tuple-element.58), channel_id=1, replica_groups=mesh['tm'=8,'batch'=4] {'tm'}, use_global_device_ids=true, to_apply=%region_15.17 | all-reduce | flops 1024 | bytes 8192 | tf_op jit(solution)/shard_map/psum | solution.py:186
  291.8 33.7 %all-reduce.20 = (f32[2,512]{1,0:T(2,128)}, f32[2,512]{1,0:T(2,128)}, f32[2,512]{1,0:T(2,128)S(1)}, f32[2,512]{1,0:T(2,128)}, f32[2,512]{1,0:T(2,128)S(1)}, /*index=5*/f32[2,512]{1,0:T(2,128)}, f32[2,512]{1,0:T(2,128)S(1)}) all-reduce(f32[2,512]{1,0:T(2,128)S(1)} %get-tuple-element.59, ...), channel_id=1, replica_groups=mesh['tm'=8,'batch'=4] {'tm'}, use_global_device_ids=true, to_apply=%region_13.15 | all-reduce | flops 7168 | bytes 57344 | tf_op jit(solution)/shard_map/psum | solution.py:186
  326.5 37.2 %all-reduce.17 = (f32[512]{0:T(512)S(1)}, f32[512]{0:T(512)S(1)}, f32[512]{0:T(512)S(1)}, f32[512]{0:T(512)S(1)}, f32[512]{0:T(512)S(1)}, /*index=5*/f32[512]{0:T(512)S(1)}, f32[512]{0:T(512)S(1)}, f32[512]{0:T(512)S(1)}) all-reduce(f32[512]{0:T(512)S(1)} %get-tuple-element.27, ...), channel_id=1, replica_groups=mesh['tm'=8,'batch'=4] {'tm','batch'}, use_global_device_ids=true, to_apply=%region_65.68 | all-reduce | flops 4096 | bytes 32768 | tf_op jit(solution)/shard_map/psum | solution.py:79
  381.4 5.4 collective-permute-start.20
  388.4 4.8 rev.4
  394.5 5.4 collective-permute-start.16
  413.6 43.4 %all-reduce.16 = (f32[512]{0:T(512)}, f32[512]{0:T(512)S(1)}, f32[512]{0:T(512)S(1)}, f32[512]{0:T(512)S(1)}, f32[512]{0:T(512)S(1)}, /*index=5*/f32[512]{0:T(512)S(1)}, f32[512]{0:T(512)S(1)}, f32[512]{0:T(512)S(1)}) all-reduce(f32[512]{0:T(512)S(1)} %get-tuple-element.51, ...), channel_id=1, replica_groups=mesh['tm'=8,'batch'=4] {'tm','batch'}, use_global_device_ids=true, to_apply=%region_69.72 | all-reduce | flops 4096 | bytes 32768 | tf_op jit(solution)/shard_map/psum | solution.py:79
  472.6 6.2 fusion.103
  478.8 5.0 fusion.104
  483.8 12.6 %bitcast_add_fusion = f32[4608,512]{1,0:T(8,128)} fusion(f32[4608,512,1,1]{1,0,3,2:T(8,128)} %fusion.104, f32[4608,512,1,1]{1,0,3,2:T(8,128)} %fusion.103, f32[4608,512,1,1]{1,0,3,2:T(8,128)S(1)} %fusion.102, bf16[2,8,8,4608]{3,2,1,0:T(8,128)(2,1)} %constant_dynamic-update-slice_fusion.63, bf16[2,8,8,512]{3,2,1,0:T(8,128)(2,1)S(1)} %multiply_convert_fusion.1), kind=kOutput, calls=%fused_computation.17 | convolution fusion | flops 611057664 | bytes 39059456 | tf_op jit(solution)/shard_map/dot_general | solution.py:103
  496.4 9.6 %copy.91 = f32[9,512,512]{1,2,0:T(8,128)} copy(f32[9,512,512]{2,1,0:T(8,128)} %bitcast.226) | data formatting | bytes 18874368 | tf_op jit(solution)/shard_map/reshape | solution.py:219
  516.0 5.0 collective-permute-start.30
  522.3 4.5 collective-permute-start.26
  528.2 4.5 collective-permute-start.22
  536.8 5.2 collective-permute-start.18
  550.4 4.7 copy.104
  569.6 29.4 %reduce-scatter.9.cloned.1.call-done = f32[9,128,512]{1,2,0:T(8,128)} async-done(((f32[9,512,512]{1,2,0:T(8,128)}), f32[9,128,512]{1,2,0:T(8,128)}) %reduce-scatter.9.cloned.1.call-update) | async-done | bytes 2359312 | tf_op jit(solution)/shard_map/reduce_scatter | solution.py:219
  619.3 47.7 %reduce-scatter.13.cloned.1.call-done = f32[64,576]{1,0:T(8,128)} async-done(((f32[512,576]{1,0:T(8,128)}), f32[64,576]{1,0:T(8,128)}) %reduce-scatter.13.cloned.1.call-update) | async-done | bytes 147472
  668.9 70.6 %reduce-scatter.11.cloned.1.call-done = f32[9,128,64]{1,2,0:T(8,128)} async-done(((f32[9,128,512]{1,2,0:T(8,128)}), f32[9,128,64]{1,2,0:T(8,128)}) %reduce-scatter.11.cloned.1.call-update) | async-done | bytes 294928 | tf_op jit(solution)/shard_map/reduce_scatter | solution.py:223
  743.0 39.5 %psum.327 = f32[]{:T(128)} all-reduce(f32[]{:T(128)S(6)} %add.600), channel_id=1, replica_groups=mesh['tm'=8,'batch'=4] {'tm','batch'}, use_global_device_ids=true, to_apply=%region_105.108 | all-reduce | flops 1 | bytes 8 | tf_op jit(solution)/shard_map/psum | solution.py:233
  (715 shorter events, 184.9 us)
Async XLA Ops:
  7.2 117.8 %all-gather.7.cloned.1.call-start = ((), (), s32[]{:S(2)}) async-start(), calls=%async_computation.5 | async-start | bytes 1327104 | tf_op jit(solution)/shard_map/all_gather | solution.py:148
  9.0 116.1 %all-gather.5.cloned.1.call-start = ((), (), s32[]{:S(2)}) async-start(), calls=%async_computation.4 | async-start | bytes 2949120 | tf_op jit(solution)/shard_map/all_gather | solution.py:152
  12.8 98.9 %collective-permute-start.12 = (bf16[2,1,8,256]{3,2,1,0:T(8,128)(2,1)S(1)}, bf16[2,1,8,256]{3,2,1,0:T(8,128)(2,1)S(1)}, u32[]{:S(2)}, u32[]{:S(2)}) collective-permute-start(bf16[2,1,8,256]{3,2,1,0:T(8,128)(2,1)S(1)} %get-tuple-element.172), channel_id=1, source_target_pairs={{0,4},{4,8},{8,12},{12,16},{16,20},{20,24},{24,28},{1,5},{5,9},{9,... | collective-permute-start | bytes 24584 | tf_op jit(solution)/shard_map/ppermute | solution.py:29
  17.7 95.3 %collective-permute-start.13 = (bf16[2,1,8,256]{3,2,1,0:T(8,128)(2,1)S(1)}, bf16[2,1,8,256]{3,2,1,0:T(8,128)(2,1)S(1)}, u32[]{:S(2)}, u32[]{:S(2)}) collective-permute-start(bf16[2,1,8,256]{3,2,1,0:T(8,128)(2,1)S(1)} %get-tuple-element.173), channel_id=1, source_target_pairs={{4,0},{8,4},{12,8},{16,12},{20,16},{24,20},{28,24},{5,1},{9,5},{13... | collective-permute-start | bytes 24584 | tf_op jit(solution)/shard_map/ppermute | solution.py:32
  19.6 98.2 %collective-permute-start.4 = (bf16[2,1,8,256]{3,2,1,0:T(8,128)(2,1)S(1)}, bf16[2,1,8,256]{3,2,1,0:T(8,128)(2,1)S(1)}, u32[]{:S(2)}, u32[]{:S(2)}) collective-permute-start(bf16[2,1,8,256]{3,2,1,0:T(8,128)(2,1)S(1)} %get-tuple-element.168), channel_id=1, source_target_pairs={{0,4},{4,8},{8,12},{12,16},{16,20},{20,24},{24,28},{1,5},{5,9},{9,... | collective-permute-start | bytes 24584 | tf_op jit(solution)/shard_map/ppermute | solution.py:29
  24.2 94.9 %collective-permute-start.5 = (bf16[2,1,8,256]{3,2,1,0:T(8,128)(2,1)S(1)}, bf16[2,1,8,256]{3,2,1,0:T(8,128)(2,1)S(1)}, u32[]{:S(2)}, u32[]{:S(2)}) collective-permute-start(bf16[2,1,8,256]{3,2,1,0:T(8,128)(2,1)S(1)} %get-tuple-element.169), channel_id=1, source_target_pairs={{4,0},{8,4},{12,8},{16,12},{20,16},{24,20},{28,24},{5,1},{9,5},{13... | collective-permute-start | bytes 24584 | tf_op jit(solution)/shard_map/ppermute | solution.py:32
  26.2 93.3 %collective-permute-start = (bf16[2,1,8,256]{3,2,1,0:T(8,128)(2,1)S(1)}, bf16[2,1,8,256]{3,2,1,0:T(8,128)(2,1)S(1)}, u32[]{:S(2)}, u32[]{:S(2)}) collective-permute-start(bf16[2,1,8,256]{3,2,1,0:T(8,128)(2,1)S(1)} %get-tuple-element.170), channel_id=1, source_target_pairs={{0,4},{4,8},{8,12},{12,16},{16,20},{20,24},{24,28},{1,5},{5,9},{9,... | collective-permute-start | bytes 24584 | tf_op jit(solution)/shard_map/ppermute | solution.py:29
  86.0 124.0 %all-gather.9.cloned.1.call-start = ((), (), s32[]{:S(2)}) async-start(), calls=%async_computation.6 | async-start | bytes 5898240 | tf_op jit(solution)/shard_map/all_gather | solution.py:153
  125.0 425.4 %reduce-scatter.7.cloned.1.call-start = ((), (), s32[]{:S(2)}) async-start(), calls=%async_computation.7 | async-start | bytes 5898240 | tf_op jit(solution)/shard_map/reduce_scatter | solution.py:218
  171.6 16.9 %collective-permute-start.10 = (bf16[2,1,8,512]{3,2,1,0:T(8,128)(2,1)S(1)}, bf16[2,1,8,512]{3,2,1,0:T(8,128)(2,1)S(1)}, u32[]{:S(2)}, u32[]{:S(2)}) collective-permute-start(bf16[2,1,8,512]{3,2,1,0:T(8,128)(2,1)S(1)} %get-tuple-element.158), channel_id=1, source_target_pairs={{0,4},{4,8},{8,12},{12,16},{16,20},{20,24},{24,28},{1,5},{5,9},{9,... | collective-permute-start | bytes 49160 | tf_op jit(solution)/shard_map/ppermute | solution.py:29
  175.8 14.0 %collective-permute-start.11 = (bf16[2,1,8,512]{3,2,1,0:T(8,128)(2,1)S(1)}, bf16[2,1,8,512]{3,2,1,0:T(8,128)(2,1)S(1)}, u32[]{:S(2)}, u32[]{:S(2)}) collective-permute-start(bf16[2,1,8,512]{3,2,1,0:T(8,128)(2,1)S(1)} %get-tuple-element.159), channel_id=1, source_target_pairs={{4,0},{8,4},{12,8},{16,12},{20,16},{24,20},{28,24},{5,1},{9,5},{13... | collective-permute-start | bytes 49160 | tf_op jit(solution)/shard_map/ppermute | solution.py:32
  177.1 18.5 %collective-permute-start.2 = (bf16[2,1,8,512]{3,2,1,0:T(8,128)(2,1)S(1)}, bf16[2,1,8,512]{3,2,1,0:T(8,128)(2,1)S(1)}, u32[]{:S(2)}, u32[]{:S(2)}) collective-permute-start(bf16[2,1,8,512]{3,2,1,0:T(8,128)(2,1)S(1)} %get-tuple-element.162), channel_id=1, source_target_pairs={{0,4},{4,8},{8,12},{12,16},{16,20},{20,24},{24,28},{1,5},{5,9},{9,... | collective-permute-start | bytes 49160 | tf_op jit(solution)/shard_map/ppermute | solution.py:29
  181.8 15.4 %collective-permute-start.3 = (bf16[2,1,8,512]{3,2,1,0:T(8,128)(2,1)S(1)}, bf16[2,1,8,512]{3,2,1,0:T(8,128)(2,1)S(1)}, u32[]{:S(2)}, u32[]{:S(2)}) collective-permute-start(bf16[2,1,8,512]{3,2,1,0:T(8,128)(2,1)S(1)} %get-tuple-element.163), channel_id=1, source_target_pairs={{4,0},{8,4},{12,8},{16,12},{20,16},{24,20},{28,24},{5,1},{9,5},{13... | collective-permute-start | bytes 49160 | tf_op jit(solution)/shard_map/ppermute | solution.py:32
  183.1 14.4 %collective-permute-start.6 = (bf16[2,1,8,512]{3,2,1,0:T(8,128)(2,1)S(1)}, bf16[2,1,8,512]{3,2,1,0:T(8,128)(2,1)S(1)}, u32[]{:S(2)}, u32[]{:S(2)}) collective-permute-start(bf16[2,1,8,512]{3,2,1,0:T(8,128)(2,1)S(1)} %get-tuple-element.160), channel_id=1, source_target_pairs={{0,4},{4,8},{8,12},{12,16},{16,20},{20,24},{24,28},{1,5},{5,9},{9,... | collective-permute-start | bytes 49160 | tf_op jit(solution)/shard_map/ppermute | solution.py:29
  367.2 26.0 %collective-permute-start.28 = (bf16[2,1,8,512]{3,2,1,0:T(8,128)(2,1)S(1)}, bf16[2,1,8,512]{3,2,1,0:T(8,128)(2,1)S(1)}, u32[]{:S(2)}, u32[]{:S(2)}) collective-permute-start(bf16[2,1,8,512]{3,2,1,0:T(8,128)(2,1)S(1)} %get-tuple-element.150), channel_id=1, source_target_pairs={{0,4},{4,8},{8,12},{12,16},{16,20},{20,24},{24,28},{1,5},{5,9},{9,... | collective-permute-start | bytes 49160 | tf_op jit(solution)/shard_map/ppermute | solution.py:29
  371.4 23.1 %collective-permute-start.29 = (bf16[2,1,8,512]{3,2,1,0:T(8,128)(2,1)S(1)}, bf16[2,1,8,512]{3,2,1,0:T(8,128)(2,1)S(1)}, u32[]{:S(2)}, u32[]{:S(2)}) collective-permute-start(bf16[2,1,8,512]{3,2,1,0:T(8,128)(2,1)S(1)} %get-tuple-element.151), channel_id=1, source_target_pairs={{4,0},{8,4},{12,8},{16,12},{20,16},{24,20},{28,24},{5,1},{9,5},{13... | collective-permute-start | bytes 49160 | tf_op jit(solution)/shard_map/ppermute | solution.py:32
  374.1 27.3 %collective-permute-start.24 = (bf16[2,1,8,512]{3,2,1,0:T(8,128)(2,1)}, bf16[2,1,8,512]{3,2,1,0:T(8,128)(2,1)S(1)}, u32[]{:S(2)}, u32[]{:S(2)}) collective-permute-start(bf16[2,1,8,512]{3,2,1,0:T(8,128)(2,1)} %get-tuple-element.152), channel_id=1, source_target_pairs={{0,4},{4,8},{8,12},{12,16},{16,20},{20,24},{24,28},{1,5},{5,9},{9,... | collective-permute-start | bytes 49160 | tf_op jit(solution)/shard_map/ppermute | solution.py:29
  378.7 24.4 %collective-permute-start.25 = (bf16[2,1,8,512]{3,2,1,0:T(8,128)(2,1)}, bf16[2,1,8,512]{3,2,1,0:T(8,128)(2,1)S(1)}, u32[]{:S(2)}, u32[]{:S(2)}) collective-permute-start(bf16[2,1,8,512]{3,2,1,0:T(8,128)(2,1)} %get-tuple-element.153), channel_id=1, source_target_pairs={{4,0},{8,4},{12,8},{16,12},{20,16},{24,20},{28,24},{5,1},{9,5},{13... | collective-permute-start | bytes 49160 | tf_op jit(solution)/shard_map/ppermute | solution.py:32
  381.4 26.2 %collective-permute-start.20 = (bf16[2,1,8,512]{3,2,1,0:T(8,128)(2,1)}, bf16[2,1,8,512]{3,2,1,0:T(8,128)(2,1)S(1)}, u32[]{:S(2)}, u32[]{:S(2)}) collective-permute-start(bf16[2,1,8,512]{3,2,1,0:T(8,128)(2,1)} %get-tuple-element.154), channel_id=1, source_target_pairs={{0,4},{4,8},{8,12},{12,16},{16,20},{20,24},{24,28},{1,5},{5,9},{9,... | collective-permute-start | bytes 49160 | tf_op jit(solution)/shard_map/ppermute | solution.py:29
  393.2 14.4 %collective-permute-start.21 = (bf16[2,1,8,512]{3,2,1,0:T(8,128)(2,1)}, bf16[2,1,8,512]{3,2,1,0:T(8,128)(2,1)S(1)}, u32[]{:S(2)}, u32[]{:S(2)}) collective-permute-start(bf16[2,1,8,512]{3,2,1,0:T(8,128)(2,1)} %get-tuple-element.155), channel_id=1, source_target_pairs={{4,0},{8,4},{12,8},{16,12},{20,16},{24,20},{28,24},{5,1},{9,5},{13... | collective-permute-start | bytes 49160 | tf_op jit(solution)/shard_map/ppermute | solution.py:32
  394.5 15.7 %collective-permute-start.16 = (bf16[2,1,8,512]{3,2,1,0:T(8,128)(2,1)}, bf16[2,1,8,512]{3,2,1,0:T(8,128)(2,1)S(1)}, u32[]{:S(2)}, u32[]{:S(2)}) collective-permute-start(bf16[2,1,8,512]{3,2,1,0:T(8,128)(2,1)} %get-tuple-element.156), channel_id=1, source_target_pairs={{0,4},{4,8},{8,12},{12,16},{16,20},{20,24},{24,28},{1,5},{5,9},{9,... | collective-permute-start | bytes 49160 | tf_op jit(solution)/shard_map/ppermute | solution.py:29
  469.5 129.6 %reduce-scatter.9.cloned.1.call-start = ((), (), s32[]{:S(2)}) async-start(), calls=%async_computation.8 | async-start | bytes 11796480 | tf_op jit(solution)/shard_map/reduce_scatter | solution.py:219
  506.1 161.0 %reduce-scatter.13.cloned.1.call-start = ((), (), s32[]{:S(2)}) async-start(), calls=%async_computation.10 | async-start | bytes 1474560
  516.0 100.9 %collective-permute-start.30 = (bf16[2,1,8,512]{3,2,1,0:T(8,128)(2,1)}, bf16[2,1,8,512]{3,2,1,0:T(8,128)(2,1)}, u32[]{:S(2)}, u32[]{:S(2)}) collective-permute-start(bf16[2,1,8,512]{3,2,1,0:T(8,128)(2,1)} %get-tuple-element.142), channel_id=1, source_target_pairs={{0,4},{4,8},{8,12},{12,16},{16,20},{20,24},{24,28},{1,5},{5,9},{9,... | collective-permute-start | bytes 49160 | tf_op jit(solution)/shard_map/ppermute | solution.py:29
  521.0 95.9 %collective-permute-start.31 = (bf16[2,1,8,512]{3,2,1,0:T(8,128)(2,1)}, bf16[2,1,8,512]{3,2,1,0:T(8,128)(2,1)S(1)}, u32[]{:S(2)}, u32[]{:S(2)}) collective-permute-start(bf16[2,1,8,512]{3,2,1,0:T(8,128)(2,1)} %get-tuple-element.143), channel_id=1, source_target_pairs={{4,0},{8,4},{12,8},{16,12},{20,16},{24,20},{28,24},{5,1},{9,5},{13... | collective-permute-start | bytes 49160 | tf_op jit(solution)/shard_map/ppermute | solution.py:32
  522.3 13.1 %collective-permute-start.26 = (bf16[2,1,8,512]{3,2,1,0:T(8,128)(2,1)S(1)}, bf16[2,1,8,512]{3,2,1,0:T(8,128)(2,1)S(1)}, u32[]{:S(2)}, u32[]{:S(2)}) collective-permute-start(bf16[2,1,8,512]{3,2,1,0:T(8,128)(2,1)S(1)} %get-tuple-element.144), channel_id=1, source_target_pairs={{0,4},{4,8},{8,12},{12,16},{16,20},{20,24},{24,28},{1,5},{5,9},{9,... | collective-permute-start | bytes 49160 | tf_op jit(solution)/shard_map/ppermute | solution.py:29
  526.9 9.9 %collective-permute-start.27 = (bf16[2,1,8,512]{3,2,1,0:T(8,128)(2,1)S(1)}, bf16[2,1,8,512]{3,2,1,0:T(8,128)(2,1)S(1)}, u32[]{:S(2)}, u32[]{:S(2)}) collective-permute-start(bf16[2,1,8,512]{3,2,1,0:T(8,128)(2,1)S(1)} %get-tuple-element.145), channel_id=1, source_target_pairs={{4,0},{8,4},{12,8},{16,12},{20,16},{24,20},{28,24},{5,1},{9,5},{13... | collective-permute-start | bytes 49160 | tf_op jit(solution)/shard_map/ppermute | solution.py:32
  528.2 15.2 %collective-permute-start.22 = (bf16[2,1,8,512]{3,2,1,0:T(8,128)(2,1)S(1)}, bf16[2,1,8,512]{3,2,1,0:T(8,128)(2,1)S(1)}, u32[]{:S(2)}, u32[]{:S(2)}) collective-permute-start(bf16[2,1,8,512]{3,2,1,0:T(8,128)(2,1)S(1)} %get-tuple-element.146), channel_id=1, source_target_pairs={{0,4},{4,8},{8,12},{12,16},{16,20},{20,24},{24,28},{1,5},{5,9},{9,... | collective-permute-start | bytes 49160 | tf_op jit(solution)/shard_map/ppermute | solution.py:29
  535.4 9.3 %collective-permute-start.23 = (bf16[2,1,8,512]{3,2,1,0:T(8,128)(2,1)S(1)}, bf16[2,1,8,512]{3,2,1,0:T(8,128)(2,1)S(1)}, u32[]{:S(2)}, u32[]{:S(2)}) collective-permute-start(bf16[2,1,8,512]{3,2,1,0:T(8,128)(2,1)S(1)} %get-tuple-element.147), channel_id=1, source_target_pairs={{4,0},{8,4},{12,8},{16,12},{20,16},{24,20},{28,24},{5,1},{9,5},{13... | collective-permute-start | bytes 49160 | tf_op jit(solution)/shard_map/ppermute | solution.py:32
  536.8 24.9 %collective-permute-start.18 = (bf16[2,1,8,512]{3,2,1,0:T(8,128)(2,1)}, bf16[2,1,8,512]{3,2,1,0:T(8,128)(2,1)}, u32[]{:S(2)}, u32[]{:S(2)}) collective-permute-start(bf16[2,1,8,512]{3,2,1,0:T(8,128)(2,1)} %get-tuple-element.148), channel_id=1, source_target_pairs={{0,4},{4,8},{8,12},{12,16},{16,20},{20,24},{24,28},{1,5},{5,9},{9,... | collective-permute-start | bytes 49160 | tf_op jit(solution)/shard_map/ppermute | solution.py:29
  543.4 18.2 %collective-permute-start.19 = (bf16[2,1,8,512]{3,2,1,0:T(8,128)(2,1)}, bf16[2,1,8,512]{3,2,1,0:T(8,128)(2,1)}, u32[]{:S(2)}, u32[]{:S(2)}) collective-permute-start(bf16[2,1,8,512]{3,2,1,0:T(8,128)(2,1)} %get-tuple-element.149), channel_id=1, source_target_pairs={{4,0},{8,4},{12,8},{16,12},{20,16},{24,20},{28,24},{5,1},{9,5},{13... | collective-permute-start | bytes 49160 | tf_op jit(solution)/shard_map/ppermute | solution.py:32
  559.3 180.2 %reduce-scatter.11.cloned.1.call-start = ((), (), s32[]{:S(2)}) async-start(), calls=%async_computation.9 | async-start | bytes 2654208 | tf_op jit(solution)/shard_map/reduce_scatter | solution.py:223
  (173 other events, 4907.2 us)
Sparse Core Ops, SparseCore 0:
  10.8 56.7 all-gather.6
  86.1 22.6 all-gather.4
  125.1 37.5 all-gather.8
  469.6 48.3 reduce-scatter.6
  520.6 78.4 reduce-scatter.8
  602.7 64.2 reduce-scatter.12
  670.9 68.4 reduce-scatter.10
where the time goes:
time: 803 us; the launch traced here: 795 us
  blocking collectives  325 us (40%)
  waiting for transfers between devices  156 us (19%)
  starting transfers between devices  99.5 us (12%)
  local copies, waits for them, and re-layouts  82.4 us (10%)
  matrix products  55.3 us (7%)
  other arithmetic  53.6 us (7%)
  between operations  22.6 us (3%)
    psum x2, blocking collectives, norm_forward(): lax.psum((jnp.sum(masked, axis=(0, 1, 2)), jnp.sum(masked * pre_norm, axi...  80.6 us
    psum x2, blocking collectives, norm_backward(): lax.psum((jnp.sum(slope_grad, axis=(0, 1, 2)), jnp.sum(slope_grad * norme...  80.5 us
    ppermute x16, starting transfers between devices, extended(): lax.ppermute(lax.slice_in_dim(block, block.shape[dim] - width, None, axis...  77.5 us
    reduce_scatter x1, waiting for transfers between devices, body(): lax.psum_scatter(batch_parts[1], 'tm', scatter_dimension=2, tiled=True)  70.6 us
    psum x2, blocking collectives, body(): lax.psum((jnp.sum(summary * pool_mask, axis=1), jnp.sum(exp_summary * poo...  54.1 us
    all_gather x1, blocking collectives, body(): lax.all_gather(low_one, 'tm', axis=2, tiled=True)  52.6 us
    unnamed x8, waiting for transfers between devices  47.8 us
    psum x1, blocking collectives, body(): grad_norm = jnp.sqrt(lax.psum(own_squares, ('tm', 'batch')))  39.5 us
  transfers between devices with their start and end apart: 39, of which 5 were waited for; matrix products, arithmetic and copies ran while one was open for 18% of the time, Pallas kernels for 0%

commit v1 on v0

--- a/solution.py
+++ b/solution.py
@@ -1,7 +1,11 @@
+import functools
+
 import jax
 import jax.numpy as jnp
 from jax import lax
-from jax.sharding import PartitionSpec as P
+from jax.experimental import pallas as pl
+from jax.experimental.pallas import tpu as pltpu
+from jax.sharding import Mesh, PartitionSpec as P
 
 C1 = 256
 C2 = 512
@@ -105,7 +109,7 @@
     )
 
 
-def body(
+def general_body(
     clip_input,
     frame_counts,
     clip_order,
@@ -254,40 +258,801 @@
     return (pooled, input_grad, grad_norm) + first_update + second_update + norm_update
 
 
+AXES = ("z", "x", "y", "core")
+BF = jnp.bfloat16
+F32 = jnp.float32
+ROWS = 512
+CLIPS_CORE = 4
+LANES = 128
+TAPS = 9
+ANY = pl.BlockSpec(memory_space=pl.ANY)
+VM = pl.BlockSpec(memory_space=pltpu.VMEM)
+SM = pl.BlockSpec(memory_space=pltpu.SMEM)
+VMEM_LIMIT = 56 * 1024 * 1024
+
+
+def shape_of(shape, dtype):
+    return jax.ShapeDtypeStruct(shape, dtype)
+
+
+def call(kernel, out, in_specs, out_specs, scratch=(), flops=0, moved=0):
+    return pl.pallas_call(
+        kernel,
+        out_shape=out,
+        in_specs=in_specs,
+        out_specs=out_specs,
+        scratch_shapes=list(scratch),
+        compiler_params=pltpu.CompilerParams(vmem_limit_bytes=VMEM_LIMIT),
+        cost_estimate=pl.CostEstimate(flops=flops, bytes_accessed=moved, transcendentals=0),
+    )
+
+
+def swap(value, axis, step=1):
+    size = lax.axis_size(axis)
+    return lax.ppermute(value, axis, [(i, i ^ step) for i in range(size)])
+
+
+def run_copies(copies, sems):
+    started = []
+    for at, (source, target) in enumerate(copies):
+        copy = pltpu.make_async_copy(source, target, sems.at[at])
+        copy.start()
+        started.append(copy)
+    for copy in started:
+        copy.wait()
+
+
+def time_shift(rows, step):
+    zero = jnp.zeros((MEL, rows.shape[1]), rows.dtype)
+    if step == 1:
+        return jnp.concatenate([rows[MEL:], zero], axis=0)
+    if step == -1:
+        return jnp.concatenate([zero, rows[:-MEL]], axis=0)
+    return rows
+
+
+def mel_shift(rows, step):
+    if step == 0:
+        return rows
+    cube = rows.reshape(rows.shape[0] // MEL, MEL, rows.shape[1])
+    turned = pltpu.roll(cube, (-step) % MEL, 1)
+    place = lax.broadcasted_iota(jnp.int32, cube.shape, 1) + step
+    keep = (place >= 0) & (place < MEL)
+    return jnp.where(keep, turned, 0.0).reshape(rows.shape)
+
+
+def valid_rows(count, width):
+    frame = lax.broadcasted_iota(jnp.int32, (ROWS, width), 0) // MEL
+    return (frame < count).astype(F32)
+
+
+def dot_nt(left, right):
+    return lax.dot_general(left, right, (((1,), (1,)), ((), ())), preferred_element_type=F32)
+
+
+def dot_nn(left, right):
+    return lax.dot_general(left, right, (((1,), (0,)), ((), ())), preferred_element_type=F32)
+
+
+def dot_tn(left, right):
+    return lax.dot_general(left, right, (((0,), (0,)), ((), ())), preferred_element_type=F32)
+
+
+def lanes_of(tap):
+    return slice(tap * LANES, (tap + 1) * LANES)
+
+
+def gather_taps(product):
+    total = None
+    for mel in range(3):
+        column = None
+        for time in range(3):
+            term = time_shift(product[:, lanes_of(3 * time + mel)], time - 1)
+            column = term if column is None else column + term
+        column = mel_shift(column, mel - 1)
+        total = column if total is None else total + column
+    return total
+
+
+def scatter_taps(grad, target, base):
+    for mel in range(3):
+        moved = mel_shift(grad, 1 - mel)
+        for time in range(3):
+            target[base : base + ROWS, lanes_of(3 * time + mel)] = time_shift(moved, 1 - time).astype(
+                BF
+            )
+
+
+def channel_sums(first, second):
+    return (jnp.sum(first, axis=0, keepdims=True), jnp.sum(second, axis=0, keepdims=True))
+
+
+def norm_rows(own_ref, other_ref, pixels):
+    mean = (own_ref[0:1, :] + other_ref[0:1, :]) / pixels
+    square = (own_ref[1:2, :] + other_ref[1:2, :]) / pixels
+    return mean, lax.rsqrt(square - mean * mean + NORM_EPS)
+
+
+def put_pair(ref, first, second):
+    ref[...] = jnp.zeros(ref.shape, F32)
+    ref[0:1, :] = first
+    ref[1:2, :] = second
+
+
+def take_kernel(ids_ref, clip_ref, *rest):
+    outs, sems = rest[:MB], rest[MB]
+    z = lax.axis_index("z")
+    copies = []
+    for step in range(MB):
+        plane = jnp.bitwise_xor(z, step)
+        for j in range(CL_MB):
+            copies.append((clip_ref.at[ids_ref[plane * CL_MB + j]], outs[step].at[j]))
+    run_copies(copies, sems)
+
+
+def weights_kernel(one_ref, two_ref, one_keep, one_send, two_keep, two_send, turned):
+    y = lax.axis_index("y")
+    for tap in range(TAPS):
+        for source, width, keep, send in (
+            (one_ref, 64, one_keep, one_send),
+            (two_ref, 128, two_keep, two_send),
+        ):
+            turned[:, 0:width] = jnp.swapaxes(source[tap], 0, 1)
+            keep[tap] = turned[pl.ds(y * 32, 32), 0:width].astype(BF)
+            send[tap] = turned[pl.ds((1 - y) * 32, 32), 0:width].astype(BF)
+
+
+def first_conv_kernel(
+    counts_ref, a0, a1, a23, b0, b1, b23, w_own, w_other, pre_ref, x_ref, weight_ref, stat_ref, low, sems
+):
+    z, x, y, core = (lax.axis_index(axis) for axis in AXES)
+    copies = []
+    for step in range(MB):
+        z_of = jnp.bitwise_xor(z, step)
+        for j, pieces in (
+            (0, ((a0, 0, x, y), (a1, 0, 1 - x, y), (a23, 0, x, 1 - y), (a23, MB, 1 - x, 1 - y))),
+            (1, ((b0, 0, x, y), (b1, 0, x, 1 - y), (b23, 0, 1 - x, y), (b23, MB, 1 - x, 1 - y))),
+        ):
+            for source, base, x_of, y_of in pieces:
+                row = pl.multiple_of((y_of * CL_MB + j) * ROWS + (z_of * 2 + x_of) * 64, 64)
+                copies.append((source.at[base + step], x_ref.at[pl.ds(row, 64), :]))
+    run = []
+    for at, (source, target) in enumerate(copies):
+        copy = pltpu.make_async_copy(source, target, sems.at[at])
+        copy.start()
+        run.append(copy)
+    place_in = lax.broadcasted_iota(jnp.int32, (256, 256), 0)
+    place_out = lax.broadcasted_iota(jnp.int32, (256, 256), 1)
+    source_in = ((place_out // 64) % 2) * 128 + (place_out // 128) * 64 + place_out % 64
+    spread = (place_in == source_in).astype(BF)
+    for step in range(MB):
+        z_of = jnp.bitwise_xor(z, step)
+        own, other = w_own[step, 0:288, :], w_other[step, 0:288, :]
+        zero, one = jnp.where(core == 0, own, other), jnp.where(core == 0, other, own)
+        both = dot_nn(jnp.concatenate([zero, one], axis=1), spread).astype(BF)
+        for tap in range(TAPS):
+            weight_ref[tap, z_of] = both[tap * 32 : (tap + 1) * 32]
+    for copy in run:
+        copy.wait()
+    weight = weight_ref[...].reshape(TAPS * LANES, C1)
+    first = jnp.zeros((1, LANES), F32)
+    second = jnp.zeros((1, LANES), F32)
+    for clip in range(CLIPS_CORE):
+        span = slice(clip * ROWS, (clip + 1) * ROWS)
+        mask = valid_rows(counts_ref[clip], C1)
+        masked = x_ref[span, :] * mask.astype(BF)
+        x_ref[span, :] = masked
+        pre = gather_taps(dot_nt(masked, weight))
+        pre_ref[span, :] = pre
+        kept = pre * mask[:, 0:LANES]
+        plus = channel_sums(kept, kept * pre)
+        first, second = first + plus[0], second + plus[1]
+    put_pair(stat_ref, first, second)
+
+
+def hidden_kernel(counts_ref, pixels_ref, pre_ref, own_ref, other_ref, gain_ref, a_ref, b_ref):
+    mean, scale = norm_rows(own_ref, other_ref, pixels_ref[0])
+    for clip in range(CLIPS_CORE):
+        pre = pre_ref[clip * ROWS : (clip + 1) * ROWS, :]
+        shaped = gain_ref[0:1, :] * ((pre - mean) * scale) + gain_ref[1:2, :]
+        value = shaped * jax.nn.sigmoid(shaped) * valid_rows(counts_ref[clip], LANES)
+        target = a_ref if clip < 2 else b_ref
+        target[(clip % 2) * ROWS : (clip % 2 + 1) * ROWS, :] = value.astype(BF)
+
+
+def second_weight_kernel(own_ref, other_ref, weight_ref, pieces, sems):
+    z, y, core = (lax.axis_index(axis) for axis in ("z", "y", "core"))
+    copies = []
+    for source, core_of in ((own_ref, core), (other_ref, 1 - core)):
+        for step in range(MB):
+            for turn in range(2):
+                y_of = jnp.bitwise_xor(y, turn)
+                copies.append(
+                    (source.at[step, turn], pieces.at[jnp.bitwise_xor(z, step), y_of * 2 + core_of])
+                )
+    run_copies(copies, sems)
+    place_in = lax.broadcasted_iota(jnp.int32, (C2, C2), 0)
+    place_out = lax.broadcasted_iota(jnp.int32, (C2, C2), 1)
+    source_in = ((place_out // 32) % 4) * 128 + (place_out // 128) * 32 + place_out % 32
+    spread = (place_in == source_in).astype(BF)
+    for step in range(MB):
+        natural = jnp.concatenate([pieces[step, part] for part in range(4)], axis=1)
+        both = dot_nn(natural, spread).astype(BF)
+        for tap in range(TAPS):
+            weight_ref[tap, step] = both[tap * 32 : (tap + 1) * 32]
+
+
+def hidden_copies(a0, a1, a23, b0, b1, b23, target):
+    x, y = lax.axis_index("x"), lax.axis_index("y")
+    copies = []
+    for source, base, half, x_of, y_of in (
+        (a0, None, 0, x, y),
+        (a1, None, 0, 1 - x, y),
+        (a23, 0, 0, x, 1 - y),
+        (a23, 1, 0, 1 - x, 1 - y),
+        (b0, None, 1, x, y),
+        (b1, None, 1, x, 1 - y),
+        (b23, 0, 1, 1 - x, y),
+        (b23, 1, 1, 1 - x, 1 - y),
+    ):
+        lane = pl.multiple_of((x_of * 2 + y_of) * LANES, LANES)
+        piece = source if base is None else source.at[base]
+        copies.append((piece, target.at[pl.ds(half * 2 * ROWS, 2 * ROWS), pl.ds(lane, LANES)]))
+    return copies
+
+
+def second_conv_kernel(
+    counts_ref, a0, a1, a23, b0, b1, b23, weight_ref, pre_ref, stat_ref, hidden, sems
+):
+    run_copies(hidden_copies(a0, a1, a23, b0, b1, b23, hidden), sems)
+    weight = weight_ref[...].reshape(TAPS * LANES, C2)
+    first = jnp.zeros((1, LANES), F32)
+    second = jnp.zeros((1, LANES), F32)
+    for clip in range(CLIPS_CORE):
+        span = slice(clip * ROWS, (clip + 1) * ROWS)
+        pre = gather_taps(dot_nt(hidden[span, :], weight))
+        pre_ref[span, :] = pre
+        kept = pre * valid_rows(counts_ref[clip], LANES)
+        plus = channel_sums(kept, kept * pre)
+        first, second = first + plus[0], second + plus[1]
+    put_pair(stat_ref, first, second)
+
+
+def pool_kernel(
+    counts_ref, pixels_ref, pre_ref, own_ref, other_ref, gain_ref, cot_ref, slope_ref, sum_ref, pooled_ref
+):
+    mean, scale = norm_rows(own_ref, other_ref, pixels_ref[0])
+    first = jnp.zeros((1, LANES), F32)
+    second = jnp.zeros((1, LANES), F32)
+    pooled_ref[...] = jnp.zeros(pooled_ref.shape, F32)
+    slots = ROWS // (2 * MEL)
+    for clip in range(CLIPS_CORE):
+        span = slice(clip * ROWS, (clip + 1) * ROWS)
+        count = counts_ref[clip]
+        mask = valid_rows(count, LANES)
+        normed = (pre_ref[span, :] - mean) * scale
+        shaped = gain_ref[2:3, :] * normed + gain_ref[3:4, :]
+        gate = jax.nn.sigmoid(shaped)
+        active = (shaped * gate * mask).reshape(slots, 2 * MEL, LANES)
+        summary = jnp.sum(active, axis=1) / (2 * MEL)
+        slot = lax.broadcasted_iota(jnp.int32, (slots, LANES), 0)
+        keep = (2 * slot + 1 < count).astype(F32)
+        raised = jnp.exp(summary)
+        exp_total = jnp.sum(raised * keep, axis=0, keepdims=True)
+        halves = (count // 2).astype(F32)
+        pooled_ref[clip : clip + 1, :] = jnp.sum(
+            summary * keep, axis=0, keepdims=True
+        ) / halves + jnp.log(exp_total / halves)
+        cot = cot_ref[clip : clip + 1, :]
+        summary_grad = keep * (cot / halves + cot * raised / exp_total) / (2 * MEL)
+        spread = jnp.broadcast_to(summary_grad[:, None, :], (slots, 2 * MEL, LANES))
+        slope = spread.reshape(ROWS, LANES) * mask * (gate * (1.0 + shaped * (1.0 - gate)))
+        slope_ref[span, :] = slope
+        plus = channel_sums(slope, slope * normed)
+        first, second = first + plus[0], second + plus[1]
+    put_pair(sum_ref, first, second)
+
+
+def pre_grad(slope, pre, mask, mean, scale, gain, sums, pixels):
+    normed = (pre - mean) * scale
+    return mask * (scale * gain) * (slope - sums[0] / pixels - normed * (sums[1] / pixels))
+
+
+def pair_sums(own_ref, other_ref):
+    return (own_ref[0:1, :] + other_ref[0:1, :], own_ref[1:2, :] + other_ref[1:2, :])
+
+
+def hidden_grad_kernel(
+    counts_ref,
+    pixels_ref,
+    slope_ref,
+    pre_ref,
+    own_ref,
+    other_ref,
+    sum_own,
+    sum_other,
+    gain_ref,
+    weight_ref,
+    grad_ref,
+    a_keep,
+    a_send,
+    b_keep,
+    b_send,
+    columns,
+    partial,
+):
+    x, y = lax.axis_index("x"), lax.axis_index("y")
+    pixels = pixels_ref[0]
+    mean, scale = norm_rows(own_ref, other_ref, pixels)
+    sums = pair_sums(sum_own, sum_other)
+    weight = weight_ref[...].reshape(TAPS * LANES, C2)
+    for clip in range(CLIPS_CORE):
+        span = slice(clip * ROWS, (clip + 1) * ROWS)
+        mask = valid_rows(counts_ref[clip], LANES)
+        grad = pre_grad(
+            slope_ref[span, :], pre_ref[span, :], mask, mean, scale, gain_ref[2:3, :], sums, pixels
+        )
+        grad_ref[span, :] = grad.astype(BF)
+        scatter_taps(grad, columns, 0)
+        partial[...] = dot_nn(columns[...], weight)
+        rows = slice((clip % 2) * ROWS, (clip % 2 + 1) * ROWS)
+        for other in range(2):
+            if clip < 2:
+                keep_lane, send_lane = x * 2 + other, (1 - x) * 2 + other
+                keep, send = a_keep, a_send
+            else:
+                keep_lane, send_lane = other * 2 + y, other * 2 + 1 - y
+                keep, send = b_keep, b_send
+            keep[other, rows, :] = partial[:, pl.ds(pl.multiple_of(keep_lane * LANES, LANES), LANES)]
+            send[other, rows, :] = partial[
+                :, pl.ds(pl.multiple_of(send_lane * LANES, LANES), LANES)
+            ].astype(BF)
+
+
+def second_weight_grad_kernel(
+    a0, a1, a23, b0, b1, b23, grad_ref, keep_ref, send_ref, hidden, columns, natural, sems
+):
+    core = lax.axis_index("core")
+    run = []
+    for at, (source, target) in enumerate(hidden_copies(a0, a1, a23, b0, b1, b23, hidden)):
+        copy = pltpu.make_async_copy(source, target, sems.at[at])
+        copy.start()
+        run.append(copy)
+    for clip in range(CLIPS_CORE):
+        grad = grad_ref[clip * ROWS : (clip + 1) * ROWS, :].astype(F32)
+        scatter_taps(grad, columns, clip * ROWS)
+    for copy in run:
+        copy.wait()
+    place_in = lax.broadcasted_iota(jnp.int32, (C2, C2), 0)
+    place_out = lax.broadcasted_iota(jnp.int32, (C2, C2), 1)
+    source_in = ((place_out // 32) % 4) * 128 + (place_out // 128) * 32 + place_out % 32
+    spread = (place_in == source_in).astype(BF)
+    for tap in range(TAPS):
+        chip = dot_tn(columns[:, lanes_of(tap)], hidden[...]).astype(BF)
+        natural[...] = dot_nn(chip, spread)
+        for y_of in range(2):
+            keep = natural[:, pl.ds(pl.multiple_of((y_of * 2 + core) * LANES, LANES), LANES)]
+            send = natural[:, pl.ds(pl.multiple_of((y_of * 2 + 1 - core) * LANES, LANES), LANES)]
+            for z_of in range(MB):
+                rows = slice(z_of * 32, (z_of + 1) * 32)
+                keep_ref[z_of, y_of, tap] = keep[rows].astype(BF)
+                send_ref[z_of, y_of, tap] = send[rows].astype(BF)
+
+
+def first_slope_kernel(
+    counts_ref,
+    pixels_ref,
+    a_keep,
+    a_got,
+    b_keep,
+    b_got,
+    pre_ref,
+    own_ref,
+    other_ref,
+    gain_ref,
+    slope_ref,
+    sum_ref,
+):
+    mean, scale = norm_rows(own_ref, other_ref, pixels_ref[0])
+    first = jnp.zeros((1, LANES), F32)
+    second = jnp.zeros((1, LANES), F32)
+    for clip in range(CLIPS_CORE):
+        span = slice(clip * ROWS, (clip + 1) * ROWS)
+        rows = slice((clip % 2) * ROWS, (clip % 2 + 1) * ROWS)
+        keep, got = (a_keep, a_got) if clip < 2 else (b_keep, b_got)
+        outer = keep[rows, :] + got[rows, :].astype(F32)
+        normed = (pre_ref[span, :] - mean) * scale
+        shaped = gain_ref[0:1, :] * normed + gain_ref[1:2, :]
+        gate = jax.nn.sigmoid(shaped)
+        slope = outer * valid_rows(counts_ref[clip], LANES) * (gate * (1.0 + shaped * (1.0 - gate)))
+        slope_ref[span, :] = slope
+        plus = channel_sums(slope, slope * normed)
+        first, second = first + plus[0], second + plus[1]
+    put_pair(sum_ref, first, second)
+
+
+def first_weight_grad_kernel(
+    counts_ref,
+    pixels_ref,
+    slope_ref,
+    pre_ref,
+    own_ref,
+    other_ref,
+    sum_own,
+    sum_other,
+    gain_ref,
+    x_ref,
+    keep_ref,
+    send_ref,
+    columns_ref,
+):
+    core = lax.axis_index("core")
+    pixels = pixels_ref[0]
+    mean, scale = norm_rows(own_ref, other_ref, pixels)
+    sums = pair_sums(sum_own, sum_other)
+    for clip in range(CLIPS_CORE):
+        span = slice(clip * ROWS, (clip + 1) * ROWS)
+        mask = valid_rows(counts_ref[clip], LANES)
+        grad = pre_grad(
+            slope_ref[span, :], pre_ref[span, :], mask, mean, scale, gain_ref[0:1, :], sums, pixels
+        )
+        scatter_taps(grad, columns_ref, clip * ROWS)
+    place_in = lax.broadcasted_iota(jnp.int32, (C1, C1), 0)
+    place_out = lax.broadcasted_iota(jnp.int32, (C1, C1), 1)
+    core_of = jnp.where(place_out < 128, core, 1 - core)
+    source_in = ((place_out // 64) % 2) * 128 + core_of * 64 + place_out % 64
+    spread = (place_in == source_in).astype(BF)
+    for tap in range(TAPS):
+        part = dot_tn(columns_ref[:, lanes_of(tap)], x_ref[...]).astype(BF)
+        both = dot_nn(part, spread)
+        for z_of in range(MB):
+            rows = slice(z_of * 32, (z_of + 1) * 32)
+            keep_ref[z_of, tap] = both[rows, 0:LANES].astype(BF)
+            send_ref[z_of, tap] = both[rows, LANES : 2 * LANES].astype(BF)
+
+
+def input_grad_kernel(columns_ref, weight_ref, a_keep, a_send, b_keep, b_send, partial):
+    x, y = lax.axis_index("x"), lax.axis_index("y")
+    weight = weight_ref[...].reshape(TAPS * LANES, C1)
+    for clip in range(CLIPS_CORE):
+        partial[clip] = dot_nn(columns_ref[clip * ROWS : (clip + 1) * ROWS, :], weight)
+    for z_of in range(MB):
+        for other in range(2):
+            keep_row = pl.multiple_of((z_of * 2 + x) * 64, 64)
+            send_row = pl.multiple_of((z_of * 2 + 1 - x) * 64, 64)
+            a_keep[other, z_of] = partial[other * CL_MB, pl.ds(keep_row, 64), :]
+            a_send[other, z_of] = partial[other * CL_MB, pl.ds(send_row, 64), :].astype(BF)
+            row = (z_of * 2 + other) * 64
+            b_keep[other, z_of] = partial[y * CL_MB + 1, row : row + 64, :]
+            b_send[other, z_of] = partial[(1 - y) * CL_MB + 1, row : row + 64, :].astype(BF)
+
+
+def pick(table, index):
+    return lax.dynamic_index_in_dim(table, index, 0, keepdims=False)
+
+
+def fast_body(
+    clip_input,
+    frame_counts,
+    clip_order,
+    cotangent,
+    kernel_one,
+    kernel_one_mean,
+    kernel_one_square,
+    kernel_two,
+    kernel_two_mean,
+    kernel_two_square,
+    norm_params,
+    norm_mean,
+    norm_square,
+):
+    z, x, y, core = (lax.axis_index(axis) for axis in AXES)
+    group = y * 2 + core
+    own_order = pick(clip_order, group)
+    pieces = call(
+        take_kernel,
+        [shape_of((CL_MB, 64, C1), BF)] * MB,
+        [SM, ANY],
+        [ANY] * MB,
+        [pltpu.SemaphoreType.DMA((MB * CL_MB,))],
+    )(own_order, clip_input.reshape(MB * CL_MB, 64, C1))
+    arrived = [pieces[0]] + [swap(pieces[step], "z", step) for step in range(1, MB)]
+
+    one_keep, one_send, two_keep, two_send = call(
+        weights_kernel,
+        [shape_of((TAPS, 32, 64), BF)] * 2 + [shape_of((TAPS, 32, 128), BF)] * 2,
+        [VM, VM],
+        [VM] * 4,
+        [pltpu.VMEM((64, 128), F32)],
+    )(kernel_one, kernel_two)
+    one_got, two_got = swap(one_send, "y"), swap(two_send, "y")
+    one_flat = jnp.where(
+        y == 0,
+        jnp.concatenate([one_keep, one_got], axis=2),
+        jnp.concatenate([one_got, one_keep], axis=2),
+    ).reshape(288, LANES)
+    low_gains = lax.dynamic_slice_in_dim(norm_params.astype(BF), y * 32, 32, 1).reshape(1, LANES)
+    one_flat = jnp.concatenate([one_flat, jnp.pad(low_gains, ((0, 15), (0, 0)))], axis=0)
+    one_all = jnp.stack([one_flat] + [swap(one_flat, "z", step) for step in range(1, MB)])
+    one_other = swap(one_all, "core")
+
+    hit = clip_order[:, :, None] == jnp.arange(MB * CL_MB, dtype=jnp.int32)
+    table = jnp.sum(hit * frame_counts.reshape(-1, 1, MB * CL_MB), axis=2)
+    plane = lax.dynamic_slice_in_dim(table.reshape(-1, MB, CL_MB), z, 1, 1)[:, 0]
+    pixels = (MEL * jnp.sum(plane)).astype(F32).reshape(1)
+    counts = lax.dynamic_slice_in_dim(plane.reshape(2, 2, CL_MB), core, 1, 1).reshape(CLIPS_CORE)
+
+    a0 = jnp.stack([piece[0] for piece in arrived])
+    b0 = jnp.stack([piece[1] for piece in arrived])
+    a1, b1 = swap(a0, "x"), swap(b0, "y")
+    a23, b23 = swap(jnp.concatenate([a0, a1]), "y"), swap(jnp.concatenate([b0, b1]), "x")
+
+    pre_one, masked, weight_one, stat_one = call(
+        first_conv_kernel,
+        [
+            shape_of((CLIPS_CORE * ROWS, LANES), F32),
+            shape_of((CLIPS_CORE * ROWS, C1), BF),
+            shape_of((TAPS, MB, 32, C1), BF),
+            shape_of((8, LANES), F32),
+        ],
+        [SM] + [ANY] * 6 + [VM, VM],
+        [VM] * 4,
+        [pltpu.VMEM((8, 128), F32), pltpu.SemaphoreType.DMA((8 * MB,))],
+    )(counts, a0, a1, a23, b0, b1, b23, one_all, one_other)
+    stat_one_other = swap(stat_one, "core")
+
+    gain_parts = one_all[:, 288, :].reshape(MB, 4, 32)
+    gain_rows = jnp.stack([pick(gain_parts, jnp.bitwise_xor(z, at)) for at in range(MB)], axis=1)
+    gains = gain_rows.reshape(4, LANES).astype(F32)
+
+    two_flat = jnp.stack([two_keep.reshape(288, LANES), two_got.reshape(288, LANES)])
+    two_all = jnp.stack([two_flat] + [swap(two_flat, "z", step) for step in range(1, MB)])
+    two_other = swap(two_all, "core")
+    weight_two = call(
+        second_weight_kernel,
+        shape_of((TAPS, MB, 32, C2), BF),
+        [ANY, ANY],
+        VM,
+        [pltpu.VMEM((MB, 4, 288, LANES), BF), pltpu.SemaphoreType.DMA((16,))],
+    )(two_all, two_other)
+
+    ha0, hb0 = call(
+        hidden_kernel,
+        [shape_of((2 * ROWS, LANES), BF)] * 2,
+        [SM, SM] + [VM] * 4,
+        [VM] * 2,
+    )(counts, pixels, pre_one, stat_one, stat_one_other, gains)
+    ha1, hb1 = swap(ha0, "x"), swap(hb0, "y")
+    ha23, hb23 = swap(jnp.stack([ha0, ha1]), "y"), swap(jnp.stack([hb0, hb1]), "x")
+    hidden_parts = (ha0, ha1, ha23, hb0, hb1, hb23)
+
+    cot_rows = jnp.take(cotangent, lax.dynamic_slice_in_dim(own_order, z * CL_MB, CL_MB, 0), axis=0)
+    cot_chips = cot_rows.reshape(CL_MB, MB, 2, 2, 32)
+    cot_x = lax.dynamic_index_in_dim(cot_chips, x, 2, keepdims=False)
+    cot_own = lax.dynamic_index_in_dim(cot_x, y, 2, keepdims=False).reshape(CL_MB, LANES)
+    cot_send = lax.dynamic_index_in_dim(cot_x, 1 - y, 2, keepdims=False).reshape(CL_MB, LANES)
+    cot_got = swap(cot_send, "y")
+    cots = jnp.where(
+        y == 0, jnp.concatenate([cot_own, cot_got]), jnp.concatenate([cot_got, cot_own])
+    )
+
+    pre_two, stat_two = call(
+        second_conv_kernel,
+        [shape_of((CLIPS_CORE * ROWS, LANES), F32), shape_of((8, LANES), F32)],
+        [SM] + [ANY] * 6 + [VM],
+        [VM] * 2,
+        [pltpu.VMEM((CLIPS_CORE * ROWS, C2), BF), pltpu.SemaphoreType.DMA((8,))],
+    )(counts, *hidden_parts, weight_two)
+    stat_two_other = swap(stat_two, "core")
+    slope_two, sum_two, pooled_own = call(
+        pool_kernel,
+        [
+            shape_of((CLIPS_CORE * ROWS, LANES), F32),
+            shape_of((8, LANES), F32),
+            shape_of((8, LANES), F32),
+        ],
+        [SM, SM] + [VM] * 5,
+        [VM] * 3,
+    )(counts, pixels, pre_two, stat_two, stat_two_other, gains, cots)
+    sum_two_other = swap(sum_two, "core")
+    grad_two, a_keep, a_send, b_keep, b_send = call(
+        hidden_grad_kernel,
+        [shape_of((CLIPS_CORE * ROWS, LANES), BF)]
+        + [shape_of((2, 2 * ROWS, LANES), F32), shape_of((2, 2 * ROWS, LANES), BF)] * 2,
+        [SM, SM] + [VM] * 8,
+        [VM] * 5,
+        [pltpu.VMEM((ROWS, TAPS * LANES), BF), pltpu.VMEM((ROWS, C2), F32)],
+    )(
+        counts,
+        pixels,
+        slope_two,
+        pre_two,
+        stat_two,
+        stat_two_other,
+        sum_two,
+        sum_two_other,
+        gains,
+        weight_two,
+    )
+    a_got, b_got = swap(a_send, "x"), swap(b_send, "y")
+    two_part, two_part_send = call(
+        second_weight_grad_kernel,
+        [shape_of((MB, 2, TAPS, 32, LANES), BF)] * 2,
+        [ANY] * 6 + [VM],
+        [VM] * 2,
+        [
+            pltpu.VMEM((CLIPS_CORE * ROWS, C2), BF),
+            pltpu.VMEM((CLIPS_CORE * ROWS, TAPS * LANES), BF),
+            pltpu.VMEM((LANES, C2), F32),
+            pltpu.SemaphoreType.DMA((8,)),
+        ],
+    )(*hidden_parts, grad_two)
+    a_mid, b_mid = a_keep + a_got.astype(F32), b_keep + b_got.astype(F32)
+    a_last = swap(pick(a_mid, 1 - y).astype(BF), "y")
+    b_last = swap(pick(b_mid, 1 - x).astype(BF), "x")
+    slope_one, sum_one = call(
+        first_slope_kernel,
+        [shape_of((CLIPS_CORE * ROWS, LANES), F32), shape_of((8, LANES), F32)],
+        [SM, SM] + [VM] * 8,
+        [VM] * 2,
+    )(
+        counts,
+        pixels,
+        pick(a_mid, y),
+        a_last,
+        pick(b_mid, x),
+        b_last,
+        pre_one,
+        stat_one,
+        stat_one_other,
+        gains,
+    )
+    sum_one_other = swap(sum_one, "core")
+    one_part, one_part_send, columns = call(
+        first_weight_grad_kernel,
+        [shape_of((MB, TAPS, 32, LANES), BF)] * 2
+        + [shape_of((CLIPS_CORE * ROWS, TAPS * LANES), BF)],
+        [SM, SM] + [VM] * 8,
+        [VM] * 3,
+    )(
+        counts,
+        pixels,
+        slope_one,
+        pre_one,
+        stat_one,
+        stat_one_other,
+        sum_one,
+        sum_one_other,
+        gains,
+        masked,
+    )
+
+    two_core = two_part.astype(F32) + swap(two_part_send, "core").astype(F32)
+    two_sum = pick(two_core, z)
+    for step in range(1, MB):
+        two_sum = two_sum + swap(
+            pick(two_core, jnp.bitwise_xor(z, step)).astype(BF), "z", step
+        ).astype(F32)
+
+    one_core = one_part.astype(F32) + swap(one_part_send, "core").astype(F32)
+    norm_rows_own = jnp.concatenate(
+        [
+            (sum_one + sum_one_other)[1:2],
+            (sum_one + sum_one_other)[0:1],
+            (sum_two + sum_two_other)[1:2],
+            (sum_two + sum_two_other)[0:1],
+        ]
+    )
+    norm_z = norm_rows_own.reshape(4, MB, 32).transpose(1, 0, 2).reshape(MB, 1, LANES)
+    norm_high = norm_z.astype(BF)
+    norm_low = (norm_z - norm_high.astype(F32)).astype(BF)
+    one_rows = jnp.concatenate(
+        [
+            one_core.reshape(MB, 288, LANES).astype(BF),
+            norm_high,
+            norm_low,
+            jnp.zeros((MB, 14, LANES), BF),
+        ],
+        axis=1,
+    )
+    one_sum = pick(one_core, z).reshape(288, LANES)
+    norm_sum = pick(norm_z, z)
+    for step in range(1, MB):
+        got = swap(pick(one_rows, jnp.bitwise_xor(z, step)), "z", step).astype(F32)
+        one_sum = one_sum + got[0:288]
+        norm_sum = norm_sum + got[288:289] + got[289:290]
+    own_squares = (
+        jnp.sum(one_sum * one_sum)
+        + jnp.sum(two_sum * two_sum)
+        + jnp.where(core == 0, jnp.sum(norm_sum * norm_sum), 0.0)
+    )
+    told = lax.all_to_all(
+        jnp.broadcast_to(own_squares, (32, LANES)), AXES, 0, 0, tiled=True
+    )
+    grad_norm = jnp.sqrt(jnp.sum(told[:, 0]))
+    factor = jnp.minimum(1.0, CLIP_NORM / (grad_norm + 1e-06))
+
+    two_shard_send = pick(two_sum, 1 - y)
+    two_shard_keep = pick(two_sum, y)
+    two_shard_got = swap(two_shard_send, "y")
+    one_cut = one_sum.reshape(TAPS, 32, LANES)
+    one_keep_sum = lax.dynamic_slice_in_dim(one_cut, y * 64, 64, 2)
+    one_send_sum = lax.dynamic_slice_in_dim(one_cut, (1 - y) * 64, 64, 2)
+    norm_keep = norm_sum.reshape(4, 32)
+    norm_got = swap(norm_keep, "y")
+    one_got_sum = swap(one_send_sum, "y")
+
+    def in_order(keep, got, axis):
+        return jnp.where(
+            y == 0, jnp.concatenate([keep, got], axis), jnp.concatenate([got, keep], axis)
+        )
+
+    grad_one_shard = jnp.swapaxes(in_order(one_keep_sum, one_got_sum, 1), 1, 2)
+    grad_two_shard = jnp.swapaxes(in_order(two_shard_keep, two_shard_got, 1), 1, 2)
+    norm_shard = in_order(norm_keep, norm_got, 1)
+
+    first_update = adam_step(
+        kernel_one, kernel_one_mean, kernel_one_square, grad_one_shard, factor, (9 * C1) ** (-0.5), WEIGHT_DECAY
+    )
+    second_update = adam_step(
+        kernel_two, kernel_two_mean, kernel_two_square, grad_two_shard, factor, (9 * C2) ** (-0.5), WEIGHT_DECAY
+    )
+    norm_update = adam_step(norm_params, norm_mean, norm_square, norm_shard, factor, GAIN_RATE, 0.0)
+
+    ia_keep, ia_send, ib_keep, ib_send = call(
+        input_grad_kernel,
+        [shape_of((2, MB, 64, C1), F32), shape_of((2, MB, 64, C1), BF)] * 2,
+        [VM, VM],
+        [VM] * 4,
+        [pltpu.VMEM((CLIPS_CORE, ROWS, C1), F32)],
+    )(columns, weight_one)
+    ia_mid = ia_keep + swap(ia_send, "x").astype(F32)
+    ib_mid = ib_keep + swap(ib_send, "y").astype(F32)
+    ia = pick(ia_mid, y) + swap(pick(ia_mid, 1 - y).astype(BF), "y").astype(F32)
+    ib = pick(ib_mid, x) + swap(pick(ib_mid, 1 - x).astype(BF), "x").astype(F32)
+    own_counts = pick(counts.reshape(2, CL_MB), y)
+    frame = (jnp.arange(MB) * 2 + x)[:, None] * 8 + jnp.arange(64)[None, :] // MEL
+    both = jnp.stack([ia, ib], axis=1)
+    masked_grad = jnp.where(
+        frame[:, None, :, None] < own_counts[None, :, None, None], both, 0.0
+    ).astype(BF)
+    final = [pick(masked_grad, z)] + [
+        swap(pick(masked_grad, jnp.bitwise_xor(z, step)), "z", step) for step in range(1, MB)
+    ]
+    stacked = jnp.stack(final)
+    ranks = jnp.argmax(own_order[None, :] == jnp.arange(MB * CL_MB)[:, None], axis=1)
+    source = jnp.bitwise_xor(ranks // CL_MB, z) * CL_MB + ranks % CL_MB
+    input_grad = jnp.take(stacked.reshape(MB * CL_MB, 8, MEL, C1), source, axis=0)
+
+    pooled_four = pooled_own[0:CLIPS_CORE].reshape(2, CL_MB, MB, 32)
+    pooled_got = swap(pick(pooled_four, 1 - y), "y")
+    pooled_y = jnp.stack(
+        [
+            jnp.where(y == 0, pick(pooled_four, y), pooled_got),
+            jnp.where(y == 0, pooled_got, pick(pooled_four, y)),
+        ],
+        axis=2,
+    )
+    pooled_x_got = swap(pooled_y, "x")
+    pooled_x = jnp.where(
+        x == 0,
+        jnp.stack([pooled_y, pooled_x_got], axis=2),
+        jnp.stack([pooled_x_got, pooled_y], axis=2),
+    ).reshape(CL_MB, C2)
+    pooled_all = jnp.stack([pooled_x] + [swap(pooled_x, "z", step) for step in range(1, MB)])
+    pooled = jnp.take(pooled_all.reshape(MB * CL_MB, C2), source, axis=0)
+    return (pooled, input_grad, grad_norm) + first_update + second_update + norm_update
+
+
 def solution(mesh):
-    in_specs = (
-        P("batch", "tm", None, None),
-        P(),
-        P(),
-        P("batch", None),
-        P(None, "batch", "tm"),
-        P(None, "batch", "tm"),
-        P(None, "batch", "tm"),
-        P(None, "batch", "tm"),
-        P(None, "batch", "tm"),
-        P(None, "batch", "tm"),
-        P(None, "tm"),
-        P(None, "tm"),
-        P(None, "tm"),
-    )
-    out_specs = (
-        P("batch", None),
-        P("batch", "tm", None, None),
-        P(),
-        P(None, "batch", "tm"),
-        P(None, "batch", "tm"),
-        P(None, "batch", "tm"),
-        P(None, "batch", "tm"),
-        P(None, "batch", "tm"),
-        P(None, "batch", "tm"),
-        P(None, "batch", "tm"),
-        P(None, "batch", "tm"),
-        P(None, "batch", "tm"),
-        P(None, "batch", "tm"),
-        P(None, "tm"),
-        P(None, "tm"),
-        P(None, "tm"),
-        P(None, "tm"),
-        P(None, "tm"),
-    )
-    return jax.shard_map(body, mesh=mesh, in_specs=in_specs, out_specs=out_specs, check_vma=False)
+    if mesh.shape["tm"] == 2 * MB and mesh.shape["batch"] == 4:
+        grid = Mesh(mesh.devices.reshape(MB, 2, 2, 2), AXES)
+        tm, batch, chosen = ("z", "x"), ("y", "core"), fast_body
+    else:
+        grid, tm, batch, chosen = mesh, "tm", "batch", general_body
+    kernels = (P(None, batch, tm),) * 3
+    norms = (P(None, tm),) * 3
+    in_specs = (P(batch, tm, None, None), P(), P(), P(batch, None)) + 2 * kernels + norms
+    out_specs = (P(batch, None), P(batch, tm, None, None), P())
+    out_specs = out_specs + (P(None, batch, tm),) * 10 + (P(None, tm),) * 5
+    return jax.shard_map(chosen, mesh=grid, in_specs=in_specs, out_specs=out_specs, check_vma=False)

time: 803 us -> 224 us (0.28)
  blocking collectives: 325 us -> 0 us
  waiting for transfers between devices: 156 us -> 45 us
  Pallas kernels: 0 us -> 66.8 us
  local copies, waits for them, and re-layouts: 82.4 us -> 20.9 us
  matrix products: 55.3 us -> 0 us
  starting transfers between devices: 99.5 us -> 64.7 us
  other arithmetic: 53.6 us -> 19.5 us
  between operations: 22.6 us -> 6.04 us
    psum x7 -> x0, blocking collectives: 255 us -> none  [the longest x2 80.6 us: norm_forward(): lax.psum((jnp.sum(masked, axis=(0, 1, 2)), jnp.sum(masked * pre_norm, axi...]
    reduce_scatter x3 -> x0, waiting for transfers between devices: 100 us -> none  [the longest x1 70.6 us: body(): lax.psum_scatter(batch_parts[1], 'tm', scatter_dimension=2, tiled=True)]
    all_gather x2 -> x0, blocking collectives: 70.7 us -> none  [the longest x1 52.6 us: body(): lax.all_gather(low_one, 'tm', axis=2, tiled=True)]
    pallas_call x0 -> x12, Pallas kernels: none -> 66.8 us  [the longest x1 9.79 us: fast_body(): call(take_kernel, [shape_of((CL_MB, 64, C1), BF)] * MB, [SM, ANY], [ANY]...]
    dot_general x24 -> x0, matrix products: 55.3 us -> none  [the longest x8 33.1 us: contract_rows(): lax.dot_general(columns, grads, (((0,), (0,)), ((), ())), preferred_eleme...]
    unnamed x8 -> x0, waiting for transfers between devices: 47.8 us -> none
    ppermute x32 -> x53, starting transfers between devices: 98.7 us -> 61.3 us  [swap(): return lax.ppermute(value, axis, [(i, i ^ step) for i in range(size)])]
    ppermute x32 -> x53, waiting for transfers between devices: 8.1 us -> 45 us  [swap(): return lax.ppermute(value, axis, [(i, i ^ step) for i in range(size)])]
  transfers between devices with their start and end apart: 39 -> 54, of which waited for: 5 -> 18; matrix products, arithmetic and copies ran while one was open for 18% -> 13% of each run, Pallas kernels for 0% -> 26%
where the time goes in v1:
time: 224 us; the launch traced here: 223 us
  Pallas kernels  66.8 us (30%)
  starting transfers between devices  64.7 us (29%)
  waiting for transfers between devices  45 us (20%)
  local copies, waits for them, and re-layouts  20.9 us (9%)
  other arithmetic  19.5 us (9%)
  between operations  6.04 us (3%)
    ppermute x53, starting transfers between devices, swap(): return lax.ppermute(value, axis, [(i, i ^ step) for i in range(size)])  61.3 us
    ppermute x53, waiting for transfers between devices, swap(): return lax.ppermute(value, axis, [(i, i ^ step) for i in range(size)])  45 us
    unnamed x91, local copies, waits for them, and re-layouts  10.4 us
    pallas_call x1, Pallas kernels, fast_body(): call(take_kernel, [shape_of((CL_MB, 64, C1), BF)] * MB, [SM, ANY], [ANY]...  9.79 us
    pallas_call x1, Pallas kernels, fast_body(): call(second_weight_grad_kernel, [shape_of((MB, 2, TAPS, 32, LANES), BF)]...  8.81 us
    pallas_call x1, Pallas kernels, fast_body(): call(first_weight_grad_kernel, [shape_of((MB, TAPS, 32, LANES), BF)] * 2...  8.48 us
    pallas_call x1, Pallas kernels, fast_body(): call(hidden_grad_kernel, [shape_of((CLIPS_CORE * ROWS, LANES), BF)] + [sh...  7.16 us
    pallas_call x1, Pallas kernels, fast_body(): call(second_conv_kernel, [shape_of((CLIPS_CORE * ROWS, LANES), F32), shap...  6.76 us
  transfers between devices with their start and end apart: 54, of which 18 were waited for; matrix products, arithmetic and copies ran while one was open for 13% of the time, Pallas kernels for 26%

profile of v1, /device:TPU:0, one launch (start us, length us, event | category | flops | bytes accessed | tf_op | source)
XLA Modules:
  0.0 222.9 jit_solution(13168456036194184064)
XLA Ops:
  0.7 2.1 copy.75.two_ref
  2.8 2.2 %shard_map.269 = (bf16[9,32,64]{2,1,0:T(8,128)(2,1)}, bf16[9,32,64]{2,1,0:T(8,128)(2,1)}, bf16[9,32,128]{2,1,0:T(8,128)(2,1)}, bf16[9,32,128]{2,1,0:T(8,128)(2,1)}) custom-call(f32[9,64,64]{2,1,0:T(8,128)} %one_ref.1, f32[9,128,64]{2,1,0:T(8,128)} %copy.75.two_ref), custom_call_target="tpu_custom_call" | custom-call | tf_op jit(solution)/shard_map/pallas_call | solution.py:761
  5.0 3.0 %collective-permute-start.7 = (bf16[9,32,64]{2,1,0:T(8,128)(2,1)}, bf16[9,32,64]{2,1,0:T(8,128)(2,1)S(1)}, u32[]{:S(2)}, u32[]{:S(2)}) collective-permute-start(bf16[9,32,64]{2,1,0:T(8,128)(2,1)} %get-tuple-element.60), channel_id=1, source_target_pairs={{0,2},{2,0},{1,3},{3,1},{4,6},{6,4},{5,7},{7,5},{8,10},{10,8},{9,1... | collective-permute-start | bytes 110600 | tf_op jit(solution)/shard_map/ppermute | solution.py:292
  8.5 9.8 %shard_map.268 = (bf16[2,64,256]{2,1,0:T(8,128)(2,1)}, bf16[2,64,256]{2,1,0:T(8,128)(2,1)}, bf16[2,64,256]{2,1,0:T(8,128)(2,1)}, bf16[2,64,256]{2,1,0:T(8,128)(2,1)}) custom-call(s32[8]{0:T(128)} %fusion.33.ids_ref, bf16[8,64,256]{2,1,0:T(8,128)(2,1)} %bitcast.150), custom_call_target="tpu_custom_call" | custom-call | tf_op jit(solution)/shard_map/pallas_call | solution.py:752
  19.9 2.6 %collective-permute-start.1 = (bf16[2,64,256]{2,1,0:T(8,128)(2,1)}, bf16[2,64,256]{2,1,0:T(8,128)(2,1)S(1)}, u32[]{:S(2)}, u32[]{:S(2)}) collective-permute-start(bf16[2,64,256]{2,1,0:T(8,128)(2,1)} %get-tuple-element.57), channel_id=1, source_target_pairs={{0,16},{8,24},{16,0},{24,8},{1,17},{9,25},{17,1},{25,9},{2,18},{10... | collective-permute-start | bytes 196616 | tf_op jit(solution)/shard_map/ppermute | solution.py:292
  30.0 3.5 %collective-permute-start.9 = (bf16[304,128]{1,0:T(8,128)(2,1)S(1)}, bf16[304,128]{1,0:T(8,128)(2,1)S(1)}, u32[]{:S(2)}, u32[]{:S(2)}) collective-permute-start(bf16[304,128]{1,0:T(8,128)(2,1)S(1)} %get-tuple-element.134), channel_id=1, source_target_pairs={{0,16},{8,24},{16,0},{24,8},{1,17},{9,25},{17,1},{25,9},{2,18},{10... | collective-permute-start | bytes 233480 | tf_op jit(solution)/shard_map/ppermute | solution.py:292
  37.5 2.2 %collective-permute-done.10 = bf16[304,128]{1,0:T(8,128)(2,1)S(1)} collective-permute-done((bf16[304,128]{1,0:T(8,128)(2,1)S(1)}, bf16[304,128]{1,0:T(8,128)(2,1)S(1)}, u32[]{:S(2)}, u32[]{:S(2)}) %collective-permute-start.10) | collective-permute-done | bytes 77856 | tf_op jit(solution)/shard_map/ppermute | solution.py:292
  43.2 3.1 %collective-permute-start.19 = (bf16[2,288,128]{2,1,0:T(8,128)(2,1)S(1)}, bf16[2,288,128]{2,1,0:T(8,128)(2,1)S(1)}, u32[]{:S(2)}, u32[]{:S(2)}) collective-permute-start(bf16[2,288,128]{2,1,0:T(8,128)(2,1)S(1)} %get-tuple-element.132), channel_id=1, source_target_pairs={{0,16},{8,24},{16,0},{24,8},{1,17},{9,25},{17,1},{25,9},{2,18},{10... | collective-permute-start | bytes 442376 | tf_op jit(solution)/shard_map/ppermute | solution.py:292
  50.7 5.4 %shard_map.270 = (f32[2048,128]{1,0:T(8,128)}, bf16[2048,256]{1,0:T(8,128)(2,1)}, bf16[9,4,32,256]{3,2,1,0:T(8,128)(2,1)}, f32[8,128]{1,0:T(8,128)}) custom-call(s32[4]{0:T(128)} %reshape.301.counts_ref, bf16[4,64,256]{2,1,0:T(8,128)(2,1)} %copy-done.17, bf16[4,64,256]{2,1,0:T(8,128)(2,1)} %copy-done.18, bf16[8,64,256]{2,1,0:T(8,128)(2,1)} %copy-done.27, ...), custom_call_target="tpu_custom_call" | custom-call | tf_op jit(solution)/shard_map/pallas_call | solution.py:790
  58.1 2.3 %shard_map.271 = (bf16[1024,128]{1,0:T(8,128)(2,1)}, bf16[1024,128]{1,0:T(8,128)(2,1)}) custom-call(s32[4]{0:T(128)} %reshape.301.counts_ref, f32[1]{0:T(128)} %bitcast.2.pixels_ref, f32[2048,128]{1,0:T(8,128)} %get-tuple-element.61.pre_ref, f32[8,128]{1,0:T(8,128)} %get-tuple-element.62.own_ref, f32[8,128]{1,0:T(8,128)} %copy-done.31, ...), custom_call_target="tpu_custom_call" | custom-call | tf_op jit(solution)/shard_map/pallas_call | solution.py:819
  63.8 5.3 %collective-permute-done.15.b1 = bf16[1024,128]{1,0:T(8,128)(2,1)S(1)} collective-permute-done((bf16[1024,128]{1,0:T(8,128)(2,1)}, bf16[1024,128]{1,0:T(8,128)(2,1)S(1)}, u32[]{:S(2)}, u32[]{:S(2)}) %collective-permute-start.15) | collective-permute-done | bytes 262176 | tf_op jit(solution)/shard_map/ppermute | solution.py:292
  74.3 3.3 %shard_map.272.weight_ref = bf16[9,4,32,512]{3,2,1,0:T(8,128)(2,1)} custom-call(bf16[4,2,288,128]{3,2,1,0:T(8,128)(2,1)} %copy-done.1, bf16[4,2,288,128]{3,2,1,0:T(8,128)(2,1)} %copy-done.14), custom_call_target="tpu_custom_call" | custom-call | tf_op jit(solution)/shard_map/pallas_call | solution.py:811
  77.7 4.7 %collective-permute-done.16.b23 = bf16[2,1024,128]{2,1,0:T(8,128)(2,1)S(1)} collective-permute-done((bf16[2,1024,128]{2,1,0:T(8,128)(2,1)S(1)}, bf16[2,1024,128]{2,1,0:T(8,128)(2,1)S(1)}, u32[]{:S(2)}, u32[]{:S(2)}) %collective-permute-start.16) | collective-permute-done | bytes 524320 | tf_op jit(solution)/shard_map/ppermute | solution.py:292
  85.1 6.8 %shard_map.273 = (f32[2048,128]{1,0:T(8,128)}, f32[8,128]{1,0:T(8,128)}) custom-call(s32[4]{0:T(128)} %reshape.301.counts_ref, bf16[1024,128]{1,0:T(8,128)(2,1)} %get-tuple-element.63.a0, bf16[1024,128]{1,0:T(8,128)(2,1)} %copy-done.5, bf16[2,1024,128]{2,1,0:T(8,128)(2,1)} %copy-done.7, bf16[1024,128]{1,0:T(8,128)(2,1)} %get-tuple-element.64.b0, ...), custom_call_target="tpu_custom_call" | custom-call | tf_op jit(solution)/shard_map/pallas_call | solution.py:839
  93.9 3.4 %shard_map.274 = (f32[2048,128]{1,0:T(8,128)}, f32[8,128]{1,0:T(8,128)}, f32[8,128]{1,0:T(8,128)}) custom-call(s32[4]{0:T(128)} %reshape.301.counts_ref, f32[1]{0:T(128)} %bitcast.2.pixels_ref, f32[2048,128]{1,0:T(8,128)} %get-tuple-element.67.pre_ref, f32[8,128]{1,0:T(8,128)} %get-tuple-element.68.own_ref, f32[8,128]{1,0:T(8,128)} %copy-done.32, ...), custom_call_target="tpu_custom_call" | custom-call | tf_op jit(solution)/shard_map/pallas_call | solution.py:847
  99.7 2.1 collective-permute-done.24
  102.9 2.5 %collective-permute-done.25 = f32[2,4,2,32]{3,2,1,0:T(2,128)S(1)} collective-permute-done((f32[2,4,2,32]{3,2,1,0:T(2,128)S(1)}, f32[2,4,2,32]{3,2,1,0:T(2,128)S(1)}, u32[]{:S(2)}, u32[]{:S(2)}) %collective-permute-start.25) | collective-permute-done | bytes 2080 | tf_op jit(solution)/shard_map/ppermute | solution.py:292
  107.2 2.8 %collective-permute-start.28 = (f32[2,512]{1,0:T(2,128)S(1)}, f32[2,512]{1,0:T(2,128)S(1)}, u32[]{:S(2)}, u32[]{:S(2)}) collective-permute-start(f32[2,512]{1,0:T(2,128)S(1)} %select_n.271), channel_id=1, source_target_pairs={{0,24},{8,16},{16,8},{24,0},{1,25},{9,17},{17,9},{25,1},{2,26},{10... | collective-permute-start | bytes 12296 | tf_op jit(solution)/shard_map/ppermute | solution.py:292
  110.7 7.2 %shard_map.275 = (bf16[2048,128]{1,0:T(8,128)(2,1)}, f32[2,1024,128]{2,1,0:T(8,128)}, bf16[2,1024,128]{2,1,0:T(8,128)(2,1)}, f32[2,1024,128]{2,1,0:T(8,128)}, bf16[2,1024,128]{2,1,0:T(8,128)(2,1)}) custom-call(s32[4]{0:T(128)} %reshape.301.counts_ref, f32[1]{0:T(128)} %bitcast.2.pixels_ref, f32[2048,128]{1,0:T(8,128)} %get-tuple-element.70.slope_ref, ...), custom_call_target="tpu_custom_call" | custom-call | tf_op jit(solution)/shard_map/pallas_call | solution.py:858
  121.0 8.8 %shard_map.279 = (bf16[4,2,9,32,128]{4,3,2,1,0:T(8,128)(2,1)}, bf16[4,2,9,32,128]{4,3,2,1,0:T(8,128)(2,1)}) custom-call(bf16[1024,128]{1,0:T(8,128)(2,1)} %get-tuple-element.63.a0, bf16[1024,128]{1,0:T(8,128)(2,1)} %copy-done.5, bf16[2,1024,128]{2,1,0:T(8,128)(2,1)} %copy-done.7, bf16[1024,128]{1,0:T(8,128)(2,1)} %get-tuple-element.64.b0, ...), custom_call_target="tpu_custom_call" | custom-call | tf_op jit(solution)/shard_map/pallas_call | solution.py:878
  136.1 2.8 %collective-permute-start.49 = (bf16[2,9,32,128]{3,2,1,0:T(8,128)(2,1)S(1)}, bf16[2,9,32,128]{3,2,1,0:T(8,128)(2,1)S(1)}, u32[]{:S(2)}, u32[]{:S(2)}) collective-permute-start(bf16[2,9,32,128]{3,2,1,0:T(8,128)(2,1)S(1)} %get-tuple-element.116), channel_id=1, source_target_pairs={{0,24},{8,16},{16,8},{24,0},{1,25},{9,17},{17,9},{25,1},{2,26},{10... | collective-permute-start | bytes 442376 | tf_op jit(solution)/shard_map/ppermute | solution.py:292
  142.2 6.4 %collective-permute-done.48 = bf16[2,9,32,128]{3,2,1,0:T(8,128)(2,1)S(1)} collective-permute-done((bf16[2,9,32,128]{3,2,1,0:T(8,128)(2,1)S(1)}, bf16[2,9,32,128]{3,2,1,0:T(8,128)(2,1)S(1)}, u32[]{:S(2)}, u32[]{:S(2)}) %collective-permute-start.48) | collective-permute-done | bytes 147488 | tf_op jit(solution)/shard_map/ppermute | solution.py:292
  150.6 3.4 %shard_map.276 = (f32[2048,128]{1,0:T(8,128)}, f32[8,128]{1,0:T(8,128)}) custom-call(s32[4]{0:T(128)} %reshape.301.counts_ref, f32[1]{0:T(128)} %bitcast.2.pixels_ref, f32[1024,128]{1,0:T(8,128)} %dynamic-slice_bitcast_fusion.1.a_keep, bf16[1024,128]{1,0:T(8,128)(2,1)} %copy-done.29, f32[1024,128]{1,0:T(8,128)} %dynamic-slice_bitcast_fusion.b_keep, ...), custom_call_target="tpu_custom_call" | custom-call | tf_op jit(solution)/shard_map/pallas_call | solution.py:893
  156.0 8.5 %shard_map.277 = (bf16[4,9,32,128]{3,2,1,0:T(8,128)(2,1)}, bf16[4,9,32,128]{3,2,1,0:T(8,128)(2,1)}, bf16[2048,1152]{1,0:T(8,128)(2,1)}) custom-call(s32[4]{0:T(128)} %reshape.301.counts_ref, f32[1]{0:T(128)} %bitcast.2.pixels_ref, f32[2048,128]{1,0:T(8,128)} %get-tuple-element.76.slope_ref, f32[2048,128]{1,0:T(8,128)} %get-tuple-element.61.pre_ref, ...), custom_call_target="tpu_custom_call" | custom-call | tf_op jit(solution)/shard_map/pallas_call | solution.py:911
  165.4 5.6 %shard_map.278 = (f32[2,4,64,256]{3,2,1,0:T(8,128)}, bf16[2,4,64,256]{3,2,1,0:T(8,128)(2,1)}, f32[2,4,64,256]{3,2,1,0:T(8,128)}, bf16[2,4,64,256]{3,2,1,0:T(8,128)(2,1)}) custom-call(bf16[2048,1152]{1,0:T(8,128)(2,1)} %get-tuple-element.79.columns_ref, bf16[9,4,32,256]{3,2,1,0:T(8,128)(2,1)} %get-tuple-element.80.weight_ref), custom_call_target="tpu_custom_call" | custom-call | tf_op jit(solution)/shard_map/pallas_call | solution.py:1002
  173.3 6.5 %collective-permute-done.35 = bf16[2,4,64,256]{3,2,1,0:T(8,128)(2,1)S(1)} collective-permute-done((bf16[2,4,64,256]{3,2,1,0:T(8,128)(2,1)}, bf16[2,4,64,256]{3,2,1,0:T(8,128)(2,1)S(1)}, u32[]{:S(2)}, u32[]{:S(2)}) %collective-permute-start.35) | collective-permute-done | bytes 262176 | tf_op jit(solution)/shard_map/ppermute | solution.py:292
  183.4 3.1 %collective-permute-start.43 = (bf16[304,128]{1,0:T(8,128)(2,1)S(1)}, bf16[304,128]{1,0:T(8,128)(2,1)S(1)}, u32[]{:S(2)}, u32[]{:S(2)}) collective-permute-start(bf16[304,128]{1,0:T(8,128)(2,1)S(1)} %get-tuple-element.120), channel_id=1, source_target_pairs={{0,8},{8,0},{16,24},{24,16},{1,9},{9,1},{17,25},{25,17},{2,10},{10... | collective-permute-start | bytes 233480 | tf_op jit(solution)/shard_map/ppermute | solution.py:292
  186.4 2.4 %collective-permute-start.45 = (bf16[304,128]{1,0:T(8,128)(2,1)S(1)}, bf16[304,128]{1,0:T(8,128)(2,1)S(1)}, u32[]{:S(2)}, u32[]{:S(2)}) collective-permute-start(bf16[304,128]{1,0:T(8,128)(2,1)S(1)} %get-tuple-element.121), channel_id=1, source_target_pairs={{0,24},{8,16},{16,8},{24,0},{1,25},{9,17},{17,9},{25,1},{2,26},{10... | collective-permute-start | bytes 233480 | tf_op jit(solution)/shard_map/ppermute | solution.py:292
  190.2 4.3 %collective-permute-done.44 = bf16[304,128]{1,0:T(8,128)(2,1)S(1)} collective-permute-done((bf16[304,128]{1,0:T(8,128)(2,1)S(1)}, bf16[304,128]{1,0:T(8,128)(2,1)S(1)}, u32[]{:S(2)}, u32[]{:S(2)}) %collective-permute-start.44) | collective-permute-done | bytes 77856 | tf_op jit(solution)/shard_map/ppermute | solution.py:292
  199.5 3.4 %all-to-all-start = ((f32[32,1,128]{2,1,0:T(1,128)}), f32[32,1,128]{2,1,0:T(1,128)S(1)}, u32[]{:S(2)}, u32[]{:S(2)}) async-start(f32[32,1,128]{2,1,0:T(1,128)} %broadcast_in_dim.68), calls=%async_computation | async-start | bytes 32768 | tf_op jit(solution)/shard_map/all_to_all | solution.py:969
  209.6 2.4 %collective-permute-start.40 = (bf16[2,64,256]{2,1,0:T(8,128)(2,1)S(1)}, bf16[2,64,256]{2,1,0:T(8,128)(2,1)}, u32[]{:S(2)}, u32[]{:S(2)}) collective-permute-start(bf16[2,64,256]{2,1,0:T(8,128)(2,1)S(1)} %get-tuple-element.127), channel_id=1, source_target_pairs={{0,16},{8,24},{16,0},{24,8},{1,17},{9,25},{17,1},{25,9},{2,18},{10... | collective-permute-start | bytes 196616 | tf_op jit(solution)/shard_map/ppermute | solution.py:292
  217.0 2.5 %collective-permute-done.41 = bf16[2,64,256]{2,1,0:T(8,128)(2,1)S(1)} collective-permute-done((bf16[2,64,256]{2,1,0:T(8,128)(2,1)S(1)}, bf16[2,64,256]{2,1,0:T(8,128)(2,1)S(1)}, u32[]{:S(2)}, u32[]{:S(2)}) %collective-permute-start.41) | collective-permute-done | bytes 65568 | tf_op jit(solution)/shard_map/ppermute | solution.py:292
  (288 shorter events, 82.5 us)
Async XLA Ops:
  5.0 22.9 %collective-permute-start.7 = (bf16[9,32,64]{2,1,0:T(8,128)(2,1)}, bf16[9,32,64]{2,1,0:T(8,128)(2,1)S(1)}, u32[]{:S(2)}, u32[]{:S(2)}) collective-permute-start(bf16[9,32,64]{2,1,0:T(8,128)(2,1)} %get-tuple-element.60), channel_id=1, source_target_pairs={{0,2},{2,0},{1,3},{3,1},{4,6},{6,4},{5,7},{7,5},{8,10},{10,8},{9,1... | collective-permute-start | bytes 110600 | tf_op jit(solution)/shard_map/ppermute | solution.py:292
  18.3 11.7 %collective-permute-start = (bf16[2,64,256]{2,1,0:T(8,128)(2,1)}, bf16[2,64,256]{2,1,0:T(8,128)(2,1)S(1)}, u32[]{:S(2)}, u32[]{:S(2)}) collective-permute-start(bf16[2,64,256]{2,1,0:T(8,128)(2,1)} %get-tuple-element.56), channel_id=1, source_target_pairs={{0,8},{8,0},{16,24},{24,16},{1,9},{9,1},{17,25},{25,17},{2,10},{10... | collective-permute-start | bytes 196616 | tf_op jit(solution)/shard_map/ppermute | solution.py:292
  19.9 13.6 %collective-permute-start.1 = (bf16[2,64,256]{2,1,0:T(8,128)(2,1)}, bf16[2,64,256]{2,1,0:T(8,128)(2,1)S(1)}, u32[]{:S(2)}, u32[]{:S(2)}) collective-permute-start(bf16[2,64,256]{2,1,0:T(8,128)(2,1)} %get-tuple-element.57), channel_id=1, source_target_pairs={{0,16},{8,24},{16,0},{24,8},{1,17},{9,25},{17,1},{25,9},{2,18},{10... | collective-permute-start | bytes 196616 | tf_op jit(solution)/shard_map/ppermute | solution.py:292
  22.5 11.1 %collective-permute-start.2 = (bf16[2,64,256]{2,1,0:T(8,128)(2,1)}, bf16[2,64,256]{2,1,0:T(8,128)(2,1)S(1)}, u32[]{:S(2)}, u32[]{:S(2)}) collective-permute-start(bf16[2,64,256]{2,1,0:T(8,128)(2,1)} %get-tuple-element.58), channel_id=1, source_target_pairs={{0,24},{8,16},{16,8},{24,0},{1,25},{9,17},{17,9},{25,1},{2,26},{10... | collective-permute-start | bytes 196616 | tf_op jit(solution)/shard_map/ppermute | solution.py:292
  22.7 20.4 %collective-permute-start.17 = (bf16[9,32,128]{2,1,0:T(8,128)(2,1)}, bf16[9,32,128]{2,1,0:T(8,128)(2,1)S(1)}, u32[]{:S(2)}, u32[]{:S(2)}) collective-permute-start(bf16[9,32,128]{2,1,0:T(8,128)(2,1)} %get-tuple-element.66), channel_id=1, source_target_pairs={{0,2},{2,0},{1,3},{3,1},{4,6},{6,4},{5,7},{7,5},{8,10},{10,8},{9,1... | collective-permute-start | bytes 221192 | tf_op jit(solution)/shard_map/ppermute | solution.py:292
  39.9 8.8 %collective-permute-start.6 = (bf16[8,64,256]{2,1,0:T(8,128)(2,1)S(1)}, bf16[8,64,256]{2,1,0:T(8,128)(2,1)S(1)}, u32[]{:S(2)}, u32[]{:S(2)}) collective-permute-start(bf16[8,64,256]{2,1,0:T(8,128)(2,1)S(1)} %constant_dynamic-update-slice_fusion.5), channel_id=1, source_target_pairs={{0,4},{4,0},{1,5},{5,1},{2,6},{6,2},{3,7},{7,3},{8,12},{12,8},{9,1... | collective-permute-start | bytes 786440 | tf_op jit(solution)/shard_map/ppermute | solution.py:292
  43.1 20.5 %collective-permute-start.18 = (bf16[2,288,128]{2,1,0:T(8,128)(2,1)S(1)}, bf16[2,288,128]{2,1,0:T(8,128)(2,1)S(1)}, u32[]{:S(2)}, u32[]{:S(2)}) collective-permute-start(bf16[2,288,128]{2,1,0:T(8,128)(2,1)S(1)} %get-tuple-element.132), channel_id=1, source_target_pairs={{0,8},{8,0},{16,24},{24,16},{1,9},{9,1},{17,25},{25,17},{2,10},{10... | collective-permute-start | bytes 442376 | tf_op jit(solution)/shard_map/ppermute | solution.py:292
  43.2 20.4 %collective-permute-start.19 = (bf16[2,288,128]{2,1,0:T(8,128)(2,1)S(1)}, bf16[2,288,128]{2,1,0:T(8,128)(2,1)S(1)}, u32[]{:S(2)}, u32[]{:S(2)}) collective-permute-start(bf16[2,288,128]{2,1,0:T(8,128)(2,1)S(1)} %get-tuple-element.132), channel_id=1, source_target_pairs={{0,16},{8,24},{16,0},{24,8},{1,17},{9,25},{17,1},{25,9},{2,18},{10... | collective-permute-start | bytes 442376 | tf_op jit(solution)/shard_map/ppermute | solution.py:292
  46.5 17.2 %collective-permute-start.20 = (bf16[2,288,128]{2,1,0:T(8,128)(2,1)S(1)}, bf16[2,288,128]{2,1,0:T(8,128)(2,1)S(1)}, u32[]{:S(2)}, u32[]{:S(2)}) collective-permute-start(bf16[2,288,128]{2,1,0:T(8,128)(2,1)S(1)} %get-tuple-element.132), channel_id=1, source_target_pairs={{0,24},{8,16},{16,8},{24,0},{1,25},{9,17},{17,9},{25,1},{2,26},{10... | collective-permute-start | bytes 442376 | tf_op jit(solution)/shard_map/ppermute | solution.py:292
  63.8 9.8 %collective-permute-start.21 = (bf16[4,2,288,128]{3,2,1,0:T(8,128)(2,1)S(1)}, bf16[4,2,288,128]{3,2,1,0:T(8,128)(2,1)S(1)}, u32[]{:S(2)}, u32[]{:S(2)}) collective-permute-start(bf16[4,2,288,128]{3,2,1,0:T(8,128)(2,1)S(1)} %pad_maximum_fusion.own_ref), channel_id=1, source_target_pairs={{0,1},{1,0},{2,3},{3,2},{4,5},{5,4},{6,7},{7,6},{8,9},{9,8},{10,11... | collective-permute-start | bytes 1769480 | tf_op jit(solution)/shard_map/ppermute | solution.py:292
  69.1 13.2 %collective-permute-start.16 = (bf16[2,1024,128]{2,1,0:T(8,128)(2,1)S(1)}, bf16[2,1024,128]{2,1,0:T(8,128)(2,1)S(1)}, u32[]{:S(2)}, u32[]{:S(2)}) collective-permute-start(bf16[2,1024,128]{2,1,0:T(8,128)(2,1)S(1)} %pad_maximum_fusion.2), channel_id=1, source_target_pairs={{0,4},{4,0},{1,5},{5,1},{2,6},{6,2},{3,7},{7,3},{8,12},{12,8},{9,1... | collective-permute-start | bytes 1572872 | tf_op jit(solution)/shard_map/ppermute | solution.py:292
  71.2 13.1 %collective-permute-start.14 = (bf16[2,1024,128]{2,1,0:T(8,128)(2,1)}, bf16[2,1024,128]{2,1,0:T(8,128)(2,1)S(1)}, u32[]{:S(2)}, u32[]{:S(2)}) collective-permute-start(bf16[2,1024,128]{2,1,0:T(8,128)(2,1)} %pad_maximum_fusion.1), channel_id=1, source_target_pairs={{0,2},{2,0},{1,3},{3,1},{4,6},{6,4},{5,7},{7,5},{8,10},{10,8},{9,1... | collective-permute-start | bytes 1572872 | tf_op jit(solution)/shard_map/ppermute | solution.py:292
  72.6 19.3 %collective-permute-start.23 = (f32[2,128]{1,0:T(2,128)S(1)}, f32[2,128]{1,0:T(2,128)S(1)}, u32[]{:S(2)}, u32[]{:S(2)}) collective-permute-start(f32[2,128]{1,0:T(2,128)S(1)} %reshape.306), channel_id=1, source_target_pairs={{0,2},{2,0},{1,3},{3,1},{4,6},{6,4},{5,7},{7,5},{8,10},{10,8},{9,1... | collective-permute-start | bytes 3080 | tf_op jit(solution)/shard_map/ppermute | solution.py:292
  105.6 24.3 %collective-permute-start.26 = (f32[2,512]{1,0:T(2,128)S(1)}, f32[2,512]{1,0:T(2,128)S(1)}, u32[]{:S(2)}, u32[]{:S(2)}) collective-permute-start(f32[2,512]{1,0:T(2,128)S(1)} %select_n.271), channel_id=1, source_target_pairs={{0,8},{8,0},{16,24},{24,16},{1,9},{9,1},{17,25},{25,17},{2,10},{10... | collective-permute-start | bytes 12296 | tf_op jit(solution)/shard_map/ppermute | solution.py:292
  105.6 24.3 %collective-permute-start.27 = (f32[2,512]{1,0:T(2,128)S(1)}, f32[2,512]{1,0:T(2,128)S(1)}, u32[]{:S(2)}, u32[]{:S(2)}) collective-permute-start(f32[2,512]{1,0:T(2,128)S(1)} %select_n.271), channel_id=1, source_target_pairs={{0,16},{8,24},{16,0},{24,8},{1,17},{9,25},{17,1},{25,9},{2,18},{10... | collective-permute-start | bytes 12296 | tf_op jit(solution)/shard_map/ppermute | solution.py:292
  107.2 22.7 %collective-permute-start.28 = (f32[2,512]{1,0:T(2,128)S(1)}, f32[2,512]{1,0:T(2,128)S(1)}, u32[]{:S(2)}, u32[]{:S(2)}) collective-permute-start(f32[2,512]{1,0:T(2,128)S(1)} %select_n.271), channel_id=1, source_target_pairs={{0,24},{8,16},{16,8},{24,0},{1,25},{9,17},{17,9},{25,1},{2,26},{10... | collective-permute-start | bytes 12296 | tf_op jit(solution)/shard_map/ppermute | solution.py:292
  117.8 13.4 %collective-permute-start.32 = (bf16[2,1024,128]{2,1,0:T(8,128)(2,1)}, bf16[2,1024,128]{2,1,0:T(8,128)(2,1)S(1)}, u32[]{:S(2)}, u32[]{:S(2)}) collective-permute-start(bf16[2,1024,128]{2,1,0:T(8,128)(2,1)} %get-tuple-element.75), channel_id=1, source_target_pairs={{0,2},{2,0},{1,3},{3,1},{4,6},{6,4},{5,7},{7,5},{8,10},{10,8},{9,1... | collective-permute-start | bytes 1572872 | tf_op jit(solution)/shard_map/ppermute | solution.py:292
  119.1 14.0 %collective-permute-start.30 = (bf16[2,1024,128]{2,1,0:T(8,128)(2,1)}, bf16[2,1024,128]{2,1,0:T(8,128)(2,1)S(1)}, u32[]{:S(2)}, u32[]{:S(2)}) collective-permute-start(bf16[2,1024,128]{2,1,0:T(8,128)(2,1)} %get-tuple-element.73), channel_id=1, source_target_pairs={{0,4},{4,0},{1,5},{5,1},{2,6},{6,2},{3,7},{7,3},{8,12},{12,8},{9,1... | collective-permute-start | bytes 1572872 | tf_op jit(solution)/shard_map/ppermute | solution.py:292
  131.4 17.8 %collective-permute-start.33 = (bf16[1024,128]{1,0:T(8,128)(2,1)S(1)}, bf16[1024,128]{1,0:T(8,128)(2,1)S(1)}, u32[]{:S(2)}, u32[]{:S(2)}) collective-permute-start(bf16[1024,128]{1,0:T(8,128)(2,1)S(1)} %fusion.10), channel_id=1, source_target_pairs={{0,4},{4,0},{1,5},{5,1},{2,6},{6,2},{3,7},{7,3},{8,12},{12,8},{9,1... | collective-permute-start | bytes 786440 | tf_op jit(solution)/shard_map/ppermute | solution.py:292
  134.5 14.0 %collective-permute-start.48 = (bf16[2,9,32,128]{3,2,1,0:T(8,128)(2,1)S(1)}, bf16[2,9,32,128]{3,2,1,0:T(8,128)(2,1)S(1)}, u32[]{:S(2)}, u32[]{:S(2)}) collective-permute-start(bf16[2,9,32,128]{3,2,1,0:T(8,128)(2,1)S(1)} %get-tuple-element.117), channel_id=1, source_target_pairs={{0,16},{8,24},{16,0},{24,8},{1,17},{9,25},{17,1},{25,9},{2,18},{10... | collective-permute-start | bytes 442376 | tf_op jit(solution)/shard_map/ppermute | solution.py:292
  136.1 12.5 %collective-permute-start.49 = (bf16[2,9,32,128]{3,2,1,0:T(8,128)(2,1)S(1)}, bf16[2,9,32,128]{3,2,1,0:T(8,128)(2,1)S(1)}, u32[]{:S(2)}, u32[]{:S(2)}) collective-permute-start(bf16[2,9,32,128]{3,2,1,0:T(8,128)(2,1)S(1)} %get-tuple-element.116), channel_id=1, source_target_pairs={{0,24},{8,16},{16,8},{24,0},{1,25},{9,17},{17,9},{25,1},{2,26},{10... | collective-permute-start | bytes 442376 | tf_op jit(solution)/shard_map/ppermute | solution.py:292
  138.9 10.3 %collective-permute-start.31 = (bf16[1024,128]{1,0:T(8,128)(2,1)S(1)}, bf16[1024,128]{1,0:T(8,128)(2,1)S(1)}, u32[]{:S(2)}, u32[]{:S(2)}) collective-permute-start(bf16[1024,128]{1,0:T(8,128)(2,1)S(1)} %fusion.9), channel_id=1, source_target_pairs={{0,2},{2,0},{1,3},{3,1},{4,6},{6,4},{5,7},{7,5},{8,10},{10,8},{9,1... | collective-permute-start | bytes 786440 | tf_op jit(solution)/shard_map/ppermute | solution.py:292
  154.1 59.2 %collective-permute-start.51 = (f32[9,32,128]{2,1,0:T(8,128)S(1)}, f32[9,32,128]{2,1,0:T(8,128)S(1)}, u32[]{:S(2)}, u32[]{:S(2)}) collective-permute-start(f32[9,32,128]{2,1,0:T(8,128)S(1)} %get-tuple-element.123), channel_id=1, source_target_pairs={{0,2},{2,0},{1,3},{3,1},{4,6},{6,4},{5,7},{7,5},{8,10},{10,8},{9,1... | collective-permute-start | bytes 442376 | tf_op jit(solution)/shard_map/ppermute | solution.py:292
  164.5 18.6 %collective-permute-start.42 = (bf16[4,9,32,128]{3,2,1,0:T(8,128)(2,1)}, bf16[4,9,32,128]{3,2,1,0:T(8,128)(2,1)S(1)}, u32[]{:S(2)}, u32[]{:S(2)}) collective-permute-start(bf16[4,9,32,128]{3,2,1,0:T(8,128)(2,1)} %get-tuple-element.86), channel_id=1, source_target_pairs={{0,1},{1,0},{2,3},{3,2},{4,5},{5,4},{6,7},{7,6},{8,9},{9,8},{10,11... | collective-permute-start | bytes 884744 | tf_op jit(solution)/shard_map/ppermute | solution.py:292
  171.0 8.8 %collective-permute-start.35 = (bf16[2,4,64,256]{3,2,1,0:T(8,128)(2,1)}, bf16[2,4,64,256]{3,2,1,0:T(8,128)(2,1)S(1)}, u32[]{:S(2)}, u32[]{:S(2)}) collective-permute-start(bf16[2,4,64,256]{3,2,1,0:T(8,128)(2,1)} %get-tuple-element.82), channel_id=1, source_target_pairs={{0,4},{4,0},{1,5},{5,1},{2,6},{6,2},{3,7},{7,3},{8,12},{12,8},{9,1... | collective-permute-start | bytes 786440 | tf_op jit(solution)/shard_map/ppermute | solution.py:292
  172.4 9.9 %collective-permute-start.37 = (bf16[2,4,64,256]{3,2,1,0:T(8,128)(2,1)}, bf16[2,4,64,256]{3,2,1,0:T(8,128)(2,1)S(1)}, u32[]{:S(2)}, u32[]{:S(2)}) collective-permute-start(bf16[2,4,64,256]{3,2,1,0:T(8,128)(2,1)} %get-tuple-element.84), channel_id=1, source_target_pairs={{0,2},{2,0},{1,3},{3,1},{4,6},{6,4},{5,7},{7,5},{8,10},{10,8},{9,1... | collective-permute-start | bytes 786440 | tf_op jit(solution)/shard_map/ppermute | solution.py:292
  181.6 24.0 %collective-permute-start.36 = (bf16[4,64,256]{2,1,0:T(8,128)(2,1)}, bf16[4,64,256]{2,1,0:T(8,128)(2,1)}, u32[]{:S(2)}, u32[]{:S(2)}) collective-permute-start(bf16[4,64,256]{2,1,0:T(8,128)(2,1)} %fusion.17), channel_id=1, source_target_pairs={{0,2},{2,0},{1,3},{3,1},{4,6},{6,4},{5,7},{7,5},{8,10},{10,8},{9,1... | collective-permute-start | bytes 393224 | tf_op jit(solution)/shard_map/ppermute | solution.py:292
  188.9 17.7 %collective-permute-start.38 = (bf16[4,64,256]{2,1,0:T(8,128)(2,1)}, bf16[4,64,256]{2,1,0:T(8,128)(2,1)}, u32[]{:S(2)}, u32[]{:S(2)}) collective-permute-start(bf16[4,64,256]{2,1,0:T(8,128)(2,1)} %fusion.18), channel_id=1, source_target_pairs={{0,4},{4,0},{1,5},{5,1},{2,6},{6,2},{3,7},{7,3},{8,12},{12,8},{9,1... | collective-permute-start | bytes 393224 | tf_op jit(solution)/shard_map/ppermute | solution.py:292
  199.5 12.4 %all-to-all-start = ((f32[32,1,128]{2,1,0:T(1,128)}), f32[32,1,128]{2,1,0:T(1,128)S(1)}, u32[]{:S(2)}, u32[]{:S(2)}) async-start(f32[32,1,128]{2,1,0:T(1,128)} %broadcast_in_dim.68), calls=%async_computation | async-start | bytes 32768 | tf_op jit(solution)/shard_map/all_to_all | solution.py:969
  203.0 11.8 %collective-permute-start.52 = (f32[4,32]{1,0:T(4,128)S(1)}, f32[4,32]{1,0:T(4,128)S(1)}, u32[]{:S(2)}, u32[]{:S(2)}) collective-permute-start(f32[4,32]{1,0:T(4,128)S(1)} %reshape.314), channel_id=1, source_target_pairs={{0,2},{2,0},{1,3},{3,1},{4,6},{6,4},{5,7},{7,5},{8,10},{10,8},{9,1... | collective-permute-start | bytes 1544 | tf_op jit(solution)/shard_map/ppermute | solution.py:292
  205.1 10.4 %collective-permute-start.50 = (f32[9,32,64]{1,2,0:T(8,128)S(1)}, f32[9,32,64]{1,2,0:T(8,128)S(1)}, u32[]{:S(2)}, u32[]{:S(2)}) collective-permute-start(f32[9,32,64]{1,2,0:T(8,128)S(1)} %copy.88), channel_id=1, source_target_pairs={{0,2},{2,0},{1,3},{3,1},{4,6},{6,4},{5,7},{7,5},{8,10},{10,8},{9,1... | collective-permute-start | bytes 221192 | tf_op jit(solution)/shard_map/ppermute | solution.py:292
  207.7 9.2 %collective-permute-start.39 = (bf16[2,64,256]{2,1,0:T(8,128)(2,1)S(1)}, bf16[2,64,256]{2,1,0:T(8,128)(2,1)S(1)}, u32[]{:S(2)}, u32[]{:S(2)}) collective-permute-start(bf16[2,64,256]{2,1,0:T(8,128)(2,1)S(1)} %get-tuple-element.128), channel_id=1, source_target_pairs={{0,8},{8,0},{16,24},{24,16},{1,9},{9,1},{17,25},{25,17},{2,10},{10... | collective-permute-start | bytes 196616 | tf_op jit(solution)/shard_map/ppermute | solution.py:292
  (64 other events, 455.4 us)

commit v2 on v0

--- a/solution.py
+++ b/solution.py
@@ -1,7 +1,11 @@
+import functools
+
 import jax
 import jax.numpy as jnp
 from jax import lax
-from jax.sharding import PartitionSpec as P
+from jax.experimental import pallas as pl
+from jax.experimental.pallas import tpu as pltpu
+from jax.sharding import Mesh, PartitionSpec as P
 
 C1 = 256
 C2 = 512
@@ -105,7 +109,7 @@
     )
 
 
-def body(
+def general_body(
     clip_input,
     frame_counts,
     clip_order,
@@ -254,40 +258,913 @@
     return (pooled, input_grad, grad_norm) + first_update + second_update + norm_update
 
 
+AXES = ("z", "x", "y", "core")
+BF = jnp.bfloat16
+F32 = jnp.float32
+ROWS = 512
+CLIPS_CORE = 4
+PIXELS = ROWS * CLIPS_CORE
+HALF = PIXELS // 2
+LANES = 128
+TAPS = 9
+CHUNK = TAPS * 32
+ANY = pl.BlockSpec(memory_space=pl.ANY)
+VM = pl.BlockSpec(memory_space=pltpu.VMEM)
+SM = pl.BlockSpec(memory_space=pltpu.SMEM)
+VMEM_LIMIT = 28 * 1024 * 1024
+
+
+def shape_of(shape, dtype=BF):
+    return jax.ShapeDtypeStruct(shape, dtype)
+
+
+def call(kernel, out, in_specs, out_specs, scratch=(), flops=0, moved=0):
+    return pl.pallas_call(
+        kernel,
+        out_shape=out,
+        in_specs=in_specs,
+        out_specs=out_specs,
+        scratch_shapes=list(scratch),
+        compiler_params=pltpu.CompilerParams(vmem_limit_bytes=VMEM_LIMIT),
+        cost_estimate=pl.CostEstimate(flops=flops, bytes_accessed=moved, transcendentals=0),
+    )
+
+
+def swap(value, axis, step=1):
+    size = lax.axis_size(axis)
+    return lax.ppermute(value, axis, [(i, i ^ step) for i in range(size)])
+
+
+def start_copies(copies, sems):
+    started = []
+    for at, (source, target) in enumerate(copies):
+        copy = pltpu.make_async_copy(source, target, sems.at[at])
+        copy.start()
+        started.append(copy)
+    return started
+
+
+def wait_all(copies):
+    for copy in copies:
+        copy.wait()
+
+
+def place(*axes):
+    found = tuple(lax.axis_index(axis) for axis in axes)
+    return found if len(found) > 1 else found[0]
+
+
+def clip_counts(order_ref, counts_ref):
+    z, core = place("z", "core")
+    counts = []
+    for group in range(2):
+        for j in range(CL_MB):
+            row = group * 2 + core
+            counts.append(counts_ref[row * 8 + order_ref[row, z * CL_MB + j]])
+    return counts
+
+
+def pixel_count(order_ref, counts_ref):
+    z = place("z")
+    total = 0
+    for row in range(4):
+        for j in range(CL_MB):
+            total = total + counts_ref[row * 8 + order_ref[row, z * CL_MB + j]]
+    return (MEL * total).astype(F32)
+
+
+def time_shift(rows, step):
+    zero = jnp.zeros((MEL, rows.shape[1]), rows.dtype)
+    if step == 1:
+        return jnp.concatenate([rows[MEL:], zero], axis=0)
+    if step == -1:
+        return jnp.concatenate([zero, rows[:-MEL]], axis=0)
+    return rows
+
+
+def mel_shift(rows, step):
+    if step == 0:
+        return rows
+    cube = rows.reshape(rows.shape[0] // MEL, MEL, rows.shape[1])
+    turned = pltpu.roll(cube, (-step) % MEL, 1)
+    bin_at = lax.broadcasted_iota(jnp.int32, cube.shape, 1) + step
+    keep = (bin_at >= 0) & (bin_at < MEL)
+    return jnp.where(keep, turned, 0.0).reshape(rows.shape)
+
+
+def valid_rows(count, width):
+    frame = lax.broadcasted_iota(jnp.int32, (ROWS, width), 0) // MEL
+    return (frame < count).astype(F32)
+
+
+def dot_nt(left, right):
+    return lax.dot_general(left, right, (((1,), (1,)), ((), ())), preferred_element_type=F32)
+
+
+def dot_nn(left, right):
+    return lax.dot_general(left, right, (((1,), (0,)), ((), ())), preferred_element_type=F32)
+
+
+def dot_tn(left, right):
+    return lax.dot_general(left, right, (((0,), (0,)), ((), ())), preferred_element_type=F32)
+
+
+def lanes_of(tap):
+    return slice(tap * LANES, (tap + 1) * LANES)
+
+
+def gather_taps(product):
+    total = None
+    for mel in range(3):
+        column = None
+        for time in range(3):
+            term = time_shift(product[:, lanes_of(3 * time + mel)], time - 1)
+            column = term if column is None else column + term
+        column = mel_shift(column, mel - 1)
+        total = column if total is None else total + column
+    return total
+
+
+def scatter_taps(grad, target, base):
+    for mel in range(3):
+        moved = mel_shift(grad, 1 - mel)
+        for time in range(3):
+            target[base : base + ROWS, lanes_of(3 * time + mel)] = time_shift(moved, 1 - time).astype(
+                BF
+            )
+
+
+def channel_sums(first, second):
+    return (jnp.sum(first, axis=0, keepdims=True), jnp.sum(second, axis=0, keepdims=True))
+
+
+def pair_sums(own_ref, other_ref):
+    return (own_ref[0:1, :] + other_ref[0:1, :], own_ref[1:2, :] + other_ref[1:2, :])
+
+
+def norm_rows(own_ref, other_ref, pixels):
+    total, squares = pair_sums(own_ref, other_ref)
+    mean = total / pixels
+    return mean, lax.rsqrt(squares / pixels - mean * mean + NORM_EPS)
+
+
+def put_pair(ref, first, second):
+    ref[...] = jnp.zeros(ref.shape, F32)
+    ref[0:1, :] = first
+    ref[1:2, :] = second
+
+
+def exchange_matrix(rows, columns, source_of):
+    row = lax.broadcasted_iota(jnp.int32, (rows, columns), 0)
+    column = lax.broadcasted_iota(jnp.int32, (rows, columns), 1)
+    return (row == source_of(column)).astype(BF)
+
+
+def block_exchange(column):
+    return ((column // 32) % 4) * 128 + (column // 128) * 32 + column % 32
+
+
+def lane_index(rows):
+    return lax.broadcasted_iota(jnp.int32, (rows, LANES), 1)
+
+
+def prepare_kernel(
+    order_ref, clip_ref, one_ref, two_ref, norm_ref, cot_ref, p0, p1, p2, p3, one_keep, one_send,
+    two_keep, two_send, gain_ref, cot_own, sems
+):
+    z, x, y, core = place(*AXES)
+    group = y * 2 + core
+    copies = []
+    for step, piece in enumerate((p0, p1, p2, p3)):
+        plane = jnp.bitwise_xor(z, step)
+        for j in range(CL_MB):
+            clip = order_ref[group, plane * CL_MB + j]
+            copies.append((clip_ref.at[clip], piece.at[j]))
+    started = start_copies(copies, sems)
+    for tap in range(TAPS):
+        turned = jnp.swapaxes(one_ref[tap], 0, 1)
+        rows = [turned[at * 16 : (at + 1) * 16] for at in range(4)]
+        low = jnp.concatenate([rows[0], rows[1]], axis=1).astype(BF)
+        high = jnp.concatenate([rows[2], rows[3]], axis=1).astype(BF)
+        span = slice(tap * 16, (tap + 1) * 16)
+        one_keep[span, :] = jnp.where(y == 0, low, high)
+        one_send[span, :] = jnp.where(y == 0, high, low)
+        low, high = two_ref[tap, 0:32, :].astype(BF), two_ref[tap, 32:64, :].astype(BF)
+        span = slice(tap * 32, (tap + 1) * 32)
+        two_keep[span, :] = jnp.where(y == 0, low, high)
+        two_send[span, :] = jnp.where(y == 0, high, low)
+    wide = jnp.concatenate([norm_ref[...], norm_ref[...]], axis=1)
+    wide = jnp.concatenate([wide, jnp.zeros((4, LANES), F32)], axis=0)
+    turned = pltpu.roll(wide, (z * 32 - y * 32) % LANES, 1)
+    gain_rows = jnp.where(lane_index(8) // 32 == z, turned, 0.0)
+    gain_ref[...] = jnp.concatenate([gain_rows, jnp.zeros((8, LANES), F32)], axis=0).astype(BF)
+
+    def cot_rows(y_of):
+        rows = []
+        for j in range(CL_MB):
+            row = cot_ref[pl.ds(order_ref[group, z * CL_MB + j], 1), :]
+            picked = jnp.zeros((1, LANES), F32)
+            for block in range(MB):
+                moved = pltpu.roll(
+                    jnp.broadcast_to(row[:, lanes_of(block)], (8, LANES)),
+                    (block * 32 - x * 64 - y_of * 32) % LANES,
+                    1,
+                )[0:1]
+                picked = jnp.where(lane_index(1) // 32 == block, moved, picked)
+            rows.append(picked)
+        return rows
+
+    own, send = cot_rows(y), cot_rows(1 - y)
+    cot_own[...] = jnp.concatenate(own + [jnp.zeros((6, LANES), F32)], axis=0)
+    high = [row.astype(BF).astype(F32) for row in send]
+    rest = [row - top for row, top in zip(send, high)]
+    middle = [row.astype(BF).astype(F32) for row in rest]
+    low = [row - top for row, top in zip(rest, middle)]
+    packed = jnp.concatenate(high + middle + low + [jnp.zeros((10, LANES), F32)], axis=0)
+    two_send[CHUNK : CHUNK + 16, :] = packed.astype(BF)
+    wait_all(started)
+
+
+def first_conv_kernel(
+    order_ref, counts_ref, a0, a1, a2, a3, b0, b1, b2, b3, o0, o1, o2, o3, s0, s1, s2, s3,
+    pre_ref, x_ref, weight_ref, stat_ref, gain_ref, sems
+):
+    z, x, y, core = place(*AXES)
+    copies = []
+    for j, pieces in (
+        (0, ((a0, x, y), (a1, 1 - x, y), (a2, x, 1 - y), (a3, 1 - x, 1 - y))),
+        (1, ((b0, x, y), (b1, x, 1 - y), (b2, 1 - x, y), (b3, 1 - x, 1 - y))),
+    ):
+        for source, x_of, y_of in pieces:
+            for step in range(MB):
+                frames = (jnp.bitwise_xor(z, step) * 2 + x_of) * 64
+                row = pl.multiple_of((y_of * CL_MB + j) * ROWS + frames, 64)
+                copies.append((source.at[step], x_ref.at[pl.ds(row, 64), :]))
+    started = start_copies(copies, sems)
+    gains = jnp.zeros((8, LANES), F32)
+    for half in range(2):
+
+        def source_of(column, half=half):
+            from_core = jnp.bitwise_xor((column // 64) % 2, core)
+            from_y = jnp.bitwise_xor(column // 128, y)
+            return from_core * 256 + from_y * 128 + half * 64 + column % 64
+
+        spread = exchange_matrix(512, C1, source_of)
+        for step, (own, other) in enumerate(((o0, s0), (o1, s1), (o2, s2), (o3, s3))):
+            z_of = jnp.bitwise_xor(z, step)
+            four = jnp.concatenate([own[0:144], own[144:288], other[0:144], other[144:288]], axis=1)
+            both = dot_nn(four, spread).astype(BF)
+            for tap in range(TAPS):
+                weight_ref[tap, z_of, half * 16 : half * 16 + 16] = both[tap * 16 : (tap + 1) * 16]
+            if half == 0:
+                gains = gains + own[CHUNK : CHUNK + 16].astype(F32)[0:8]
+    gain_ref[...] = gains
+    counts = clip_counts(order_ref, counts_ref)
+    wait_all(started)
+    weight = weight_ref[...].reshape(TAPS * LANES, C1)
+    first = jnp.zeros((1, LANES), F32)
+    second = jnp.zeros((1, LANES), F32)
+    for clip in range(CLIPS_CORE):
+        span = slice(clip * ROWS, (clip + 1) * ROWS)
+        mask = valid_rows(counts[clip], C1)
+        masked = x_ref[span, :] * mask.astype(BF)
+        x_ref[span, :] = masked
+        pre = gather_taps(dot_nt(masked, weight))
+        pre_ref[span, :] = pre
+        kept = pre * mask[:, 0:LANES]
+        plus = channel_sums(kept, kept * pre)
+        first, second = first + plus[0], second + plus[1]
+    put_pair(stat_ref, first, second)
+
+
+def hidden_kernel(order_ref, counts_ref, pre_ref, own_ref, other_ref, gain_ref, a_ref, b_ref):
+    mean, scale = norm_rows(own_ref, other_ref, pixel_count(order_ref, counts_ref))
+    counts = clip_counts(order_ref, counts_ref)
+    for clip in range(CLIPS_CORE):
+        pre = pre_ref[clip * ROWS : (clip + 1) * ROWS, :]
+        shaped = gain_ref[0:1, :] * ((pre - mean) * scale) + gain_ref[1:2, :]
+        value = shaped * jax.nn.sigmoid(shaped) * valid_rows(counts[clip], LANES)
+        target = a_ref if clip < 2 else b_ref
+        target[(clip % 2) * ROWS : (clip % 2 + 1) * ROWS, :] = value.astype(BF)
+
+
+def second_weight_kernel(o0, o1, o2, o3, s0, s1, s2, s3, weight_ref, pieces, sems):
+    z, y, core = place("z", "y", "core")
+    copies = []
+    for step, (own, other) in enumerate(((o0, s0), (o1, s1), (o2, s2), (o3, s3))):
+        for source, core_of in ((own, core), (other, 1 - core)):
+            for turn in range(2):
+                part = jnp.bitwise_xor(y, turn) * 2 + core_of
+                copies.append(
+                    (
+                        source.at[pl.ds(turn * CHUNK, CHUNK), :],
+                        pieces.at[jnp.bitwise_xor(z, step), part],
+                    )
+                )
+    started = start_copies(copies, sems)
+    spread = exchange_matrix(C2, C2, block_exchange)
+    wait_all(started)
+    for z_of in range(MB):
+        natural = jnp.concatenate([pieces[z_of, part] for part in range(4)], axis=1)
+        both = dot_nn(natural, spread).astype(BF)
+        for tap in range(TAPS):
+            weight_ref[tap, z_of] = both[tap * 32 : (tap + 1) * 32]
+
+
+def hidden_copies(parts, target):
+    x, y = place("x", "y")
+    chips = ((x, y), (1 - x, y), (x, 1 - y), (1 - x, 1 - y), (x, y), (x, 1 - y), (1 - x, y), (1 - x, 1 - y))
+    copies = []
+    for at, (source, (x_of, y_of)) in enumerate(zip(parts, chips)):
+        lane = pl.multiple_of((x_of * 2 + y_of) * LANES, LANES)
+        copies.append((source, target.at[pl.ds((at // 4) * HALF, HALF), pl.ds(lane, LANES)]))
+    return copies
+
+
+def second_conv_kernel(order_ref, counts_ref, *rest):
+    parts, (weight_ref, pre_ref, stat_ref, hidden, sems) = rest[:8], rest[8:]
+    started = start_copies(hidden_copies(parts, hidden), sems)
+    counts = clip_counts(order_ref, counts_ref)
+    weight = weight_ref[...].reshape(TAPS * LANES, C2)
+    wait_all(started)
+    first = jnp.zeros((1, LANES), F32)
+    second = jnp.zeros((1, LANES), F32)
+    for clip in range(CLIPS_CORE):
+        span = slice(clip * ROWS, (clip + 1) * ROWS)
+        pre = gather_taps(dot_nt(hidden[span, :], weight))
+        pre_ref[span, :] = pre
+        kept = pre * valid_rows(counts[clip], LANES)
+        plus = channel_sums(kept, kept * pre)
+        first, second = first + plus[0], second + plus[1]
+    put_pair(stat_ref, first, second)
+
+
+def pool_kernel(
+    order_ref, counts_ref, pre_ref, own_ref, other_ref, gain_ref, cot_own, cot_got,
+    slope_ref, sum_ref, pooled_ref
+):
+    y = place("y")
+    counts = clip_counts(order_ref, counts_ref)
+    mean, scale = norm_rows(own_ref, other_ref, pixel_count(order_ref, counts_ref))
+    first = jnp.zeros((1, LANES), F32)
+    second = jnp.zeros((1, LANES), F32)
+    slots = ROWS // (2 * MEL)
+    got = cot_got[CHUNK : CHUNK + 16, :].astype(F32)
+    pooled = []
+    for clip in range(CLIPS_CORE):
+        span = slice(clip * ROWS, (clip + 1) * ROWS)
+        count = counts[clip]
+        j = clip % CL_MB
+        told = got[j : j + 1] + got[2 + j : 3 + j] + got[4 + j : 5 + j]
+        cot = jnp.where(y == clip // CL_MB, cot_own[j : j + 1, :], told)
+        mask = valid_rows(count, LANES)
+        normed = (pre_ref[span, :] - mean) * scale
+        shaped = gain_ref[2:3, :] * normed + gain_ref[3:4, :]
+        gate = jax.nn.sigmoid(shaped)
+        active = (shaped * gate * mask).reshape(slots, 2 * MEL, LANES)
+        summary = jnp.sum(active, axis=1) / (2 * MEL)
+        slot = lax.broadcasted_iota(jnp.int32, (slots, LANES), 0)
+        keep = (2 * slot + 1 < count).astype(F32)
+        raised = jnp.exp(summary)
+        exp_total = jnp.sum(raised * keep, axis=0, keepdims=True)
+        halves = (count // 2).astype(F32)
+        pooled.append(
+            jnp.sum(summary * keep, axis=0, keepdims=True) / halves + jnp.log(exp_total / halves)
+        )
+        summary_grad = keep * (cot / halves + cot * raised / exp_total) / (2 * MEL)
+        spread = jnp.broadcast_to(summary_grad[:, None, :], (slots, 2 * MEL, LANES))
+        slope = spread.reshape(ROWS, LANES) * mask * (gate * (1.0 + shaped * (1.0 - gate)))
+        slope_ref[span, :] = slope
+        plus = channel_sums(slope, slope * normed)
+        first, second = first + plus[0], second + plus[1]
+    put_pair(sum_ref, first, second)
+    high = [row.astype(BF).astype(F32) for row in pooled]
+    low = [row - top for row, top in zip(pooled, high)]
+    rows = jnp.concatenate(high + low + [jnp.zeros((8, LANES), F32)], axis=0)
+    pooled_ref[...] = rows.astype(BF)
+
+
+def pre_grad(slope, pre, mask, mean, scale, gain, sums, pixels):
+    normed = (pre - mean) * scale
+    return mask * (scale * gain) * (slope - sums[0] / pixels - normed * (sums[1] / pixels))
+
+
+def hidden_grad_kernel(
+    order_ref, counts_ref, slope_ref, pre_ref, own_ref, other_ref, sum_own, sum_other, gain_ref,
+    weight_ref, pooled_ref, grad_ref, a_own, a_mid, a_far, a_near, b_own, b_mid, b_far, b_near,
+    columns, partial
+):
+    x, y = place("x", "y")
+    counts = clip_counts(order_ref, counts_ref)
+    pixels = pixel_count(order_ref, counts_ref)
+    mean, scale = norm_rows(own_ref, other_ref, pixels)
+    sums = pair_sums(sum_own, sum_other)
+    weight = weight_ref[...].reshape(TAPS * LANES, C2)
+    a_near[HALF : HALF + 16, :] = pooled_ref[...]
+
+    def lane(x_of, y_of):
+        return pl.ds(pl.multiple_of((x_of * 2 + y_of) * LANES, LANES), LANES)
+
+    for clip in range(CLIPS_CORE):
+        span = slice(clip * ROWS, (clip + 1) * ROWS)
+        mask = valid_rows(counts[clip], LANES)
+        grad = pre_grad(
+            slope_ref[span, :], pre_ref[span, :], mask, mean, scale, gain_ref[2:3, :], sums, pixels
+        )
+        grad_ref[span, :] = grad.astype(BF)
+        scatter_taps(grad, columns, 0)
+        partial[...] = dot_nn(columns[...], weight)
+        rows = slice((clip % 2) * ROWS, (clip % 2 + 1) * ROWS)
+        far = partial[:, lane(1 - x, 1 - y)].astype(BF)
+        if clip < 2:
+            a_own[rows, :] = partial[:, lane(x, y)]
+            a_mid[rows, :] = partial[:, lane(x, 1 - y)]
+            a_near[rows, :] = partial[:, lane(1 - x, y)].astype(BF)
+            a_far[rows, :] = far
+        else:
+            b_own[rows, :] = partial[:, lane(x, y)]
+            b_mid[rows, :] = partial[:, lane(1 - x, y)]
+            b_near[rows, :] = partial[:, lane(x, 1 - y)].astype(BF)
+            b_far[rows, :] = far
+
+
+def pass_on_kernel(a_mid, a_got, b_mid, b_got, a_next, b_next):
+    a_next[...] = (a_mid[...] + a_got[...].astype(F32)).astype(BF)
+    b_next[...] = (b_mid[...] + b_got[...].astype(F32)).astype(BF)
+
+
+def second_weight_grad_kernel(*rest):
+    parts, (grad_ref, keep_ref, send_ref, hidden, columns, natural, sems) = rest[:8], rest[8:]
+    core = place("core")
+    started = start_copies(hidden_copies(parts, hidden), sems)
+    for clip in range(CLIPS_CORE):
+        grad = grad_ref[clip * ROWS : (clip + 1) * ROWS, :].astype(F32)
+        scatter_taps(grad, columns, clip * ROWS)
+    spread = exchange_matrix(C2, C2, block_exchange)
+    wait_all(started)
+    for tap in range(TAPS):
+        chip = dot_tn(columns[:, lanes_of(tap)], hidden[...]).astype(BF)
+        natural[...] = dot_nn(chip, spread)
+        for y_of in range(2):
+            keep = natural[:, pl.ds(pl.multiple_of((y_of * 2 + core) * LANES, LANES), LANES)]
+            send = natural[:, pl.ds(pl.multiple_of((y_of * 2 + 1 - core) * LANES, LANES), LANES)]
+            for z_of in range(MB):
+                rows = slice(z_of * 32, (z_of + 1) * 32)
+                target = slice(tap * 32, (tap + 1) * 32)
+                keep_ref[z_of, y_of, target] = keep[rows].astype(BF)
+                send_ref[z_of, y_of, target] = send[rows].astype(BF)
+
+
+def second_core_kernel(keep_ref, got_ref, own_ref, n1, n2, n3):
+    z = place("z")
+    own_ref[...] = keep_ref[z].astype(F32) + got_ref[z].astype(F32)
+    for step, target in ((1, n1), (2, n2), (3, n3)):
+        at = jnp.bitwise_xor(z, step)
+        target[...] = (keep_ref[at].astype(F32) + got_ref[at].astype(F32)).astype(BF)
+
+
+def second_sum_kernel(own_ref, g1, g2, g3, keep_ref, send_ref, square_ref):
+    y = place("y")
+    total = own_ref[...] + g1[...].astype(F32) + g2[...].astype(F32) + g3[...].astype(F32)
+    keep_ref[...] = jnp.where(y == 0, total[0], total[1])
+    send_ref[...] = jnp.where(y == 0, total[1], total[0])
+    square_ref[...] = jnp.sum(total * total, axis=(0, 1), keepdims=False)[None, :] * jnp.ones((8, 1), F32)
+
+
+def first_slope_kernel(
+    order_ref, counts_ref, a_own, a_near, a_last, b_own, b_near, b_last, pre_ref, own_ref, other_ref,
+    gain_ref, slope_ref, sum_ref
+):
+    counts = clip_counts(order_ref, counts_ref)
+    mean, scale = norm_rows(own_ref, other_ref, pixel_count(order_ref, counts_ref))
+    first = jnp.zeros((1, LANES), F32)
+    second = jnp.zeros((1, LANES), F32)
+    for clip in range(CLIPS_CORE):
+        span = slice(clip * ROWS, (clip + 1) * ROWS)
+        rows = slice((clip % 2) * ROWS, (clip % 2 + 1) * ROWS)
+        own, near, last = (a_own, a_near, a_last) if clip < 2 else (b_own, b_near, b_last)
+        outer = own[rows, :] + near[rows, :].astype(F32) + last[rows, :].astype(F32)
+        normed = (pre_ref[span, :] - mean) * scale
+        shaped = gain_ref[0:1, :] * normed + gain_ref[1:2, :]
+        gate = jax.nn.sigmoid(shaped)
+        slope = outer * valid_rows(counts[clip], LANES) * (gate * (1.0 + shaped * (1.0 - gate)))
+        slope_ref[span, :] = slope
+        plus = channel_sums(slope, slope * normed)
+        first, second = first + plus[0], second + plus[1]
+    put_pair(sum_ref, first, second)
+
+
+def first_weight_grad_kernel(
+    order_ref, counts_ref, slope_ref, pre_ref, own_ref, other_ref, sum_own, sum_other, gain_ref, x_ref,
+    keep_ref, send_ref, grad_ref, columns
+):
+    core = place("core")
+    counts = clip_counts(order_ref, counts_ref)
+    pixels = pixel_count(order_ref, counts_ref)
+    mean, scale = norm_rows(own_ref, other_ref, pixels)
+    sums = pair_sums(sum_own, sum_other)
+    for clip in range(CLIPS_CORE):
+        span = slice(clip * ROWS, (clip + 1) * ROWS)
+        mask = valid_rows(counts[clip], LANES)
+        grad = pre_grad(
+            slope_ref[span, :], pre_ref[span, :], mask, mean, scale, gain_ref[0:1, :], sums, pixels
+        )
+        grad_ref[span, :] = grad.astype(BF)
+        scatter_taps(grad, columns, clip * ROWS)
+
+    def source_of(column):
+        core_of = jnp.where(column < 128, core, 1 - core)
+        return ((column // 64) % 2) * 128 + core_of * 64 + column % 64
+
+    spread = exchange_matrix(C1, C1, source_of)
+    for tap in range(TAPS):
+        part = dot_tn(columns[:, lanes_of(tap)], x_ref[...]).astype(BF)
+        both = dot_nn(part, spread).astype(BF)
+        for z_of in range(MB):
+            rows = slice(z_of * 32, (z_of + 1) * 32)
+            target = slice(tap * 32, (tap + 1) * 32)
+            keep_ref[z_of, target] = both[rows, 0:LANES]
+            send_ref[z_of, target] = both[rows, LANES : 2 * LANES]
+
+
+def first_core_kernel(
+    keep_ref, got_ref, one_own, one_other, two_own, two_other, pooled_own, pooled_near, pooled_last,
+    own_ref, n0, n1, n2, n3, scratch
+):
+    z, x, y = place("z", "x", "y")
+    own_ref[...] = keep_ref[z].astype(F32) + got_ref[z].astype(F32)
+    one, two = pair_sums(one_own, one_other), pair_sums(two_own, two_other)
+    sums = jnp.concatenate([one[1], one[0], two[1], two[0]], axis=0)
+    high = sums.astype(BF).astype(F32)
+    norm_tile = jnp.concatenate([high, sums - high, jnp.zeros((8, LANES), F32)], axis=0).astype(BF)
+    last = pooled_last[HALF : HALF + 32, :].astype(F32)
+    near = pooled_near[HALF : HALF + 16, :].astype(F32)
+    own = pooled_own[...].astype(F32)
+    for rows, x_of, y_of in (
+        (own, x, y),
+        (near, 1 - x, y),
+        (last[0:16], x, 1 - y),
+        (last[16:32], 1 - x, 1 - y),
+    ):
+        for part in range(2):
+            for j in range(CL_MB):
+                row = jnp.where(
+                    y == 0, rows[part * 4 + j : part * 4 + j + 1], rows[part * 4 + 2 + j : part * 4 + 3 + j]
+                )
+                scratch[pl.ds((x_of * 2 + y_of) * 4 + part * 2 + j, 1), :] = row
+    pooled_tile = scratch[...].astype(BF)
+    for step, target in ((0, n0), (1, n1), (2, n2), (3, n3)):
+        at = jnp.bitwise_xor(z, step)
+        target[0:CHUNK, :] = (keep_ref[at].astype(F32) + got_ref[at].astype(F32)).astype(BF)
+        target[CHUNK : CHUNK + 16, :] = norm_tile
+        target[CHUNK + 16 : CHUNK + 32, :] = pooled_tile
+
+
+def first_sum_kernel(own_ref, n0, g1, g2, g3, square_two, told_ref, keep_ref, send_ref, norm_ref):
+    z, y, core = place("z", "y", "core")
+    total = own_ref[...]
+    norm = n0[CHUNK : CHUNK + 16, :].astype(F32)
+    for got in (g1, g2, g3):
+        total = total + got[0:CHUNK, :].astype(F32)
+        norm = norm + got[CHUNK : CHUNK + 16, :].astype(F32)
+    norm = norm[0:4] + norm[4:8]
+    mine = (lane_index(4) // 32 == z) & (core == 0)
+    squares = jnp.sum(total * total, axis=0, keepdims=True) + jnp.sum(
+        jnp.where(mine, norm * norm, 0.0), axis=0, keepdims=True
+    )
+    told_ref[...] = jnp.broadcast_to(squares + square_two[0:1, :], told_ref.shape)
+    turned = pltpu.roll(total, 64, 1)
+    low = jnp.where(y == 0, total, turned)
+    high = jnp.where(y == 0, turned, total)
+    left = lane_index(144) < 64
+    keep_ref[...] = jnp.where(left, low[0:144], pltpu.roll(low[144:288], 64, 1))
+    send_ref[0:144, :] = jnp.where(left, high[0:144], pltpu.roll(high[144:288], 64, 1))
+    rows = jnp.concatenate([norm, jnp.zeros((4, LANES), F32)], axis=0)
+    send_ref[144:152, :] = rows
+    norm_ref[...] = rows
+
+
+def shard_kernel(keep_ref, got_ref, norm_ref, one_ref, norm_out):
+    z, y = place("z", "y")
+    keep, got = keep_ref[...], got_ref[0:144, :]
+    first, second = jnp.where(y == 0, keep, got), jnp.where(y == 0, got, keep)
+    spans = []
+    for half in (first, second):
+        spans.append(jnp.concatenate([half[:, 0:64], half[:, 64:128]], axis=0))
+    for tap in range(TAPS):
+        rows = [span[tap * 32 : (tap + 1) * 32] for span in spans]
+        one_ref[tap] = jnp.swapaxes(jnp.concatenate(rows, axis=0), 0, 1)
+    keep, got = norm_ref[...], got_ref[144:152, :]
+    first, second = jnp.where(y == 0, keep, got), jnp.where(y == 0, got, keep)
+    low = pltpu.roll(first, (0 - z * 32) % LANES, 1)
+    high = pltpu.roll(second, (32 - z * 32) % LANES, 1)
+    norm_out[...] = jnp.where(lane_index(8) < 32, low, high)[0:4, 0:64]
+
+
+def input_grad_kernel(
+    grad_ref, weight_ref, a_own, a_mid, a_far, a_near, b_own, b_mid, b_far, b_near, columns, partial
+):
+    x, y = place("x", "y")
+    weight = weight_ref[...].reshape(TAPS * LANES, C1)
+    for clip in range(CLIPS_CORE):
+        grad = grad_ref[clip * ROWS : (clip + 1) * ROWS, :].astype(F32)
+        scatter_taps(grad, columns, 0)
+        partial[clip] = dot_nn(columns[...], weight)
+
+    def part(x_of, y_of, j, z_of):
+        return partial[y_of * CL_MB + j, pl.ds(pl.multiple_of((z_of * 2 + x_of) * 64, 64), 64), :]
+
+    for z_of in range(MB):
+        a_own[z_of] = part(x, y, 0, z_of)
+        a_mid[z_of] = part(x, 1 - y, 0, z_of)
+        a_near[z_of] = part(1 - x, y, 0, z_of).astype(BF)
+        a_far[z_of] = part(1 - x, 1 - y, 0, z_of).astype(BF)
+        b_own[z_of] = part(x, y, 1, z_of)
+        b_mid[z_of] = part(1 - x, y, 1, z_of)
+        b_near[z_of] = part(x, 1 - y, 1, z_of).astype(BF)
+        b_far[z_of] = part(1 - x, 1 - y, 1, z_of).astype(BF)
+
+
+def input_sum_kernel(order_ref, counts_ref, a_own, a_near, a_last, b_own, b_near, b_last, f0, f1, f2, f3):
+    z, x, y, core = place(*AXES)
+    row = y * 2 + core
+    for j, (own, near, last) in enumerate(((a_own, a_near, a_last), (b_own, b_near, b_last))):
+        count = counts_ref[row * 8 + order_ref[row, z * CL_MB + j]]
+        for step, target in enumerate((f0, f1, f2, f3)):
+            at = jnp.bitwise_xor(z, step)
+            total = own[at] + near[at].astype(F32) + last[at].astype(F32)
+            frame = (at * 2 + x) * 8 + lax.broadcasted_iota(jnp.int32, (64, C1), 0) // MEL
+            target[j] = jnp.where(frame < count, total, 0.0).astype(BF)
+
+
+def finish_kernel(order_ref, f0, g1, g2, g3, n0, n1, n2, n3, grad_ref, pooled_ref, scratch):
+    z, y, core = place("z", "y", "core")
+    row = y * 2 + core
+    for step, (piece, told) in enumerate(((f0, n0), (g1, n1), (g2, n2), (g3, n3))):
+        at = jnp.bitwise_xor(z, step)
+        rows = told[CHUNK + 16 : CHUNK + 32, :].astype(F32)
+        for j in range(CL_MB):
+            clip = order_ref[row, at * CL_MB + j]
+            grad_ref[clip] = piece[j]
+            for part in range(2):
+                chips = [rows[chip * 4 + part * 2 + j : chip * 4 + part * 2 + j + 1] for chip in range(4)]
+                scratch[part, pl.ds(clip, 1), :] = jnp.concatenate(chips, axis=1)
+    spread = exchange_matrix(C2, C2, block_exchange)
+    pooled_ref[...] = dot_nn(scratch[0].astype(BF), spread) + dot_nn(scratch[1].astype(BF), spread)
+
+
+def spread_plane(a0, b0):
+    a1, b1 = swap(a0, "x"), swap(b0, "y")
+    a2, b2 = swap(a0, "y"), swap(b0, "x")
+    a3, b3 = swap(a1, "y"), swap(b1, "x")
+    return (a0, a1, a2, a3, b0, b1, b2, b3)
+
+
+def fast_body(
+    clip_input,
+    frame_counts,
+    clip_order,
+    cotangent,
+    kernel_one,
+    kernel_one_mean,
+    kernel_one_square,
+    kernel_two,
+    kernel_two_mean,
+    kernel_two_square,
+    norm_params,
+    norm_mean,
+    norm_square,
+):
+    table = (clip_order, frame_counts)
+    p0, p1, p2, p3, one_keep, one_send, two_keep, two_send, gain_rows, cot_own = call(
+        prepare_kernel,
+        [shape_of((CL_MB, 64, C1))] * MB
+        + [shape_of((144, LANES))] * 2
+        + [shape_of((CHUNK, LANES)), shape_of((CHUNK + 16, LANES)), shape_of((16, LANES))]
+        + [shape_of((8, LANES), F32)],
+        [SM, ANY, VM, VM, VM, VM],
+        [VM] * 10,
+        [pltpu.SemaphoreType.DMA((MB * CL_MB,))],
+    )(
+        clip_order,
+        clip_input.reshape(MB * CL_MB, 64, C1),
+        kernel_one,
+        jnp.swapaxes(kernel_two, 1, 2),
+        norm_params,
+        cotangent,
+    )
+    arrived = [p0] + [swap(piece, "z", step) for step, piece in ((1, p1), (2, p2), (3, p3))]
+    one_got = swap(one_send, "y")
+    two_got = swap(two_send, "y")
+    a0 = jnp.stack([piece[0] for piece in arrived])
+    b0 = jnp.stack([piece[1] for piece in arrived])
+    inputs = spread_plane(a0, b0)
+
+    one_flat = jnp.concatenate([one_keep, one_got, gain_rows])
+    one_parts = [one_flat] + [swap(one_flat, "z", step) for step in range(1, MB)]
+    one_others = [swap(part, "core") for part in one_parts]
+    pre_one, masked, weight_one, stat_one, gains = call(
+        first_conv_kernel,
+        [
+            shape_of((PIXELS, LANES), F32),
+            shape_of((PIXELS, C1)),
+            shape_of((TAPS, MB, 32, C1)),
+            shape_of((8, LANES), F32),
+            shape_of((8, LANES), F32),
+        ],
+        [SM, SM] + [ANY] * 8 + [VM] * 8,
+        [VM] * 5,
+        [pltpu.SemaphoreType.DMA((8 * MB,))],
+        flops=2 * PIXELS * C1 * TAPS * LANES,
+    )(*table, *inputs, *one_parts, *one_others)
+    stat_one_other = swap(stat_one, "core")
+
+    two_flat = jnp.concatenate([two_keep, two_got[0:CHUNK]])
+    two_parts = [two_flat] + [swap(two_flat, "z", step) for step in range(1, MB)]
+    two_others = [swap(part, "core") for part in two_parts]
+    weight_two = call(
+        second_weight_kernel,
+        shape_of((TAPS, MB, 32, C2)),
+        [ANY] * 8,
+        VM,
+        [pltpu.VMEM((MB, 4, CHUNK, LANES), BF), pltpu.SemaphoreType.DMA((16,))],
+        flops=2 * TAPS * LANES * C2 * C2,
+    )(*two_parts, *two_others)
+
+    ha0, hb0 = call(
+        hidden_kernel, [shape_of((HALF, LANES))] * 2, [SM, SM] + [VM] * 4, [VM] * 2
+    )(*table, pre_one, stat_one, stat_one_other, gains)
+    hidden_parts = spread_plane(ha0, hb0)
+
+    pre_two, stat_two = call(
+        second_conv_kernel,
+        [shape_of((PIXELS, LANES), F32), shape_of((8, LANES), F32)],
+        [SM, SM] + [ANY] * 8 + [VM],
+        [VM] * 2,
+        [pltpu.VMEM((PIXELS, C2), BF), pltpu.SemaphoreType.DMA((8,))],
+        flops=2 * PIXELS * C2 * TAPS * LANES,
+    )(*table, *hidden_parts, weight_two)
+    stat_two_other = swap(stat_two, "core")
+    slope_two, sum_two, pooled_own = call(
+        pool_kernel,
+        [shape_of((PIXELS, LANES), F32), shape_of((8, LANES), F32), shape_of((16, LANES))],
+        [SM, SM] + [VM] * 6,
+        [VM] * 3,
+    )(*table, pre_two, stat_two, stat_two_other, gains, cot_own, two_got)
+    sum_two_other = swap(sum_two, "core")
+    grad_two, a_own, a_mid, a_far, a_near, b_own, b_mid, b_far, b_near = call(
+        hidden_grad_kernel,
+        [shape_of((PIXELS, LANES))]
+        + [shape_of((HALF, LANES), F32)] * 2
+        + [shape_of((HALF, LANES)), shape_of((HALF + 16, LANES))]
+        + [shape_of((HALF, LANES), F32)] * 2
+        + [shape_of((HALF, LANES))] * 2,
+        [SM, SM] + [VM] * 9,
+        [VM] * 9,
+        [pltpu.VMEM((ROWS, TAPS * LANES), BF), pltpu.VMEM((ROWS, C2), F32)],
+        flops=2 * PIXELS * C2 * TAPS * LANES,
+    )(
+        *table, slope_two, pre_two, stat_two, stat_two_other, sum_two, sum_two_other, gains,
+        weight_two, pooled_own,
+    )
+    a_got, b_got = swap(a_far, "x"), swap(b_far, "y")
+    a_near, b_near = swap(a_near, "x"), swap(b_near, "y")
+    two_part, two_part_send = call(
+        second_weight_grad_kernel,
+        [shape_of((MB, 2, CHUNK, LANES))] * 2,
+        [ANY] * 8 + [VM],
+        [VM] * 2,
+        [
+            pltpu.VMEM((PIXELS, C2), BF),
+            pltpu.VMEM((PIXELS, TAPS * LANES), BF),
+            pltpu.VMEM((LANES, C2), F32),
+            pltpu.SemaphoreType.DMA((8,)),
+        ],
+        flops=2 * PIXELS * C2 * TAPS * LANES,
+    )(*hidden_parts, grad_two)
+    a_next, b_next = call(
+        pass_on_kernel, [shape_of((HALF, LANES))] * 2, [VM] * 4, [VM] * 2
+    )(a_mid, a_got, b_mid, b_got)
+    a_next = jnp.concatenate([a_next, pooled_own, a_near[HALF:]])
+    a_last, b_last = swap(a_next, "y"), swap(b_next, "x")
+    slope_one, sum_one = call(
+        first_slope_kernel,
+        [shape_of((PIXELS, LANES), F32), shape_of((8, LANES), F32)],
+        [SM, SM] + [VM] * 10,
+        [VM] * 2,
+    )(*table, a_own, a_near, a_last, b_own, b_near, b_last, pre_one, stat_one, stat_one_other, gains)
+    sum_one_other = swap(sum_one, "core")
+    one_part, one_part_send, grad_one = call(
+        first_weight_grad_kernel,
+        [shape_of((MB, CHUNK, LANES))] * 2 + [shape_of((PIXELS, LANES))],
+        [SM, SM] + [VM] * 8,
+        [VM] * 3,
+        [pltpu.VMEM((PIXELS, TAPS * LANES), BF)],
+        flops=2 * PIXELS * C1 * TAPS * LANES,
+    )(
+        *table, slope_one, pre_one, stat_one, stat_one_other, sum_one, sum_one_other, gains, masked
+    )
+
+    two_own, t1, t2, t3 = call(
+        second_core_kernel,
+        [shape_of((2, CHUNK, LANES), F32)] + [shape_of((2, CHUNK, LANES))] * 3,
+        [VM] * 2,
+        [VM] * 4,
+    )(two_part, swap(two_part_send, "core"))
+    two_keep_sum, two_send_sum, square_two = call(
+        second_sum_kernel,
+        [shape_of((CHUNK, LANES), F32)] * 2 + [shape_of((8, LANES), F32)],
+        [VM] * 4,
+        [VM] * 3,
+    )(two_own, swap(t1, "z", 1), swap(t2, "z", 2), swap(t3, "z", 3))
+    two_got_sum = swap(two_send_sum, "y")
+
+    one_own, n0, n1, n2, n3 = call(
+        first_core_kernel,
+        [shape_of((CHUNK, LANES), F32)] + [shape_of((CHUNK + 32, LANES))] * MB,
+        [VM] * 9,
+        [VM] * 5,
+        [pltpu.VMEM((16, LANES), F32)],
+    )(
+        one_part, swap(one_part_send, "core"), sum_one, sum_one_other, sum_two, sum_two_other,
+        pooled_own, a_near, a_last,
+    )
+    g1, g2, g3 = swap(n1, "z", 1), swap(n2, "z", 2), swap(n3, "z", 3)
+    told, one_keep_sum, one_send_sum, norm_sum = call(
+        first_sum_kernel,
+        [
+            shape_of((32, LANES), F32),
+            shape_of((144, LANES), F32),
+            shape_of((152, LANES), F32),
+            shape_of((8, LANES), F32),
+        ],
+        [VM] * 6,
+        [VM] * 4,
+    )(one_own, n0, g1, g2, g3, square_two)
+    told = lax.all_to_all(told, AXES, 0, 0, tiled=True)
+    grad_norm = jnp.sqrt(jnp.sum(told))
+    factor = jnp.minimum(1.0, CLIP_NORM / (grad_norm + 1e-06))
+    one_got_sum = swap(one_send_sum, "y")
+    grad_one_shard, norm_shard = call(
+        shard_kernel,
+        [shape_of((TAPS, 64, 64), F32), shape_of((4, 64), F32)],
+        [VM] * 3,
+        [VM] * 2,
+    )(one_keep_sum, one_got_sum, norm_sum)
+    y = lax.axis_index("y")
+    cut = (TAPS, 32, LANES)
+    keep, got = two_keep_sum.reshape(cut), two_got_sum.reshape(cut)
+    grad_two_shard = jnp.where(
+        y == 0, jnp.concatenate([keep, got], axis=1), jnp.concatenate([got, keep], axis=1)
+    )
+    grad_two_shard = jnp.swapaxes(grad_two_shard, 1, 2)
+
+    first_update = adam_step(
+        kernel_one, kernel_one_mean, kernel_one_square, grad_one_shard, factor, (9 * C1) ** (-0.5), WEIGHT_DECAY
+    )
+    second_update = adam_step(
+        kernel_two, kernel_two_mean, kernel_two_square, grad_two_shard, factor, (9 * C2) ** (-0.5), WEIGHT_DECAY
+    )
+    norm_update = adam_step(norm_params, norm_mean, norm_square, norm_shard, factor, GAIN_RATE, 0.0)
+
+    block = (MB, 64, C1)
+    ia_own, ia_mid, ia_far, ia_near, ib_own, ib_mid, ib_far, ib_near = call(
+        input_grad_kernel,
+        ([shape_of(block, F32)] * 2 + [shape_of(block)] * 2) * 2,
+        [VM, VM],
+        [VM] * 8,
+        [pltpu.VMEM((ROWS, TAPS * LANES), BF), pltpu.VMEM((CLIPS_CORE, ROWS, C1), F32)],
+        flops=2 * PIXELS * C1 * TAPS * LANES,
+    )(grad_one, weight_one)
+    ia_got, ib_got = swap(ia_far, "x"), swap(ib_far, "y")
+    ia_near, ib_near = swap(ia_near, "x"), swap(ib_near, "y")
+    ia_next, ib_next = call(pass_on_kernel, [shape_of(block)] * 2, [VM] * 4, [VM] * 2)(
+        ia_mid, ia_got, ib_mid, ib_got
+    )
+    ia_last, ib_last = swap(ia_next, "y"), swap(ib_next, "x")
+    f0, f1, f2, f3 = call(
+        input_sum_kernel, [shape_of((CL_MB, 64, C1))] * MB, [SM, SM] + [VM] * 6, [VM] * 4
+    )(*table, ia_own, ia_near, ia_last, ib_own, ib_near, ib_last)
+    input_grad, pooled = call(
+        finish_kernel,
+        [shape_of((MB * CL_MB, 64, C1)), shape_of((MB * CL_MB, C2), F32)],
+        [SM] + [VM] * 8,
+        [VM] * 2,
+        [pltpu.VMEM((2, MB * CL_MB, C2), F32)],
+    )(clip_order, f0, swap(f1, "z", 1), swap(f2, "z", 2), swap(f3, "z", 3), n0, g1, g2, g3)
+    input_grad = input_grad.reshape(clip_input.shape)
+    return (pooled, input_grad, grad_norm) + first_update + second_update + norm_update
+
+
 def solution(mesh):
-    in_specs = (
-        P("batch", "tm", None, None),
-        P(),
-        P(),
-        P("batch", None),
-        P(None, "batch", "tm"),
-        P(None, "batch", "tm"),
-        P(None, "batch", "tm"),
-        P(None, "batch", "tm"),
-        P(None, "batch", "tm"),
-        P(None, "batch", "tm"),
-        P(None, "tm"),
-        P(None, "tm"),
-        P(None, "tm"),
-    )
-    out_specs = (
-        P("batch", None),
-        P("batch", "tm", None, None),
-        P(),
-        P(None, "batch", "tm"),
-        P(None, "batch", "tm"),
-        P(None, "batch", "tm"),
-        P(None, "batch", "tm"),
-        P(None, "batch", "tm"),
-        P(None, "batch", "tm"),
-        P(None, "batch", "tm"),
-        P(None, "batch", "tm"),
-        P(None, "batch", "tm"),
-        P(None, "batch", "tm"),
-        P(None, "tm"),
-        P(None, "tm"),
-        P(None, "tm"),
-        P(None, "tm"),
-        P(None, "tm"),
-    )
-    return jax.shard_map(body, mesh=mesh, in_specs=in_specs, out_specs=out_specs, check_vma=False)
+    if mesh.shape["tm"] == 2 * MB and mesh.shape["batch"] == 4:
+        grid = Mesh(mesh.devices.reshape(MB, 2, 2, 2), AXES)
+        tm, batch, chosen = ("z", "x"), ("y", "core"), fast_body
+    else:
+        grid, tm, batch, chosen = mesh, "tm", "batch", general_body
+    kernels = (P(None, batch, tm),) * 3
+    norms = (P(None, tm),) * 3
+    in_specs = (P(batch, tm, None, None), P(), P(), P(batch, None)) + 2 * kernels + norms
+    out_specs = (P(batch, None), P(batch, tm, None, None), P())
+    out_specs = out_specs + (P(None, batch, tm),) * 10 + (P(None, tm),) * 5
+    return jax.shard_map(chosen, mesh=grid, in_specs=in_specs, out_specs=out_specs, check_vma=False)

time: 803 us -> 168 us (0.21)
  blocking collectives: 325 us -> 0 us
  waiting for transfers between devices: 156 us -> 53.1 us
  local copies, waits for them, and re-layouts: 82.4 us -> 5.06 us
  matrix products: 55.3 us -> 0 us
  other arithmetic: 53.6 us -> 3.6 us
  Pallas kernels: 0 us -> 38 us
  starting transfers between devices: 99.5 us -> 64.7 us
  between operations: 22.6 us -> 2.97 us
    psum x7 -> x0, blocking collectives: 255 us -> none  [the longest x2 80.6 us: norm_forward(): lax.psum((jnp.sum(masked, axis=(0, 1, 2)), jnp.sum(masked * pre_norm, axi...]
    reduce_scatter x3 -> x0, waiting for transfers between devices: 100 us -> none  [the longest x1 70.6 us: body(): lax.psum_scatter(batch_parts[1], 'tm', scatter_dimension=2, tiled=True)]
    all_gather x2 -> x0, blocking collectives: 70.7 us -> none  [the longest x1 52.6 us: body(): lax.all_gather(low_one, 'tm', axis=2, tiled=True)]
    dot_general x24 -> x0, matrix products: 55.3 us -> none  [the longest x8 33.1 us: contract_rows(): lax.dot_general(columns, grads, (((0,), (0,)), ((), ())), preferred_eleme...]
    unnamed x8 -> x0, waiting for transfers between devices: 47.8 us -> none
    ppermute x32 -> x60, waiting for transfers between devices: 8.1 us -> 49.3 us  [swap(): return lax.ppermute(value, axis, [(i, i ^ step) for i in range(size)])]
    ppermute x32 -> x60, starting transfers between devices: 98.7 us -> 60.4 us  [swap(): return lax.ppermute(value, axis, [(i, i ^ step) for i in range(size)])]
    pallas_call x0 -> x20, Pallas kernels: none -> 38 us  [the longest x1 6.41 us: fast_body(): call(second_weight_grad_kernel, [shape_of((MB, 2, CHUNK, LANES))] * 2, [A...]
  transfers between devices with their start and end apart: 39 -> 61, of which waited for: 5 -> 22; matrix products, arithmetic and copies ran while one was open for 18% -> 1% of each run, Pallas kernels for 0% -> 16%
where the time goes in v2:
time: 168 us; the launch traced here: 167 us
  starting transfers between devices  64.7 us (39%)
  waiting for transfers between devices  53.1 us (32%)
  Pallas kernels  38 us (23%)
  local copies, waits for them, and re-layouts  5.06 us (3%)
  other arithmetic  3.6 us (2%)
  between operations  2.97 us (2%)
    ppermute x60, starting transfers between devices, swap(): return lax.ppermute(value, axis, [(i, i ^ step) for i in range(size)])  60.4 us
    ppermute x60, waiting for transfers between devices, swap(): return lax.ppermute(value, axis, [(i, i ^ step) for i in range(size)])  49.3 us
    pallas_call x1, Pallas kernels, fast_body(): call(second_weight_grad_kernel, [shape_of((MB, 2, CHUNK, LANES))] * 2, [A...  6.41 us
    unnamed x36, local copies, waits for them, and re-layouts  5.02 us
    pallas_call x1, Pallas kernels, fast_body(): call(first_weight_grad_kernel, [shape_of((MB, CHUNK, LANES))] * 2 + [shap...  4.77 us
    pallas_call x1, Pallas kernels, fast_body(): call(first_conv_kernel, [shape_of((PIXELS, LANES), F32), shape_of((PIXELS...  4.73 us
    pallas_call x1, Pallas kernels, fast_body(): call(hidden_grad_kernel, [shape_of((PIXELS, LANES))] + [shape_of((HALF, L...  4.42 us
    all_to_all x1, starting transfers between devices, fast_body(): told = lax.all_to_all(told, AXES, 0, 0, tiled=True)  4.31 us
  transfers between devices with their start and end apart: 61, of which 22 were waited for; matrix products, arithmetic and copies ran while one was open for 1% of the time, Pallas kernels for 16%

profile of v2, /device:TPU:0, one launch (start us, length us, event | category | flops | bytes accessed | tf_op | source)
XLA Modules:
  0.0 167.5 jit_solution(966913665989173066)
XLA Ops:
  6.9 3.1 %collective-permute-start = (bf16[2,64,256]{2,1,0:T(8,128)(2,1)S(1)}, bf16[2,64,256]{2,1,0:T(8,128)(2,1)S(1)}, u32[]{:S(2)}, u32[]{:S(2)}) collective-permute-start(bf16[2,64,256]{2,1,0:T(8,128)(2,1)S(1)} %get-tuple-element.93), channel_id=1, source_target_pairs={{0,8},{8,0},{16,24},{24,16},{1,9},{9,1},{17,25},{25,17},{2,10},{10... | collective-permute-start | bytes 196616 | tf_op jit(solution)/shard_map/ppermute | solution.py:295
  10.0 2.6 %collective-permute-start.1 = (bf16[2,64,256]{2,1,0:T(8,128)(2,1)S(1)}, bf16[2,64,256]{2,1,0:T(8,128)(2,1)S(1)}, u32[]{:S(2)}, u32[]{:S(2)}) collective-permute-start(bf16[2,64,256]{2,1,0:T(8,128)(2,1)S(1)} %get-tuple-element.94), channel_id=1, source_target_pairs={{0,16},{8,24},{16,0},{24,8},{1,17},{9,25},{17,1},{25,9},{2,18},{10... | collective-permute-start | bytes 196616 | tf_op jit(solution)/shard_map/ppermute | solution.py:295
  12.6 1.7 %collective-permute-start.9 = (bf16[144,128]{1,0:T(8,128)(2,1)S(1)}, bf16[144,128]{1,0:T(8,128)(2,1)S(1)}, u32[]{:S(2)}, u32[]{:S(2)}) collective-permute-start(bf16[144,128]{1,0:T(8,128)(2,1)S(1)} %get-tuple-element.97), channel_id=1, source_target_pairs={{0,2},{2,0},{1,3},{3,1},{4,6},{6,4},{5,7},{7,5},{8,10},{10,8},{9,1... | collective-permute-start | bytes 110600 | tf_op jit(solution)/shard_map/ppermute | solution.py:295
  14.7 2.2 %collective-permute-done.9 = bf16[144,128]{1,0:T(8,128)(2,1)S(1)} collective-permute-done((bf16[144,128]{1,0:T(8,128)(2,1)S(1)}, bf16[144,128]{1,0:T(8,128)(2,1)S(1)}, u32[]{:S(2)}, u32[]{:S(2)}) %collective-permute-start.9) | collective-permute-done | bytes 36896 | tf_op jit(solution)/shard_map/ppermute | solution.py:295
  17.7 3.5 %collective-permute-start.11 = (bf16[304,128]{1,0:T(8,128)(2,1)S(1)}, bf16[304,128]{1,0:T(8,128)(2,1)S(1)}, u32[]{:S(2)}, u32[]{:S(2)}) collective-permute-start(bf16[304,128]{1,0:T(8,128)(2,1)S(1)} %constant_dynamic-update-slice_fusion.o0), channel_id=1, source_target_pairs={{0,16},{8,24},{16,0},{24,8},{1,17},{9,25},{17,1},{25,9},{2,18},{10... | collective-permute-start | bytes 233480 | tf_op jit(solution)/shard_map/ppermute | solution.py:295
  23.0 1.6 collective-permute-start.3
  25.2 2.2 %collective-permute-done.12.o3 = bf16[304,128]{1,0:T(8,128)(2,1)S(1)} collective-permute-done((bf16[304,128]{1,0:T(8,128)(2,1)S(1)}, bf16[304,128]{1,0:T(8,128)(2,1)S(1)}, u32[]{:S(2)}, u32[]{:S(2)}) %collective-permute-start.12) | collective-permute-done | bytes 77856 | tf_op jit(solution)/shard_map/ppermute | solution.py:295
  33.7 1.7 %collective-permute-start.26 = (bf16[576,128]{1,0:T(8,128)(2,1)S(1)}, bf16[576,128]{1,0:T(8,128)(2,1)S(1)}, u32[]{:S(2)}, u32[]{:S(2)}) collective-permute-start(bf16[576,128]{1,0:T(8,128)(2,1)S(1)} %pad_maximum_fusion.1.o0), channel_id=1, source_target_pairs={{0,16},{8,24},{16,0},{24,8},{1,17},{9,25},{17,1},{25,9},{2,18},{10... | collective-permute-start | bytes 442376 | tf_op jit(solution)/shard_map/ppermute | solution.py:295
  37.4 4.7 %shard_map.269 = (f32[2048,128]{1,0:T(8,128)S(1)}, bf16[2048,256]{1,0:T(8,128)(2,1)S(1)}, bf16[9,4,32,256]{3,2,1,0:T(8,128)(2,1)S(1)}, f32[8,128]{1,0:T(8,128)S(1)}, f32[8,128]{1,0:T(8,128)S(1)}) custom-call(s32[4,8]{1,0:T(4,128)S(1)} %copy-done.5, s32[32]{0:T(128)S(1)} %copy-done.8, bf16[4,64,256]{2,1,0:T(8,128)(2,1)S(1)} %pad_maximum_fusion.2.a0, ...), custom_call_target="tpu_custom_call" | custom-call | flops 1207959552 | tf_op jit(solution)/shard_map/pallas_call | solution.py:966
  47.7 5.9 %collective-permute-done.27.o3 = bf16[576,128]{1,0:T(8,128)(2,1)S(1)} collective-permute-done((bf16[576,128]{1,0:T(8,128)(2,1)S(1)}, bf16[576,128]{1,0:T(8,128)(2,1)S(1)}, u32[]{:S(2)}, u32[]{:S(2)}) %collective-permute-start.27) | collective-permute-done | bytes 147488 | tf_op jit(solution)/shard_map/ppermute | solution.py:295
  59.0 2.8 %shard_map.271.rest_8_.weight_ref = bf16[9,4,32,512]{3,2,1,0:T(8,128)(2,1)S(1)} custom-call(bf16[576,128]{1,0:T(8,128)(2,1)S(1)} %pad_maximum_fusion.1.o0, bf16[576,128]{1,0:T(8,128)(2,1)S(1)} %collective-permute-done.25.o1, bf16[576,128]{1,0:T(8,128)(2,1)S(1)} %collective-permute-done.26.o2, bf16[576,128]{1,0:T(8,128)(2,1)S(1)} %collective-permute-done.27.o3, ...), custom_call_target="tpu_custom_call" | custom-call | flops 603979776 | tf_op jit(solution)/shard_map/pallas_call | solution.py:985
  63.4 4.6 %collective-permute-done.20.rest_3_ = bf16[1024,128]{1,0:T(8,128)(2,1)S(1)} collective-permute-done((bf16[1024,128]{1,0:T(8,128)(2,1)S(1)}, bf16[1024,128]{1,0:T(8,128)(2,1)S(1)}, u32[]{:S(2)}, u32[]{:S(2)}) %collective-permute-start.20) | collective-permute-done | bytes 262176 | tf_op jit(solution)/shard_map/ppermute | solution.py:295
  68.3 4.0 %shard_map.272 = (f32[2048,128]{1,0:T(8,128)S(1)}, f32[8,128]{1,0:T(8,128)S(1)}) custom-call(s32[4,8]{1,0:T(4,128)S(1)} %copy-done.6, s32[32]{0:T(128)S(1)} %copy-done.8, bf16[1024,128]{1,0:T(8,128)(2,1)S(1)} %get-tuple-element.102.rest_0_, bf16[1024,128]{1,0:T(8,128)(2,1)S(1)} %collective-permute-done.18.rest_1_, ...), custom_call_target="tpu_custom_call" | custom-call | flops 2415919104 | tf_op jit(solution)/shard_map/pallas_call | solution.py:999
  73.5 1.7 %shard_map.273 = (f32[2048,128]{1,0:T(8,128)S(1)}, f32[8,128]{1,0:T(8,128)S(1)}, bf16[16,128]{1,0:T(8,128)(2,1)S(1)}) custom-call(s32[4,8]{1,0:T(4,128)S(1)} %copy-done.6, s32[32]{0:T(128)S(1)} %copy-done.8, f32[2048,128]{1,0:T(8,128)S(1)} %get-tuple-element.106.pre_ref, f32[8,128]{1,0:T(8,128)S(1)} %get-tuple-element.107.own_ref, ...), custom_call_target="tpu_custom_call" | custom-call | tf_op jit(solution)/shard_map/pallas_call | solution.py:1008
  76.5 4.4 %shard_map.274 = (bf16[2048,128]{1,0:T(8,128)(2,1)S(1)}, f32[1024,128]{1,0:T(8,128)S(1)}, f32[1024,128]{1,0:T(8,128)S(1)}, bf16[1024,128]{1,0:T(8,128)(2,1)S(1)}...) custom-call(s32[4,8]{1,0:T(4,128)S(1)} %copy-done.6, ...), custom_call_target="tpu_custom_call" | custom-call | flops 2415919104 | tf_op jit(solution)/shard_map/pallas_call | solution.py:1015
  84.4 6.4 %shard_map.283 = (bf16[4,2,288,128]{3,2,1,0:T(8,128)(2,1)S(1)}, bf16[4,2,288,128]{3,2,1,0:T(8,128)(2,1)S(1)}) custom-call(bf16[1024,128]{1,0:T(8,128)(2,1)S(1)} %get-tuple-element.102.rest_0_, bf16[1024,128]{1,0:T(8,128)(2,1)S(1)} %collective-permute-done.18.rest_1_, bf16[1024,128]{1,0:T(8,128)(2,1)S(1)} %collective-permute-done.19.rest_2_, ...), custom_call_target="tpu_custom_call" | custom-call | flops 2415919104 | tf_op jit(solution)/shard_map/pallas_call | solution.py:1032
  90.9 4.1 %collective-permute-done.35.a_got = bf16[1024,128]{1,0:T(8,128)(2,1)S(1)} collective-permute-done((bf16[1024,128]{1,0:T(8,128)(2,1)S(1)}, bf16[1024,128]{1,0:T(8,128)(2,1)S(1)}, u32[]{:S(2)}, u32[]{:S(2)}) %collective-permute-start.35) | collective-permute-done | bytes 262176 | tf_op jit(solution)/shard_map/ppermute | solution.py:295
  98.8 9.8 %collective-permute-done.38.b_near = bf16[1024,128]{1,0:T(8,128)(2,1)S(1)} collective-permute-done((bf16[1024,128]{1,0:T(8,128)(2,1)S(1)}, bf16[1024,128]{1,0:T(8,128)(2,1)S(1)}, u32[]{:S(2)}, u32[]{:S(2)}) %collective-permute-start.38) | collective-permute-done | bytes 262176 | tf_op jit(solution)/shard_map/ppermute | solution.py:295
  111.2 4.8 %shard_map.277 = (bf16[4,288,128]{2,1,0:T(8,128)(2,1)S(1)}, bf16[4,288,128]{2,1,0:T(8,128)(2,1)S(1)}, bf16[2048,128]{1,0:T(8,128)(2,1)S(1)}) custom-call(s32[4,8]{1,0:T(4,128)S(1)} %copy-done.6, s32[32]{0:T(128)S(1)} %copy-done.8, f32[2048,128]{1,0:T(8,128)S(1)} %get-tuple-element.122.slope_ref, f32[2048,128]{1,0:T(8,128)S(1)} %get-tuple-element.99.pre_ref, ...), custom_call_target="tpu_custom_call" | custom-call | flops 1207959552 | tf_op jit(solution)/shard_map/pallas_call | solution.py:1057
  116.2 1.9 %shard_map.278 = (f32[4,64,256]{2,1,0:T(8,128)S(1)}, f32[4,64,256]{2,1,0:T(8,128)S(1)}, bf16[4,64,256]{2,1,0:T(8,128)(2,1)S(1)}, bf16[4,64,256]{2,1,0:T(8,128)(2...) custom-call(bf16[2048,128]{1,0:T(8,128)(2,1)S(1)} %get-tuple-element, ...), custom_call_target="tpu_custom_call" | custom-call | flops 1207959552 | tf_op jit(solution)/shard_map/pallas_call | solution.py:1131
  118.1 1.6 collective-permute-start.42
  122.5 1.8 %collective-permute-done.42.a_got = bf16[4,64,256]{2,1,0:T(8,128)(2,1)S(1)} collective-permute-done((bf16[4,64,256]{2,1,0:T(8,128)(2,1)S(1)}, bf16[4,64,256]{2,1,0:T(8,128)(2,1)S(1)}, u32[]{:S(2)}, u32[]{:S(2)}) %collective-permute-start.42) | collective-permute-done | bytes 131104 | tf_op jit(solution)/shard_map/ppermute | solution.py:295
  124.3 1.9 %collective-permute-start.56 = (bf16[2,288,128]{2,1,0:T(8,128)(2,1)S(1)}, bf16[2,288,128]{2,1,0:T(8,128)(2,1)S(1)}, u32[]{:S(2)}, u32[]{:S(2)}) collective-permute-start(bf16[2,288,128]{2,1,0:T(8,128)(2,1)S(1)} %get-tuple-element.155), channel_id=1, source_target_pairs={{0,16},{8,24},{16,0},{24,8},{1,17},{9,25},{17,1},{25,9},{2,18},{10... | collective-permute-start | bytes 442376 | tf_op jit(solution)/shard_map/ppermute | solution.py:295
  127.4 1.6 collective-permute-start.45
  129.5 1.6 collective-permute-start.46
  131.3 6.2 %collective-permute-done.56.g2 = bf16[2,288,128]{2,1,0:T(8,128)(2,1)S(1)} collective-permute-done((bf16[2,288,128]{2,1,0:T(8,128)(2,1)S(1)}, bf16[2,288,128]{2,1,0:T(8,128)(2,1)S(1)}, u32[]{:S(2)}, u32[]{:S(2)}) %collective-permute-start.56) | collective-permute-done | bytes 147488 | tf_op jit(solution)/shard_map/ppermute | solution.py:295
  137.5 2.9 %collective-permute-start.52 = (bf16[320,128]{1,0:T(8,128)(2,1)S(1)}, bf16[320,128]{1,0:T(8,128)(2,1)S(1)}, u32[]{:S(2)}, u32[]{:S(2)}) collective-permute-start(bf16[320,128]{1,0:T(8,128)(2,1)S(1)} %get-tuple-element.145), channel_id=1, source_target_pairs={{0,16},{8,24},{16,0},{24,8},{1,17},{9,25},{17,1},{25,9},{2,18},{10... | collective-permute-start | bytes 245768 | tf_op jit(solution)/shard_map/ppermute | solution.py:295
  141.5 2.9 %collective-permute-start.53 = (bf16[320,128]{1,0:T(8,128)(2,1)S(1)}, bf16[320,128]{1,0:T(8,128)(2,1)S(1)}, u32[]{:S(2)}, u32[]{:S(2)}) collective-permute-start(bf16[320,128]{1,0:T(8,128)(2,1)S(1)} %get-tuple-element.146), channel_id=1, source_target_pairs={{0,24},{8,16},{16,8},{24,0},{1,25},{9,17},{17,9},{25,1},{2,26},{10... | collective-permute-start | bytes 245768 | tf_op jit(solution)/shard_map/ppermute | solution.py:295
  146.7 2.9 %collective-permute-start.49 = (bf16[2,64,256]{2,1,0:T(8,128)(2,1)S(1)}, bf16[2,64,256]{2,1,0:T(8,128)(2,1)S(1)}, u32[]{:S(2)}, u32[]{:S(2)}) collective-permute-start(bf16[2,64,256]{2,1,0:T(8,128)(2,1)S(1)} %get-tuple-element.140), channel_id=1, source_target_pairs={{0,24},{8,16},{16,8},{24,0},{1,25},{9,17},{17,9},{25,1},{2,26},{10... | collective-permute-start | bytes 196616 | tf_op jit(solution)/shard_map/ppermute | solution.py:295
  150.3 4.3 %all-to-all-start = ((f32[32,1,128]{2,1,0:T(1,128)}), f32[32,1,128]{2,1,0:T(1,128)S(1)}, u32[]{:S(2)}, u32[]{:S(2)}) async-start(f32[32,1,128]{2,1,0:T(1,128)} %bitcast.4), calls=%async_computation | async-start | bytes 32768 | tf_op jit(solution)/shard_map/all_to_all | solution.py:1104
  154.6 1.8 %collective-permute-start.58 = (f32[152,128]{1,0:T(8,128)S(1)}, f32[152,128]{1,0:T(8,128)S(1)}, u32[]{:S(2)}, u32[]{:S(2)}) collective-permute-start(f32[152,128]{1,0:T(8,128)S(1)} %get-tuple-element.160), channel_id=1, source_target_pairs={{0,2},{2,0},{1,3},{3,1},{4,6},{6,4},{5,7},{7,5},{8,10},{10,8},{9,1... | collective-permute-start | bytes 233480 | tf_op jit(solution)/shard_map/ppermute | solution.py:295
  158.0 3.7 %all-to-all-done = f32[32,1,128]{2,1,0:T(1,128)S(1)} async-done(((f32[32,1,128]{2,1,0:T(1,128)}), f32[32,1,128]{2,1,0:T(1,128)S(1)}, u32[]{:S(2)}, u32[]{:S(2)}) %all-to-all-start) | async-done | bytes 16416 | tf_op jit(solution)/shard_map/all_to_all | solution.py:1104
  (161 shorter events, 57.4 us)
Async XLA Ops:
  6.9 10.7 %collective-permute-start = (bf16[2,64,256]{2,1,0:T(8,128)(2,1)S(1)}, bf16[2,64,256]{2,1,0:T(8,128)(2,1)S(1)}, u32[]{:S(2)}, u32[]{:S(2)}) collective-permute-start(bf16[2,64,256]{2,1,0:T(8,128)(2,1)S(1)} %get-tuple-element.93), channel_id=1, source_target_pairs={{0,8},{8,0},{16,24},{24,16},{1,9},{9,1},{17,25},{25,17},{2,10},{10... | collective-permute-start | bytes 196616 | tf_op jit(solution)/shard_map/ppermute | solution.py:295
  10.0 11.1 %collective-permute-start.1 = (bf16[2,64,256]{2,1,0:T(8,128)(2,1)S(1)}, bf16[2,64,256]{2,1,0:T(8,128)(2,1)S(1)}, u32[]{:S(2)}, u32[]{:S(2)}) collective-permute-start(bf16[2,64,256]{2,1,0:T(8,128)(2,1)S(1)} %get-tuple-element.94), channel_id=1, source_target_pairs={{0,16},{8,24},{16,0},{24,8},{1,17},{9,25},{17,1},{25,9},{2,18},{10... | collective-permute-start | bytes 196616 | tf_op jit(solution)/shard_map/ppermute | solution.py:295
  12.6 8.8 %collective-permute-start.2 = (bf16[2,64,256]{2,1,0:T(8,128)(2,1)S(1)}, bf16[2,64,256]{2,1,0:T(8,128)(2,1)S(1)}, u32[]{:S(2)}, u32[]{:S(2)}) collective-permute-start(bf16[2,64,256]{2,1,0:T(8,128)(2,1)S(1)} %get-tuple-element.95), channel_id=1, source_target_pairs={{0,24},{8,16},{16,8},{24,0},{1,25},{9,17},{17,9},{25,1},{2,26},{10... | collective-permute-start | bytes 196616 | tf_op jit(solution)/shard_map/ppermute | solution.py:295
  21.5 8.9 %collective-permute-start.6 = (bf16[4,64,256]{2,1,0:T(8,128)(2,1)S(1)}, bf16[4,64,256]{2,1,0:T(8,128)(2,1)S(1)}, u32[]{:S(2)}, u32[]{:S(2)}) collective-permute-start(bf16[4,64,256]{2,1,0:T(8,128)(2,1)S(1)} %pad_maximum_fusion.3.b0), channel_id=1, source_target_pairs={{0,2},{2,0},{1,3},{3,1},{4,6},{6,4},{5,7},{7,5},{8,10},{10,8},{9,1... | collective-permute-start | bytes 393224 | tf_op jit(solution)/shard_map/ppermute | solution.py:295
  32.8 14.4 %collective-permute-start.25 = (bf16[576,128]{1,0:T(8,128)(2,1)S(1)}, bf16[576,128]{1,0:T(8,128)(2,1)S(1)}, u32[]{:S(2)}, u32[]{:S(2)}) collective-permute-start(bf16[576,128]{1,0:T(8,128)(2,1)S(1)} %pad_maximum_fusion.1.o0), channel_id=1, source_target_pairs={{0,8},{8,0},{16,24},{24,16},{1,9},{9,1},{17,25},{25,17},{2,10},{10... | collective-permute-start | bytes 442376 | tf_op jit(solution)/shard_map/ppermute | solution.py:295
  33.7 13.5 %collective-permute-start.26 = (bf16[576,128]{1,0:T(8,128)(2,1)S(1)}, bf16[576,128]{1,0:T(8,128)(2,1)S(1)}, u32[]{:S(2)}, u32[]{:S(2)}) collective-permute-start(bf16[576,128]{1,0:T(8,128)(2,1)S(1)} %pad_maximum_fusion.1.o0), channel_id=1, source_target_pairs={{0,16},{8,24},{16,0},{24,8},{1,17},{9,25},{17,1},{25,9},{2,18},{10... | collective-permute-start | bytes 442376 | tf_op jit(solution)/shard_map/ppermute | solution.py:295
  44.3 11.4 %collective-permute-start.18 = (bf16[1024,128]{1,0:T(8,128)(2,1)S(1)}, bf16[1024,128]{1,0:T(8,128)(2,1)S(1)}, u32[]{:S(2)}, u32[]{:S(2)}) collective-permute-start(bf16[1024,128]{1,0:T(8,128)(2,1)S(1)} %get-tuple-element.102.rest_0_), channel_id=1, source_target_pairs={{0,4},{4,0},{1,5},{5,1},{2,6},{6,2},{3,7},{7,3},{8,12},{12,8},{9,1... | collective-permute-start | bytes 786440 | tf_op jit(solution)/shard_map/ppermute | solution.py:295
  44.9 12.2 %collective-permute-start.21 = (bf16[1024,128]{1,0:T(8,128)(2,1)S(1)}, bf16[1024,128]{1,0:T(8,128)(2,1)S(1)}, u32[]{:S(2)}, u32[]{:S(2)}) collective-permute-start(bf16[1024,128]{1,0:T(8,128)(2,1)S(1)} %get-tuple-element.103.rest_4_), channel_id=1, source_target_pairs={{0,2},{2,0},{1,3},{3,1},{4,6},{6,4},{5,7},{7,5},{8,10},{10,8},{9,1... | collective-permute-start | bytes 786440 | tf_op jit(solution)/shard_map/ppermute | solution.py:295
  53.6 9.1 %collective-permute-start.19 = (bf16[1024,128]{1,0:T(8,128)(2,1)S(1)}, bf16[1024,128]{1,0:T(8,128)(2,1)S(1)}, u32[]{:S(2)}, u32[]{:S(2)}) collective-permute-start(bf16[1024,128]{1,0:T(8,128)(2,1)S(1)} %get-tuple-element.102.rest_0_), channel_id=1, source_target_pairs={{0,2},{2,0},{1,3},{3,1},{4,6},{6,4},{5,7},{7,5},{8,10},{10,8},{9,1... | collective-permute-start | bytes 786440 | tf_op jit(solution)/shard_map/ppermute | solution.py:295
  54.2 9.1 %collective-permute-start.22 = (bf16[1024,128]{1,0:T(8,128)(2,1)S(1)}, bf16[1024,128]{1,0:T(8,128)(2,1)S(1)}, u32[]{:S(2)}, u32[]{:S(2)}) collective-permute-start(bf16[1024,128]{1,0:T(8,128)(2,1)S(1)} %get-tuple-element.103.rest_4_), channel_id=1, source_target_pairs={{0,4},{4,0},{1,5},{5,1},{2,6},{6,2},{3,7},{7,3},{8,12},{12,8},{9,1... | collective-permute-start | bytes 786440 | tf_op jit(solution)/shard_map/ppermute | solution.py:295
  55.7 12.2 %collective-permute-start.20 = (bf16[1024,128]{1,0:T(8,128)(2,1)S(1)}, bf16[1024,128]{1,0:T(8,128)(2,1)S(1)}, u32[]{:S(2)}, u32[]{:S(2)}) collective-permute-start(bf16[1024,128]{1,0:T(8,128)(2,1)S(1)} %collective-permute-done.18.rest_1_), channel_id=1, source_target_pairs={{0,2},{2,0},{1,3},{3,1},{4,6},{6,4},{5,7},{7,5},{8,10},{10,8},{9,1... | collective-permute-start | bytes 786440 | tf_op jit(solution)/shard_map/ppermute | solution.py:295
  57.1 11.1 %collective-permute-start.23 = (bf16[1024,128]{1,0:T(8,128)(2,1)S(1)}, bf16[1024,128]{1,0:T(8,128)(2,1)S(1)}, u32[]{:S(2)}, u32[]{:S(2)}) collective-permute-start(bf16[1024,128]{1,0:T(8,128)(2,1)S(1)} %collective-permute-done.21.rest_5_), channel_id=1, source_target_pairs={{0,4},{4,0},{1,5},{5,1},{2,6},{6,2},{3,7},{7,3},{8,12},{12,8},{9,1... | collective-permute-start | bytes 786440 | tf_op jit(solution)/shard_map/ppermute | solution.py:295
  80.9 14.3 %collective-permute-start.34 = (bf16[1040,128]{1,0:T(8,128)(2,1)S(1)}, bf16[1040,128]{1,0:T(8,128)(2,1)S(1)}, u32[]{:S(2)}, u32[]{:S(2)}) collective-permute-start(bf16[1040,128]{1,0:T(8,128)(2,1)S(1)} %get-tuple-element.113), channel_id=1, source_target_pairs={{0,4},{4,0},{1,5},{5,1},{2,6},{6,2},{3,7},{7,3},{8,12},{12,8},{9,1... | collective-permute-start | bytes 798728 | tf_op jit(solution)/shard_map/ppermute | solution.py:295
  82.5 12.6 %collective-permute-start.35 = (bf16[1024,128]{1,0:T(8,128)(2,1)S(1)}, bf16[1024,128]{1,0:T(8,128)(2,1)S(1)}, u32[]{:S(2)}, u32[]{:S(2)}) collective-permute-start(bf16[1024,128]{1,0:T(8,128)(2,1)S(1)} %get-tuple-element.115), channel_id=1, source_target_pairs={{0,4},{4,0},{1,5},{5,1},{2,6},{6,2},{3,7},{7,3},{8,12},{12,8},{9,1... | collective-permute-start | bytes 786440 | tf_op jit(solution)/shard_map/ppermute | solution.py:295
  83.0 12.1 %collective-permute-start.36 = (bf16[1024,128]{1,0:T(8,128)(2,1)S(1)}, bf16[1024,128]{1,0:T(8,128)(2,1)S(1)}, u32[]{:S(2)}, u32[]{:S(2)}) collective-permute-start(bf16[1024,128]{1,0:T(8,128)(2,1)S(1)} %get-tuple-element.117), channel_id=1, source_target_pairs={{0,2},{2,0},{1,3},{3,1},{4,6},{6,4},{5,7},{7,5},{8,10},{10,8},{9,1... | collective-permute-start | bytes 786440 | tf_op jit(solution)/shard_map/ppermute | solution.py:295
  90.8 30.8 %collective-permute-start.54 = (bf16[4,2,288,128]{3,2,1,0:T(8,128)(2,1)S(1)}, bf16[4,2,288,128]{3,2,1,0:T(8,128)(2,1)S(1)}, u32[]{:S(2)}, u32[]{:S(2)}) collective-permute-start(bf16[4,2,288,128]{3,2,1,0:T(8,128)(2,1)S(1)} %get-tuple-element.152), channel_id=1, source_target_pairs={{0,1},{1,0},{2,3},{3,2},{4,5},{5,4},{6,7},{7,6},{8,9},{9,8},{10,11... | collective-permute-start | bytes 1769480 | tf_op jit(solution)/shard_map/ppermute | solution.py:295
  95.2 13.4 %collective-permute-start.37 = (bf16[1056,128]{1,0:T(8,128)(2,1)S(1)}, bf16[1056,128]{1,0:T(8,128)(2,1)S(1)}, u32[]{:S(2)}, u32[]{:S(2)}) collective-permute-start(bf16[1056,128]{1,0:T(8,128)(2,1)S(1)} %pad_maximum_fusion), channel_id=1, source_target_pairs={{0,2},{2,0},{1,3},{3,1},{4,6},{6,4},{5,7},{7,5},{8,10},{10,8},{9,1... | collective-permute-start | bytes 811016 | tf_op jit(solution)/shard_map/ppermute | solution.py:295
  96.7 11.9 %collective-permute-start.38 = (bf16[1024,128]{1,0:T(8,128)(2,1)S(1)}, bf16[1024,128]{1,0:T(8,128)(2,1)S(1)}, u32[]{:S(2)}, u32[]{:S(2)}) collective-permute-start(bf16[1024,128]{1,0:T(8,128)(2,1)S(1)} %get-tuple-element.120), channel_id=1, source_target_pairs={{0,2},{2,0},{1,3},{3,1},{4,6},{6,4},{5,7},{7,5},{8,10},{10,8},{9,1... | collective-permute-start | bytes 786440 | tf_op jit(solution)/shard_map/ppermute | solution.py:295
  97.3 11.3 %collective-permute-start.39 = (bf16[1024,128]{1,0:T(8,128)(2,1)S(1)}, bf16[1024,128]{1,0:T(8,128)(2,1)S(1)}, u32[]{:S(2)}, u32[]{:S(2)}) collective-permute-start(bf16[1024,128]{1,0:T(8,128)(2,1)S(1)} %get-tuple-element.121), channel_id=1, source_target_pairs={{0,4},{4,0},{1,5},{5,1},{2,6},{6,2},{3,7},{7,3},{8,12},{12,8},{9,1... | collective-permute-start | bytes 786440 | tf_op jit(solution)/shard_map/ppermute | solution.py:295
  116.0 13.5 %collective-permute-start.50 = (bf16[4,288,128]{2,1,0:T(8,128)(2,1)S(1)}, bf16[4,288,128]{2,1,0:T(8,128)(2,1)S(1)}, u32[]{:S(2)}, u32[]{:S(2)}) collective-permute-start(bf16[4,288,128]{2,1,0:T(8,128)(2,1)S(1)} %get-tuple-element.142), channel_id=1, source_target_pairs={{0,1},{1,0},{2,3},{3,2},{4,5},{5,4},{6,7},{7,6},{8,9},{9,8},{10,11... | collective-permute-start | bytes 884744 | tf_op jit(solution)/shard_map/ppermute | solution.py:295
  124.3 13.1 %collective-permute-start.56 = (bf16[2,288,128]{2,1,0:T(8,128)(2,1)S(1)}, bf16[2,288,128]{2,1,0:T(8,128)(2,1)S(1)}, u32[]{:S(2)}, u32[]{:S(2)}) collective-permute-start(bf16[2,288,128]{2,1,0:T(8,128)(2,1)S(1)} %get-tuple-element.155), channel_id=1, source_target_pairs={{0,16},{8,24},{16,0},{24,8},{1,17},{9,25},{17,1},{25,9},{2,18},{10... | collective-permute-start | bytes 442376 | tf_op jit(solution)/shard_map/ppermute | solution.py:295
  126.2 11.3 %collective-permute-start.57 = (bf16[2,288,128]{2,1,0:T(8,128)(2,1)S(1)}, bf16[2,288,128]{2,1,0:T(8,128)(2,1)S(1)}, u32[]{:S(2)}, u32[]{:S(2)}) collective-permute-start(bf16[2,288,128]{2,1,0:T(8,128)(2,1)S(1)} %get-tuple-element.156), channel_id=1, source_target_pairs={{0,24},{8,16},{16,8},{24,0},{1,25},{9,17},{17,9},{25,1},{2,26},{10... | collective-permute-start | bytes 442376 | tf_op jit(solution)/shard_map/ppermute | solution.py:295
  127.4 13.2 %collective-permute-start.45 = (bf16[4,64,256]{2,1,0:T(8,128)(2,1)S(1)}, bf16[4,64,256]{2,1,0:T(8,128)(2,1)S(1)}, u32[]{:S(2)}, u32[]{:S(2)}) collective-permute-start(bf16[4,64,256]{2,1,0:T(8,128)(2,1)S(1)} %get-tuple-element.135), channel_id=1, source_target_pairs={{0,2},{2,0},{1,3},{3,1},{4,6},{6,4},{5,7},{7,5},{8,10},{10,8},{9,1... | collective-permute-start | bytes 393224 | tf_op jit(solution)/shard_map/ppermute | solution.py:295
  129.0 12.5 %collective-permute-start.44 = (bf16[4,64,256]{2,1,0:T(8,128)(2,1)S(1)}, bf16[4,64,256]{2,1,0:T(8,128)(2,1)S(1)}, u32[]{:S(2)}, u32[]{:S(2)}) collective-permute-start(bf16[4,64,256]{2,1,0:T(8,128)(2,1)S(1)} %get-tuple-element.133), channel_id=1, source_target_pairs={{0,2},{2,0},{1,3},{3,1},{4,6},{6,4},{5,7},{7,5},{8,10},{10,8},{9,1... | collective-permute-start | bytes 393224 | tf_op jit(solution)/shard_map/ppermute | solution.py:295
  129.5 14.9 %collective-permute-start.46 = (bf16[4,64,256]{2,1,0:T(8,128)(2,1)S(1)}, bf16[4,64,256]{2,1,0:T(8,128)(2,1)S(1)}, u32[]{:S(2)}, u32[]{:S(2)}) collective-permute-start(bf16[4,64,256]{2,1,0:T(8,128)(2,1)S(1)} %get-tuple-element.136), channel_id=1, source_target_pairs={{0,4},{4,0},{1,5},{5,1},{2,6},{6,2},{3,7},{7,3},{8,12},{12,8},{9,1... | collective-permute-start | bytes 393224 | tf_op jit(solution)/shard_map/ppermute | solution.py:295
  137.5 9.2 %collective-permute-start.52 = (bf16[320,128]{1,0:T(8,128)(2,1)S(1)}, bf16[320,128]{1,0:T(8,128)(2,1)S(1)}, u32[]{:S(2)}, u32[]{:S(2)}) collective-permute-start(bf16[320,128]{1,0:T(8,128)(2,1)S(1)} %get-tuple-element.145), channel_id=1, source_target_pairs={{0,16},{8,24},{16,0},{24,8},{1,17},{9,25},{17,1},{25,9},{2,18},{10... | collective-permute-start | bytes 245768 | tf_op jit(solution)/shard_map/ppermute | solution.py:295
  140.6 22.5 %collective-permute-start.59 = (f32[288,128]{1,0:T(8,128)S(1)}, f32[288,128]{1,0:T(8,128)S(1)}, u32[]{:S(2)}, u32[]{:S(2)}) collective-permute-start(f32[288,128]{1,0:T(8,128)S(1)} %get-tuple-element.164), channel_id=1, source_target_pairs={{0,2},{2,0},{1,3},{3,1},{4,6},{6,4},{5,7},{7,5},{8,10},{10,8},{9,1... | collective-permute-start | bytes 442376 | tf_op jit(solution)/shard_map/ppermute | solution.py:295
  145.1 11.3 %collective-permute-start.47 = (bf16[2,64,256]{2,1,0:T(8,128)(2,1)S(1)}, bf16[2,64,256]{2,1,0:T(8,128)(2,1)S(1)}, u32[]{:S(2)}, u32[]{:S(2)}) collective-permute-start(bf16[2,64,256]{2,1,0:T(8,128)(2,1)S(1)} %get-tuple-element.138), channel_id=1, source_target_pairs={{0,8},{8,0},{16,24},{24,16},{1,9},{9,1},{17,25},{25,17},{2,10},{10... | collective-permute-start | bytes 196616 | tf_op jit(solution)/shard_map/ppermute | solution.py:295
  145.2 11.3 %collective-permute-start.48 = (bf16[2,64,256]{2,1,0:T(8,128)(2,1)S(1)}, bf16[2,64,256]{2,1,0:T(8,128)(2,1)S(1)}, u32[]{:S(2)}, u32[]{:S(2)}) collective-permute-start(bf16[2,64,256]{2,1,0:T(8,128)(2,1)S(1)} %get-tuple-element.139), channel_id=1, source_target_pairs={{0,16},{8,24},{16,0},{24,8},{1,17},{9,25},{17,1},{25,9},{2,18},{10... | collective-permute-start | bytes 196616 | tf_op jit(solution)/shard_map/ppermute | solution.py:295
  146.7 9.8 %collective-permute-start.49 = (bf16[2,64,256]{2,1,0:T(8,128)(2,1)S(1)}, bf16[2,64,256]{2,1,0:T(8,128)(2,1)S(1)}, u32[]{:S(2)}, u32[]{:S(2)}) collective-permute-start(bf16[2,64,256]{2,1,0:T(8,128)(2,1)S(1)} %get-tuple-element.140), channel_id=1, source_target_pairs={{0,24},{8,16},{16,8},{24,0},{1,25},{9,17},{17,9},{25,1},{2,26},{10... | collective-permute-start | bytes 196616 | tf_op jit(solution)/shard_map/ppermute | solution.py:295
  150.3 11.4 %all-to-all-start = ((f32[32,1,128]{2,1,0:T(1,128)}), f32[32,1,128]{2,1,0:T(1,128)S(1)}, u32[]{:S(2)}, u32[]{:S(2)}) async-start(f32[32,1,128]{2,1,0:T(1,128)} %bitcast.4), calls=%async_computation | async-start | bytes 32768 | tf_op jit(solution)/shard_map/all_to_all | solution.py:1104
  154.6 9.7 %collective-permute-start.58 = (f32[152,128]{1,0:T(8,128)S(1)}, f32[152,128]{1,0:T(8,128)S(1)}, u32[]{:S(2)}, u32[]{:S(2)}) collective-permute-start(f32[152,128]{1,0:T(8,128)S(1)} %get-tuple-element.160), channel_id=1, source_target_pairs={{0,2},{2,0},{1,3},{3,1},{4,6},{6,4},{5,7},{7,5},{8,10},{10,8},{9,1... | collective-permute-start | bytes 233480 | tf_op jit(solution)/shard_map/ppermute | solution.py:295
  (46 other events, 290.5 us)

commit v3 on v2

--- a/solution.py
+++ b/solution.py
@@ -7,6 +7,7 @@
 from jax.experimental.pallas import tpu as pltpu
 from jax.sharding import Mesh, PartitionSpec as P
 
+OPT = {'flop': 200000000.0, 'zorder': [2, 3, 1], 'merge_w': False, 'w1_after_in': False, 'core_w1': 1, 'core_w1_after_xy': False, 'fwd_after_core_w1': False, 'w2_after': 0, 'w2_before': 1, 'core_w2_after': 1, 'kw2_after': False, 'rs': 'two', 'pass_after_g2': True, 'pass_after_near': False, 'core_g2_after': True, 'k5_after': True, 'core1_after_g2': False, 'core_g1_after_g2': True, 'a2a_after_core1': False, 'sum_after_f': False, 'sum_after_y': True, 'f_after_sum': False, 'told_after_f': True, 'core_w1_after': 0, 'y2_after': 1}
 C1 = 256
 C2 = 512
 MEL = 8
@@ -271,22 +272,26 @@
 ANY = pl.BlockSpec(memory_space=pl.ANY)
 VM = pl.BlockSpec(memory_space=pltpu.VMEM)
 SM = pl.BlockSpec(memory_space=pltpu.SMEM)
-VMEM_LIMIT = 28 * 1024 * 1024
+HB = pl.BlockSpec(memory_space=pltpu.HBM)
+VMEM_LIMIT = 16 * 1024 * 1024
 
 
 def shape_of(shape, dtype=BF):
     return jax.ShapeDtypeStruct(shape, dtype)
 
 
-def call(kernel, out, in_specs, out_specs, scratch=(), flops=0, moved=0):
+def call(kernel, out, in_specs, out_specs, scratch=(), limit=VMEM_LIMIT):
+    cost = COSTS[kernel]
     return pl.pallas_call(
         kernel,
         out_shape=out,
         in_specs=in_specs,
         out_specs=out_specs,
         scratch_shapes=list(scratch),
-        compiler_params=pltpu.CompilerParams(vmem_limit_bytes=VMEM_LIMIT),
-        cost_estimate=pl.CostEstimate(flops=flops, bytes_accessed=moved, transcendentals=0),
+        compiler_params=pltpu.CompilerParams(vmem_limit_bytes=limit),
+        cost_estimate=pl.CostEstimate(
+            flops=int(cost * FLOP_SCALE), bytes_accessed=int(cost * BYTE_SCALE), transcendentals=0
+        ),
     )
 
 
@@ -295,10 +300,10 @@
     return lax.ppermute(value, axis, [(i, i ^ step) for i in range(size)])
 
 
-def start_copies(copies, sems):
+def start_copies(copies, sems, base=0):
     started = []
     for at, (source, target) in enumerate(copies):
-        copy = pltpu.make_async_copy(source, target, sems.at[at])
+        copy = pltpu.make_async_copy(source, target, sems.at[base + at])
         copy.start()
         started.append(copy)
     return started
@@ -314,23 +319,41 @@
     return found if len(found) > 1 else found[0]
 
 
-def clip_counts(order_ref, counts_ref):
+def after(value, *others):
+    return lax.optimization_barrier((value,) + others)[0]
+
+
+def pin(name, value, *others):
+    return after(value, *others) if OPT[name] else value
+
+
+def steps_of():
+    return OPT["zorder"]
+
+
+def write_facts(order_ref, counts_ref, facts_ref):
     z, core = place("z", "core")
-    counts = []
-    for group in range(2):
-        for j in range(CL_MB):
-            row = group * 2 + core
-            counts.append(counts_ref[row * 8 + order_ref[row, z * CL_MB + j]])
-    return counts
-
-
-def pixel_count(order_ref, counts_ref):
-    z = place("z")
+    row_of = lax.broadcasted_iota(jnp.int32, (8, LANES), 0)
+    facts = jnp.zeros((8, LANES), jnp.int32)
     total = 0
     for row in range(4):
         for j in range(CL_MB):
             total = total + counts_ref[row * 8 + order_ref[row, z * CL_MB + j]]
-    return (MEL * total).astype(F32)
+    facts = jnp.where(row_of == 4, MEL * total, facts)
+    for group in range(2):
+        for j in range(CL_MB):
+            row = group * 2 + core
+            count = counts_ref[row * 8 + order_ref[row, z * CL_MB + j]]
+            facts = jnp.where(row_of == group * CL_MB + j, count, facts)
+    facts_ref[...] = facts
+
+
+def count_row(facts_ref, clip):
+    return facts_ref[clip : clip + 1, :]
+
+
+def pixel_row(facts_ref):
+    return facts_ref[4:5, :].astype(F32)
 
 
 def time_shift(rows, step):
@@ -352,9 +375,9 @@
     return jnp.where(keep, turned, 0.0).reshape(rows.shape)
 
 
-def valid_rows(count, width):
-    frame = lax.broadcasted_iota(jnp.int32, (ROWS, width), 0) // MEL
-    return (frame < count).astype(F32)
+def valid_rows(facts_ref, clip):
+    frame = lax.broadcasted_iota(jnp.int32, (ROWS, LANES), 0) // MEL
+    return (frame < count_row(facts_ref, clip)).astype(F32)
 
 
 def dot_nt(left, right):
@@ -429,18 +452,23 @@
 
 
 def prepare_kernel(
-    order_ref, clip_ref, one_ref, two_ref, norm_ref, cot_ref, p0, p1, p2, p3, one_keep, one_send,
-    two_keep, two_send, gain_ref, cot_own, sems
+    order_ref, counts_ref, clip_ref, one_in, two_in, norm_in, cot_in, p0, p1, p2, p3, one_keep,
+    two_keep, send_ref, gain_ref, cot_own, facts_ref, one_ref, two_ref, norm_ref, cot_ref, sems
 ):
     z, x, y, core = place(*AXES)
     group = y * 2 + core
+    loads = start_copies(
+        [(one_in, one_ref), (two_in, two_ref), (norm_in, norm_ref), (cot_in, cot_ref)], sems
+    )
     copies = []
     for step, piece in enumerate((p0, p1, p2, p3)):
         plane = jnp.bitwise_xor(z, step)
         for j in range(CL_MB):
             clip = order_ref[group, plane * CL_MB + j]
             copies.append((clip_ref.at[clip], piece.at[j]))
-    started = start_copies(copies, sems)
+    started = start_copies(copies, sems, 4)
+    write_facts(order_ref, counts_ref, facts_ref)
+    wait_all(loads)
     for tap in range(TAPS):
         turned = jnp.swapaxes(one_ref[tap], 0, 1)
         rows = [turned[at * 16 : (at + 1) * 16] for at in range(4)]
@@ -448,11 +476,12 @@
         high = jnp.concatenate([rows[2], rows[3]], axis=1).astype(BF)
         span = slice(tap * 16, (tap + 1) * 16)
         one_keep[span, :] = jnp.where(y == 0, low, high)
-        one_send[span, :] = jnp.where(y == 0, high, low)
+        send_ref[span, :] = jnp.where(y == 0, high, low)
         low, high = two_ref[tap, 0:32, :].astype(BF), two_ref[tap, 32:64, :].astype(BF)
         span = slice(tap * 32, (tap + 1) * 32)
         two_keep[span, :] = jnp.where(y == 0, low, high)
-        two_send[span, :] = jnp.where(y == 0, high, low)
+        span = slice(144 + tap * 32, 144 + (tap + 1) * 32)
+        send_ref[span, :] = jnp.where(y == 0, high, low)
     wide = jnp.concatenate([norm_ref[...], norm_ref[...]], axis=1)
     wide = jnp.concatenate([wide, jnp.zeros((4, LANES), F32)], axis=0)
     turned = pltpu.roll(wide, (z * 32 - y * 32) % LANES, 1)
@@ -481,25 +510,25 @@
     middle = [row.astype(BF).astype(F32) for row in rest]
     low = [row - top for row, top in zip(rest, middle)]
     packed = jnp.concatenate(high + middle + low + [jnp.zeros((10, LANES), F32)], axis=0)
-    two_send[CHUNK : CHUNK + 16, :] = packed.astype(BF)
+    send_ref[144 + CHUNK : 160 + CHUNK, :] = packed.astype(BF)
     wait_all(started)
 
 
 def first_conv_kernel(
-    order_ref, counts_ref, a0, a1, a2, a3, b0, b1, b2, b3, o0, o1, o2, o3, s0, s1, s2, s3,
+    facts_ref, a0, a1, a23, b0, b1, b23, o0, o1, o2, o3, others,
     pre_ref, x_ref, weight_ref, stat_ref, gain_ref, sems
 ):
     z, x, y, core = place(*AXES)
     copies = []
     for j, pieces in (
-        (0, ((a0, x, y), (a1, 1 - x, y), (a2, x, 1 - y), (a3, 1 - x, 1 - y))),
-        (1, ((b0, x, y), (b1, x, 1 - y), (b2, 1 - x, y), (b3, 1 - x, 1 - y))),
+        (0, ((a0, 0, x, y), (a1, 0, 1 - x, y), (a23, 0, x, 1 - y), (a23, MB, 1 - x, 1 - y))),
+        (1, ((b0, 0, x, y), (b1, 0, x, 1 - y), (b23, 0, 1 - x, y), (b23, MB, 1 - x, 1 - y))),
     ):
-        for source, x_of, y_of in pieces:
+        for source, base, x_of, y_of in pieces:
             for step in range(MB):
                 frames = (jnp.bitwise_xor(z, step) * 2 + x_of) * 64
                 row = pl.multiple_of((y_of * CL_MB + j) * ROWS + frames, 64)
-                copies.append((source.at[step], x_ref.at[pl.ds(row, 64), :]))
+                copies.append((source.at[base + step], x_ref.at[pl.ds(row, 64), :]))
     started = start_copies(copies, sems)
     gains = jnp.zeros((8, LANES), F32)
     for half in range(2):
@@ -510,8 +539,9 @@
             return from_core * 256 + from_y * 128 + half * 64 + column % 64
 
         spread = exchange_matrix(512, C1, source_of)
-        for step, (own, other) in enumerate(((o0, s0), (o1, s1), (o2, s2), (o3, s3))):
+        for step, own in enumerate((o0, o1, o2, o3)):
             z_of = jnp.bitwise_xor(z, step)
+            other = others[step * 304 : step * 304 + 288]
             four = jnp.concatenate([own[0:144], own[144:288], other[0:144], other[144:288]], axis=1)
             both = dot_nn(four, spread).astype(BF)
             for tap in range(TAPS):
@@ -519,45 +549,43 @@
             if half == 0:
                 gains = gains + own[CHUNK : CHUNK + 16].astype(F32)[0:8]
     gain_ref[...] = gains
-    counts = clip_counts(order_ref, counts_ref)
     wait_all(started)
     weight = weight_ref[...].reshape(TAPS * LANES, C1)
     first = jnp.zeros((1, LANES), F32)
     second = jnp.zeros((1, LANES), F32)
     for clip in range(CLIPS_CORE):
         span = slice(clip * ROWS, (clip + 1) * ROWS)
-        mask = valid_rows(counts[clip], C1)
-        masked = x_ref[span, :] * mask.astype(BF)
+        mask = valid_rows(facts_ref, clip)
+        masked = x_ref[span, :] * jnp.concatenate([mask, mask], axis=1).astype(BF)
         x_ref[span, :] = masked
         pre = gather_taps(dot_nt(masked, weight))
         pre_ref[span, :] = pre
-        kept = pre * mask[:, 0:LANES]
+        kept = pre * mask
         plus = channel_sums(kept, kept * pre)
         first, second = first + plus[0], second + plus[1]
     put_pair(stat_ref, first, second)
 
 
-def hidden_kernel(order_ref, counts_ref, pre_ref, own_ref, other_ref, gain_ref, a_ref, b_ref):
-    mean, scale = norm_rows(own_ref, other_ref, pixel_count(order_ref, counts_ref))
-    counts = clip_counts(order_ref, counts_ref)
+def hidden_kernel(facts_ref, pre_ref, own_ref, other_ref, gain_ref, a_ref, b_ref):
+    mean, scale = norm_rows(own_ref, other_ref, pixel_row(facts_ref))
     for clip in range(CLIPS_CORE):
         pre = pre_ref[clip * ROWS : (clip + 1) * ROWS, :]
         shaped = gain_ref[0:1, :] * ((pre - mean) * scale) + gain_ref[1:2, :]
-        value = shaped * jax.nn.sigmoid(shaped) * valid_rows(counts[clip], LANES)
+        value = shaped * jax.nn.sigmoid(shaped) * valid_rows(facts_ref, clip)
         target = a_ref if clip < 2 else b_ref
         target[(clip % 2) * ROWS : (clip % 2 + 1) * ROWS, :] = value.astype(BF)
 
 
-def second_weight_kernel(o0, o1, o2, o3, s0, s1, s2, s3, weight_ref, pieces, sems):
+def second_weight_kernel(own_ref, other_ref, weight_ref, pieces, sems):
     z, y, core = place("z", "y", "core")
     copies = []
-    for step, (own, other) in enumerate(((o0, s0), (o1, s1), (o2, s2), (o3, s3))):
-        for source, core_of in ((own, core), (other, 1 - core)):
+    for step in range(MB):
+        for source, core_of in ((own_ref, core), (other_ref, 1 - core)):
             for turn in range(2):
                 part = jnp.bitwise_xor(y, turn) * 2 + core_of
                 copies.append(
                     (
-                        source.at[pl.ds(turn * CHUNK, CHUNK), :],
+                        source.at[pl.ds((step * 2 + turn) * CHUNK, CHUNK), :],
                         pieces.at[jnp.bitwise_xor(z, step), part],
                     )
                 )
@@ -581,10 +609,9 @@
     return copies
 
 
-def second_conv_kernel(order_ref, counts_ref, *rest):
+def second_conv_kernel(facts_ref, *rest):
     parts, (weight_ref, pre_ref, stat_ref, hidden, sems) = rest[:8], rest[8:]
     started = start_copies(hidden_copies(parts, hidden), sems)
-    counts = clip_counts(order_ref, counts_ref)
     weight = weight_ref[...].reshape(TAPS * LANES, C2)
     wait_all(started)
     first = jnp.zeros((1, LANES), F32)
@@ -593,31 +620,30 @@
         span = slice(clip * ROWS, (clip + 1) * ROWS)
         pre = gather_taps(dot_nt(hidden[span, :], weight))
         pre_ref[span, :] = pre
-        kept = pre * valid_rows(counts[clip], LANES)
+        kept = pre * valid_rows(facts_ref, clip)
         plus = channel_sums(kept, kept * pre)
         first, second = first + plus[0], second + plus[1]
     put_pair(stat_ref, first, second)
 
 
 def pool_kernel(
-    order_ref, counts_ref, pre_ref, own_ref, other_ref, gain_ref, cot_own, cot_got,
+    facts_ref, pre_ref, own_ref, other_ref, gain_ref, cot_own, cot_got,
     slope_ref, sum_ref, pooled_ref
 ):
     y = place("y")
-    counts = clip_counts(order_ref, counts_ref)
-    mean, scale = norm_rows(own_ref, other_ref, pixel_count(order_ref, counts_ref))
+    mean, scale = norm_rows(own_ref, other_ref, pixel_row(facts_ref))
     first = jnp.zeros((1, LANES), F32)
     second = jnp.zeros((1, LANES), F32)
     slots = ROWS // (2 * MEL)
-    got = cot_got[CHUNK : CHUNK + 16, :].astype(F32)
+    got = cot_got[144 + CHUNK : 160 + CHUNK, :].astype(F32)
     pooled = []
     for clip in range(CLIPS_CORE):
         span = slice(clip * ROWS, (clip + 1) * ROWS)
-        count = counts[clip]
+        count = count_row(facts_ref, clip)
         j = clip % CL_MB
         told = got[j : j + 1] + got[2 + j : 3 + j] + got[4 + j : 5 + j]
         cot = jnp.where(y == clip // CL_MB, cot_own[j : j + 1, :], told)
-        mask = valid_rows(count, LANES)
+        mask = valid_rows(facts_ref, clip)
         normed = (pre_ref[span, :] - mean) * scale
         shaped = gain_ref[2:3, :] * normed + gain_ref[3:4, :]
         gate = jax.nn.sigmoid(shaped)
@@ -649,78 +675,121 @@
     return mask * (scale * gain) * (slope - sums[0] / pixels - normed * (sums[1] / pixels))
 
 
-def hidden_grad_kernel(
-    order_ref, counts_ref, slope_ref, pre_ref, own_ref, other_ref, sum_own, sum_other, gain_ref,
-    weight_ref, pooled_ref, grad_ref, a_own, a_mid, a_far, a_near, b_own, b_mid, b_far, b_near,
-    columns, partial
+def grad_columns_kernel(
+    facts_ref, slope_ref, pre_ref, own_ref, other_ref, sum_own, sum_other, gain_ref, weight_ref,
+    columns, a_far, b_far
 ):
     x, y = place("x", "y")
-    counts = clip_counts(order_ref, counts_ref)
-    pixels = pixel_count(order_ref, counts_ref)
+    pixels = pixel_row(facts_ref)
+    mean, scale = norm_rows(own_ref, other_ref, pixels)
+    sums = pair_sums(sum_own, sum_other)
+    lane = pl.multiple_of(((1 - x) * 2 + 1 - y) * LANES, LANES)
+    weight = weight_ref[:, :, :, pl.ds(lane, LANES)].reshape(TAPS * LANES, LANES)
+    for clip in range(CLIPS_CORE):
+        span = slice(clip * ROWS, (clip + 1) * ROWS)
+        mask = valid_rows(facts_ref, clip)
+        grad = pre_grad(
+            slope_ref[span, :], pre_ref[span, :], mask, mean, scale, gain_ref[2:3, :], sums, pixels
+        )
+        scatter_taps(grad, columns, clip * ROWS)
+        rows = slice((clip % 2) * ROWS, (clip % 2 + 1) * ROWS)
+        target = a_far if clip < 2 else b_far
+        target[rows, :] = dot_nn(columns[span, :], weight).astype(BF)
+
+
+def hidden_grad_kernel(
+    columns, weight_ref, pooled_ref, a_own, a_mid, a_near, b_own, b_mid, b_near, partial
+):
+    x, y = place("x", "y")
+    weight = weight_ref[...].reshape(TAPS * LANES, C2)
+    a_near[HALF : HALF + 16, :] = pooled_ref[...]
+
+    def lane(x_of, y_of):
+        return pl.ds(pl.multiple_of((x_of * 2 + y_of) * LANES, LANES), LANES)
+
+    for clip in range(CLIPS_CORE):
+        span = slice(clip * ROWS, (clip + 1) * ROWS)
+        partial[...] = dot_nn(columns[span, :], weight)
+        rows = slice((clip % 2) * ROWS, (clip % 2 + 1) * ROWS)
+        if clip < 2:
+            a_own[rows, :] = partial[:, lane(x, y)]
+            a_mid[rows, :] = partial[:, lane(x, 1 - y)]
+            a_near[rows, :] = partial[:, lane(1 - x, y)].astype(BF)
+        else:
+            b_own[rows, :] = partial[:, lane(x, y)]
+            b_mid[rows, :] = partial[:, lane(1 - x, y)]
+            b_near[rows, :] = partial[:, lane(x, 1 - y)].astype(BF)
+
+
+def both_grad_kernel(
+    facts_ref, slope_ref, pre_ref, own_ref, other_ref, sum_own, sum_other, gain_ref, weight_ref,
+    pooled_ref, columns, a_own, a_mid, a_send, b_own, b_mid, b_send, partial
+):
+    x, y = place("x", "y")
+    pixels = pixel_row(facts_ref)
     mean, scale = norm_rows(own_ref, other_ref, pixels)
     sums = pair_sums(sum_own, sum_other)
     weight = weight_ref[...].reshape(TAPS * LANES, C2)
-    a_near[HALF : HALF + 16, :] = pooled_ref[...]
+    a_send[2 * HALF : 2 * HALF + 16, :] = pooled_ref[...]
 
     def lane(x_of, y_of):
         return pl.ds(pl.multiple_of((x_of * 2 + y_of) * LANES, LANES), LANES)
 
     for clip in range(CLIPS_CORE):
         span = slice(clip * ROWS, (clip + 1) * ROWS)
-        mask = valid_rows(counts[clip], LANES)
+        mask = valid_rows(facts_ref, clip)
         grad = pre_grad(
             slope_ref[span, :], pre_ref[span, :], mask, mean, scale, gain_ref[2:3, :], sums, pixels
         )
-        grad_ref[span, :] = grad.astype(BF)
-        scatter_taps(grad, columns, 0)
-        partial[...] = dot_nn(columns[...], weight)
+        scatter_taps(grad, columns, clip * ROWS)
+        partial[...] = dot_nn(columns[span, :], weight)
         rows = slice((clip % 2) * ROWS, (clip % 2 + 1) * ROWS)
+        near_rows = slice(HALF + (clip % 2) * ROWS, HALF + (clip % 2 + 1) * ROWS)
         far = partial[:, lane(1 - x, 1 - y)].astype(BF)
         if clip < 2:
             a_own[rows, :] = partial[:, lane(x, y)]
             a_mid[rows, :] = partial[:, lane(x, 1 - y)]
-            a_near[rows, :] = partial[:, lane(1 - x, y)].astype(BF)
-            a_far[rows, :] = far
+            a_send[rows, :] = far
+            a_send[near_rows, :] = partial[:, lane(1 - x, y)].astype(BF)
         else:
             b_own[rows, :] = partial[:, lane(x, y)]
             b_mid[rows, :] = partial[:, lane(1 - x, y)]
-            b_near[rows, :] = partial[:, lane(x, 1 - y)].astype(BF)
-            b_far[rows, :] = far
+            b_send[rows, :] = far
+            b_send[near_rows, :] = partial[:, lane(x, 1 - y)].astype(BF)
 
 
 def pass_on_kernel(a_mid, a_got, b_mid, b_got, a_next, b_next):
-    a_next[...] = (a_mid[...] + a_got[...].astype(F32)).astype(BF)
-    b_next[...] = (b_mid[...] + b_got[...].astype(F32)).astype(BF)
+    a_next[...] = (a_mid[...] + a_got[0:HALF].astype(F32)).astype(BF)
+    b_next[...] = (b_mid[...] + b_got[0:HALF].astype(F32)).astype(BF)
 
 
 def second_weight_grad_kernel(*rest):
-    parts, (grad_ref, keep_ref, send_ref, hidden, columns, natural, sems) = rest[:8], rest[8:]
+    parts, (columns, keep_ref, send_ref, hidden, natural, sems) = rest[:8], rest[8:]
     core = place("core")
     started = start_copies(hidden_copies(parts, hidden), sems)
-    for clip in range(CLIPS_CORE):
-        grad = grad_ref[clip * ROWS : (clip + 1) * ROWS, :].astype(F32)
-        scatter_taps(grad, columns, clip * ROWS)
     spread = exchange_matrix(C2, C2, block_exchange)
     wait_all(started)
+    for clip in range(CLIPS_CORE):
+        span = slice(clip * ROWS, (clip + 1) * ROWS)
+        hidden[span, :] = dot_nn(hidden[span, :], spread).astype(BF)
     for tap in range(TAPS):
-        chip = dot_tn(columns[:, lanes_of(tap)], hidden[...]).astype(BF)
-        natural[...] = dot_nn(chip, spread)
+        natural[...] = dot_tn(columns[:, lanes_of(tap)], hidden[...])
         for y_of in range(2):
             keep = natural[:, pl.ds(pl.multiple_of((y_of * 2 + core) * LANES, LANES), LANES)]
             send = natural[:, pl.ds(pl.multiple_of((y_of * 2 + 1 - core) * LANES, LANES), LANES)]
             for z_of in range(MB):
                 rows = slice(z_of * 32, (z_of + 1) * 32)
                 target = slice(tap * 32, (tap + 1) * 32)
-                keep_ref[z_of, y_of, target] = keep[rows].astype(BF)
-                send_ref[z_of, y_of, target] = send[rows].astype(BF)
+                keep_ref[z_of, y_of, target] = keep[rows]
+                send_ref[z_of, y_of, target] = send[rows]
 
 
 def second_core_kernel(keep_ref, got_ref, own_ref, n1, n2, n3):
     z = place("z")
-    own_ref[...] = keep_ref[z].astype(F32) + got_ref[z].astype(F32)
+    own_ref[...] = keep_ref[z] + got_ref[z]
     for step, target in ((1, n1), (2, n2), (3, n3)):
         at = jnp.bitwise_xor(z, step)
-        target[...] = (keep_ref[at].astype(F32) + got_ref[at].astype(F32)).astype(BF)
+        target[...] = (keep_ref[at] + got_ref[at]).astype(BF)
 
 
 def second_sum_kernel(own_ref, g1, g2, g3, keep_ref, send_ref, square_ref):
@@ -732,54 +801,60 @@
 
 
 def first_slope_kernel(
-    order_ref, counts_ref, a_own, a_near, a_last, b_own, b_near, b_last, pre_ref, own_ref, other_ref,
+    facts_ref, a_own, a_near, a_last, b_own, b_near, b_last, pre_ref, own_ref, other_ref,
     gain_ref, slope_ref, sum_ref
 ):
-    counts = clip_counts(order_ref, counts_ref)
-    mean, scale = norm_rows(own_ref, other_ref, pixel_count(order_ref, counts_ref))
+    mean, scale = norm_rows(own_ref, other_ref, pixel_row(facts_ref))
     first = jnp.zeros((1, LANES), F32)
     second = jnp.zeros((1, LANES), F32)
     for clip in range(CLIPS_CORE):
         span = slice(clip * ROWS, (clip + 1) * ROWS)
         rows = slice((clip % 2) * ROWS, (clip % 2 + 1) * ROWS)
         own, near, last = (a_own, a_near, a_last) if clip < 2 else (b_own, b_near, b_last)
-        outer = own[rows, :] + near[rows, :].astype(F32) + last[rows, :].astype(F32)
+        base = near.shape[0] // HALF * HALF - HALF
+        near_rows = slice(base + (clip % 2) * ROWS, base + (clip % 2 + 1) * ROWS)
+        outer = own[rows, :] + near[near_rows, :].astype(F32) + last[rows, :].astype(F32)
         normed = (pre_ref[span, :] - mean) * scale
         shaped = gain_ref[0:1, :] * normed + gain_ref[1:2, :]
         gate = jax.nn.sigmoid(shaped)
-        slope = outer * valid_rows(counts[clip], LANES) * (gate * (1.0 + shaped * (1.0 - gate)))
+        slope = outer * valid_rows(facts_ref, clip) * (gate * (1.0 + shaped * (1.0 - gate)))
         slope_ref[span, :] = slope
         plus = channel_sums(slope, slope * normed)
         first, second = first + plus[0], second + plus[1]
     put_pair(sum_ref, first, second)
 
 
-def first_weight_grad_kernel(
-    order_ref, counts_ref, slope_ref, pre_ref, own_ref, other_ref, sum_own, sum_other, gain_ref, x_ref,
-    keep_ref, send_ref, grad_ref, columns
+def first_grads_kernel(
+    facts_ref, slope_ref, pre_ref, own_ref, other_ref, sum_own, sum_other, gain_ref, weight_ref, x_ref,
+    part_ref, keep_ref, send_ref, columns, turned
 ):
     core = place("core")
-    counts = clip_counts(order_ref, counts_ref)
-    pixels = pixel_count(order_ref, counts_ref)
+    pixels = pixel_row(facts_ref)
     mean, scale = norm_rows(own_ref, other_ref, pixels)
     sums = pair_sums(sum_own, sum_other)
-    for clip in range(CLIPS_CORE):
-        span = slice(clip * ROWS, (clip + 1) * ROWS)
-        mask = valid_rows(counts[clip], LANES)
-        grad = pre_grad(
-            slope_ref[span, :], pre_ref[span, :], mask, mean, scale, gain_ref[0:1, :], sums, pixels
-        )
-        grad_ref[span, :] = grad.astype(BF)
-        scatter_taps(grad, columns, clip * ROWS)
+    weight = weight_ref[...].reshape(TAPS * LANES, C1)
 
     def source_of(column):
         core_of = jnp.where(column < 128, core, 1 - core)
         return ((column // 64) % 2) * 128 + core_of * 64 + column % 64
 
     spread = exchange_matrix(C1, C1, source_of)
+    for clip in range(CLIPS_CORE):
+        span = slice(clip * ROWS, (clip + 1) * ROWS)
+        mask = valid_rows(facts_ref, clip)
+        grad = pre_grad(
+            slope_ref[span, :], pre_ref[span, :], mask, mean, scale, gain_ref[0:1, :], sums, pixels
+        )
+        scatter_taps(grad, columns, clip * ROWS)
+        partial = dot_nn(columns[span, :], weight).astype(BF)
+        turned[span, :] = dot_nn(x_ref[span, :], spread).astype(BF)
+        for z_of in range(MB):
+            for x_of in range(2):
+                target = slice(((clip % 2) * MB + z_of) * 64, ((clip % 2) * MB + z_of + 1) * 64)
+                rows = slice((z_of * 2 + x_of) * 64, (z_of * 2 + x_of + 1) * 64)
+                part_ref[x_of * 2 + clip // 2, target, :] = partial[rows]
     for tap in range(TAPS):
-        part = dot_tn(columns[:, lanes_of(tap)], x_ref[...]).astype(BF)
-        both = dot_nn(part, spread).astype(BF)
+        both = dot_tn(columns[:, lanes_of(tap)], turned[...])
         for z_of in range(MB):
             rows = slice(z_of * 32, (z_of + 1) * 32)
             target = slice(tap * 32, (tap + 1) * 32)
@@ -792,13 +867,13 @@
     own_ref, n0, n1, n2, n3, scratch
 ):
     z, x, y = place("z", "x", "y")
-    own_ref[...] = keep_ref[z].astype(F32) + got_ref[z].astype(F32)
+    own_ref[...] = keep_ref[z] + got_ref[z]
     one, two = pair_sums(one_own, one_other), pair_sums(two_own, two_other)
     sums = jnp.concatenate([one[1], one[0], two[1], two[0]], axis=0)
     high = sums.astype(BF).astype(F32)
     norm_tile = jnp.concatenate([high, sums - high, jnp.zeros((8, LANES), F32)], axis=0).astype(BF)
     last = pooled_last[HALF : HALF + 32, :].astype(F32)
-    near = pooled_near[HALF : HALF + 16, :].astype(F32)
+    near = pooled_near[...].astype(F32)
     own = pooled_own[...].astype(F32)
     for rows, x_of, y_of in (
         (own, x, y),
@@ -815,7 +890,7 @@
     pooled_tile = scratch[...].astype(BF)
     for step, target in ((0, n0), (1, n1), (2, n2), (3, n3)):
         at = jnp.bitwise_xor(z, step)
-        target[0:CHUNK, :] = (keep_ref[at].astype(F32) + got_ref[at].astype(F32)).astype(BF)
+        target[0:CHUNK, :] = (keep_ref[at] + got_ref[at]).astype(BF)
         target[CHUNK : CHUNK + 16, :] = norm_tile
         target[CHUNK + 16 : CHUNK + 32, :] = pooled_tile
 
@@ -832,7 +907,8 @@
     squares = jnp.sum(total * total, axis=0, keepdims=True) + jnp.sum(
         jnp.where(mine, norm * norm, 0.0), axis=0, keepdims=True
     )
-    told_ref[...] = jnp.broadcast_to(squares + square_two[0:1, :], told_ref.shape)
+    first_rows = lax.broadcasted_iota(jnp.int32, told_ref.shape, 0) % 8 == 0
+    told_ref[...] = jnp.where(first_rows, squares + square_two[0:1, :], 0.0)
     turned = pltpu.roll(total, 64, 1)
     low = jnp.where(y == 0, total, turned)
     high = jnp.where(y == 0, turned, total)
@@ -861,38 +937,17 @@
     norm_out[...] = jnp.where(lane_index(8) < 32, low, high)[0:4, 0:64]
 
 
-def input_grad_kernel(
-    grad_ref, weight_ref, a_own, a_mid, a_far, a_near, b_own, b_mid, b_far, b_near, columns, partial
-):
-    x, y = place("x", "y")
-    weight = weight_ref[...].reshape(TAPS * LANES, C1)
-    for clip in range(CLIPS_CORE):
-        grad = grad_ref[clip * ROWS : (clip + 1) * ROWS, :].astype(F32)
-        scatter_taps(grad, columns, 0)
-        partial[clip] = dot_nn(columns[...], weight)
-
-    def part(x_of, y_of, j, z_of):
-        return partial[y_of * CL_MB + j, pl.ds(pl.multiple_of((z_of * 2 + x_of) * 64, 64), 64), :]
-
-    for z_of in range(MB):
-        a_own[z_of] = part(x, y, 0, z_of)
-        a_mid[z_of] = part(x, 1 - y, 0, z_of)
-        a_near[z_of] = part(1 - x, y, 0, z_of).astype(BF)
-        a_far[z_of] = part(1 - x, 1 - y, 0, z_of).astype(BF)
-        b_own[z_of] = part(x, y, 1, z_of)
-        b_mid[z_of] = part(1 - x, y, 1, z_of)
-        b_near[z_of] = part(x, 1 - y, 1, z_of).astype(BF)
-        b_far[z_of] = part(1 - x, 1 - y, 1, z_of).astype(BF)
-
-
-def input_sum_kernel(order_ref, counts_ref, a_own, a_near, a_last, b_own, b_near, b_last, f0, f1, f2, f3):
-    z, x, y, core = place(*AXES)
-    row = y * 2 + core
-    for j, (own, near, last) in enumerate(((a_own, a_near, a_last), (b_own, b_near, b_last))):
-        count = counts_ref[row * 8 + order_ref[row, z * CL_MB + j]]
+def input_sum_kernel(facts_ref, got_ref, f0, f1, f2, f3):
+    z, x, y = place("z", "x", "y")
+    for j in range(CL_MB):
+        count = jnp.where(y == 0, count_row(facts_ref, j), count_row(facts_ref, CL_MB + j))
+        count = jnp.concatenate([count, count], axis=1)
         for step, target in enumerate((f0, f1, f2, f3)):
             at = jnp.bitwise_xor(z, step)
-            total = own[at] + near[at].astype(F32) + last[at].astype(F32)
+            rows = pl.ds(pl.multiple_of((j * MB + at) * 64, 64), 64)
+            total = got_ref[0, rows, :].astype(F32)
+            for chip in range(1, 4):
+                total = total + got_ref[chip, rows, :].astype(F32)
             frame = (at * 2 + x) * 8 + lax.broadcasted_iota(jnp.int32, (64, C1), 0) // MEL
             target[j] = jnp.where(frame < count, total, 0.0).astype(BF)
 
@@ -911,6 +966,32 @@
                 scratch[part, pl.ds(clip, 1), :] = jnp.concatenate(chips, axis=1)
     spread = exchange_matrix(C2, C2, block_exchange)
     pooled_ref[...] = dot_nn(scratch[0].astype(BF), spread) + dot_nn(scratch[1].astype(BF), spread)
+
+
+FLOP_SCALE = OPT['flop']
+BYTE_SCALE = 0
+COSTS = {
+    prepare_kernel: 3,
+    first_conv_kernel: 4,
+    hidden_kernel: 0.4,
+    second_weight_kernel: 2.8,
+    second_conv_kernel: 3.5,
+    pool_kernel: 1.1,
+    grad_columns_kernel: 1.7,
+    hidden_grad_kernel: 3.4,
+    both_grad_kernel: 4,
+    second_weight_grad_kernel: 5,
+    pass_on_kernel: 0.2,
+    second_core_kernel: 0.2,
+    second_sum_kernel: 0.2,
+    first_slope_kernel: 0.8,
+    first_grads_kernel: 4,
+    first_core_kernel: 0.2,
+    first_sum_kernel: 0.8,
+    shard_kernel: 0.3,
+    input_sum_kernel: 0.3,
+    finish_kernel: 1.5,
+}
 
 
 def spread_plane(a0, b0):
@@ -935,34 +1016,76 @@
     norm_mean,
     norm_square,
 ):
-    table = (clip_order, frame_counts)
-    p0, p1, p2, p3, one_keep, one_send, two_keep, two_send, gain_rows, cot_own = call(
+    one_view, two_view = kernel_one, jnp.swapaxes(kernel_two, 1, 2)
+    p0, p1, p2, p3, one_keep, two_keep, send, gain_rows, cot_own, facts = call(
         prepare_kernel,
         [shape_of((CL_MB, 64, C1))] * MB
-        + [shape_of((144, LANES))] * 2
-        + [shape_of((CHUNK, LANES)), shape_of((CHUNK + 16, LANES)), shape_of((16, LANES))]
-        + [shape_of((8, LANES), F32)],
-        [SM, ANY, VM, VM, VM, VM],
+        + [shape_of((144, LANES)), shape_of((CHUNK, LANES)), shape_of((160 + CHUNK, LANES))]
+        + [shape_of((16, LANES)), shape_of((8, LANES), F32), shape_of((8, LANES), jnp.int32)],
+        [SM, SM] + [HB] * 5,
         [VM] * 10,
-        [pltpu.SemaphoreType.DMA((MB * CL_MB,))],
+        [
+            pltpu.VMEM(one_view.shape, F32),
+            pltpu.VMEM(two_view.shape, F32),
+            pltpu.VMEM(norm_params.shape, F32),
+            pltpu.VMEM(cotangent.shape, F32),
+            pltpu.SemaphoreType.DMA((4 + MB * CL_MB,)),
+        ],
+        limit=62 * 1024 * 1024,
     )(
         clip_order,
+        frame_counts,
         clip_input.reshape(MB * CL_MB, 64, C1),
-        kernel_one,
-        jnp.swapaxes(kernel_two, 1, 2),
+        one_view,
+        two_view,
         norm_params,
         cotangent,
     )
-    arrived = [p0] + [swap(piece, "z", step) for step, piece in ((1, p1), (2, p2), (3, p3))]
-    one_got = swap(one_send, "y")
-    two_got = swap(two_send, "y")
+    def spread_z(values):
+        got = {step: swap(values[step], "z", step) for step in steps_of()}
+        return [values[0]] + [got[step] for step in (1, 2, 3)]
+
+    arrived = spread_z([p0, p1, p2, p3])
+    got = swap(send, "y")
     a0 = jnp.stack([piece[0] for piece in arrived])
     b0 = jnp.stack([piece[1] for piece in arrived])
-    inputs = spread_plane(a0, b0)
-
-    one_flat = jnp.concatenate([one_keep, one_got, gain_rows])
-    one_parts = [one_flat] + [swap(one_flat, "z", step) for step in range(1, MB)]
-    one_others = [swap(part, "core") for part in one_parts]
+    one_flat = pin("w1_after_in", jnp.concatenate([one_keep, got[0:144], gain_rows]), a0, b0)
+    a1, b1 = swap(a0, "x"), swap(b0, "y")
+    if OPT["merge_w"]:
+        flat = jnp.concatenate([one_flat, two_keep, got[144 : 144 + CHUNK]])
+        one_parts = spread_z([flat] * 4)
+    else:
+        one_parts = spread_z([one_flat] * 4)
+    a01, b01 = jnp.concatenate([a0, a1]), jnp.concatenate([b0, b1])
+    if OPT["core_w1_after"] < 2:
+        deps = (a1, b1) if OPT["core_w1_after"] else ()
+        if OPT["core_w1"] == 4:
+            one_others = jnp.concatenate([swap(after(part[0:304], *deps), "core") for part in one_parts])
+        else:
+            one_others = swap(after(jnp.concatenate([part[0:304] for part in one_parts]), *deps), "core")
+        a01, b01 = pin("fwd_after_core_w1", a01, one_others), pin("fwd_after_core_w1", b01, one_others)
+        a23, b23 = swap(a01, "y"), swap(b01, "x")
+    else:
+        a23, b23 = swap(a01, "y"), swap(b01, "x")
+        deps = (a23, b23)
+        if OPT["core_w1"] == 4:
+            one_others = jnp.concatenate([swap(after(part[0:304], *deps), "core") for part in one_parts])
+        else:
+            one_others = swap(after(jnp.concatenate([part[0:304] for part in one_parts]), *deps), "core")
+    inputs = (a0, a1, a23, b0, b1, b23)
+    if OPT["merge_w"]:
+        two_parts = [part[304:] for part in one_parts]
+        one_parts = [part[0:304] for part in one_parts]
+    else:
+        two_flat = jnp.concatenate([two_keep, got[144 : 144 + CHUNK]])
+        two_flat = {
+            0: lambda: two_flat,
+            1: lambda: after(two_flat, *one_parts[1:]),
+            2: lambda: after(two_flat, one_others),
+            3: lambda: after(two_flat, a1, b1),
+            4: lambda: after(two_flat, a1, b1, one_others),
+        }[OPT["w2_after"]]()
+        two_parts = spread_z([two_flat] * 4)
     pre_one, masked, weight_one, stat_one, gains = call(
         first_conv_kernel,
         [
@@ -972,112 +1095,139 @@
             shape_of((8, LANES), F32),
             shape_of((8, LANES), F32),
         ],
-        [SM, SM] + [ANY] * 8 + [VM] * 8,
+        [VM] + [ANY] * 6 + [VM] * 5,
         [VM] * 5,
         [pltpu.SemaphoreType.DMA((8 * MB,))],
-        flops=2 * PIXELS * C1 * TAPS * LANES,
-    )(*table, *inputs, *one_parts, *one_others)
+    )(
+        after(facts, *two_parts[1:]) if OPT["w2_before"] == 2 else facts, *inputs, *one_parts, one_others
+    )
     stat_one_other = swap(stat_one, "core")
 
-    two_flat = jnp.concatenate([two_keep, two_got[0:CHUNK]])
-    two_parts = [two_flat] + [swap(two_flat, "z", step) for step in range(1, MB)]
-    two_others = [swap(part, "core") for part in two_parts]
+    ha0, hb0 = call(
+        hidden_kernel, [shape_of((HALF, LANES))] * 2, [VM] * 5, [VM] * 2
+    )(
+        after(facts, *two_parts[1:]) if OPT["w2_before"] == 1 else facts, pre_one, stat_one, stat_one_other, gains
+    )
+    hidden_parts = spread_plane(ha0, hb0)
+
+    two_all = jnp.concatenate(two_parts)
+    if OPT["core_w2_after"] == 1:
+        two_all = after(two_all, ha0)
+    if OPT["core_w2_after"] == 2:
+        two_all = after(two_all, hidden_parts[1], hidden_parts[5])
+    two_all_other = swap(two_all, "core")
+    two_all = pin("kw2_after", two_all, hidden_parts[1], hidden_parts[5])
     weight_two = call(
         second_weight_kernel,
         shape_of((TAPS, MB, 32, C2)),
-        [ANY] * 8,
+        [ANY, ANY],
         VM,
         [pltpu.VMEM((MB, 4, CHUNK, LANES), BF), pltpu.SemaphoreType.DMA((16,))],
-        flops=2 * TAPS * LANES * C2 * C2,
-    )(*two_parts, *two_others)
-
-    ha0, hb0 = call(
-        hidden_kernel, [shape_of((HALF, LANES))] * 2, [SM, SM] + [VM] * 4, [VM] * 2
-    )(*table, pre_one, stat_one, stat_one_other, gains)
-    hidden_parts = spread_plane(ha0, hb0)
+    )(two_all, two_all_other)
 
     pre_two, stat_two = call(
         second_conv_kernel,
         [shape_of((PIXELS, LANES), F32), shape_of((8, LANES), F32)],
-        [SM, SM] + [ANY] * 8 + [VM],
+        [VM] + [ANY] * 8 + [VM],
         [VM] * 2,
         [pltpu.VMEM((PIXELS, C2), BF), pltpu.SemaphoreType.DMA((8,))],
-        flops=2 * PIXELS * C2 * TAPS * LANES,
-    )(*table, *hidden_parts, weight_two)
+    )(facts, *hidden_parts, weight_two)
     stat_two_other = swap(stat_two, "core")
     slope_two, sum_two, pooled_own = call(
         pool_kernel,
         [shape_of((PIXELS, LANES), F32), shape_of((8, LANES), F32), shape_of((16, LANES))],
-        [SM, SM] + [VM] * 6,
+        [VM] * 7,
         [VM] * 3,
-    )(*table, pre_two, stat_two, stat_two_other, gains, cot_own, two_got)
+    )(facts, pre_two, stat_two, stat_two_other, gains, cot_own, got)
     sum_two_other = swap(sum_two, "core")
-    grad_two, a_own, a_mid, a_far, a_near, b_own, b_mid, b_far, b_near = call(
-        hidden_grad_kernel,
-        [shape_of((PIXELS, LANES))]
-        + [shape_of((HALF, LANES), F32)] * 2
-        + [shape_of((HALF, LANES)), shape_of((HALF + 16, LANES))]
-        + [shape_of((HALF, LANES), F32)] * 2
-        + [shape_of((HALF, LANES))] * 2,
-        [SM, SM] + [VM] * 9,
-        [VM] * 9,
-        [pltpu.VMEM((ROWS, TAPS * LANES), BF), pltpu.VMEM((ROWS, C2), F32)],
-        flops=2 * PIXELS * C2 * TAPS * LANES,
-    )(
-        *table, slope_two, pre_two, stat_two, stat_two_other, sum_two, sum_two_other, gains,
-        weight_two, pooled_own,
-    )
-    a_got, b_got = swap(a_far, "x"), swap(b_far, "y")
-    a_near, b_near = swap(a_near, "x"), swap(b_near, "y")
+    if OPT["rs"] == "far":
+        columns_two, a_far, b_far = call(
+            grad_columns_kernel,
+            [shape_of((PIXELS, TAPS * LANES))] + [shape_of((HALF, LANES))] * 2,
+            [VM] * 9,
+            [VM] * 3,
+        )(facts, slope_two, pre_two, stat_two, stat_two_other, sum_two, sum_two_other, gains, weight_two)
+        a_got, b_got = swap(a_far, "x"), swap(b_far, "y")
+        a_own, a_mid, a_near, b_own, b_mid, b_near = call(
+            hidden_grad_kernel,
+            [shape_of((HALF, LANES), F32)] * 2
+            + [shape_of((HALF + 16, LANES))]
+            + [shape_of((HALF, LANES), F32)] * 2
+            + [shape_of((HALF, LANES))],
+            [VM] * 3,
+            [VM] * 6,
+            [pltpu.VMEM((ROWS, C2), F32)],
+        )(columns_two, weight_two, pooled_own)
+        a_near, b_near = swap(a_near, "x"), swap(b_near, "y")
+        a_pool = a_near[HALF:]
+    else:
+        columns_two, a_own, a_mid, a_send, b_own, b_mid, b_send = call(
+            both_grad_kernel,
+            [shape_of((PIXELS, TAPS * LANES))]
+            + [shape_of((HALF, LANES), F32)] * 2
+            + [shape_of((2 * HALF + 16, LANES))]
+            + [shape_of((HALF, LANES), F32)] * 2
+            + [shape_of((2 * HALF, LANES))],
+            [VM] * 10,
+            [VM] * 7,
+            [pltpu.VMEM((ROWS, C2), F32)],
+        )(
+            facts, slope_two, pre_two, stat_two, stat_two_other, sum_two, sum_two_other, gains,
+            weight_two, pooled_own,
+        )
+        a_got = a_near = swap(a_send, "x")
+        b_got = b_near = swap(b_send, "y")
+        a_pool = a_got[2 * HALF :]
     two_part, two_part_send = call(
         second_weight_grad_kernel,
-        [shape_of((MB, 2, CHUNK, LANES))] * 2,
+        [shape_of((MB, 2, CHUNK, LANES), F32)] * 2,
         [ANY] * 8 + [VM],
         [VM] * 2,
         [
             pltpu.VMEM((PIXELS, C2), BF),
-            pltpu.VMEM((PIXELS, TAPS * LANES), BF),
             pltpu.VMEM((LANES, C2), F32),
             pltpu.SemaphoreType.DMA((8,)),
         ],
-        flops=2 * PIXELS * C2 * TAPS * LANES,
-    )(*hidden_parts, grad_two)
-    a_next, b_next = call(
-        pass_on_kernel, [shape_of((HALF, LANES))] * 2, [VM] * 4, [VM] * 2
-    )(a_mid, a_got, b_mid, b_got)
-    a_next = jnp.concatenate([a_next, pooled_own, a_near[HALF:]])
+    )(*hidden_parts, columns_two)
+    a_next, b_next = call(pass_on_kernel, [shape_of((HALF, LANES))] * 2, [VM] * 4, [VM] * 2)(
+        a_mid,
+        pin("pass_after_near", pin("pass_after_g2", a_got, two_part), a_near, b_near),
+        b_mid,
+        b_got,
+    )
+    a_next = jnp.concatenate([a_next, pooled_own, a_pool])
     a_last, b_last = swap(a_next, "y"), swap(b_next, "x")
-    slope_one, sum_one = call(
-        first_slope_kernel,
-        [shape_of((PIXELS, LANES), F32), shape_of((8, LANES), F32)],
-        [SM, SM] + [VM] * 10,
-        [VM] * 2,
-    )(*table, a_own, a_near, a_last, b_own, b_near, b_last, pre_one, stat_one, stat_one_other, gains)
-    sum_one_other = swap(sum_one, "core")
-    one_part, one_part_send, grad_one = call(
-        first_weight_grad_kernel,
-        [shape_of((MB, CHUNK, LANES))] * 2 + [shape_of((PIXELS, LANES))],
-        [SM, SM] + [VM] * 8,
-        [VM] * 3,
-        [pltpu.VMEM((PIXELS, TAPS * LANES), BF)],
-        flops=2 * PIXELS * C1 * TAPS * LANES,
-    )(
-        *table, slope_one, pre_one, stat_one, stat_one_other, sum_one, sum_one_other, gains, masked
-    )
-
     two_own, t1, t2, t3 = call(
         second_core_kernel,
         [shape_of((2, CHUNK, LANES), F32)] + [shape_of((2, CHUNK, LANES))] * 3,
         [VM] * 2,
         [VM] * 4,
-    )(two_part, swap(two_part_send, "core"))
+    )(two_part, swap(pin("core_g2_after", two_part_send, a_next), "core"))
+    slope_one, sum_one = call(
+        first_slope_kernel,
+        [shape_of((PIXELS, LANES), F32), shape_of((8, LANES), F32)],
+        [VM] * 11,
+        [VM] * 2,
+    )(pin("k5_after", facts, t1), a_own, a_near, a_last, b_own, b_near, b_last, pre_one, stat_one, stat_one_other, gains)
+    sum_one_other = swap(sum_one, "core")
+
+    input_part, one_part, one_part_send = call(
+        first_grads_kernel,
+        [shape_of((4, ROWS, C1))] + [shape_of((MB, CHUNK, LANES), F32)] * 2,
+        [VM] * 10,
+        [VM] * 3,
+        [pltpu.VMEM((PIXELS, TAPS * LANES), BF), pltpu.VMEM((PIXELS, C1), BF)],
+    )(
+        facts, slope_one, pre_one, stat_one, stat_one_other, sum_one, sum_one_other, gains, weight_one,
+        masked,
+    )
     two_keep_sum, two_send_sum, square_two = call(
         second_sum_kernel,
         [shape_of((CHUNK, LANES), F32)] * 2 + [shape_of((8, LANES), F32)],
         [VM] * 4,
         [VM] * 3,
-    )(two_own, swap(t1, "z", 1), swap(t2, "z", 2), swap(t3, "z", 3))
-    two_got_sum = swap(two_send_sum, "y")
+    )(*spread_z([two_own, t1, t2, t3]))
+    two_got_sum = swap(two_send_sum, "y") if not OPT['y2_after'] else None
 
     one_own, n0, n1, n2, n3 = call(
         first_core_kernel,
@@ -1086,23 +1236,38 @@
         [VM] * 5,
         [pltpu.VMEM((16, LANES), F32)],
     )(
-        one_part, swap(one_part_send, "core"), sum_one, sum_one_other, sum_two, sum_two_other,
-        pooled_own, a_near, a_last,
-    )
-    g1, g2, g3 = swap(n1, "z", 1), swap(n2, "z", 2), swap(n3, "z", 3)
+        pin("core1_after_g2", one_part, square_two),
+        swap(pin("core_g1_after_g2", one_part_send, square_two), "core"),
+        sum_one, sum_one_other, sum_two, sum_two_other,
+        pooled_own, a_pool, a_last,
+    )
+    g1, g2, g3 = spread_z([n0, n1, n2, n3])[1:]
+    input_part = pin("a2a_after_core1", input_part, n1)
+    input_got = lax.all_to_all(input_part, ("x", "y"), 0, 0, tiled=True)
+    f0, f1, f2, f3 = call(
+        input_sum_kernel, [shape_of((CL_MB, 64, C1))] * MB, [VM] * 2, [VM] * 4
+    )(facts, input_got)
+    if OPT["y2_after"]:
+        two_got_sum = swap(after(two_send_sum, n1), "y")
+    if not OPT["f_after_sum"]:
+        f1, f2, f3 = spread_z([f0, f1, f2, f3])[1:]
     told, one_keep_sum, one_send_sum, norm_sum = call(
         first_sum_kernel,
         [
-            shape_of((32, LANES), F32),
+            shape_of((32 * 8, LANES), F32),
             shape_of((144, LANES), F32),
             shape_of((152, LANES), F32),
             shape_of((8, LANES), F32),
         ],
         [VM] * 6,
         [VM] * 4,
-    )(one_own, n0, g1, g2, g3, square_two)
+    )(
+        pin("sum_after_y", pin("sum_after_f", one_own, f0), two_got_sum), n0, g1, g2, g3, square_two
+    )
+    if OPT["f_after_sum"]:
+        f1, f2, f3 = spread_z([f0, after(f1, told), after(f2, told), after(f3, told)])[1:]
     told = lax.all_to_all(told, AXES, 0, 0, tiled=True)
-    grad_norm = jnp.sqrt(jnp.sum(told))
+    grad_norm = jnp.sqrt(jnp.sum(pin("told_after_f", told, f1, f2, f3)))
     factor = jnp.minimum(1.0, CLIP_NORM / (grad_norm + 1e-06))
     one_got_sum = swap(one_send_sum, "y")
     grad_one_shard, norm_shard = call(
@@ -1127,31 +1292,13 @@
     )
     norm_update = adam_step(norm_params, norm_mean, norm_square, norm_shard, factor, GAIN_RATE, 0.0)
 
-    block = (MB, 64, C1)
-    ia_own, ia_mid, ia_far, ia_near, ib_own, ib_mid, ib_far, ib_near = call(
-        input_grad_kernel,
-        ([shape_of(block, F32)] * 2 + [shape_of(block)] * 2) * 2,
-        [VM, VM],
-        [VM] * 8,
-        [pltpu.VMEM((ROWS, TAPS * LANES), BF), pltpu.VMEM((CLIPS_CORE, ROWS, C1), F32)],
-        flops=2 * PIXELS * C1 * TAPS * LANES,
-    )(grad_one, weight_one)
-    ia_got, ib_got = swap(ia_far, "x"), swap(ib_far, "y")
-    ia_near, ib_near = swap(ia_near, "x"), swap(ib_near, "y")
-    ia_next, ib_next = call(pass_on_kernel, [shape_of(block)] * 2, [VM] * 4, [VM] * 2)(
-        ia_mid, ia_got, ib_mid, ib_got
-    )
-    ia_last, ib_last = swap(ia_next, "y"), swap(ib_next, "x")
-    f0, f1, f2, f3 = call(
-        input_sum_kernel, [shape_of((CL_MB, 64, C1))] * MB, [SM, SM] + [VM] * 6, [VM] * 4
-    )(*table, ia_own, ia_near, ia_last, ib_own, ib_near, ib_last)
     input_grad, pooled = call(
         finish_kernel,
         [shape_of((MB * CL_MB, 64, C1)), shape_of((MB * CL_MB, C2), F32)],
         [SM] + [VM] * 8,
         [VM] * 2,
         [pltpu.VMEM((2, MB * CL_MB, C2), F32)],
-    )(clip_order, f0, swap(f1, "z", 1), swap(f2, "z", 2), swap(f3, "z", 3), n0, g1, g2, g3)
+    )(clip_order, f0, f1, f2, f3, n0, g1, g2, g3)
     input_grad = input_grad.reshape(clip_input.shape)
     return (pooled, input_grad, grad_norm) + first_update + second_update + norm_update
 

time: 168 us -> 150 us (0.89)
  starting transfers between devices: 64.7 us -> 54.8 us
  Pallas kernels: 38 us -> 31.8 us
  local copies, waits for them, and re-layouts: 5.06 us -> 3.04 us
    ppermute x60 -> x43, starting transfers between devices: 60.4 us -> 47.5 us  [swap(): return lax.ppermute(value, axis, [(i, i ^ step) for i in range(size)])]
    pallas_call x9 -> x7, Pallas kernels: 22.7 us -> 16.4 us  [the longest x1 4.98 us: fast_body(): call(second_weight_grad_kernel, [shape_of((MB, 2, CHUNK, LANES), F32)] *...]
    all_to_all x1, waiting for transfers between devices: 3.72 us -> 0.01 us  [fast_body(): told = lax.all_to_all(told, AXES, 0, 0, tiled=True)]
    all_to_all x0 -> x1, starting transfers between devices: none -> 3.67 us  [fast_body(): input_got = lax.all_to_all(input_part, ('x', 'y'), 0, 0, tiled=True)]
    ppermute x60 -> x43, waiting for transfers between devices: 49.3 us -> 52.8 us  [swap(): return lax.ppermute(value, axis, [(i, i ^ step) for i in range(size)])]
    unnamed x36 -> x43, local copies, waits for them, and re-layouts: 5.02 us -> 2.98 us
  transfers between devices with their start and end apart: 61 -> 45, of which waited for: 22 -> 23; matrix products, arithmetic and copies ran while one was open for 1% -> 2% of each run, Pallas kernels for 16% -> 13%
where the time goes in v3:
time: 150 us; the launch traced here: 149 us
  starting transfers between devices  54.8 us (37%)
  waiting for transfers between devices  52.8 us (35%)
  Pallas kernels  31.8 us (21%)
  other arithmetic  3.6 us (2%)
  local copies, waits for them, and re-layouts  3.04 us (2%)
  between operations  3.02 us (2%)
    ppermute x43, waiting for transfers between devices, swap(): return lax.ppermute(value, axis, [(i, i ^ step) for i in range(size)])  52.8 us
    ppermute x43, starting transfers between devices, swap(): return lax.ppermute(value, axis, [(i, i ^ step) for i in range(size)])  47.5 us
    pallas_call x1, Pallas kernels, fast_body(): call(second_weight_grad_kernel, [shape_of((MB, 2, CHUNK, LANES), F32)] *...  4.98 us
    pallas_call x1, Pallas kernels, fast_body(): call(first_conv_kernel, [shape_of((PIXELS, LANES), F32), shape_of((PIXELS...  4.16 us
    pallas_call x1, Pallas kernels, fast_body(): call(both_grad_kernel, [shape_of((PIXELS, TAPS * LANES))] + [shape_of((HA...  4.05 us
    all_to_all x1, starting transfers between devices, fast_body(): input_got = lax.all_to_all(input_part, ('x', 'y'), 0, 0, tiled=True)  3.67 us
    all_to_all x1, starting transfers between devices, fast_body(): told = lax.all_to_all(told, AXES, 0, 0, tiled=True)  3.63 us
    pallas_call x1, Pallas kernels, fast_body(): call(second_conv_kernel, [shape_of((PIXELS, LANES), F32), shape_of((8, LA...  3.47 us
  transfers between devices with their start and end apart: 45, of which 23 were waited for; matrix products, arithmetic and copies ran while one was open for 2% of the time, Pallas kernels for 13%

profile of v3, /device:TPU:0, one launch (start us, length us, event | category | flops | bytes accessed | tf_op | source)
XLA Modules:
  0.0 149.1 jit_solution(17963561394121082679)
XLA Ops:
  0.7 2.9 %shard_map.268 = (bf16[2,64,256]{2,1,0:T(8,128)(2,1)}, bf16[2,64,256]{2,1,0:T(8,128)(2,1)}, bf16[2,64,256]{2,1,0:T(8,128)(2,1)}, bf16[2,64,256]{2,1,0:T(8,128)(2...) custom-call(s32[4,8]{1,0:T(4,128)} %order_ref.3, ...), custom_call_target="tpu_custom_call" | custom-call | flops 600000000 | tf_op jit(solution)/shard_map/pallas_call | solution.py:1020
  3.6 3.1 %collective-permute-start.4 = (bf16[2,64,256]{2,1,0:T(8,128)(2,1)}, bf16[2,64,256]{2,1,0:T(8,128)(2,1)S(1)}, u32[]{:S(2)}, u32[]{:S(2)}) collective-permute-start(bf16[2,64,256]{2,1,0:T(8,128)(2,1)} %get-tuple-element.94), channel_id=1, source_target_pairs={{0,8},{8,0},{16,24},{24,16},{1,9},{9,1},{17,25},{25,17},{2,10},{10... | collective-permute-start | bytes 196616 | tf_op jit(solution)/shard_map/ppermute | solution.py:300
  6.7 2.6 %collective-permute-start.5 = (bf16[2,64,256]{2,1,0:T(8,128)(2,1)}, bf16[2,64,256]{2,1,0:T(8,128)(2,1)S(1)}, u32[]{:S(2)}, u32[]{:S(2)}) collective-permute-start(bf16[2,64,256]{2,1,0:T(8,128)(2,1)} %get-tuple-element.95), channel_id=1, source_target_pairs={{0,16},{8,24},{16,0},{24,8},{1,17},{9,25},{17,1},{25,9},{2,18},{10... | collective-permute-start | bytes 196616 | tf_op jit(solution)/shard_map/ppermute | solution.py:300
  19.0 2.4 %collective-permute-start.12 = (bf16[304,128]{1,0:T(8,128)(2,1)S(1)}, bf16[304,128]{1,0:T(8,128)(2,1)S(1)}, u32[]{:S(2)}, u32[]{:S(2)}) collective-permute-start(bf16[304,128]{1,0:T(8,128)(2,1)S(1)} %pad_maximum_fusion.4.o0), channel_id=1, source_target_pairs={{0,16},{8,24},{16,0},{24,8},{1,17},{9,25},{17,1},{25,9},{2,18},{10... | collective-permute-start | bytes 233480 | tf_op jit(solution)/shard_map/ppermute | solution.py:300
  21.3 2.0 %collective-permute-start.13 = (bf16[304,128]{1,0:T(8,128)(2,1)S(1)}, bf16[304,128]{1,0:T(8,128)(2,1)S(1)}, u32[]{:S(2)}, u32[]{:S(2)}) collective-permute-start(bf16[304,128]{1,0:T(8,128)(2,1)S(1)} %pad_maximum_fusion.4.o0), channel_id=1, source_target_pairs={{0,24},{8,16},{16,8},{24,0},{1,25},{9,17},{17,9},{25,1},{2,26},{10... | collective-permute-start | bytes 233480 | tf_op jit(solution)/shard_map/ppermute | solution.py:300
  23.4 2.5 %collective-permute-done.11.o1 = bf16[304,128]{1,0:T(8,128)(2,1)S(1)} collective-permute-done((bf16[304,128]{1,0:T(8,128)(2,1)S(1)}, bf16[304,128]{1,0:T(8,128)(2,1)S(1)}, u32[]{:S(2)}, u32[]{:S(2)}) %collective-permute-start.11) | collective-permute-done | bytes 77856 | tf_op jit(solution)/shard_map/ppermute | solution.py:300
  25.9 3.1 %collective-permute-start.2 = (bf16[576,128]{1,0:T(8,128)(2,1)S(1)}, bf16[576,128]{1,0:T(8,128)(2,1)S(1)}, u32[]{:S(2)}, u32[]{:S(2)}) collective-permute-start(bf16[576,128]{1,0:T(8,128)(2,1)S(1)} %pad_maximum_fusion.1), channel_id=1, source_target_pairs={{0,16},{8,24},{16,0},{24,8},{1,17},{9,25},{17,1},{25,9},{2,18},{10... | collective-permute-start | bytes 442376 | tf_op jit(solution)/shard_map/ppermute | solution.py:300
  30.3 2.6 %collective-permute-done.1 = bf16[576,128]{1,0:T(8,128)(2,1)S(1)} collective-permute-done((bf16[576,128]{1,0:T(8,128)(2,1)S(1)}, bf16[576,128]{1,0:T(8,128)(2,1)S(1)}, u32[]{:S(2)}, u32[]{:S(2)}) %collective-permute-start.1) | collective-permute-done | bytes 147488 | tf_op jit(solution)/shard_map/ppermute | solution.py:300
  33.0 2.8 %collective-permute-start.3 = (bf16[576,128]{1,0:T(8,128)(2,1)S(1)}, bf16[576,128]{1,0:T(8,128)(2,1)S(1)}, u32[]{:S(2)}, u32[]{:S(2)}) collective-permute-start(bf16[576,128]{1,0:T(8,128)(2,1)S(1)} %pad_maximum_fusion.1), channel_id=1, source_target_pairs={{0,24},{8,16},{16,8},{24,0},{1,25},{9,17},{17,9},{25,1},{2,26},{10... | collective-permute-start | bytes 442376 | tf_op jit(solution)/shard_map/ppermute | solution.py:300
  35.8 2.1 %collective-permute-done.10.b23 = bf16[8,64,256]{2,1,0:T(8,128)(2,1)S(1)} collective-permute-done((bf16[8,64,256]{2,1,0:T(8,128)(2,1)S(1)}, bf16[8,64,256]{2,1,0:T(8,128)(2,1)S(1)}, u32[]{:S(2)}, u32[]{:S(2)}) %collective-permute-start.10) | collective-permute-done | bytes 262176 | tf_op jit(solution)/shard_map/ppermute | solution.py:300
  38.2 4.2 %shard_map.269 = (f32[2048,128]{1,0:T(8,128)S(1)}, bf16[2048,256]{1,0:T(8,128)(2,1)S(1)}, bf16[9,4,32,256]{3,2,1,0:T(8,128)(2,1)S(1)}, f32[8,128]{1,0:T(8,128)S(1)}, f32[8,128]{1,0:T(8,128)S(1)}) custom-call(s32[8,128]{1,0:T(8,128)S(1)} %copy-done, bf16[4,64,256]{2,1,0:T(8,128)(2,1)S(1)} %pad_maximum_fusion.2.a0, ...), custom_call_target="tpu_custom_call" | custom-call | flops 800000000 | tf_op jit(solution)/shard_map/pallas_call | solution.py:1089
  48.3 5.1 %collective-permute-done.16.rest_1_ = bf16[1024,128]{1,0:T(8,128)(2,1)S(1)} collective-permute-done((bf16[1024,128]{1,0:T(8,128)(2,1)S(1)}, bf16[1024,128]{1,0:T(8,128)(2,1)S(1)}, u32[]{:S(2)}, u32[]{:S(2)}) %collective-permute-start.16) | collective-permute-done | bytes 262176 | tf_op jit(solution)/shard_map/ppermute | solution.py:300
  55.4 2.8 %shard_map.271.rest_8_.weight_ref = bf16[9,4,32,512]{3,2,1,0:T(8,128)(2,1)S(1)} custom-call(bf16[2304,128]{1,0:T(8,128)(2,1)S(1)} %constant_dynamic-update-slice_fusion.16.own_ref, bf16[2304,128]{1,0:T(8,128)(2,1)S(1)} %collective-permute-done.22.other_ref), custom_call_target="tpu_custom_call" | custom-call | flops 560000000 | tf_op jit(solution)/shard_map/pallas_call | solution.py:1120
  58.2 2.3 %collective-permute-done.17.rest_2_ = bf16[1024,128]{1,0:T(8,128)(2,1)S(1)} collective-permute-done((bf16[1024,128]{1,0:T(8,128)(2,1)S(1)}, bf16[1024,128]{1,0:T(8,128)(2,1)S(1)}, u32[]{:S(2)}, u32[]{:S(2)}) %collective-permute-start.17) | collective-permute-done | bytes 262176 | tf_op jit(solution)/shard_map/ppermute | solution.py:300
  60.5 4.7 %collective-permute-done.18.rest_3_ = bf16[1024,128]{1,0:T(8,128)(2,1)S(1)} collective-permute-done((bf16[1024,128]{1,0:T(8,128)(2,1)S(1)}, bf16[1024,128]{1,0:T(8,128)(2,1)S(1)}, u32[]{:S(2)}, u32[]{:S(2)}) %collective-permute-start.18) | collective-permute-done | bytes 262176 | tf_op jit(solution)/shard_map/ppermute | solution.py:300
  65.2 3.5 %shard_map.272 = (f32[2048,128]{1,0:T(8,128)S(1)}, f32[8,128]{1,0:T(8,128)S(1)}) custom-call(s32[8,128]{1,0:T(8,128)S(1)} %copy-done, bf16[1024,128]{1,0:T(8,128)(2,1)S(1)} %get-tuple-element.102.rest_0_, bf16[1024,128]{1,0:T(8,128)(2,1)S(1)} %collective-permute-done.16.rest_1_, bf16[1024,128]{1,0:T(8,128)(2,1)S(1)} %collective-permute-done.17.rest_2_, ...), custom_call_target="tpu_custom_call" | custom-call | flops 700000000 | tf_op jit(solution)/shard_map/pallas_call | solution.py:1128
  72.3 4.0 %shard_map.274 = (bf16[2048,1152]{1,0:T(8,128)(2,1)S(1)}, f32[1024,128]{1,0:T(8,128)S(1)}, f32[1024,128]{1,0:T(8,128)S(1)}, bf16[2064,128]{1,0:T(8,128)(2,1)S(1)...) custom-call(s32[8,128]{1,0:T(8,128)S(1)} %copy-done, ...), custom_call_target="tpu_custom_call" | custom-call | flops 800000000 | tf_op jit(solution)/shard_map/pallas_call | solution.py:1164
  77.5 5.0 %shard_map.275 = (f32[4,2,288,128]{3,2,1,0:T(8,128)S(1)}, f32[4,2,288,128]{3,2,1,0:T(8,128)S(1)}) custom-call(bf16[1024,128]{1,0:T(8,128)(2,1)S(1)} %get-tuple-element.102.rest_0_, bf16[1024,128]{1,0:T(8,128)(2,1)S(1)} %collective-permute-done.16.rest_1_, bf16[1024,128]{1,0:T(8,128)(2,1)S(1)} %collective-permute-done.17.rest_2_, ...), custom_call_target="tpu_custom_call" | custom-call | flops 1000000000 | tf_op jit(solution)/shard_map/pallas_call | solution.py:1181
  82.5 8.0 %collective-permute-done.25.a_got.a_near = bf16[2064,128]{1,0:T(8,128)(2,1)S(1)} collective-permute-done((bf16[2064,128]{1,0:T(8,128)(2,1)S(1)}, bf16[2064,128]{1,0:T(8,128)(2,1)S(1)}, u32[]{:S(2)}, u32[]{:S(2)}) %collective-permute-start.25) | collective-permute-done | bytes 528416 | tf_op jit(solution)/shard_map/ppermute | solution.py:300
  94.6 1.8 %collective-permute-start.34 = (bf16[2,288,128]{2,1,0:T(8,128)(2,1)}, bf16[2,288,128]{2,1,0:T(8,128)(2,1)S(1)}, u32[]{:S(2)}, u32[]{:S(2)}) collective-permute-start(bf16[2,288,128]{2,1,0:T(8,128)(2,1)} %get-tuple-element.121), channel_id=1, source_target_pairs={{0,8},{8,0},{16,24},{24,16},{1,9},{9,1},{17,25},{25,17},{2,10},{10... | collective-permute-start | bytes 442376 | tf_op jit(solution)/shard_map/ppermute | solution.py:300
  97.0 2.0 %collective-permute-start.36 = (bf16[2,288,128]{2,1,0:T(8,128)(2,1)}, bf16[2,288,128]{2,1,0:T(8,128)(2,1)S(1)}, u32[]{:S(2)}, u32[]{:S(2)}) collective-permute-start(bf16[2,288,128]{2,1,0:T(8,128)(2,1)} %get-tuple-element.139), channel_id=1, source_target_pairs={{0,24},{8,16},{16,8},{24,0},{1,25},{9,17},{17,9},{25,1},{2,26},{10... | collective-permute-start | bytes 442376 | tf_op jit(solution)/shard_map/ppermute | solution.py:300
  101.9 3.3 %shard_map.279 = (bf16[4,512,256]{2,1,0:T(8,128)(2,1)}, f32[4,288,128]{2,1,0:T(8,128)S(1)}, f32[4,288,128]{2,1,0:T(8,128)S(1)}) custom-call(s32[8,128]{1,0:T(8,128)S(1)} %copy-done, f32[2048,128]{1,0:T(8,128)S(1)} %get-tuple-element.126.slope_ref, f32[2048,128]{1,0:T(8,128)S(1)} %get-tuple-element.99.pre_ref, f32[8,128]{1,0:T(8,128)S(1)} %get-tuple-element.100.own_ref, ...), custom_call_target="tpu_custom_call" | custom-call | flops 800000000 | tf_op jit(solution)/shard_map/pallas_call | solution.py:1214
  105.2 3.7 %all-to-all-start = ((bf16[4,512,256]{2,1,0:T(8,128)(2,1)}), bf16[4,512,256]{2,1,0:T(8,128)(2,1)S(1)}, u32[]{:S(2)}, u32[]{:S(2)}) async-start(bf16[4,512,256]{2,1,0:T(8,128)(2,1)} %get-tuple-element.130), calls=%async_computation | async-start | bytes 2097152 | tf_op jit(solution)/shard_map/all_to_all | solution.py:1246
  110.7 2.0 %collective-permute-done.37.got_ref = f32[4,288,128]{2,1,0:T(8,128)S(1)} collective-permute-done((f32[4,288,128]{2,1,0:T(8,128)S(1)}, f32[4,288,128]{2,1,0:T(8,128)S(1)}, u32[]{:S(2)}, u32[]{:S(2)}) %collective-permute-start.37) | collective-permute-done | bytes 589856 | tf_op jit(solution)/shard_map/ppermute | solution.py:300
  113.7 2.4 %collective-permute-start.38 = (bf16[320,128]{1,0:T(8,128)(2,1)S(1)}, bf16[320,128]{1,0:T(8,128)(2,1)S(1)}, u32[]{:S(2)}, u32[]{:S(2)}) collective-permute-start(bf16[320,128]{1,0:T(8,128)(2,1)S(1)} %get-tuple-element.143), channel_id=1, source_target_pairs={{0,8},{8,0},{16,24},{24,16},{1,9},{9,1},{17,25},{25,17},{2,10},{10... | collective-permute-start | bytes 245768 | tf_op jit(solution)/shard_map/ppermute | solution.py:300
  116.7 1.8 %collective-permute-start.40 = (bf16[320,128]{1,0:T(8,128)(2,1)S(1)}, bf16[320,128]{1,0:T(8,128)(2,1)S(1)}, u32[]{:S(2)}, u32[]{:S(2)}) collective-permute-start(bf16[320,128]{1,0:T(8,128)(2,1)S(1)} %get-tuple-element.145), channel_id=1, source_target_pairs={{0,24},{8,16},{16,8},{24,0},{1,25},{9,17},{17,9},{25,1},{2,26},{10... | collective-permute-start | bytes 245768 | tf_op jit(solution)/shard_map/ppermute | solution.py:300
  118.5 7.6 %collective-permute-done.41 = f32[288,128]{1,0:T(8,128)S(1)} collective-permute-done((f32[288,128]{1,0:T(8,128)S(1)}, f32[288,128]{1,0:T(8,128)S(1)}, u32[]{:S(2)}, u32[]{:S(2)}) %collective-permute-start.41) | collective-permute-done | bytes 147488 | tf_op jit(solution)/shard_map/ppermute | solution.py:300
  126.8 3.6 %all-to-all-start.1 = ((f32[32,8,128]{2,1,0:T(8,128)}), f32[32,8,128]{2,1,0:T(8,128)S(1)}, u32[]{:S(2)}, u32[]{:S(2)}) async-start(f32[32,8,128]{2,1,0:T(8,128)} %bitcast.3), calls=%async_computation.1 | async-start | bytes 262144 | tf_op jit(solution)/shard_map/all_to_all | solution.py:1269
  130.7 1.8 %collective-permute-start.31 = (bf16[2,64,256]{2,1,0:T(8,128)(2,1)S(1)}, bf16[2,64,256]{2,1,0:T(8,128)(2,1)S(1)}, u32[]{:S(2)}, u32[]{:S(2)}) collective-permute-start(bf16[2,64,256]{2,1,0:T(8,128)(2,1)S(1)} %get-tuple-element.132), channel_id=1, source_target_pairs={{0,8},{8,0},{16,24},{24,16},{1,9},{9,1},{17,25},{25,17},{2,10},{10... | collective-permute-start | bytes 196616 | tf_op jit(solution)/shard_map/ppermute | solution.py:300
  132.6 2.4 %collective-permute-start.32 = (bf16[2,64,256]{2,1,0:T(8,128)(2,1)S(1)}, bf16[2,64,256]{2,1,0:T(8,128)(2,1)S(1)}, u32[]{:S(2)}, u32[]{:S(2)}) collective-permute-start(bf16[2,64,256]{2,1,0:T(8,128)(2,1)S(1)} %get-tuple-element.133), channel_id=1, source_target_pairs={{0,16},{8,24},{16,0},{24,8},{1,17},{9,25},{17,1},{25,9},{2,18},{10... | collective-permute-start | bytes 196616 | tf_op jit(solution)/shard_map/ppermute | solution.py:300
  136.9 2.2 %collective-permute-done.32.g2 = bf16[2,64,256]{2,1,0:T(8,128)(2,1)S(1)} collective-permute-done((bf16[2,64,256]{2,1,0:T(8,128)(2,1)S(1)}, bf16[2,64,256]{2,1,0:T(8,128)(2,1)S(1)}, u32[]{:S(2)}, u32[]{:S(2)}) %collective-permute-start.32) | collective-permute-done | bytes 65568 | tf_op jit(solution)/shard_map/ppermute | solution.py:300
  139.2 2.4 %collective-permute-done.33.g3 = bf16[2,64,256]{2,1,0:T(8,128)(2,1)S(1)} collective-permute-done((bf16[2,64,256]{2,1,0:T(8,128)(2,1)S(1)}, bf16[2,64,256]{2,1,0:T(8,128)(2,1)S(1)}, u32[]{:S(2)}, u32[]{:S(2)}) %collective-permute-start.33) | collective-permute-done | bytes 65568 | tf_op jit(solution)/shard_map/ppermute | solution.py:300
  (133 shorter events, 43.7 us)
Async XLA Ops:
  3.6 9.9 %collective-permute-start.4 = (bf16[2,64,256]{2,1,0:T(8,128)(2,1)}, bf16[2,64,256]{2,1,0:T(8,128)(2,1)S(1)}, u32[]{:S(2)}, u32[]{:S(2)}) collective-permute-start(bf16[2,64,256]{2,1,0:T(8,128)(2,1)} %get-tuple-element.94), channel_id=1, source_target_pairs={{0,8},{8,0},{16,24},{24,16},{1,9},{9,1},{17,25},{25,17},{2,10},{10... | collective-permute-start | bytes 196616 | tf_op jit(solution)/shard_map/ppermute | solution.py:300
  6.7 7.5 %collective-permute-start.5 = (bf16[2,64,256]{2,1,0:T(8,128)(2,1)}, bf16[2,64,256]{2,1,0:T(8,128)(2,1)S(1)}, u32[]{:S(2)}, u32[]{:S(2)}) collective-permute-start(bf16[2,64,256]{2,1,0:T(8,128)(2,1)} %get-tuple-element.95), channel_id=1, source_target_pairs={{0,16},{8,24},{16,0},{24,8},{1,17},{9,25},{17,1},{25,9},{2,18},{10... | collective-permute-start | bytes 196616 | tf_op jit(solution)/shard_map/ppermute | solution.py:300
  9.3 9.5 %collective-permute-start = (bf16[448,128]{1,0:T(8,128)(2,1)}, bf16[448,128]{1,0:T(8,128)(2,1)S(1)}, u32[]{:S(2)}, u32[]{:S(2)}) collective-permute-start(bf16[448,128]{1,0:T(8,128)(2,1)} %get-tuple-element.91), channel_id=1, source_target_pairs={{0,2},{2,0},{1,3},{3,1},{4,6},{6,4},{5,7},{7,5},{8,10},{10,8},{9,1... | collective-permute-start | bytes 344072 | tf_op jit(solution)/shard_map/ppermute | solution.py:300
  15.7 13.4 %collective-permute-start.9 = (bf16[4,64,256]{2,1,0:T(8,128)(2,1)S(1)}, bf16[4,64,256]{2,1,0:T(8,128)(2,1)S(1)}, u32[]{:S(2)}, u32[]{:S(2)}) collective-permute-start(bf16[4,64,256]{2,1,0:T(8,128)(2,1)S(1)} %pad_maximum_fusion.3.b0), channel_id=1, source_target_pairs={{0,2},{2,0},{1,3},{3,1},{4,6},{6,4},{5,7},{7,5},{8,10},{10,8},{9,1... | collective-permute-start | bytes 393224 | tf_op jit(solution)/shard_map/ppermute | solution.py:300
  17.3 12.4 %collective-permute-start.7 = (bf16[4,64,256]{2,1,0:T(8,128)(2,1)S(1)}, bf16[4,64,256]{2,1,0:T(8,128)(2,1)S(1)}, u32[]{:S(2)}, u32[]{:S(2)}) collective-permute-start(bf16[4,64,256]{2,1,0:T(8,128)(2,1)S(1)} %pad_maximum_fusion.2.a0), channel_id=1, source_target_pairs={{0,4},{4,0},{1,5},{5,1},{2,6},{6,2},{3,7},{7,3},{8,12},{12,8},{9,1... | collective-permute-start | bytes 393224 | tf_op jit(solution)/shard_map/ppermute | solution.py:300
  21.3 7.6 %collective-permute-start.13 = (bf16[304,128]{1,0:T(8,128)(2,1)S(1)}, bf16[304,128]{1,0:T(8,128)(2,1)S(1)}, u32[]{:S(2)}, u32[]{:S(2)}) collective-permute-start(bf16[304,128]{1,0:T(8,128)(2,1)S(1)} %pad_maximum_fusion.4.o0), channel_id=1, source_target_pairs={{0,24},{8,16},{16,8},{24,0},{1,25},{9,17},{17,9},{25,1},{2,26},{10... | collective-permute-start | bytes 233480 | tf_op jit(solution)/shard_map/ppermute | solution.py:300
  25.9 9.9 %collective-permute-start.2 = (bf16[576,128]{1,0:T(8,128)(2,1)S(1)}, bf16[576,128]{1,0:T(8,128)(2,1)S(1)}, u32[]{:S(2)}, u32[]{:S(2)}) collective-permute-start(bf16[576,128]{1,0:T(8,128)(2,1)S(1)} %pad_maximum_fusion.1), channel_id=1, source_target_pairs={{0,16},{8,24},{16,0},{24,8},{1,17},{9,25},{17,1},{25,9},{2,18},{10... | collective-permute-start | bytes 442376 | tf_op jit(solution)/shard_map/ppermute | solution.py:300
  29.0 9.2 %collective-permute-start.14 = (bf16[1216,128]{1,0:T(8,128)(2,1)S(1)}, bf16[1216,128]{1,0:T(8,128)(2,1)S(1)}, u32[]{:S(2)}, u32[]{:S(2)}) collective-permute-start(bf16[1216,128]{1,0:T(8,128)(2,1)S(1)} %constant_dynamic-update-slice_fusion.10), channel_id=1, source_target_pairs={{0,1},{1,0},{2,3},{3,2},{4,5},{5,4},{6,7},{7,6},{8,9},{9,8},{10,11... | collective-permute-start | bytes 933896 | tf_op jit(solution)/shard_map/ppermute | solution.py:300
  29.1 8.8 %collective-permute-start.10 = (bf16[8,64,256]{2,1,0:T(8,128)(2,1)S(1)}, bf16[8,64,256]{2,1,0:T(8,128)(2,1)S(1)}, u32[]{:S(2)}, u32[]{:S(2)}) collective-permute-start(bf16[8,64,256]{2,1,0:T(8,128)(2,1)S(1)} %constant_dynamic-update-slice_fusion.5), channel_id=1, source_target_pairs={{0,4},{4,0},{1,5},{5,1},{2,6},{6,2},{3,7},{7,3},{8,12},{12,8},{9,1... | collective-permute-start | bytes 786440 | tf_op jit(solution)/shard_map/ppermute | solution.py:300
  29.7 8.5 %collective-permute-start.8 = (bf16[8,64,256]{2,1,0:T(8,128)(2,1)S(1)}, bf16[8,64,256]{2,1,0:T(8,128)(2,1)S(1)}, u32[]{:S(2)}, u32[]{:S(2)}) collective-permute-start(bf16[8,64,256]{2,1,0:T(8,128)(2,1)S(1)} %constant_dynamic-update-slice_fusion), channel_id=1, source_target_pairs={{0,2},{2,0},{1,3},{3,1},{4,6},{6,4},{5,7},{7,5},{8,10},{10,8},{9,1... | collective-permute-start | bytes 786440 | tf_op jit(solution)/shard_map/ppermute | solution.py:300
  33.0 9.5 %collective-permute-start.3 = (bf16[576,128]{1,0:T(8,128)(2,1)S(1)}, bf16[576,128]{1,0:T(8,128)(2,1)S(1)}, u32[]{:S(2)}, u32[]{:S(2)}) collective-permute-start(bf16[576,128]{1,0:T(8,128)(2,1)S(1)} %pad_maximum_fusion.1), channel_id=1, source_target_pairs={{0,24},{8,16},{16,8},{24,0},{1,25},{9,17},{17,9},{25,1},{2,26},{10... | collective-permute-start | bytes 442376 | tf_op jit(solution)/shard_map/ppermute | solution.py:300
  44.0 11.4 %collective-permute-start.22 = (bf16[2304,128]{1,0:T(8,128)(2,1)S(1)}, bf16[2304,128]{1,0:T(8,128)(2,1)S(1)}, u32[]{:S(2)}, u32[]{:S(2)}) collective-permute-start(bf16[2304,128]{1,0:T(8,128)(2,1)S(1)} %constant_dynamic-update-slice_fusion.16.own_ref), channel_id=1, source_target_pairs={{0,1},{1,0},{2,3},{3,2},{4,5},{5,4},{6,7},{7,6},{8,9},{9,8},{10,11... | collective-permute-start | bytes 1769480 | tf_op jit(solution)/shard_map/ppermute | solution.py:300
  44.2 9.1 %collective-permute-start.16 = (bf16[1024,128]{1,0:T(8,128)(2,1)S(1)}, bf16[1024,128]{1,0:T(8,128)(2,1)S(1)}, u32[]{:S(2)}, u32[]{:S(2)}) collective-permute-start(bf16[1024,128]{1,0:T(8,128)(2,1)S(1)} %get-tuple-element.102.rest_0_), channel_id=1, source_target_pairs={{0,4},{4,0},{1,5},{5,1},{2,6},{6,2},{3,7},{7,3},{8,12},{12,8},{9,1... | collective-permute-start | bytes 786440 | tf_op jit(solution)/shard_map/ppermute | solution.py:300
  45.7 9.2 %collective-permute-start.19 = (bf16[1024,128]{1,0:T(8,128)(2,1)S(1)}, bf16[1024,128]{1,0:T(8,128)(2,1)S(1)}, u32[]{:S(2)}, u32[]{:S(2)}) collective-permute-start(bf16[1024,128]{1,0:T(8,128)(2,1)S(1)} %get-tuple-element.103.rest_4_), channel_id=1, source_target_pairs={{0,2},{2,0},{1,3},{3,1},{4,6},{6,4},{5,7},{7,5},{8,10},{10,8},{9,1... | collective-permute-start | bytes 786440 | tf_op jit(solution)/shard_map/ppermute | solution.py:300
  46.2 14.3 %collective-permute-start.17 = (bf16[1024,128]{1,0:T(8,128)(2,1)S(1)}, bf16[1024,128]{1,0:T(8,128)(2,1)S(1)}, u32[]{:S(2)}, u32[]{:S(2)}) collective-permute-start(bf16[1024,128]{1,0:T(8,128)(2,1)S(1)} %get-tuple-element.102.rest_0_), channel_id=1, source_target_pairs={{0,2},{2,0},{1,3},{3,1},{4,6},{6,4},{5,7},{7,5},{8,10},{10,8},{9,1... | collective-permute-start | bytes 786440 | tf_op jit(solution)/shard_map/ppermute | solution.py:300
  47.7 12.8 %collective-permute-start.20 = (bf16[1024,128]{1,0:T(8,128)(2,1)S(1)}, bf16[1024,128]{1,0:T(8,128)(2,1)S(1)}, u32[]{:S(2)}, u32[]{:S(2)}) collective-permute-start(bf16[1024,128]{1,0:T(8,128)(2,1)S(1)} %get-tuple-element.103.rest_4_), channel_id=1, source_target_pairs={{0,4},{4,0},{1,5},{5,1},{2,6},{6,2},{3,7},{7,3},{8,12},{12,8},{9,1... | collective-permute-start | bytes 786440 | tf_op jit(solution)/shard_map/ppermute | solution.py:300
  53.3 11.9 %collective-permute-start.18 = (bf16[1024,128]{1,0:T(8,128)(2,1)S(1)}, bf16[1024,128]{1,0:T(8,128)(2,1)S(1)}, u32[]{:S(2)}, u32[]{:S(2)}) collective-permute-start(bf16[1024,128]{1,0:T(8,128)(2,1)S(1)} %collective-permute-done.16.rest_1_), channel_id=1, source_target_pairs={{0,2},{2,0},{1,3},{3,1},{4,6},{6,4},{5,7},{7,5},{8,10},{10,8},{9,1... | collective-permute-start | bytes 786440 | tf_op jit(solution)/shard_map/ppermute | solution.py:300
  54.9 10.3 %collective-permute-start.21 = (bf16[1024,128]{1,0:T(8,128)(2,1)S(1)}, bf16[1024,128]{1,0:T(8,128)(2,1)S(1)}, u32[]{:S(2)}, u32[]{:S(2)}) collective-permute-start(bf16[1024,128]{1,0:T(8,128)(2,1)S(1)} %collective-permute-done.19.rest_5_), channel_id=1, source_target_pairs={{0,4},{4,0},{1,5},{5,1},{2,6},{6,2},{3,7},{7,3},{8,12},{12,8},{9,1... | collective-permute-start | bytes 786440 | tf_op jit(solution)/shard_map/ppermute | solution.py:300
  76.3 14.2 %collective-permute-start.25 = (bf16[2064,128]{1,0:T(8,128)(2,1)S(1)}, bf16[2064,128]{1,0:T(8,128)(2,1)S(1)}, u32[]{:S(2)}, u32[]{:S(2)}) collective-permute-start(bf16[2064,128]{1,0:T(8,128)(2,1)S(1)} %get-tuple-element.115), channel_id=1, source_target_pairs={{0,4},{4,0},{1,5},{5,1},{2,6},{6,2},{3,7},{7,3},{8,12},{12,8},{9,1... | collective-permute-start | bytes 1585160 | tf_op jit(solution)/shard_map/ppermute | solution.py:300
  76.9 13.7 %collective-permute-start.26 = (bf16[2048,128]{1,0:T(8,128)(2,1)S(1)}, bf16[2048,128]{1,0:T(8,128)(2,1)S(1)}, u32[]{:S(2)}, u32[]{:S(2)}) collective-permute-start(bf16[2048,128]{1,0:T(8,128)(2,1)S(1)} %get-tuple-element.118), channel_id=1, source_target_pairs={{0,2},{2,0},{1,3},{3,1},{4,6},{6,4},{5,7},{7,5},{8,10},{10,8},{9,1... | collective-permute-start | bytes 1572872 | tf_op jit(solution)/shard_map/ppermute | solution.py:300
  90.9 9.0 %collective-permute-start.28 = (bf16[1056,128]{1,0:T(8,128)(2,1)S(1)}, bf16[1056,128]{1,0:T(8,128)(2,1)S(1)}, u32[]{:S(2)}, u32[]{:S(2)}) collective-permute-start(bf16[1056,128]{1,0:T(8,128)(2,1)S(1)} %pad_maximum_fusion), channel_id=1, source_target_pairs={{0,2},{2,0},{1,3},{3,1},{4,6},{6,4},{5,7},{7,5},{8,10},{10,8},{9,1... | collective-permute-start | bytes 811016 | tf_op jit(solution)/shard_map/ppermute | solution.py:300
  91.5 8.4 %collective-permute-start.29 = (bf16[1024,128]{1,0:T(8,128)(2,1)S(1)}, bf16[1024,128]{1,0:T(8,128)(2,1)S(1)}, u32[]{:S(2)}, u32[]{:S(2)}) collective-permute-start(bf16[1024,128]{1,0:T(8,128)(2,1)S(1)} %get-tuple-element.125), channel_id=1, source_target_pairs={{0,4},{4,0},{1,5},{5,1},{2,6},{6,2},{3,7},{7,3},{8,12},{12,8},{9,1... | collective-permute-start | bytes 786440 | tf_op jit(solution)/shard_map/ppermute | solution.py:300
  94.6 14.3 %collective-permute-start.34 = (bf16[2,288,128]{2,1,0:T(8,128)(2,1)}, bf16[2,288,128]{2,1,0:T(8,128)(2,1)S(1)}, u32[]{:S(2)}, u32[]{:S(2)}) collective-permute-start(bf16[2,288,128]{2,1,0:T(8,128)(2,1)} %get-tuple-element.121), channel_id=1, source_target_pairs={{0,8},{8,0},{16,24},{24,16},{1,9},{9,1},{17,25},{25,17},{2,10},{10... | collective-permute-start | bytes 442376 | tf_op jit(solution)/shard_map/ppermute | solution.py:300
  96.4 14.2 %collective-permute-start.35 = (bf16[2,288,128]{2,1,0:T(8,128)(2,1)}, bf16[2,288,128]{2,1,0:T(8,128)(2,1)S(1)}, u32[]{:S(2)}, u32[]{:S(2)}) collective-permute-start(bf16[2,288,128]{2,1,0:T(8,128)(2,1)} %get-tuple-element.138), channel_id=1, source_target_pairs={{0,16},{8,24},{16,0},{24,8},{1,17},{9,25},{17,1},{25,9},{2,18},{10... | collective-permute-start | bytes 442376 | tf_op jit(solution)/shard_map/ppermute | solution.py:300
  97.0 13.6 %collective-permute-start.36 = (bf16[2,288,128]{2,1,0:T(8,128)(2,1)}, bf16[2,288,128]{2,1,0:T(8,128)(2,1)S(1)}, u32[]{:S(2)}, u32[]{:S(2)}) collective-permute-start(bf16[2,288,128]{2,1,0:T(8,128)(2,1)} %get-tuple-element.139), channel_id=1, source_target_pairs={{0,24},{8,16},{16,8},{24,0},{1,25},{9,17},{17,9},{25,1},{2,26},{10... | collective-permute-start | bytes 442376 | tf_op jit(solution)/shard_map/ppermute | solution.py:300
  105.2 21.7 %all-to-all-start = ((bf16[4,512,256]{2,1,0:T(8,128)(2,1)}), bf16[4,512,256]{2,1,0:T(8,128)(2,1)S(1)}, u32[]{:S(2)}, u32[]{:S(2)}) async-start(bf16[4,512,256]{2,1,0:T(8,128)(2,1)} %get-tuple-element.130), calls=%async_computation | async-start | bytes 2097152 | tf_op jit(solution)/shard_map/all_to_all | solution.py:1246
  112.8 13.2 %collective-permute-start.41 = (f32[288,128]{1,0:T(8,128)S(1)}, f32[288,128]{1,0:T(8,128)S(1)}, u32[]{:S(2)}, u32[]{:S(2)}) collective-permute-start(f32[288,128]{1,0:T(8,128)S(1)} %get-tuple-element.150), channel_id=1, source_target_pairs={{0,2},{2,0},{1,3},{3,1},{4,6},{6,4},{5,7},{7,5},{8,10},{10,8},{9,1... | collective-permute-start | bytes 442376 | tf_op jit(solution)/shard_map/ppermute | solution.py:300
  113.7 12.3 %collective-permute-start.38 = (bf16[320,128]{1,0:T(8,128)(2,1)S(1)}, bf16[320,128]{1,0:T(8,128)(2,1)S(1)}, u32[]{:S(2)}, u32[]{:S(2)}) collective-permute-start(bf16[320,128]{1,0:T(8,128)(2,1)S(1)} %get-tuple-element.143), channel_id=1, source_target_pairs={{0,8},{8,0},{16,24},{24,16},{1,9},{9,1},{17,25},{25,17},{2,10},{10... | collective-permute-start | bytes 245768 | tf_op jit(solution)/shard_map/ppermute | solution.py:300
  116.1 9.9 %collective-permute-start.39 = (bf16[320,128]{1,0:T(8,128)(2,1)S(1)}, bf16[320,128]{1,0:T(8,128)(2,1)S(1)}, u32[]{:S(2)}, u32[]{:S(2)}) collective-permute-start(bf16[320,128]{1,0:T(8,128)(2,1)S(1)} %get-tuple-element.144), channel_id=1, source_target_pairs={{0,16},{8,24},{16,0},{24,8},{1,17},{9,25},{17,1},{25,9},{2,18},{10... | collective-permute-start | bytes 245768 | tf_op jit(solution)/shard_map/ppermute | solution.py:300
  116.7 9.4 %collective-permute-start.40 = (bf16[320,128]{1,0:T(8,128)(2,1)S(1)}, bf16[320,128]{1,0:T(8,128)(2,1)S(1)}, u32[]{:S(2)}, u32[]{:S(2)}) collective-permute-start(bf16[320,128]{1,0:T(8,128)(2,1)S(1)} %get-tuple-element.145), channel_id=1, source_target_pairs={{0,24},{8,16},{16,8},{24,0},{1,25},{9,17},{17,9},{25,1},{2,26},{10... | collective-permute-start | bytes 245768 | tf_op jit(solution)/shard_map/ppermute | solution.py:300
  126.8 16.5 %all-to-all-start.1 = ((f32[32,8,128]{2,1,0:T(8,128)}), f32[32,8,128]{2,1,0:T(8,128)S(1)}, u32[]{:S(2)}, u32[]{:S(2)}) async-start(f32[32,8,128]{2,1,0:T(8,128)} %bitcast.3), calls=%async_computation.1 | async-start | bytes 262144 | tf_op jit(solution)/shard_map/all_to_all | solution.py:1269
  135.2 7.9 %collective-permute-start.42 = (f32[152,128]{1,0:T(8,128)S(1)}, f32[152,128]{1,0:T(8,128)S(1)}, u32[]{:S(2)}, u32[]{:S(2)}) collective-permute-start(f32[152,128]{1,0:T(8,128)S(1)} %get-tuple-element.155), channel_id=1, source_target_pairs={{0,2},{2,0},{1,3},{3,1},{4,6},{6,4},{5,7},{7,5},{8,10},{10,8},{9,1... | collective-permute-start | bytes 233480 | tf_op jit(solution)/shard_map/ppermute | solution.py:300
  (28 other events, 259.3 us)

commit v4 on v3

--- a/solution.py
+++ b/solution.py
@@ -7,7 +7,7 @@
 from jax.experimental.pallas import tpu as pltpu
 from jax.sharding import Mesh, PartitionSpec as P
 
-OPT = {'flop': 200000000.0, 'zorder': [2, 3, 1], 'merge_w': False, 'w1_after_in': False, 'core_w1': 1, 'core_w1_after_xy': False, 'fwd_after_core_w1': False, 'w2_after': 0, 'w2_before': 1, 'core_w2_after': 1, 'kw2_after': False, 'rs': 'two', 'pass_after_g2': True, 'pass_after_near': False, 'core_g2_after': True, 'k5_after': True, 'core1_after_g2': False, 'core_g1_after_g2': True, 'a2a_after_core1': False, 'sum_after_f': False, 'sum_after_y': True, 'f_after_sum': False, 'told_after_f': True, 'core_w1_after': 0, 'y2_after': 1}
+OPT = {'flop': 0, 'zorder': [2, 3, 1], 'merge_w': False, 'w1_after_in': False, 'core_w1': 1, 'core_w1_after': 0, 'fwd_after_core_w1': False, 'w2_after': 1, 'w2_before': 1, 'core_w2_after': 1, 'kw2_after': False, 'rs': 'two', 'pass_after_g2': True, 'pass_after_near': False, 'k5_after': True, 'core1_after_g2': False, 'core_g1_after_g2': True, 'a2a_after_core1': False, 'sum_after_f': False, 'f_after_sum': False, 'told_after_f': False, 'prep_after_take': True, 'finish_last': True, 'split_first': True, 'split_conv': True, 'ki_after_kg': False, 'load': False, 'a2a_after_g2': False, 'core_g2': 0, 'adam_limit': 62}
 C1 = 256
 C2 = 512
 MEL = 8
@@ -281,7 +281,7 @@
 
 
 def call(kernel, out, in_specs, out_specs, scratch=(), limit=VMEM_LIMIT):
-    cost = COSTS[kernel]
+    cost = COSTS[kernel] * OPT.get(kernel.__name__, 1)
     return pl.pallas_call(
         kernel,
         out_shape=out,
@@ -331,21 +331,33 @@
     return OPT["zorder"]
 
 
+def order_entry(order, row, column):
+    row_of = lax.broadcasted_iota(jnp.int32, order.shape, 0)
+    column_of = lax.broadcasted_iota(jnp.int32, order.shape, 1)
+    chosen = jnp.where((row_of == row) & (column_of == column), order, 0).astype(F32)
+    return jnp.sum(jnp.sum(chosen, axis=1, keepdims=True), axis=0, keepdims=True)
+
+
 def write_facts(order_ref, counts_ref, facts_ref):
-    z, core = place("z", "core")
-    row_of = lax.broadcasted_iota(jnp.int32, (8, LANES), 0)
-    facts = jnp.zeros((8, LANES), jnp.int32)
-    total = 0
+    z, y, core = place("z", "y", "core")
+    order, counts = order_ref[...], counts_ref[...]
+    column_of = lax.broadcasted_iota(jnp.int32, counts.shape, 1)
+    row_of = lax.broadcasted_iota(jnp.int32, (16, LANES), 0)
+    facts = jnp.zeros((16, LANES), F32)
+    total = jnp.zeros((1, 1), F32)
     for row in range(4):
         for j in range(CL_MB):
-            total = total + counts_ref[row * 8 + order_ref[row, z * CL_MB + j]]
+            clip = order_entry(order, row, z * CL_MB + j).astype(jnp.int32) + row * 8
+            count = jnp.sum(
+                jnp.where(column_of == clip, counts, 0).astype(F32), axis=1, keepdims=True
+            )
+            total = total + count
+            target = jnp.where(row % 2 == core, row // 2 * CL_MB + j, -1)
+            facts = jnp.where(row_of == target, count, facts)
     facts = jnp.where(row_of == 4, MEL * total, facts)
-    for group in range(2):
-        for j in range(CL_MB):
-            row = group * 2 + core
-            count = counts_ref[row * 8 + order_ref[row, z * CL_MB + j]]
-            facts = jnp.where(row_of == group * CL_MB + j, count, facts)
-    facts_ref[...] = facts
+    for slot in range(MB * CL_MB):
+        facts = jnp.where(row_of == 8 + slot, order_entry(order, y * 2 + core, slot), facts)
+    facts_ref[...] = facts.astype(jnp.int32)
 
 
 def count_row(facts_ref, clip):
@@ -451,8 +463,18 @@
     return lax.broadcasted_iota(jnp.int32, (rows, LANES), 1)
 
 
+def take_kernel(order_ref, clip_ref, p0, p1, p2, p3):
+    z, y, core = place("z", "y", "core")
+    order = order_ref[...]
+    for step, piece in enumerate((p0, p1, p2, p3)):
+        plane = jnp.bitwise_xor(z, step)
+        for j in range(CL_MB):
+            clip = order_entry(order, y * 2 + core, plane * CL_MB + j)[0, 0].astype(jnp.int32)
+            piece[j] = clip_ref[clip]
+
+
 def prepare_kernel(
-    order_ref, counts_ref, clip_ref, one_in, two_in, norm_in, cot_in, p0, p1, p2, p3, one_keep,
+    order_ref, counts_ref, one_in, two_in, norm_in, cot_in, one_keep,
     two_keep, send_ref, gain_ref, cot_own, facts_ref, one_ref, two_ref, norm_ref, cot_ref, sems
 ):
     z, x, y, core = place(*AXES)
@@ -460,13 +482,6 @@
     loads = start_copies(
         [(one_in, one_ref), (two_in, two_ref), (norm_in, norm_ref), (cot_in, cot_ref)], sems
     )
-    copies = []
-    for step, piece in enumerate((p0, p1, p2, p3)):
-        plane = jnp.bitwise_xor(z, step)
-        for j in range(CL_MB):
-            clip = order_ref[group, plane * CL_MB + j]
-            copies.append((clip_ref.at[clip], piece.at[j]))
-    started = start_copies(copies, sems, 4)
     write_facts(order_ref, counts_ref, facts_ref)
     wait_all(loads)
     for tap in range(TAPS):
@@ -491,7 +506,8 @@
     def cot_rows(y_of):
         rows = []
         for j in range(CL_MB):
-            row = cot_ref[pl.ds(order_ref[group, z * CL_MB + j], 1), :]
+            clip = order_entry(order_ref[...], group, z * CL_MB + j)[0, 0].astype(jnp.int32)
+            row = cot_ref[pl.ds(clip, 1), :]
             picked = jnp.zeros((1, LANES), F32)
             for block in range(MB):
                 moved = pltpu.roll(
@@ -511,12 +527,33 @@
     low = [row - top for row, top in zip(rest, middle)]
     packed = jnp.concatenate(high + middle + low + [jnp.zeros((10, LANES), F32)], axis=0)
     send_ref[144 + CHUNK : 160 + CHUNK, :] = packed.astype(BF)
-    wait_all(started)
+
+
+def first_weight_kernel(o0, o1, o2, o3, others, weight_ref, gain_ref):
+    z, y, core = place("z", "y", "core")
+    gains = jnp.zeros((8, LANES), F32)
+    for half in range(2):
+
+        def source_of(column, half=half):
+            from_core = jnp.bitwise_xor((column // 64) % 2, core)
+            from_y = jnp.bitwise_xor(column // 128, y)
+            return from_core * 256 + from_y * 128 + half * 64 + column % 64
+
+        spread = exchange_matrix(512, C1, source_of)
+        for step, own in enumerate((o0, o1, o2, o3)):
+            z_of = jnp.bitwise_xor(z, step)
+            other = others[step * 304 : step * 304 + 288]
+            four = jnp.concatenate([own[0:144], own[144:288], other[0:144], other[144:288]], axis=1)
+            both = dot_nn(four, spread).astype(BF)
+            for tap in range(TAPS):
+                weight_ref[tap, z_of, half * 16 : half * 16 + 16] = both[tap * 16 : (tap + 1) * 16]
+            if half == 0:
+                gains = gains + own[CHUNK : CHUNK + 16].astype(F32)[0:8]
+    gain_ref[...] = gains
 
 
 def first_conv_kernel(
-    facts_ref, a0, a1, a23, b0, b1, b23, o0, o1, o2, o3, others,
-    pre_ref, x_ref, weight_ref, stat_ref, gain_ref, sems
+    facts_ref, a0, a1, a23, b0, b1, b23, weight_ref, pre_ref, x_ref, stat_ref, sems
 ):
     z, x, y, core = place(*AXES)
     copies = []
@@ -530,25 +567,6 @@
                 row = pl.multiple_of((y_of * CL_MB + j) * ROWS + frames, 64)
                 copies.append((source.at[base + step], x_ref.at[pl.ds(row, 64), :]))
     started = start_copies(copies, sems)
-    gains = jnp.zeros((8, LANES), F32)
-    for half in range(2):
-
-        def source_of(column, half=half):
-            from_core = jnp.bitwise_xor((column // 64) % 2, core)
-            from_y = jnp.bitwise_xor(column // 128, y)
-            return from_core * 256 + from_y * 128 + half * 64 + column % 64
-
-        spread = exchange_matrix(512, C1, source_of)
-        for step, own in enumerate((o0, o1, o2, o3)):
-            z_of = jnp.bitwise_xor(z, step)
-            other = others[step * 304 : step * 304 + 288]
-            four = jnp.concatenate([own[0:144], own[144:288], other[0:144], other[144:288]], axis=1)
-            both = dot_nn(four, spread).astype(BF)
-            for tap in range(TAPS):
-                weight_ref[tap, z_of, half * 16 : half * 16 + 16] = both[tap * 16 : (tap + 1) * 16]
-            if half == 0:
-                gains = gains + own[CHUNK : CHUNK + 16].astype(F32)[0:8]
-    gain_ref[...] = gains
     wait_all(started)
     weight = weight_ref[...].reshape(TAPS * LANES, C1)
     first = jnp.zeros((1, LANES), F32)
@@ -576,25 +594,18 @@
         target[(clip % 2) * ROWS : (clip % 2 + 1) * ROWS, :] = value.astype(BF)
 
 
-def second_weight_kernel(own_ref, other_ref, weight_ref, pieces, sems):
+def second_weight_kernel(own_ref, other_ref, weight_ref):
     z, y, core = place("z", "y", "core")
-    copies = []
+    spread = exchange_matrix(C2, C2, block_exchange)
     for step in range(MB):
-        for source, core_of in ((own_ref, core), (other_ref, 1 - core)):
-            for turn in range(2):
-                part = jnp.bitwise_xor(y, turn) * 2 + core_of
-                copies.append(
-                    (
-                        source.at[pl.ds((step * 2 + turn) * CHUNK, CHUNK), :],
-                        pieces.at[jnp.bitwise_xor(z, step), part],
-                    )
-                )
-    started = start_copies(copies, sems)
-    spread = exchange_matrix(C2, C2, block_exchange)
-    wait_all(started)
-    for z_of in range(MB):
-        natural = jnp.concatenate([pieces[z_of, part] for part in range(4)], axis=1)
-        both = dot_nn(natural, spread).astype(BF)
+        z_of = jnp.bitwise_xor(z, step)
+        spans = [slice((step * 2 + turn) * CHUNK, (step * 2 + turn + 1) * CHUNK) for turn in range(2)]
+        parts = []
+        for y_of in range(2):
+            own = jnp.where(y == y_of, own_ref[spans[0]], own_ref[spans[1]])
+            other = jnp.where(y == y_of, other_ref[spans[0]], other_ref[spans[1]])
+            parts += [jnp.where(core == 0, own, other), jnp.where(core == 0, other, own)]
+        both = dot_nn(jnp.concatenate(parts, axis=1), spread).astype(BF)
         for tap in range(TAPS):
             weight_ref[tap, z_of] = both[tap * 32 : (tap + 1) * 32]
 
@@ -619,6 +630,44 @@
     for clip in range(CLIPS_CORE):
         span = slice(clip * ROWS, (clip + 1) * ROWS)
         pre = gather_taps(dot_nt(hidden[span, :], weight))
+        pre_ref[span, :] = pre
+        kept = pre * valid_rows(facts_ref, clip)
+        plus = channel_sums(kept, kept * pre)
+        first, second = first + plus[0], second + plus[1]
+    put_pair(stat_ref, first, second)
+
+
+def near_conv_kernel(a0, a1, a2, b0, b1, b2, weight_ref, pre_ref):
+    x, y = place("x", "y")
+
+    def lane(x_of, y_of):
+        return pl.ds(pl.multiple_of((x_of * 2 + y_of) * LANES, LANES), LANES)
+
+    weight = jnp.concatenate(
+        [
+            weight_ref[:, :, :, lane(*chip)].reshape(TAPS * LANES, LANES)
+            for chip in ((x, y), (1 - x, y), (x, 1 - y))
+        ],
+        axis=1,
+    )
+    for clip in range(CLIPS_CORE):
+        parts = (a0, a1, a2) if clip < 2 else (b0, b2, b1)
+        rows = slice((clip % 2) * ROWS, (clip % 2 + 1) * ROWS)
+        three = jnp.concatenate([part[rows, :] for part in parts], axis=1)
+        pre_ref[clip * ROWS : (clip + 1) * ROWS, :] = gather_taps(dot_nt(three, weight))
+
+
+def far_conv_kernel(facts_ref, a3, b3, weight_ref, near_ref, pre_ref, stat_ref):
+    x, y = place("x", "y")
+    lane = pl.multiple_of(((1 - x) * 2 + 1 - y) * LANES, LANES)
+    weight = weight_ref[:, :, :, pl.ds(lane, LANES)].reshape(TAPS * LANES, LANES)
+    first = jnp.zeros((1, LANES), F32)
+    second = jnp.zeros((1, LANES), F32)
+    for clip in range(CLIPS_CORE):
+        span = slice(clip * ROWS, (clip + 1) * ROWS)
+        part = a3 if clip < 2 else b3
+        rows = slice((clip % 2) * ROWS, (clip % 2 + 1) * ROWS)
+        pre = near_ref[span, :] + gather_taps(dot_nt(part[rows, :], weight))
         pre_ref[span, :] = pre
         kept = pre * valid_rows(facts_ref, clip)
         plus = channel_sums(kept, kept * pre)
@@ -764,7 +813,8 @@
 
 
 def second_weight_grad_kernel(*rest):
-    parts, (columns, keep_ref, send_ref, hidden, natural, sems) = rest[:8], rest[8:]
+    parts, columns, keeps, sends = rest[:8], rest[8], rest[9:12], rest[12:15]
+    hidden, natural, sems = rest[15:]
     core = place("core")
     started = start_copies(hidden_copies(parts, hidden), sems)
     spread = exchange_matrix(C2, C2, block_exchange)
@@ -774,22 +824,25 @@
         hidden[span, :] = dot_nn(hidden[span, :], spread).astype(BF)
     for tap in range(TAPS):
         natural[...] = dot_tn(columns[:, lanes_of(tap)], hidden[...])
+        keep_ref, send_ref = keeps[tap // 3], sends[tap // 3]
+        target = slice(tap % 3 * 32, (tap % 3 + 1) * 32)
         for y_of in range(2):
             keep = natural[:, pl.ds(pl.multiple_of((y_of * 2 + core) * LANES, LANES), LANES)]
             send = natural[:, pl.ds(pl.multiple_of((y_of * 2 + 1 - core) * LANES, LANES), LANES)]
             for z_of in range(MB):
                 rows = slice(z_of * 32, (z_of + 1) * 32)
-                target = slice(tap * 32, (tap + 1) * 32)
                 keep_ref[z_of, y_of, target] = keep[rows]
                 send_ref[z_of, y_of, target] = send[rows]
 
 
-def second_core_kernel(keep_ref, got_ref, own_ref, n1, n2, n3):
+def second_core_kernel(k0, k1, k2, g0, g1, g2, own_ref, n1, n2, n3):
     z = place("z")
-    own_ref[...] = keep_ref[z] + got_ref[z]
-    for step, target in ((1, n1), (2, n2), (3, n3)):
-        at = jnp.bitwise_xor(z, step)
-        target[...] = (keep_ref[at] + got_ref[at]).astype(BF)
+    for third, (keep_ref, got_ref) in enumerate(((k0, g0), (k1, g1), (k2, g2))):
+        rows = slice(third * 96, (third + 1) * 96)
+        own_ref[:, rows] = keep_ref[z] + got_ref[z]
+        for step, target in ((1, n1), (2, n2), (3, n3)):
+            at = jnp.bitwise_xor(z, step)
+            target[:, rows] = (keep_ref[at] + got_ref[at]).astype(BF)
 
 
 def second_sum_kernel(own_ref, g1, g2, g3, keep_ref, send_ref, square_ref):
@@ -860,6 +913,48 @@
             target = slice(tap * 32, (tap + 1) * 32)
             keep_ref[z_of, target] = both[rows, 0:LANES]
             send_ref[z_of, target] = both[rows, LANES : 2 * LANES]
+
+
+def first_weight_grad_kernel(
+    facts_ref, slope_ref, pre_ref, own_ref, other_ref, sum_own, sum_other, gain_ref, x_ref,
+    columns, keep_ref, send_ref, turned
+):
+    core = place("core")
+    pixels = pixel_row(facts_ref)
+    mean, scale = norm_rows(own_ref, other_ref, pixels)
+    sums = pair_sums(sum_own, sum_other)
+
+    def source_of(column):
+        core_of = jnp.where(column < 128, core, 1 - core)
+        return ((column // 64) % 2) * 128 + core_of * 64 + column % 64
+
+    spread = exchange_matrix(C1, C1, source_of)
+    for clip in range(CLIPS_CORE):
+        span = slice(clip * ROWS, (clip + 1) * ROWS)
+        mask = valid_rows(facts_ref, clip)
+        grad = pre_grad(
+            slope_ref[span, :], pre_ref[span, :], mask, mean, scale, gain_ref[0:1, :], sums, pixels
+        )
+        scatter_taps(grad, columns, clip * ROWS)
+        turned[span, :] = dot_nn(x_ref[span, :], spread).astype(BF)
+    for tap in range(TAPS):
+        both = dot_tn(columns[:, lanes_of(tap)], turned[...])
+        for z_of in range(MB):
+            rows = slice(z_of * 32, (z_of + 1) * 32)
+            target = slice(tap * 32, (tap + 1) * 32)
+            keep_ref[z_of, target] = both[rows, 0:LANES]
+            send_ref[z_of, target] = both[rows, LANES : 2 * LANES]
+
+
+def input_grad_kernel(columns, weight_ref, part_ref):
+    weight = weight_ref[...].reshape(TAPS * LANES, C1)
+    for clip in range(CLIPS_CORE):
+        partial = dot_nn(columns[clip * ROWS : (clip + 1) * ROWS, :], weight).astype(BF)
+        for z_of in range(MB):
+            for x_of in range(2):
+                target = slice(((clip % 2) * MB + z_of) * 64, ((clip % 2) * MB + z_of + 1) * 64)
+                rows = slice((z_of * 2 + x_of) * 64, (z_of * 2 + x_of + 1) * 64)
+                part_ref[x_of * 2 + clip // 2, target, :] = partial[rows]
 
 
 def first_core_kernel(
@@ -895,7 +990,7 @@
         target[CHUNK + 16 : CHUNK + 32, :] = pooled_tile
 
 
-def first_sum_kernel(own_ref, n0, g1, g2, g3, square_two, told_ref, keep_ref, send_ref, norm_ref):
+def first_sum_kernel(own_ref, n0, g1, g2, g3, square_two, two_send, told_ref, keep_ref, send_ref, norm_ref):
     z, y, core = place("z", "y", "core")
     total = own_ref[...]
     norm = n0[CHUNK : CHUNK + 16, :].astype(F32)
@@ -917,24 +1012,53 @@
     send_ref[0:144, :] = jnp.where(left, high[0:144], pltpu.roll(high[144:288], 64, 1))
     rows = jnp.concatenate([norm, jnp.zeros((4, LANES), F32)], axis=0)
     send_ref[144:152, :] = rows
+    send_ref[152 : 152 + CHUNK, :] = two_send[...]
     norm_ref[...] = rows
 
 
-def shard_kernel(keep_ref, got_ref, norm_ref, one_ref, norm_out):
+def load_kernel(*refs):
+    half = (len(refs) - 1) // 2
+    wait_all(start_copies(list(zip(refs[:half], refs[half : 2 * half])), refs[-1]))
+
+
+def adam_write(refs, outs, gradient, factor, step_rate, decay_rate, at):
+    weight, moment, square = (ref[at] for ref in refs)
+    clipped = gradient * factor
+    moment_new = BETA_ONE * moment + (1.0 - BETA_ONE) * clipped
+    square_new = BETA_TWO * square + (1.0 - BETA_TWO) * clipped * clipped
+    corrected = moment_new * (1.0 / (1.0 - BETA_ONE**STEP))
+    scaled = jnp.sqrt(square_new * (1.0 / (1.0 - BETA_TWO**STEP))) + ADAM_EPS
+    weight_new = weight - step_rate * (corrected / scaled + decay_rate * weight)
+    for out, value in zip(outs, (clipped, moment_new, square_new, weight_new, weight_new.astype(BF))):
+        out[at] = value
+
+
+def adam_kernel(told_ref, keep_ref, got_ref, norm_ref, two_keep, *refs):
     z, y = place("z", "y")
+    one, two, norm, outs = refs[0:3], refs[3:6], refs[6:9], refs[9:]
+    norm_out, one_out, two_out, small_out = outs[0], outs[1:6], outs[6:11], outs[11:16]
+    told = jnp.sum(told_ref[...], axis=0, keepdims=True)
+    length = jnp.sqrt(jnp.sum(told, axis=1, keepdims=True))
+    norm_out[...] = length
+    factor = jnp.minimum(1.0, CLIP_NORM / (length + 1e-06))
     keep, got = keep_ref[...], got_ref[0:144, :]
     first, second = jnp.where(y == 0, keep, got), jnp.where(y == 0, got, keep)
-    spans = []
-    for half in (first, second):
-        spans.append(jnp.concatenate([half[:, 0:64], half[:, 64:128]], axis=0))
+    spans = [jnp.concatenate([half[:, 0:64], half[:, 64:128]], axis=0) for half in (first, second)]
     for tap in range(TAPS):
-        rows = [span[tap * 32 : (tap + 1) * 32] for span in spans]
-        one_ref[tap] = jnp.swapaxes(jnp.concatenate(rows, axis=0), 0, 1)
+        rows = slice(tap * 32, (tap + 1) * 32)
+        gradient = jnp.swapaxes(jnp.concatenate([span[rows] for span in spans], axis=0), 0, 1)
+        adam_write(one, one_out, gradient, factor, (9 * C1) ** (-0.5), WEIGHT_DECAY, tap)
+        keep, got = two_keep[rows, :], got_ref[152 + tap * 32 : 152 + (tap + 1) * 32, :]
+        gradient = jnp.concatenate(
+            [jnp.where(y == 0, keep, got), jnp.where(y == 0, got, keep)], axis=0
+        )
+        adam_write(two, two_out, gradient, factor, (9 * C2) ** (-0.5), WEIGHT_DECAY, tap)
     keep, got = norm_ref[...], got_ref[144:152, :]
     first, second = jnp.where(y == 0, keep, got), jnp.where(y == 0, got, keep)
     low = pltpu.roll(first, (0 - z * 32) % LANES, 1)
     high = pltpu.roll(second, (32 - z * 32) % LANES, 1)
-    norm_out[...] = jnp.where(lane_index(8) < 32, low, high)[0:4, 0:64]
+    gradient = jnp.where(lane_index(8) < 32, low, high)[0:4, 0:64]
+    adam_write(norm, small_out, gradient, factor, GAIN_RATE, 0.0, slice(None))
 
 
 def input_sum_kernel(facts_ref, got_ref, f0, f1, f2, f3):
@@ -952,14 +1076,13 @@
             target[j] = jnp.where(frame < count, total, 0.0).astype(BF)
 
 
-def finish_kernel(order_ref, f0, g1, g2, g3, n0, n1, n2, n3, grad_ref, pooled_ref, scratch):
-    z, y, core = place("z", "y", "core")
-    row = y * 2 + core
+def finish_kernel(facts_ref, f0, g1, g2, g3, n0, n1, n2, n3, grad_ref, pooled_ref, scratch):
+    z = place("z")
     for step, (piece, told) in enumerate(((f0, n0), (g1, n1), (g2, n2), (g3, n3))):
         at = jnp.bitwise_xor(z, step)
         rows = told[CHUNK + 16 : CHUNK + 32, :].astype(F32)
         for j in range(CL_MB):
-            clip = order_ref[row, at * CL_MB + j]
+            clip = facts_ref[pl.ds(8 + at * CL_MB + j, 1), :][0, 0]
             grad_ref[clip] = piece[j]
             for part in range(2):
                 chips = [rows[chip * 4 + part * 2 + j : chip * 4 + part * 2 + j + 1] for chip in range(4)]
@@ -971,11 +1094,15 @@
 FLOP_SCALE = OPT['flop']
 BYTE_SCALE = 0
 COSTS = {
-    prepare_kernel: 3,
+    take_kernel: 1,
+    prepare_kernel: 2,
+    first_weight_kernel: 1,
     first_conv_kernel: 4,
     hidden_kernel: 0.4,
     second_weight_kernel: 2.8,
     second_conv_kernel: 3.5,
+    near_conv_kernel: 3,
+    far_conv_kernel: 2,
     pool_kernel: 1.1,
     grad_columns_kernel: 1.7,
     hidden_grad_kernel: 3.4,
@@ -986,9 +1113,12 @@
     second_sum_kernel: 0.2,
     first_slope_kernel: 0.8,
     first_grads_kernel: 4,
+    first_weight_grad_kernel: 2,
+    input_grad_kernel: 1.5,
     first_core_kernel: 0.2,
     first_sum_kernel: 0.8,
-    shard_kernel: 0.3,
+    adam_kernel: 2,
+    load_kernel: 1,
     input_sum_kernel: 0.3,
     finish_kernel: 1.5,
 }
@@ -1017,30 +1147,27 @@
     norm_square,
 ):
     one_view, two_view = kernel_one, jnp.swapaxes(kernel_two, 1, 2)
-    p0, p1, p2, p3, one_keep, two_keep, send, gain_rows, cot_own, facts = call(
+    p0, p1, p2, p3 = call(
+        take_kernel, [shape_of((CL_MB, 64, C1))] * MB, [VM] * 2, [VM] * MB, limit=62 * 1024 * 1024
+    )(clip_order, clip_input.reshape(MB * CL_MB, 64, C1))
+    one_keep, two_keep, send, gain_rows, cot_own, facts = call(
         prepare_kernel,
-        [shape_of((CL_MB, 64, C1))] * MB
-        + [shape_of((144, LANES)), shape_of((CHUNK, LANES)), shape_of((160 + CHUNK, LANES))]
-        + [shape_of((16, LANES)), shape_of((8, LANES), F32), shape_of((8, LANES), jnp.int32)],
-        [SM, SM] + [HB] * 5,
-        [VM] * 10,
+        [shape_of((144, LANES)), shape_of((CHUNK, LANES)), shape_of((160 + CHUNK, LANES))]
+        + [shape_of((16, LANES)), shape_of((8, LANES), F32), shape_of((16, LANES), jnp.int32)],
+        [VM, VM] + [HB] * 4,
+        [VM] * 6,
         [
             pltpu.VMEM(one_view.shape, F32),
             pltpu.VMEM(two_view.shape, F32),
             pltpu.VMEM(norm_params.shape, F32),
             pltpu.VMEM(cotangent.shape, F32),
-            pltpu.SemaphoreType.DMA((4 + MB * CL_MB,)),
+            pltpu.SemaphoreType.DMA((4,)),
         ],
         limit=62 * 1024 * 1024,
     )(
-        clip_order,
-        frame_counts,
-        clip_input.reshape(MB * CL_MB, 64, C1),
-        one_view,
-        two_view,
-        norm_params,
-        cotangent,
-    )
+        pin("prep_after_take", clip_order, p0), frame_counts.reshape(1, 32), one_view, two_view, norm_params, cotangent
+    )
+
     def spread_z(values):
         got = {step: swap(values[step], "z", step) for step in steps_of()}
         return [values[0]] + [got[step] for step in (1, 2, 3)]
@@ -1086,20 +1213,20 @@
             4: lambda: after(two_flat, a1, b1, one_others),
         }[OPT["w2_after"]]()
         two_parts = spread_z([two_flat] * 4)
-    pre_one, masked, weight_one, stat_one, gains = call(
+    weight_one, gains = call(
+        first_weight_kernel,
+        [shape_of((TAPS, MB, 32, C1)), shape_of((8, LANES), F32)],
+        [VM] * 5,
+        [VM] * 2,
+    )(*one_parts, one_others)
+    pre_one, masked, stat_one = call(
         first_conv_kernel,
-        [
-            shape_of((PIXELS, LANES), F32),
-            shape_of((PIXELS, C1)),
-            shape_of((TAPS, MB, 32, C1)),
-            shape_of((8, LANES), F32),
-            shape_of((8, LANES), F32),
-        ],
-        [VM] + [ANY] * 6 + [VM] * 5,
-        [VM] * 5,
+        [shape_of((PIXELS, LANES), F32), shape_of((PIXELS, C1)), shape_of((8, LANES), F32)],
+        [VM] + [ANY] * 6 + [VM],
+        [VM] * 3,
         [pltpu.SemaphoreType.DMA((8 * MB,))],
     )(
-        after(facts, *two_parts[1:]) if OPT["w2_before"] == 2 else facts, *inputs, *one_parts, one_others
+        after(facts, *two_parts[1:]) if OPT["w2_before"] == 2 else facts, *inputs, weight_one
     )
     stat_one_other = swap(stat_one, "core")
 
@@ -1118,20 +1245,28 @@
     two_all_other = swap(two_all, "core")
     two_all = pin("kw2_after", two_all, hidden_parts[1], hidden_parts[5])
     weight_two = call(
-        second_weight_kernel,
-        shape_of((TAPS, MB, 32, C2)),
-        [ANY, ANY],
-        VM,
-        [pltpu.VMEM((MB, 4, CHUNK, LANES), BF), pltpu.SemaphoreType.DMA((16,))],
+        second_weight_kernel, shape_of((TAPS, MB, 32, C2)), [VM, VM], VM
     )(two_all, two_all_other)
 
-    pre_two, stat_two = call(
-        second_conv_kernel,
-        [shape_of((PIXELS, LANES), F32), shape_of((8, LANES), F32)],
-        [VM] + [ANY] * 8 + [VM],
-        [VM] * 2,
-        [pltpu.VMEM((PIXELS, C2), BF), pltpu.SemaphoreType.DMA((8,))],
-    )(facts, *hidden_parts, weight_two)
+    if OPT["split_conv"]:
+        ha = hidden_parts
+        near_two = call(near_conv_kernel, shape_of((PIXELS, LANES), F32), [VM] * 7, VM)(
+            ha[0], ha[1], ha[2], ha[4], ha[5], ha[6], weight_two
+        )
+        pre_two, stat_two = call(
+            far_conv_kernel,
+            [shape_of((PIXELS, LANES), F32), shape_of((8, LANES), F32)],
+            [VM] * 5,
+            [VM] * 2,
+        )(facts, ha[3], ha[7], weight_two, near_two)
+    else:
+        pre_two, stat_two = call(
+            second_conv_kernel,
+            [shape_of((PIXELS, LANES), F32), shape_of((8, LANES), F32)],
+            [VM] + [ANY] * 8 + [VM],
+            [VM] * 2,
+            [pltpu.VMEM((PIXELS, C2), BF), pltpu.SemaphoreType.DMA((8,))],
+        )(facts, *hidden_parts, weight_two)
     stat_two_other = swap(stat_two, "core")
     slope_two, sum_two, pooled_own = call(
         pool_kernel,
@@ -1178,31 +1313,42 @@
         a_got = a_near = swap(a_send, "x")
         b_got = b_near = swap(b_send, "y")
         a_pool = a_got[2 * HALF :]
-    two_part, two_part_send = call(
+    thirds = call(
         second_weight_grad_kernel,
-        [shape_of((MB, 2, CHUNK, LANES), F32)] * 2,
+        [shape_of((MB, 2, 96, LANES), F32)] * 6,
         [ANY] * 8 + [VM],
-        [VM] * 2,
+        [VM] * 6,
         [
             pltpu.VMEM((PIXELS, C2), BF),
             pltpu.VMEM((LANES, C2), F32),
             pltpu.SemaphoreType.DMA((8,)),
         ],
     )(*hidden_parts, columns_two)
+
+    def sum_cores(*deps):
+        sends = [after(part, *deps) if deps else part for part in thirds[3:6]]
+        return call(
+            second_core_kernel,
+            [shape_of((2, CHUNK, LANES), F32)] + [shape_of((2, CHUNK, LANES))] * 3,
+            [VM] * 6,
+            [VM] * 4,
+        )(*thirds[0:3], *[swap(part, "core") for part in sends])
+
+    if OPT["core_g2"] == 0:
+        two_own, t1, t2, t3 = sum_cores()
+        a_got = after(a_got, t1)
+    else:
+        a_got = pin("pass_after_g2", a_got, thirds[0])
     a_next, b_next = call(pass_on_kernel, [shape_of((HALF, LANES))] * 2, [VM] * 4, [VM] * 2)(
         a_mid,
-        pin("pass_after_near", pin("pass_after_g2", a_got, two_part), a_near, b_near),
+        pin("pass_after_near", a_got, a_near, b_near),
         b_mid,
         b_got,
     )
     a_next = jnp.concatenate([a_next, pooled_own, a_pool])
     a_last, b_last = swap(a_next, "y"), swap(b_next, "x")
-    two_own, t1, t2, t3 = call(
-        second_core_kernel,
-        [shape_of((2, CHUNK, LANES), F32)] + [shape_of((2, CHUNK, LANES))] * 3,
-        [VM] * 2,
-        [VM] * 4,
-    )(two_part, swap(pin("core_g2_after", two_part_send, a_next), "core"))
+    if OPT["core_g2"] == 1:
+        two_own, t1, t2, t3 = sum_cores(a_next)
     slope_one, sum_one = call(
         first_slope_kernel,
         [shape_of((PIXELS, LANES), F32), shape_of((8, LANES), F32)],
@@ -1211,23 +1357,35 @@
     )(pin("k5_after", facts, t1), a_own, a_near, a_last, b_own, b_near, b_last, pre_one, stat_one, stat_one_other, gains)
     sum_one_other = swap(sum_one, "core")
 
-    input_part, one_part, one_part_send = call(
-        first_grads_kernel,
-        [shape_of((4, ROWS, C1))] + [shape_of((MB, CHUNK, LANES), F32)] * 2,
-        [VM] * 10,
-        [VM] * 3,
-        [pltpu.VMEM((PIXELS, TAPS * LANES), BF), pltpu.VMEM((PIXELS, C1), BF)],
-    )(
-        facts, slope_one, pre_one, stat_one, stat_one_other, sum_one, sum_one_other, gains, weight_one,
-        masked,
-    )
+    if OPT["split_first"]:
+        columns_one, one_part, one_part_send = call(
+            first_weight_grad_kernel,
+            [shape_of((PIXELS, TAPS * LANES))] + [shape_of((MB, CHUNK, LANES), F32)] * 2,
+            [VM] * 9,
+            [VM] * 3,
+            [pltpu.VMEM((PIXELS, C1), BF)],
+        )(facts, slope_one, pre_one, stat_one, stat_one_other, sum_one, sum_one_other, gains, masked)
+        input_part = call(input_grad_kernel, shape_of((4, ROWS, C1)), [VM] * 2, VM)(
+            pin("ki_after_kg", columns_one, one_part), weight_one
+        )
+    else:
+        input_part, one_part, one_part_send = call(
+            first_grads_kernel,
+            [shape_of((4, ROWS, C1))] + [shape_of((MB, CHUNK, LANES), F32)] * 2,
+            [VM] * 10,
+            [VM] * 3,
+            [pltpu.VMEM((PIXELS, TAPS * LANES), BF), pltpu.VMEM((PIXELS, C1), BF)],
+        )(
+            facts, slope_one, pre_one, stat_one, stat_one_other, sum_one, sum_one_other, gains, weight_one,
+            masked,
+        )
+
     two_keep_sum, two_send_sum, square_two = call(
         second_sum_kernel,
         [shape_of((CHUNK, LANES), F32)] * 2 + [shape_of((8, LANES), F32)],
         [VM] * 4,
         [VM] * 3,
     )(*spread_z([two_own, t1, t2, t3]))
-    two_got_sum = swap(two_send_sum, "y") if not OPT['y2_after'] else None
 
     one_own, n0, n1, n2, n3 = call(
         first_core_kernel,
@@ -1242,13 +1400,11 @@
         pooled_own, a_pool, a_last,
     )
     g1, g2, g3 = spread_z([n0, n1, n2, n3])[1:]
-    input_part = pin("a2a_after_core1", input_part, n1)
+    input_part = pin("a2a_after_g2", pin("a2a_after_core1", input_part, n1), square_two)
     input_got = lax.all_to_all(input_part, ("x", "y"), 0, 0, tiled=True)
     f0, f1, f2, f3 = call(
         input_sum_kernel, [shape_of((CL_MB, 64, C1))] * MB, [VM] * 2, [VM] * 4
     )(facts, input_got)
-    if OPT["y2_after"]:
-        two_got_sum = swap(after(two_send_sum, n1), "y")
     if not OPT["f_after_sum"]:
         f1, f2, f3 = spread_z([f0, f1, f2, f3])[1:]
     told, one_keep_sum, one_send_sum, norm_sum = call(
@@ -1256,49 +1412,65 @@
         [
             shape_of((32 * 8, LANES), F32),
             shape_of((144, LANES), F32),
-            shape_of((152, LANES), F32),
+            shape_of((152 + CHUNK, LANES), F32),
             shape_of((8, LANES), F32),
         ],
-        [VM] * 6,
+        [VM] * 7,
         [VM] * 4,
     )(
-        pin("sum_after_y", pin("sum_after_f", one_own, f0), two_got_sum), n0, g1, g2, g3, square_two
+        pin("sum_after_f", one_own, f0), n0, g1, g2, g3, square_two, two_send_sum
     )
     if OPT["f_after_sum"]:
         f1, f2, f3 = spread_z([f0, after(f1, told), after(f2, told), after(f3, told)])[1:]
     told = lax.all_to_all(told, AXES, 0, 0, tiled=True)
-    grad_norm = jnp.sqrt(jnp.sum(pin("told_after_f", told, f1, f2, f3)))
-    factor = jnp.minimum(1.0, CLIP_NORM / (grad_norm + 1e-06))
     one_got_sum = swap(one_send_sum, "y")
-    grad_one_shard, norm_shard = call(
-        shard_kernel,
-        [shape_of((TAPS, 64, 64), F32), shape_of((4, 64), F32)],
-        [VM] * 3,
-        [VM] * 2,
-    )(one_keep_sum, one_got_sum, norm_sum)
-    y = lax.axis_index("y")
-    cut = (TAPS, 32, LANES)
-    keep, got = two_keep_sum.reshape(cut), two_got_sum.reshape(cut)
-    grad_two_shard = jnp.where(
-        y == 0, jnp.concatenate([keep, got], axis=1), jnp.concatenate([got, keep], axis=1)
-    )
-    grad_two_shard = jnp.swapaxes(grad_two_shard, 1, 2)
-
-    first_update = adam_step(
-        kernel_one, kernel_one_mean, kernel_one_square, grad_one_shard, factor, (9 * C1) ** (-0.5), WEIGHT_DECAY
-    )
-    second_update = adam_step(
-        kernel_two, kernel_two_mean, kernel_two_square, grad_two_shard, factor, (9 * C2) ** (-0.5), WEIGHT_DECAY
-    )
-    norm_update = adam_step(norm_params, norm_mean, norm_square, norm_shard, factor, GAIN_RATE, 0.0)
-
+    one_shapes = [shape_of(one_view.shape, F32)] * 4 + [shape_of(one_view.shape)]
+    two_shapes = [shape_of(two_view.shape, F32)] * 4 + [shape_of(two_view.shape)]
+    norm_shapes = [shape_of(norm_params.shape, F32)] * 4 + [shape_of(norm_params.shape)]
+    state = (
+        kernel_one,
+        kernel_one_mean,
+        kernel_one_square,
+        two_view,
+        jnp.swapaxes(kernel_two_mean, 1, 2),
+        jnp.swapaxes(kernel_two_square, 1, 2),
+        norm_params,
+        norm_mean,
+        norm_square,
+    )
+    if OPT["load"]:
+        state = (after(state[0], hidden_parts[1], hidden_parts[5]),) + state[1:]
+        state = call(
+            load_kernel,
+            [shape_of(part.shape, F32) for part in state],
+            [HB] * 9,
+            [VM] * 9,
+            [pltpu.SemaphoreType.DMA((9,))],
+        )(*state)
+    updates = call(
+        adam_kernel,
+        [shape_of((1, 1), F32)] + one_shapes + two_shapes + norm_shapes,
+        [VM] * 14,
+        [VM] * 16,
+        limit=OPT['adam_limit'] * 1024 * 1024,
+    )(
+        pin("told_after_f", told, f1, f2, f3),
+        one_keep_sum,
+        one_got_sum,
+        norm_sum,
+        two_keep_sum,
+        *state,
+    )
+    grad_norm = updates[0].reshape(())
+    first_update, norm_update = tuple(updates[1:6]), tuple(updates[11:16])
+    second_update = tuple(jnp.swapaxes(part, 1, 2) for part in updates[6:11])
     input_grad, pooled = call(
         finish_kernel,
         [shape_of((MB * CL_MB, 64, C1)), shape_of((MB * CL_MB, C2), F32)],
-        [SM] + [VM] * 8,
+        [VM] * 9,
         [VM] * 2,
         [pltpu.VMEM((2, MB * CL_MB, C2), F32)],
-    )(clip_order, f0, f1, f2, f3, n0, g1, g2, g3)
+    )(facts, pin("finish_last", f0, updates[0]), f1, f2, f3, n0, g1, g2, g3)
     input_grad = input_grad.reshape(clip_input.shape)
     return (pooled, input_grad, grad_norm) + first_update + second_update + norm_update
 

time: 150 us -> 143 us (0.953)
  waiting for transfers between devices: 52.8 us -> 41.7 us
  Pallas kernels: 31.8 us -> 37.1 us
  starting transfers between devices: 54.8 us -> 58.8 us
  other arithmetic: 3.6 us -> 0.12 us
  between operations: 3.02 us -> 1.07 us
    ppermute x43 -> x44, waiting for transfers between devices: 52.8 us -> 41.7 us  [swap(): return lax.ppermute(value, axis, [(i, i ^ step) for i in range(size)])]
    pallas_call x7 -> x11, Pallas kernels: 18.5 us -> 24.7 us  [the longest x1 5.14 us: fast_body(): call(second_weight_grad_kernel, [shape_of((MB, 2, 96, LANES), F32)] * 6,...]
    convert_element_type x3 -> x0, other arithmetic: 2.89 us -> none  [adam_step(): weight_new.astype(jnp.bfloat16)]
    ppermute x43 -> x44, starting transfers between devices: 47.5 us -> 50.1 us  [swap(): return lax.ppermute(value, axis, [(i, i ^ step) for i in range(size)])]
    all_to_all x1, starting transfers between devices: 3.63 us -> 5.26 us  [fast_body(): told = lax.all_to_all(told, AXES, 0, 0, tiled=True)]
    unnamed x43 -> x29, local copies, waits for them, and re-layouts: 2.98 us -> 3.68 us
  transfers between devices with their start and end apart: 45 -> 46, of which waited for: 23 -> 21; matrix products, arithmetic and copies ran while one was open for 2% -> 1% of each run, Pallas kernels for 13% -> 19%
where the time goes in v4:
time: 143 us
  starting transfers between devices  58.8 us (41%)
  waiting for transfers between devices  41.7 us (29%)
  Pallas kernels  37.1 us (26%)
  local copies, waits for them, and re-layouts  3.72 us (3%)
    ppermute x44, starting transfers between devices, swap(): return lax.ppermute(value, axis, [(i, i ^ step) for i in range(size)])  50.1 us
    ppermute x44, waiting for transfers between devices, swap(): return lax.ppermute(value, axis, [(i, i ^ step) for i in range(size)])  41.7 us
    all_to_all x1, starting transfers between devices, fast_body(): told = lax.all_to_all(told, AXES, 0, 0, tiled=True)  5.26 us
    pallas_call x1, Pallas kernels, fast_body(): call(second_weight_grad_kernel, [shape_of((MB, 2, 96, LANES), F32)] * 6,...  5.14 us
    pallas_call x1, Pallas kernels, fast_body(): call(both_grad_kernel, [shape_of((PIXELS, TAPS * LANES))] + [shape_of((HA...  4.04 us
    pallas_call x1, Pallas kernels, fast_body(): call(first_conv_kernel, [shape_of((PIXELS, LANES), F32), shape_of((PIXELS...  3.84 us
    unnamed x29, local copies, waits for them, and re-layouts  3.68 us
    pallas_call x1, Pallas kernels, fast_body(): call(adam_kernel, [shape_of((1, 1), F32)] + one_shapes + two_shapes + nor...  3.53 us
  transfers between devices with their start and end apart: 46, of which 21 were waited for; matrix products, arithmetic and copies ran while one was open for 1% of the time, Pallas kernels for 19%

profile of v4, /device:TPU:0, one launch (start us, length us, event | category | flops | bytes accessed | tf_op | source)
XLA Modules:
  0.0 142.6 jit_solution(8832990471190024099)
XLA Ops:
  2.5 3.0 %collective-permute-start.7 = (bf16[2,64,256]{2,1,0:T(8,128)(2,1)}, bf16[2,64,256]{2,1,0:T(8,128)(2,1)S(1)}, u32[]{:S(2)}, u32[]{:S(2)}) collective-permute-start(bf16[2,64,256]{2,1,0:T(8,128)(2,1)} %get-tuple-element.115), channel_id=1, source_target_pairs={{0,8},{8,0},{16,24},{24,16},{1,9},{9,1},{17,25},{25,17},{2,10},{10... | collective-permute-start | bytes 196616 | tf_op jit(solution)/shard_map/ppermute | solution.py:300
  5.5 2.6 %collective-permute-start.8 = (bf16[2,64,256]{2,1,0:T(8,128)(2,1)}, bf16[2,64,256]{2,1,0:T(8,128)(2,1)S(1)}, u32[]{:S(2)}, u32[]{:S(2)}) collective-permute-start(bf16[2,64,256]{2,1,0:T(8,128)(2,1)} %get-tuple-element.116), channel_id=1, source_target_pairs={{0,16},{8,24},{16,0},{24,8},{1,17},{9,25},{17,1},{25,9},{2,18},{10... | collective-permute-start | bytes 196616 | tf_op jit(solution)/shard_map/ppermute | solution.py:300
  8.1 2.8 %shard_map.269 = (bf16[144,128]{1,0:T(8,128)(2,1)}, bf16[288,128]{1,0:T(8,128)(2,1)}, bf16[448,128]{1,0:T(8,128)(2,1)}, bf16[16,128]{1,0:T(8,128)(2,1)}, f32[8,128]{1,0:T(8,128)}, /*index=5*/s32[16,128]{1,0:T(8,128)}) custom-call(s32[4,8]{1,0:T(4,128)} %order_ref.2, s32[1,32]{1,0:T(1,128)} %bitcast.20, f32[9,64,64]{2,1,0:T(8,128)} %refs_0_.1, ...), custom_call_target="tpu_custom_call" | custom-call | tf_op jit(solution)/shard_map/pallas_call | solution.py:1153
  10.9 1.8 %collective-permute-start = (bf16[448,128]{1,0:T(8,128)(2,1)}, bf16[448,128]{1,0:T(8,128)(2,1)S(1)}, u32[]{:S(2)}, u32[]{:S(2)}) collective-permute-start(bf16[448,128]{1,0:T(8,128)(2,1)} %get-tuple-element.110), channel_id=1, source_target_pairs={{0,2},{2,0},{1,3},{3,1},{4,6},{6,4},{5,7},{7,5},{8,10},{10,8},{9,1... | collective-permute-start | bytes 344072 | tf_op jit(solution)/shard_map/ppermute | solution.py:300
  17.6 2.6 %collective-permute-start.3 = (bf16[304,128]{1,0:T(8,128)(2,1)S(1)}, bf16[304,128]{1,0:T(8,128)(2,1)S(1)}, u32[]{:S(2)}, u32[]{:S(2)}) collective-permute-start(bf16[304,128]{1,0:T(8,128)(2,1)S(1)} %pad_maximum_fusion.5.o0), channel_id=1, source_target_pairs={{0,24},{8,16},{16,8},{24,0},{1,25},{9,17},{17,9},{25,1},{2,26},{10... | collective-permute-start | bytes 233480 | tf_op jit(solution)/shard_map/ppermute | solution.py:300
  20.2 1.8 %collective-permute-start.1 = (bf16[304,128]{1,0:T(8,128)(2,1)S(1)}, bf16[304,128]{1,0:T(8,128)(2,1)S(1)}, u32[]{:S(2)}, u32[]{:S(2)}) collective-permute-start(bf16[304,128]{1,0:T(8,128)(2,1)S(1)} %pad_maximum_fusion.5.o0), channel_id=1, source_target_pairs={{0,8},{8,0},{16,24},{24,16},{1,9},{9,1},{17,25},{25,17},{2,10},{10... | collective-permute-start | bytes 233480 | tf_op jit(solution)/shard_map/ppermute | solution.py:300
  22.1 3.0 %collective-permute-done.1.o1 = bf16[304,128]{1,0:T(8,128)(2,1)S(1)} collective-permute-done((bf16[304,128]{1,0:T(8,128)(2,1)S(1)}, bf16[304,128]{1,0:T(8,128)(2,1)S(1)}, u32[]{:S(2)}, u32[]{:S(2)}) %collective-permute-start.1) | collective-permute-done | bytes 77856 | tf_op jit(solution)/shard_map/ppermute | solution.py:300
  27.2 2.4 %collective-permute-start.11 = (bf16[8,64,256]{2,1,0:T(8,128)(2,1)S(1)}, bf16[8,64,256]{2,1,0:T(8,128)(2,1)S(1)}, u32[]{:S(2)}, u32[]{:S(2)}) collective-permute-start(bf16[8,64,256]{2,1,0:T(8,128)(2,1)S(1)} %constant_dynamic-update-slice_fusion), channel_id=1, source_target_pairs={{0,2},{2,0},{1,3},{3,1},{4,6},{6,4},{5,7},{7,5},{8,10},{10,8},{9,1... | collective-permute-start | bytes 786440 | tf_op jit(solution)/shard_map/ppermute | solution.py:300
  29.6 1.8 %collective-permute-start.6 = (bf16[576,128]{1,0:T(8,128)(2,1)S(1)}, bf16[576,128]{1,0:T(8,128)(2,1)S(1)}, u32[]{:S(2)}, u32[]{:S(2)}) collective-permute-start(bf16[576,128]{1,0:T(8,128)(2,1)S(1)} %pad_maximum_fusion.2), channel_id=1, source_target_pairs={{0,24},{8,16},{16,8},{24,0},{1,25},{9,17},{17,9},{25,1},{2,26},{10... | collective-permute-start | bytes 442376 | tf_op jit(solution)/shard_map/ppermute | solution.py:300
  31.9 2.1 %collective-permute-start.4 = (bf16[576,128]{1,0:T(8,128)(2,1)S(1)}, bf16[576,128]{1,0:T(8,128)(2,1)S(1)}, u32[]{:S(2)}, u32[]{:S(2)}) collective-permute-start(bf16[576,128]{1,0:T(8,128)(2,1)S(1)} %pad_maximum_fusion.2), channel_id=1, source_target_pairs={{0,8},{8,0},{16,24},{24,16},{1,9},{9,1},{17,25},{25,17},{2,10},{10... | collective-permute-start | bytes 442376 | tf_op jit(solution)/shard_map/ppermute | solution.py:300
  36.2 3.8 %shard_map.271 = (f32[2048,128]{1,0:T(8,128)S(1)}, bf16[2048,256]{1,0:T(8,128)(2,1)S(1)}, f32[8,128]{1,0:T(8,128)S(1)}) custom-call(s32[16,128]{1,0:T(8,128)S(1)} %copy-done, bf16[4,64,256]{2,1,0:T(8,128)(2,1)S(1)} %pad_maximum_fusion.3.a0, bf16[4,64,256]{2,1,0:T(8,128)(2,1)S(1)} %collective-permute-done.10.a1, ...), custom_call_target="tpu_custom_call" | custom-call | tf_op jit(solution)/shard_map/pallas_call | solution.py:1222
  40.2 4.9 %collective-permute-done.5 = bf16[576,128]{1,0:T(8,128)(2,1)S(1)} collective-permute-done((bf16[576,128]{1,0:T(8,128)(2,1)S(1)}, bf16[576,128]{1,0:T(8,128)(2,1)S(1)}, u32[]{:S(2)}, u32[]{:S(2)}) %collective-permute-start.5) | collective-permute-done | bytes 147488 | tf_op jit(solution)/shard_map/ppermute | solution.py:300
  49.8 5.1 %collective-permute-done.19.b1.rest_5_ = bf16[1024,128]{1,0:T(8,128)(2,1)S(1)} collective-permute-done((bf16[1024,128]{1,0:T(8,128)(2,1)S(1)}, bf16[1024,128]{1,0:T(8,128)(2,1)S(1)}, u32[]{:S(2)}, u32[]{:S(2)}) %collective-permute-start.19) | collective-permute-done | bytes 262176 | tf_op jit(solution)/shard_map/ppermute | solution.py:300
  57.7 3.1 %collective-permute-done.20.b2.rest_6_ = bf16[1024,128]{1,0:T(8,128)(2,1)S(1)} collective-permute-done((bf16[1024,128]{1,0:T(8,128)(2,1)S(1)}, bf16[1024,128]{1,0:T(8,128)(2,1)S(1)}, u32[]{:S(2)}, u32[]{:S(2)}) %collective-permute-start.20) | collective-permute-done | bytes 262176 | tf_op jit(solution)/shard_map/ppermute | solution.py:300
  60.8 2.9 %shard_map.274.near_ref = f32[2048,128]{1,0:T(8,128)S(1)} custom-call(bf16[1024,128]{1,0:T(8,128)(2,1)S(1)} %get-tuple-element.122.a0.rest_0_, bf16[1024,128]{1,0:T(8,128)(2,1)S(1)} %collective-permute-done.16.a1.rest_1_, bf16[1024,128]{1,0:T(8,128)(2,1)S(1)} %collective-permute-done.17.a2.rest_2_, bf16[1024,128]{1,0:T(8,128)(2,1)S(1)} %get-tuple-element.123.b0.rest_4_, ...), custom_call_target="tpu_custom_call" | custom-call | tf_op jit(solution)/shard_map/pallas_call | solution.py:1253
  63.7 1.9 %collective-permute-done.21.b3.rest_7_ = bf16[1024,128]{1,0:T(8,128)(2,1)S(1)} collective-permute-done((bf16[1024,128]{1,0:T(8,128)(2,1)S(1)}, bf16[1024,128]{1,0:T(8,128)(2,1)S(1)}, u32[]{:S(2)}, u32[]{:S(2)}) %collective-permute-start.21) | collective-permute-done | bytes 262176 | tf_op jit(solution)/shard_map/ppermute | solution.py:300
  70.7 4.0 %shard_map.277 = (bf16[2048,1152]{1,0:T(8,128)(2,1)S(1)}, f32[1024,128]{1,0:T(8,128)S(1)}, f32[1024,128]{1,0:T(8,128)S(1)}, bf16[2064,128]{1,0:T(8,128)(2,1)S(1)...) custom-call(s32[16,128]{1,0:T(8,128)S(1)} %copy-done, ...), custom_call_target="tpu_custom_call" | custom-call | tf_op jit(solution)/shard_map/pallas_call | solution.py:1299
  76.9 5.1 %shard_map.278 = (f32[4,2,96,128]{3,2,1,0:T(8,128)S(1)}, f32[4,2,96,128]{3,2,1,0:T(8,128)S(1)}, f32[4,2,96,128]{3,2,1,0:T(8,128)S(1)}, f32[4,2,96,128]{3,2,1,0:T...) custom-call(bf16[1024,128]{1,0:T(8,128)(2,1)S(1)} %get-tuple-element.122.a0.rest_0_, ...), custom_call_target="tpu_custom_call" | custom-call | tf_op jit(solution)/shard_map/pallas_call | solution.py:1316
  85.8 3.1 %collective-permute-done.28.a_got.a_near = bf16[2064,128]{1,0:T(8,128)(2,1)S(1)} collective-permute-done((bf16[2064,128]{1,0:T(8,128)(2,1)S(1)}, bf16[2064,128]{1,0:T(8,128)(2,1)S(1)}, u32[]{:S(2)}, u32[]{:S(2)}) %collective-permute-start.28) | collective-permute-done | bytes 528416 | tf_op jit(solution)/shard_map/ppermute | solution.py:300
  92.6 2.6 %collective-permute-start.35 = (bf16[2,288,128]{2,1,0:T(8,128)(2,1)}, bf16[2,288,128]{2,1,0:T(8,128)(2,1)S(1)}, u32[]{:S(2)}, u32[]{:S(2)}) collective-permute-start(bf16[2,288,128]{2,1,0:T(8,128)(2,1)} %get-tuple-element.158), channel_id=1, source_target_pairs={{0,24},{8,16},{16,8},{24,0},{1,25},{9,17},{17,9},{25,1},{2,26},{10... | collective-permute-start | bytes 442376 | tf_op jit(solution)/shard_map/ppermute | solution.py:300
  96.0 2.1 %collective-permute-done.31.b_last = bf16[1024,128]{1,0:T(8,128)(2,1)S(1)} collective-permute-done((bf16[1024,128]{1,0:T(8,128)(2,1)S(1)}, bf16[1024,128]{1,0:T(8,128)(2,1)S(1)}, u32[]{:S(2)}, u32[]{:S(2)}) %collective-permute-start.31) | collective-permute-done | bytes 262176 | tf_op jit(solution)/shard_map/ppermute | solution.py:300
  100.2 2.4 %shard_map.282 = (bf16[2048,1152]{1,0:T(8,128)(2,1)S(1)}, f32[4,288,128]{2,1,0:T(8,128)S(1)}, f32[4,288,128]{2,1,0:T(8,128)S(1)}) custom-call(s32[16,128]{1,0:T(8,128)S(1)} %copy-done, f32[2048,128]{1,0:T(8,128)S(1)} %get-tuple-element.149.slope_ref, f32[2048,128]{1,0:T(8,128)S(1)} %get-tuple-element.119.pre_ref, f32[8,128]{1,0:T(8,128)S(1)} %get-tuple-element.120.own_ref, ...), custom_call_target="tpu_custom_call" | custom-call | tf_op jit(solution)/shard_map/pallas_call | solution.py:1361
  102.6 2.5 %shard_map.283 = bf16[4,512,256]{2,1,0:T(8,128)(2,1)} custom-call(bf16[2048,1152]{1,0:T(8,128)(2,1)S(1)} %get-tuple-element.152.columns, bf16[9,4,32,256]{3,2,1,0:T(8,128)(2,1)S(1)} %get-tuple-element.118.weight_ref), custom_call_target="tpu_custom_call" | custom-call | tf_op jit(solution)/shard_map/pallas_call | solution.py:1368
  105.1 3.5 %all-to-all-start = ((bf16[4,512,256]{2,1,0:T(8,128)(2,1)}), bf16[4,512,256]{2,1,0:T(8,128)(2,1)S(1)}, u32[]{:S(2)}, u32[]{:S(2)}) async-start(bf16[4,512,256]{2,1,0:T(8,128)(2,1)} %shard_map.283), calls=%async_computation | async-start | bytes 2097152 | tf_op jit(solution)/shard_map/all_to_all | solution.py:1404
  109.6 1.8 %collective-permute-done.36.got_ref = f32[4,288,128]{2,1,0:T(8,128)S(1)} collective-permute-done((f32[4,288,128]{2,1,0:T(8,128)S(1)}, f32[4,288,128]{2,1,0:T(8,128)S(1)}, u32[]{:S(2)}, u32[]{:S(2)}) %collective-permute-start.36) | collective-permute-done | bytes 589856 | tf_op jit(solution)/shard_map/ppermute | solution.py:300
  111.6 3.2 %collective-permute-start.38 = (bf16[320,128]{1,0:T(8,128)(2,1)S(1)}, bf16[320,128]{1,0:T(8,128)(2,1)S(1)}, u32[]{:S(2)}, u32[]{:S(2)}) collective-permute-start(bf16[320,128]{1,0:T(8,128)(2,1)S(1)} %get-tuple-element.164), channel_id=1, source_target_pairs={{0,16},{8,24},{16,0},{24,8},{1,17},{9,25},{17,1},{25,9},{2,18},{10... | collective-permute-start | bytes 245768 | tf_op jit(solution)/shard_map/ppermute | solution.py:300
  117.4 4.2 %collective-permute-done.38.g2.n2 = bf16[320,128]{1,0:T(8,128)(2,1)S(1)} collective-permute-done((bf16[320,128]{1,0:T(8,128)(2,1)S(1)}, bf16[320,128]{1,0:T(8,128)(2,1)S(1)}, u32[]{:S(2)}, u32[]{:S(2)}) %collective-permute-start.38) | collective-permute-done | bytes 81952 | tf_op jit(solution)/shard_map/ppermute | solution.py:300
  123.0 5.3 %all-to-all-start.1 = ((f32[32,8,128]{2,1,0:T(8,128)}), f32[32,8,128]{2,1,0:T(8,128)S(1)}, u32[]{:S(2)}, u32[]{:S(2)}) async-start(f32[32,8,128]{2,1,0:T(8,128)} %bitcast.3), calls=%async_computation.1 | async-start | bytes 262144 | tf_op jit(solution)/shard_map/all_to_all | solution.py:1425
  128.2 1.8 %collective-permute-start.40 = (f32[440,128]{1,0:T(8,128)S(1)}, f32[440,128]{1,0:T(8,128)S(1)}, u32[]{:S(2)}, u32[]{:S(2)}) collective-permute-start(f32[440,128]{1,0:T(8,128)S(1)} %get-tuple-element.169), channel_id=1, source_target_pairs={{0,2},{2,0},{1,3},{3,1},{4,6},{6,4},{5,7},{7,5},{8,10},{10,8},{9,1... | collective-permute-start | bytes 675848 | tf_op jit(solution)/shard_map/ppermute | solution.py:300
  131.8 2.4 %collective-permute-start.42 = (bf16[2,64,256]{2,1,0:T(8,128)(2,1)S(1)}, bf16[2,64,256]{2,1,0:T(8,128)(2,1)S(1)}, u32[]{:S(2)}, u32[]{:S(2)}) collective-permute-start(bf16[2,64,256]{2,1,0:T(8,128)(2,1)S(1)} %get-tuple-element.175), channel_id=1, source_target_pairs={{0,16},{8,24},{16,0},{24,8},{1,17},{9,25},{17,1},{25,9},{2,18},{10... | collective-permute-start | bytes 196616 | tf_op jit(solution)/shard_map/ppermute | solution.py:300
  134.7 2.6 %collective-permute-done.40.got_ref = f32[440,128]{1,0:T(8,128)S(1)} collective-permute-done((f32[440,128]{1,0:T(8,128)S(1)}, f32[440,128]{1,0:T(8,128)S(1)}, u32[]{:S(2)}, u32[]{:S(2)}) %collective-permute-start.40) | collective-permute-done | bytes 225312 | tf_op jit(solution)/shard_map/ppermute | solution.py:300
  138.0 3.5 %shard_map.288 = (f32[1,1]{1,0:T(1,128)}, f32[9,64,64]{2,1,0:T(8,128)}, f32[9,64,64]{2,1,0:T(8,128)}, f32[9,64,64]{2,1,0:T(8,128)}, f32[9,64,64]{2,1,0:T(8,128)}...) custom-call(f32[256,128]{1,0:T(8,128)} %bitcast.16, ...), custom_call_target="tpu_custom_call" | custom-call | tf_op jit(solution)/shard_map/pallas_call | solution.py:1450
  (122 shorter events, 45.3 us)
Async XLA Ops:
  2.5 11.8 %collective-permute-start.7 = (bf16[2,64,256]{2,1,0:T(8,128)(2,1)}, bf16[2,64,256]{2,1,0:T(8,128)(2,1)S(1)}, u32[]{:S(2)}, u32[]{:S(2)}) collective-permute-start(bf16[2,64,256]{2,1,0:T(8,128)(2,1)} %get-tuple-element.115), channel_id=1, source_target_pairs={{0,8},{8,0},{16,24},{24,16},{1,9},{9,1},{17,25},{25,17},{2,10},{10... | collective-permute-start | bytes 196616 | tf_op jit(solution)/shard_map/ppermute | solution.py:300
  5.5 8.8 %collective-permute-start.8 = (bf16[2,64,256]{2,1,0:T(8,128)(2,1)}, bf16[2,64,256]{2,1,0:T(8,128)(2,1)S(1)}, u32[]{:S(2)}, u32[]{:S(2)}) collective-permute-start(bf16[2,64,256]{2,1,0:T(8,128)(2,1)} %get-tuple-element.116), channel_id=1, source_target_pairs={{0,16},{8,24},{16,0},{24,8},{1,17},{9,25},{17,1},{25,9},{2,18},{10... | collective-permute-start | bytes 196616 | tf_op jit(solution)/shard_map/ppermute | solution.py:300
  14.4 12.8 %collective-permute-start.10 = (bf16[4,64,256]{2,1,0:T(8,128)(2,1)S(1)}, bf16[4,64,256]{2,1,0:T(8,128)(2,1)S(1)}, u32[]{:S(2)}, u32[]{:S(2)}) collective-permute-start(bf16[4,64,256]{2,1,0:T(8,128)(2,1)S(1)} %pad_maximum_fusion.3.a0), channel_id=1, source_target_pairs={{0,4},{4,0},{1,5},{5,1},{2,6},{6,2},{3,7},{7,3},{8,12},{12,8},{9,1... | collective-permute-start | bytes 393224 | tf_op jit(solution)/shard_map/ppermute | solution.py:300
  16.0 10.3 %collective-permute-start.12 = (bf16[4,64,256]{2,1,0:T(8,128)(2,1)S(1)}, bf16[4,64,256]{2,1,0:T(8,128)(2,1)S(1)}, u32[]{:S(2)}, u32[]{:S(2)}) collective-permute-start(bf16[4,64,256]{2,1,0:T(8,128)(2,1)S(1)} %pad_maximum_fusion.4.b0), channel_id=1, source_target_pairs={{0,2},{2,0},{1,3},{3,1},{4,6},{6,4},{5,7},{7,5},{8,10},{10,8},{9,1... | collective-permute-start | bytes 393224 | tf_op jit(solution)/shard_map/ppermute | solution.py:300
  17.6 8.5 %collective-permute-start.3 = (bf16[304,128]{1,0:T(8,128)(2,1)S(1)}, bf16[304,128]{1,0:T(8,128)(2,1)S(1)}, u32[]{:S(2)}, u32[]{:S(2)}) collective-permute-start(bf16[304,128]{1,0:T(8,128)(2,1)S(1)} %pad_maximum_fusion.5.o0), channel_id=1, source_target_pairs={{0,24},{8,16},{16,8},{24,0},{1,25},{9,17},{17,9},{25,1},{2,26},{10... | collective-permute-start | bytes 233480 | tf_op jit(solution)/shard_map/ppermute | solution.py:300
  26.3 8.8 %collective-permute-start.13 = (bf16[8,64,256]{2,1,0:T(8,128)(2,1)S(1)}, bf16[8,64,256]{2,1,0:T(8,128)(2,1)S(1)}, u32[]{:S(2)}, u32[]{:S(2)}) collective-permute-start(bf16[8,64,256]{2,1,0:T(8,128)(2,1)S(1)} %constant_dynamic-update-slice_fusion.5), channel_id=1, source_target_pairs={{0,4},{4,0},{1,5},{5,1},{2,6},{6,2},{3,7},{7,3},{8,12},{12,8},{9,1... | collective-permute-start | bytes 786440 | tf_op jit(solution)/shard_map/ppermute | solution.py:300
  27.2 9.1 %collective-permute-start.11 = (bf16[8,64,256]{2,1,0:T(8,128)(2,1)S(1)}, bf16[8,64,256]{2,1,0:T(8,128)(2,1)S(1)}, u32[]{:S(2)}, u32[]{:S(2)}) collective-permute-start(bf16[8,64,256]{2,1,0:T(8,128)(2,1)S(1)} %constant_dynamic-update-slice_fusion), channel_id=1, source_target_pairs={{0,2},{2,0},{1,3},{3,1},{4,6},{6,4},{5,7},{7,5},{8,10},{10,8},{9,1... | collective-permute-start | bytes 786440 | tf_op jit(solution)/shard_map/ppermute | solution.py:300
  29.6 10.6 %collective-permute-start.6 = (bf16[576,128]{1,0:T(8,128)(2,1)S(1)}, bf16[576,128]{1,0:T(8,128)(2,1)S(1)}, u32[]{:S(2)}, u32[]{:S(2)}) collective-permute-start(bf16[576,128]{1,0:T(8,128)(2,1)S(1)} %pad_maximum_fusion.2), channel_id=1, source_target_pairs={{0,24},{8,16},{16,8},{24,0},{1,25},{9,17},{17,9},{25,1},{2,26},{10... | collective-permute-start | bytes 442376 | tf_op jit(solution)/shard_map/ppermute | solution.py:300
  31.4 13.7 %collective-permute-start.5 = (bf16[576,128]{1,0:T(8,128)(2,1)S(1)}, bf16[576,128]{1,0:T(8,128)(2,1)S(1)}, u32[]{:S(2)}, u32[]{:S(2)}) collective-permute-start(bf16[576,128]{1,0:T(8,128)(2,1)S(1)} %pad_maximum_fusion.2), channel_id=1, source_target_pairs={{0,16},{8,24},{16,0},{24,8},{1,17},{9,25},{17,1},{25,9},{2,18},{10... | collective-permute-start | bytes 442376 | tf_op jit(solution)/shard_map/ppermute | solution.py:300
  31.9 13.2 %collective-permute-start.4 = (bf16[576,128]{1,0:T(8,128)(2,1)S(1)}, bf16[576,128]{1,0:T(8,128)(2,1)S(1)}, u32[]{:S(2)}, u32[]{:S(2)}) collective-permute-start(bf16[576,128]{1,0:T(8,128)(2,1)S(1)} %pad_maximum_fusion.2), channel_id=1, source_target_pairs={{0,8},{8,0},{16,24},{24,16},{1,9},{9,1},{17,25},{25,17},{2,10},{10... | collective-permute-start | bytes 442376 | tf_op jit(solution)/shard_map/ppermute | solution.py:300
  45.6 11.3 %collective-permute-start.22 = (bf16[2304,128]{1,0:T(8,128)(2,1)S(1)}, bf16[2304,128]{1,0:T(8,128)(2,1)S(1)}, u32[]{:S(2)}, u32[]{:S(2)}) collective-permute-start(bf16[2304,128]{1,0:T(8,128)(2,1)S(1)} %pad_maximum_fusion.own_ref), channel_id=1, source_target_pairs={{0,1},{1,0},{2,3},{3,2},{4,5},{5,4},{6,7},{7,6},{8,9},{9,8},{10,11... | collective-permute-start | bytes 1769480 | tf_op jit(solution)/shard_map/ppermute | solution.py:300
  45.7 9.2 %collective-permute-start.19 = (bf16[1024,128]{1,0:T(8,128)(2,1)S(1)}, bf16[1024,128]{1,0:T(8,128)(2,1)S(1)}, u32[]{:S(2)}, u32[]{:S(2)}) collective-permute-start(bf16[1024,128]{1,0:T(8,128)(2,1)S(1)} %get-tuple-element.123.b0.rest_4_), channel_id=1, source_target_pairs={{0,2},{2,0},{1,3},{3,1},{4,6},{6,4},{5,7},{7,5},{8,10},{10,8},{9,1... | collective-permute-start | bytes 786440 | tf_op jit(solution)/shard_map/ppermute | solution.py:300
  46.0 9.2 %collective-permute-start.16 = (bf16[1024,128]{1,0:T(8,128)(2,1)S(1)}, bf16[1024,128]{1,0:T(8,128)(2,1)S(1)}, u32[]{:S(2)}, u32[]{:S(2)}) collective-permute-start(bf16[1024,128]{1,0:T(8,128)(2,1)S(1)} %get-tuple-element.122.a0.rest_0_), channel_id=1, source_target_pairs={{0,4},{4,0},{1,5},{5,1},{2,6},{6,2},{3,7},{7,3},{8,12},{12,8},{9,1... | collective-permute-start | bytes 786440 | tf_op jit(solution)/shard_map/ppermute | solution.py:300
  46.3 14.5 %collective-permute-start.20 = (bf16[1024,128]{1,0:T(8,128)(2,1)S(1)}, bf16[1024,128]{1,0:T(8,128)(2,1)S(1)}, u32[]{:S(2)}, u32[]{:S(2)}) collective-permute-start(bf16[1024,128]{1,0:T(8,128)(2,1)S(1)} %get-tuple-element.123.b0.rest_4_), channel_id=1, source_target_pairs={{0,4},{4,0},{1,5},{5,1},{2,6},{6,2},{3,7},{7,3},{8,12},{12,8},{9,1... | collective-permute-start | bytes 786440 | tf_op jit(solution)/shard_map/ppermute | solution.py:300
  48.1 12.7 %collective-permute-start.17 = (bf16[1024,128]{1,0:T(8,128)(2,1)S(1)}, bf16[1024,128]{1,0:T(8,128)(2,1)S(1)}, u32[]{:S(2)}, u32[]{:S(2)}) collective-permute-start(bf16[1024,128]{1,0:T(8,128)(2,1)S(1)} %get-tuple-element.122.a0.rest_0_), channel_id=1, source_target_pairs={{0,2},{2,0},{1,3},{3,1},{4,6},{6,4},{5,7},{7,5},{8,10},{10,8},{9,1... | collective-permute-start | bytes 786440 | tf_op jit(solution)/shard_map/ppermute | solution.py:300
  54.8 10.8 %collective-permute-start.21 = (bf16[1024,128]{1,0:T(8,128)(2,1)S(1)}, bf16[1024,128]{1,0:T(8,128)(2,1)S(1)}, u32[]{:S(2)}, u32[]{:S(2)}) collective-permute-start(bf16[1024,128]{1,0:T(8,128)(2,1)S(1)} %collective-permute-done.19.b1.rest_5_), channel_id=1, source_target_pairs={{0,4},{4,0},{1,5},{5,1},{2,6},{6,2},{3,7},{7,3},{8,12},{12,8},{9,1... | collective-permute-start | bytes 786440 | tf_op jit(solution)/shard_map/ppermute | solution.py:300
  55.2 10.5 %collective-permute-start.18 = (bf16[1024,128]{1,0:T(8,128)(2,1)S(1)}, bf16[1024,128]{1,0:T(8,128)(2,1)S(1)}, u32[]{:S(2)}, u32[]{:S(2)}) collective-permute-start(bf16[1024,128]{1,0:T(8,128)(2,1)S(1)} %collective-permute-done.16.a1.rest_1_), channel_id=1, source_target_pairs={{0,2},{2,0},{1,3},{3,1},{4,6},{6,4},{5,7},{7,5},{8,10},{10,8},{9,1... | collective-permute-start | bytes 786440 | tf_op jit(solution)/shard_map/ppermute | solution.py:300
  74.8 14.2 %collective-permute-start.28 = (bf16[2064,128]{1,0:T(8,128)(2,1)S(1)}, bf16[2064,128]{1,0:T(8,128)(2,1)S(1)}, u32[]{:S(2)}, u32[]{:S(2)}) collective-permute-start(bf16[2064,128]{1,0:T(8,128)(2,1)S(1)} %get-tuple-element.141), channel_id=1, source_target_pairs={{0,4},{4,0},{1,5},{5,1},{2,6},{6,2},{3,7},{7,3},{8,12},{12,8},{9,1... | collective-permute-start | bytes 1585160 | tf_op jit(solution)/shard_map/ppermute | solution.py:300
  75.2 13.8 %collective-permute-start.29 = (bf16[2048,128]{1,0:T(8,128)(2,1)S(1)}, bf16[2048,128]{1,0:T(8,128)(2,1)S(1)}, u32[]{:S(2)}, u32[]{:S(2)}) collective-permute-start(bf16[2048,128]{1,0:T(8,128)(2,1)S(1)} %get-tuple-element.145), channel_id=1, source_target_pairs={{0,2},{2,0},{1,3},{3,1},{4,6},{6,4},{5,7},{7,5},{8,10},{10,8},{9,1... | collective-permute-start | bytes 1572872 | tf_op jit(solution)/shard_map/ppermute | solution.py:300
  89.1 9.1 %collective-permute-start.30 = (bf16[1056,128]{1,0:T(8,128)(2,1)S(1)}, bf16[1056,128]{1,0:T(8,128)(2,1)S(1)}, u32[]{:S(2)}, u32[]{:S(2)}) collective-permute-start(bf16[1056,128]{1,0:T(8,128)(2,1)S(1)} %pad_maximum_fusion.1), channel_id=1, source_target_pairs={{0,2},{2,0},{1,3},{3,1},{4,6},{6,4},{5,7},{7,5},{8,10},{10,8},{9,1... | collective-permute-start | bytes 811016 | tf_op jit(solution)/shard_map/ppermute | solution.py:300
  90.9 7.3 %collective-permute-start.31 = (bf16[1024,128]{1,0:T(8,128)(2,1)S(1)}, bf16[1024,128]{1,0:T(8,128)(2,1)S(1)}, u32[]{:S(2)}, u32[]{:S(2)}) collective-permute-start(bf16[1024,128]{1,0:T(8,128)(2,1)S(1)} %get-tuple-element.148), channel_id=1, source_target_pairs={{0,4},{4,0},{1,5},{5,1},{2,6},{6,2},{3,7},{7,3},{8,12},{12,8},{9,1... | collective-permute-start | bytes 786440 | tf_op jit(solution)/shard_map/ppermute | solution.py:300
  92.6 16.1 %collective-permute-start.34 = (bf16[2,288,128]{2,1,0:T(8,128)(2,1)}, bf16[2,288,128]{2,1,0:T(8,128)(2,1)S(1)}, u32[]{:S(2)}, u32[]{:S(2)}) collective-permute-start(bf16[2,288,128]{2,1,0:T(8,128)(2,1)} %get-tuple-element.157), channel_id=1, source_target_pairs={{0,16},{8,24},{16,0},{24,8},{1,17},{9,25},{17,1},{25,9},{2,18},{10... | collective-permute-start | bytes 442376 | tf_op jit(solution)/shard_map/ppermute | solution.py:300
  92.6 16.1 %collective-permute-start.35 = (bf16[2,288,128]{2,1,0:T(8,128)(2,1)}, bf16[2,288,128]{2,1,0:T(8,128)(2,1)S(1)}, u32[]{:S(2)}, u32[]{:S(2)}) collective-permute-start(bf16[2,288,128]{2,1,0:T(8,128)(2,1)} %get-tuple-element.158), channel_id=1, source_target_pairs={{0,24},{8,16},{16,8},{24,0},{1,25},{9,17},{17,9},{25,1},{2,26},{10... | collective-permute-start | bytes 442376 | tf_op jit(solution)/shard_map/ppermute | solution.py:300
  95.2 13.5 %collective-permute-start.33 = (bf16[2,288,128]{2,1,0:T(8,128)(2,1)S(1)}, bf16[2,288,128]{2,1,0:T(8,128)(2,1)S(1)}, u32[]{:S(2)}, u32[]{:S(2)}) collective-permute-start(bf16[2,288,128]{2,1,0:T(8,128)(2,1)S(1)} %get-tuple-element.138), channel_id=1, source_target_pairs={{0,8},{8,0},{16,24},{24,16},{1,9},{9,1},{17,25},{25,17},{2,10},{10... | collective-permute-start | bytes 442376 | tf_op jit(solution)/shard_map/ppermute | solution.py:300
  105.1 17.8 %all-to-all-start = ((bf16[4,512,256]{2,1,0:T(8,128)(2,1)}), bf16[4,512,256]{2,1,0:T(8,128)(2,1)S(1)}, u32[]{:S(2)}, u32[]{:S(2)}) async-start(bf16[4,512,256]{2,1,0:T(8,128)(2,1)} %shard_map.283), calls=%async_computation | async-start | bytes 2097152 | tf_op jit(solution)/shard_map/all_to_all | solution.py:1404
  111.6 9.9 %collective-permute-start.38 = (bf16[320,128]{1,0:T(8,128)(2,1)S(1)}, bf16[320,128]{1,0:T(8,128)(2,1)S(1)}, u32[]{:S(2)}, u32[]{:S(2)}) collective-permute-start(bf16[320,128]{1,0:T(8,128)(2,1)S(1)} %get-tuple-element.164), channel_id=1, source_target_pairs={{0,16},{8,24},{16,0},{24,8},{1,17},{9,25},{17,1},{25,9},{2,18},{10... | collective-permute-start | bytes 245768 | tf_op jit(solution)/shard_map/ppermute | solution.py:300
  114.8 6.7 %collective-permute-start.39 = (bf16[320,128]{1,0:T(8,128)(2,1)S(1)}, bf16[320,128]{1,0:T(8,128)(2,1)S(1)}, u32[]{:S(2)}, u32[]{:S(2)}) collective-permute-start(bf16[320,128]{1,0:T(8,128)(2,1)S(1)} %get-tuple-element.165), channel_id=1, source_target_pairs={{0,24},{8,16},{16,8},{24,0},{1,25},{9,17},{17,9},{25,1},{2,26},{10... | collective-permute-start | bytes 245768 | tf_op jit(solution)/shard_map/ppermute | solution.py:300
  123.0 14.4 %all-to-all-start.1 = ((f32[32,8,128]{2,1,0:T(8,128)}), f32[32,8,128]{2,1,0:T(8,128)S(1)}, u32[]{:S(2)}, u32[]{:S(2)}) async-start(f32[32,8,128]{2,1,0:T(8,128)} %bitcast.3), calls=%async_computation.1 | async-start | bytes 262144 | tf_op jit(solution)/shard_map/all_to_all | solution.py:1425
  128.2 9.1 %collective-permute-start.40 = (f32[440,128]{1,0:T(8,128)S(1)}, f32[440,128]{1,0:T(8,128)S(1)}, u32[]{:S(2)}, u32[]{:S(2)}) collective-permute-start(f32[440,128]{1,0:T(8,128)S(1)} %get-tuple-element.169), channel_id=1, source_target_pairs={{0,2},{2,0},{1,3},{3,1},{4,6},{6,4},{5,7},{7,5},{8,10},{10,8},{9,1... | collective-permute-start | bytes 675848 | tf_op jit(solution)/shard_map/ppermute | solution.py:300
  130.2 11.3 %collective-permute-start.41 = (bf16[2,64,256]{2,1,0:T(8,128)(2,1)S(1)}, bf16[2,64,256]{2,1,0:T(8,128)(2,1)S(1)}, u32[]{:S(2)}, u32[]{:S(2)}) collective-permute-start(bf16[2,64,256]{2,1,0:T(8,128)(2,1)S(1)} %get-tuple-element.174), channel_id=1, source_target_pairs={{0,8},{8,0},{16,24},{24,16},{1,9},{9,1},{17,25},{25,17},{2,10},{10... | collective-permute-start | bytes 196616 | tf_op jit(solution)/shard_map/ppermute | solution.py:300
  131.8 9.8 %collective-permute-start.42 = (bf16[2,64,256]{2,1,0:T(8,128)(2,1)S(1)}, bf16[2,64,256]{2,1,0:T(8,128)(2,1)S(1)}, u32[]{:S(2)}, u32[]{:S(2)}) collective-permute-start(bf16[2,64,256]{2,1,0:T(8,128)(2,1)S(1)} %get-tuple-element.175), channel_id=1, source_target_pairs={{0,16},{8,24},{16,0},{24,8},{1,17},{9,25},{17,1},{25,9},{2,18},{10... | collective-permute-start | bytes 196616 | tf_op jit(solution)/shard_map/ppermute | solution.py:300
  134.2 7.4 %collective-permute-start.43 = (bf16[2,64,256]{2,1,0:T(8,128)(2,1)S(1)}, bf16[2,64,256]{2,1,0:T(8,128)(2,1)S(1)}, u32[]{:S(2)}, u32[]{:S(2)}) collective-permute-start(bf16[2,64,256]{2,1,0:T(8,128)(2,1)S(1)} %get-tuple-element.176), channel_id=1, source_target_pairs={{0,24},{8,16},{16,8},{24,0},{1,25},{9,17},{17,9},{25,1},{2,26},{10... | collective-permute-start | bytes 196616 | tf_op jit(solution)/shard_map/ppermute | solution.py:300
  (24 other events, 120.2 us)

commit v5 on v4

--- a/solution.py
+++ b/solution.py
@@ -7,7 +7,7 @@
 from jax.experimental.pallas import tpu as pltpu
 from jax.sharding import Mesh, PartitionSpec as P
 
-OPT = {'flop': 0, 'zorder': [2, 3, 1], 'merge_w': False, 'w1_after_in': False, 'core_w1': 1, 'core_w1_after': 0, 'fwd_after_core_w1': False, 'w2_after': 1, 'w2_before': 1, 'core_w2_after': 1, 'kw2_after': False, 'rs': 'two', 'pass_after_g2': True, 'pass_after_near': False, 'k5_after': True, 'core1_after_g2': False, 'core_g1_after_g2': True, 'a2a_after_core1': False, 'sum_after_f': False, 'f_after_sum': False, 'told_after_f': False, 'prep_after_take': True, 'finish_last': True, 'split_first': True, 'split_conv': True, 'ki_after_kg': False, 'load': False, 'a2a_after_g2': False, 'core_g2': 0, 'adam_limit': 62}
+OPT = {'flop': 0, 'zorder': [2, 3, 1], 'merge_w': False, 'w1_after_in': False, 'core_w1': 4, 'core_w1_after': 0, 'fwd_after_core_w1': False, 'w2_after': 1, 'w2_before': 1, 'core_w2_after': 1, 'kw2_after': False, 'rs': 'two', 'pass_after_g2': True, 'pass_after_near': False, 'k5_after': True, 'core1_after_g2': False, 'core_g1_after_g2': True, 'a2a_after_core1': False, 'sum_after_f': False, 'f_after_sum': False, 'told_after_f': False, 'prep_after_take': True, 'finish_last': True, 'split_first': True, 'split_conv': True, 'ki_after_kg': False, 'load': False, 'a2a_after_g2': False, 'core_g2': 0, 'adam_limit': 62, 'pad_p': 32, 'pad_s': 48, 'y2_after': True, 'sum_after_y2': False, 'pooled_after': True, 'zin_after_prep': False, 'pad_in': 16, 'y2_after_y1': True, 'take_limit': 16, 'prep_limit': 62}
 C1 = 256
 C2 = 512
 MEL = 8
@@ -281,7 +281,6 @@
 
 
 def call(kernel, out, in_specs, out_specs, scratch=(), limit=VMEM_LIMIT):
-    cost = COSTS[kernel] * OPT.get(kernel.__name__, 1)
     return pl.pallas_call(
         kernel,
         out_shape=out,
@@ -289,10 +288,21 @@
         out_specs=out_specs,
         scratch_shapes=list(scratch),
         compiler_params=pltpu.CompilerParams(vmem_limit_bytes=limit),
-        cost_estimate=pl.CostEstimate(
-            flops=int(cost * FLOP_SCALE), bytes_accessed=int(cost * BYTE_SCALE), transcendentals=0
-        ),
-    )
+        cost_estimate=pl.CostEstimate(flops=0, bytes_accessed=0, transcendentals=0),
+    )
+
+
+def join_kernel(*refs):
+    base = 0
+    for ref in refs[:-1]:
+        refs[-1][base : base + ref.shape[0]] = ref[...]
+        base += ref.shape[0]
+
+
+def join(*parts):
+    rows = sum(part.shape[0] for part in parts)
+    out = shape_of((rows,) + parts[0].shape[1:], parts[0].dtype)
+    return call(join_kernel, out, [VM] * len(parts), VM)(*parts)
 
 
 def swap(value, axis, step=1):
@@ -470,7 +480,8 @@
         plane = jnp.bitwise_xor(z, step)
         for j in range(CL_MB):
             clip = order_entry(order, y * 2 + core, plane * CL_MB + j)[0, 0].astype(jnp.int32)
-            piece[j] = clip_ref[clip]
+            piece[j * 64 : (j + 1) * 64, :] = clip_ref[clip]
+        piece[CL_MB * 64 :, :] = jnp.zeros((piece.shape[0] - CL_MB * 64, C1), BF)
 
 
 def prepare_kernel(
@@ -529,7 +540,8 @@
     send_ref[144 + CHUNK : 160 + CHUNK, :] = packed.astype(BF)
 
 
-def first_weight_kernel(o0, o1, o2, o3, others, weight_ref, gain_ref):
+def first_weight_kernel(o0, o1, o2, o3, others, facts_in, weight_ref, gain_ref, facts_ref):
+    facts_ref[...] = facts_in[...]
     z, y, core = place("z", "y", "core")
     gains = jnp.zeros((8, LANES), F32)
     for half in range(2):
@@ -553,53 +565,58 @@
 
 
 def first_conv_kernel(
-    facts_ref, a0, a1, a23, b0, b1, b23, weight_ref, pre_ref, x_ref, stat_ref, sems
+    facts_ref, a0, a1, a23, b0, b1, b23, weight_ref, pre_ref, x_ref, stat_ref
 ):
-    z, x, y, core = place(*AXES)
-    copies = []
+    z, x, y = place("z", "x", "y")
+    frame = lax.broadcasted_iota(jnp.int32, (64, LANES), 0) // MEL
     for j, pieces in (
         (0, ((a0, 0, x, y), (a1, 0, 1 - x, y), (a23, 0, x, 1 - y), (a23, MB, 1 - x, 1 - y))),
         (1, ((b0, 0, x, y), (b1, 0, x, 1 - y), (b23, 0, 1 - x, y), (b23, MB, 1 - x, 1 - y))),
     ):
         for source, base, x_of, y_of in pieces:
+            count = facts_ref[pl.ds(y_of * CL_MB + j, 1), :]
             for step in range(MB):
-                frames = (jnp.bitwise_xor(z, step) * 2 + x_of) * 64
-                row = pl.multiple_of((y_of * CL_MB + j) * ROWS + frames, 64)
-                copies.append((source.at[base + step], x_ref.at[pl.ds(row, 64), :]))
-    started = start_copies(copies, sems)
-    wait_all(started)
+                frames = (jnp.bitwise_xor(z, step) * 2 + x_of) * 8
+                mask = (frame + frames < count).astype(F32).astype(BF)
+                row = pl.multiple_of((y_of * CL_MB + j) * ROWS + frames * MEL, 64)
+                x_ref[pl.ds(row, 64), :] = source[base + step] * jnp.concatenate([mask, mask], axis=1)
     weight = weight_ref[...].reshape(TAPS * LANES, C1)
     first = jnp.zeros((1, LANES), F32)
     second = jnp.zeros((1, LANES), F32)
     for clip in range(CLIPS_CORE):
         span = slice(clip * ROWS, (clip + 1) * ROWS)
-        mask = valid_rows(facts_ref, clip)
-        masked = x_ref[span, :] * jnp.concatenate([mask, mask], axis=1).astype(BF)
-        x_ref[span, :] = masked
-        pre = gather_taps(dot_nt(masked, weight))
+        pre = gather_taps(dot_nt(x_ref[span, :], weight))
         pre_ref[span, :] = pre
-        kept = pre * mask
+        kept = pre * valid_rows(facts_ref, clip)
         plus = channel_sums(kept, kept * pre)
         first, second = first + plus[0], second + plus[1]
     put_pair(stat_ref, first, second)
 
 
-def hidden_kernel(facts_ref, pre_ref, own_ref, other_ref, gain_ref, a_ref, b_ref):
+def stack_kernel(p0, p1, p2, p3, a_ref, b_ref):
+    for step, piece in enumerate((p0, p1, p2, p3)):
+        a_ref[step] = piece[0:64]
+        b_ref[step] = piece[64:128]
+
+
+def hidden_kernel(facts_ref, pre_ref, own_ref, other_ref, gain_ref, *outs):
     mean, scale = norm_rows(own_ref, other_ref, pixel_row(facts_ref))
     for clip in range(CLIPS_CORE):
         pre = pre_ref[clip * ROWS : (clip + 1) * ROWS, :]
         shaped = gain_ref[0:1, :] * ((pre - mean) * scale) + gain_ref[1:2, :]
         value = shaped * jax.nn.sigmoid(shaped) * valid_rows(facts_ref, clip)
-        target = a_ref if clip < 2 else b_ref
-        target[(clip % 2) * ROWS : (clip % 2 + 1) * ROWS, :] = value.astype(BF)
-
-
-def second_weight_kernel(own_ref, other_ref, weight_ref):
+        for target in outs[clip // 2 * 2 : clip // 2 * 2 + 2]:
+            target[(clip % 2) * ROWS : (clip % 2 + 1) * ROWS, :] = value.astype(BF)
+    for target in outs:
+        target[HALF:, :] = jnp.zeros((target.shape[0] - HALF, LANES), BF)
+
+
+def second_weight_kernel(o0, o1, o2, o3, s0, s1, s2, s3, weight_ref):
     z, y, core = place("z", "y", "core")
     spread = exchange_matrix(C2, C2, block_exchange)
-    for step in range(MB):
+    spans = [slice(0, CHUNK), slice(CHUNK, 2 * CHUNK)]
+    for step, (own_ref, other_ref) in enumerate(((o0, s0), (o1, s1), (o2, s2), (o3, s3))):
         z_of = jnp.bitwise_xor(z, step)
-        spans = [slice((step * 2 + turn) * CHUNK, (step * 2 + turn + 1) * CHUNK) for turn in range(2)]
         parts = []
         for y_of in range(2):
             own = jnp.where(y == y_of, own_ref[spans[0]], own_ref[spans[1]])
@@ -616,7 +633,9 @@
     copies = []
     for at, (source, (x_of, y_of)) in enumerate(zip(parts, chips)):
         lane = pl.multiple_of((x_of * 2 + y_of) * LANES, LANES)
-        copies.append((source, target.at[pl.ds((at // 4) * HALF, HALF), pl.ds(lane, LANES)]))
+        copies.append(
+            (source.at[pl.ds(0, HALF)], target.at[pl.ds((at // 4) * HALF, HALF), pl.ds(lane, LANES)])
+        )
     return copies
 
 
@@ -772,18 +791,17 @@
 
 def both_grad_kernel(
     facts_ref, slope_ref, pre_ref, own_ref, other_ref, sum_own, sum_other, gain_ref, weight_ref,
-    pooled_ref, columns, a_own, a_mid, a_send, b_own, b_mid, b_send, partial
+    pooled_ref, columns, a_own, a_mid, a_send, b_own, b_mid, b_send, weight
 ):
     x, y = place("x", "y")
     pixels = pixel_row(facts_ref)
     mean, scale = norm_rows(own_ref, other_ref, pixels)
     sums = pair_sums(sum_own, sum_other)
-    weight = weight_ref[...].reshape(TAPS * LANES, C2)
     a_send[2 * HALF : 2 * HALF + 16, :] = pooled_ref[...]
 
-    def lane(x_of, y_of):
-        return pl.ds(pl.multiple_of((x_of * 2 + y_of) * LANES, LANES), LANES)
-
+    for at, (x_of, y_of) in enumerate(((x, y), (x, 1 - y), (1 - x, y), (1 - x, 1 - y))):
+        lane = pl.multiple_of((x_of * 2 + y_of) * LANES, LANES)
+        weight[:, lanes_of(at)] = weight_ref[:, :, :, pl.ds(lane, LANES)].reshape(TAPS * LANES, LANES)
     for clip in range(CLIPS_CORE):
         span = slice(clip * ROWS, (clip + 1) * ROWS)
         mask = valid_rows(facts_ref, clip)
@@ -791,24 +809,26 @@
             slope_ref[span, :], pre_ref[span, :], mask, mean, scale, gain_ref[2:3, :], sums, pixels
         )
         scatter_taps(grad, columns, clip * ROWS)
-        partial[...] = dot_nn(columns[span, :], weight)
+        partial = dot_nn(columns[span, :], weight[...])
         rows = slice((clip % 2) * ROWS, (clip % 2 + 1) * ROWS)
         near_rows = slice(HALF + (clip % 2) * ROWS, HALF + (clip % 2 + 1) * ROWS)
-        far = partial[:, lane(1 - x, 1 - y)].astype(BF)
+        far = partial[:, lanes_of(3)].astype(BF)
         if clip < 2:
-            a_own[rows, :] = partial[:, lane(x, y)]
-            a_mid[rows, :] = partial[:, lane(x, 1 - y)]
+            a_own[rows, :] = partial[:, lanes_of(0)]
+            a_mid[rows, :] = partial[:, lanes_of(1)]
             a_send[rows, :] = far
-            a_send[near_rows, :] = partial[:, lane(1 - x, y)].astype(BF)
+            a_send[near_rows, :] = partial[:, lanes_of(2)].astype(BF)
         else:
-            b_own[rows, :] = partial[:, lane(x, y)]
-            b_mid[rows, :] = partial[:, lane(1 - x, y)]
+            b_own[rows, :] = partial[:, lanes_of(0)]
+            b_mid[rows, :] = partial[:, lanes_of(2)]
             b_send[rows, :] = far
-            b_send[near_rows, :] = partial[:, lane(x, 1 - y)].astype(BF)
-
-
-def pass_on_kernel(a_mid, a_got, b_mid, b_got, a_next, b_next):
-    a_next[...] = (a_mid[...] + a_got[0:HALF].astype(F32)).astype(BF)
+            b_send[near_rows, :] = partial[:, lanes_of(1)].astype(BF)
+
+
+def pass_on_kernel(a_mid, a_got, b_mid, b_got, pooled_ref, a_next, b_next):
+    a_next[HALF : HALF + 16, :] = pooled_ref[...]
+    a_next[HALF + 16 : HALF + 32, :] = a_got[2 * HALF : 2 * HALF + 16]
+    a_next[0:HALF, :] = (a_mid[...] + a_got[0:HALF].astype(F32)).astype(BF)
     b_next[...] = (b_mid[...] + b_got[0:HALF].astype(F32)).astype(BF)
 
 
@@ -849,7 +869,7 @@
     y = place("y")
     total = own_ref[...] + g1[...].astype(F32) + g2[...].astype(F32) + g3[...].astype(F32)
     keep_ref[...] = jnp.where(y == 0, total[0], total[1])
-    send_ref[...] = jnp.where(y == 0, total[1], total[0])
+    send_ref[...] = jnp.where(y == 0, total[1], total[0]).astype(BF)
     square_ref[...] = jnp.sum(total * total, axis=(0, 1), keepdims=False)[None, :] * jnp.ones((8, 1), F32)
 
 
@@ -990,7 +1010,7 @@
         target[CHUNK + 16 : CHUNK + 32, :] = pooled_tile
 
 
-def first_sum_kernel(own_ref, n0, g1, g2, g3, square_two, two_send, told_ref, keep_ref, send_ref, norm_ref):
+def first_sum_kernel(own_ref, n0, g1, g2, g3, square_two, told_ref, keep_ref, send_ref, norm_ref):
     z, y, core = place("z", "y", "core")
     total = own_ref[...]
     norm = n0[CHUNK : CHUNK + 16, :].astype(F32)
@@ -1012,7 +1032,6 @@
     send_ref[0:144, :] = jnp.where(left, high[0:144], pltpu.roll(high[144:288], 64, 1))
     rows = jnp.concatenate([norm, jnp.zeros((4, LANES), F32)], axis=0)
     send_ref[144:152, :] = rows
-    send_ref[152 : 152 + CHUNK, :] = two_send[...]
     norm_ref[...] = rows
 
 
@@ -1033,7 +1052,7 @@
         out[at] = value
 
 
-def adam_kernel(told_ref, keep_ref, got_ref, norm_ref, two_keep, *refs):
+def adam_kernel(told_ref, keep_ref, got_ref, norm_ref, two_keep, two_got, *refs):
     z, y = place("z", "y")
     one, two, norm, outs = refs[0:3], refs[3:6], refs[6:9], refs[9:]
     norm_out, one_out, two_out, small_out = outs[0], outs[1:6], outs[6:11], outs[11:16]
@@ -1048,7 +1067,7 @@
         rows = slice(tap * 32, (tap + 1) * 32)
         gradient = jnp.swapaxes(jnp.concatenate([span[rows] for span in spans], axis=0), 0, 1)
         adam_write(one, one_out, gradient, factor, (9 * C1) ** (-0.5), WEIGHT_DECAY, tap)
-        keep, got = two_keep[rows, :], got_ref[152 + tap * 32 : 152 + (tap + 1) * 32, :]
+        keep, got = two_keep[rows, :], two_got[rows, :].astype(F32)
         gradient = jnp.concatenate(
             [jnp.where(y == 0, keep, got), jnp.where(y == 0, got, keep)], axis=0
         )
@@ -1076,52 +1095,27 @@
             target[j] = jnp.where(frame < count, total, 0.0).astype(BF)
 
 
-def finish_kernel(facts_ref, f0, g1, g2, g3, n0, n1, n2, n3, grad_ref, pooled_ref, scratch):
+def finish_kernel(facts_ref, f0, g1, g2, g3, grad_ref):
     z = place("z")
-    for step, (piece, told) in enumerate(((f0, n0), (g1, n1), (g2, n2), (g3, n3))):
+    for step, piece in enumerate((f0, g1, g2, g3)):
+        at = jnp.bitwise_xor(z, step)
+        for j in range(CL_MB):
+            clip = facts_ref[pl.ds(8 + at * CL_MB + j, 1), :][0, 0]
+            grad_ref[clip] = piece[j]
+
+
+def pooled_kernel(facts_ref, n0, n1, n2, n3, pooled_ref, scratch):
+    z = place("z")
+    for step, told in enumerate((n0, n1, n2, n3)):
         at = jnp.bitwise_xor(z, step)
         rows = told[CHUNK + 16 : CHUNK + 32, :].astype(F32)
         for j in range(CL_MB):
             clip = facts_ref[pl.ds(8 + at * CL_MB + j, 1), :][0, 0]
-            grad_ref[clip] = piece[j]
             for part in range(2):
                 chips = [rows[chip * 4 + part * 2 + j : chip * 4 + part * 2 + j + 1] for chip in range(4)]
                 scratch[part, pl.ds(clip, 1), :] = jnp.concatenate(chips, axis=1)
     spread = exchange_matrix(C2, C2, block_exchange)
     pooled_ref[...] = dot_nn(scratch[0].astype(BF), spread) + dot_nn(scratch[1].astype(BF), spread)
-
-
-FLOP_SCALE = OPT['flop']
-BYTE_SCALE = 0
-COSTS = {
-    take_kernel: 1,
-    prepare_kernel: 2,
-    first_weight_kernel: 1,
-    first_conv_kernel: 4,
-    hidden_kernel: 0.4,
-    second_weight_kernel: 2.8,
-    second_conv_kernel: 3.5,
-    near_conv_kernel: 3,
-    far_conv_kernel: 2,
-    pool_kernel: 1.1,
-    grad_columns_kernel: 1.7,
-    hidden_grad_kernel: 3.4,
-    both_grad_kernel: 4,
-    second_weight_grad_kernel: 5,
-    pass_on_kernel: 0.2,
-    second_core_kernel: 0.2,
-    second_sum_kernel: 0.2,
-    first_slope_kernel: 0.8,
-    first_grads_kernel: 4,
-    first_weight_grad_kernel: 2,
-    input_grad_kernel: 1.5,
-    first_core_kernel: 0.2,
-    first_sum_kernel: 0.8,
-    adam_kernel: 2,
-    load_kernel: 1,
-    input_sum_kernel: 0.3,
-    finish_kernel: 1.5,
-}
 
 
 def spread_plane(a0, b0):
@@ -1148,7 +1142,7 @@
 ):
     one_view, two_view = kernel_one, jnp.swapaxes(kernel_two, 1, 2)
     p0, p1, p2, p3 = call(
-        take_kernel, [shape_of((CL_MB, 64, C1))] * MB, [VM] * 2, [VM] * MB, limit=62 * 1024 * 1024
+        take_kernel, [shape_of((CL_MB * 64 + OPT['pad_in'], C1))] * MB, [VM] * 2, [VM] * MB, limit=OPT['take_limit'] * 1024 * 1024
     )(clip_order, clip_input.reshape(MB * CL_MB, 64, C1))
     one_keep, two_keep, send, gain_rows, cot_own, facts = call(
         prepare_kernel,
@@ -1163,7 +1157,7 @@
             pltpu.VMEM(cotangent.shape, F32),
             pltpu.SemaphoreType.DMA((4,)),
         ],
-        limit=62 * 1024 * 1024,
+        limit=OPT['prep_limit'] * 1024 * 1024,
     )(
         pin("prep_after_take", clip_order, p0), frame_counts.reshape(1, 32), one_view, two_view, norm_params, cotangent
     )
@@ -1172,81 +1166,67 @@
         got = {step: swap(values[step], "z", step) for step in steps_of()}
         return [values[0]] + [got[step] for step in (1, 2, 3)]
 
+    p1, p2, p3 = (pin("zin_after_prep", part, send) for part in (p1, p2, p3))
     arrived = spread_z([p0, p1, p2, p3])
     got = swap(send, "y")
-    a0 = jnp.stack([piece[0] for piece in arrived])
-    b0 = jnp.stack([piece[1] for piece in arrived])
-    one_flat = pin("w1_after_in", jnp.concatenate([one_keep, got[0:144], gain_rows]), a0, b0)
+    a0, b0 = call(stack_kernel, [shape_of((MB, 64, C1))] * 2, [VM] * 4, [VM] * 2)(*arrived)
+    one_flat = pin("w1_after_in", join(one_keep, got[0:144], gain_rows), a0, b0)
     a1, b1 = swap(a0, "x"), swap(b0, "y")
-    if OPT["merge_w"]:
-        flat = jnp.concatenate([one_flat, two_keep, got[144 : 144 + CHUNK]])
-        one_parts = spread_z([flat] * 4)
+    one_parts = spread_z([one_flat] * 4)
+    a01, b01 = join(a0, a1), join(b0, b1)
+    deps = (a1, b1) if OPT["core_w1_after"] == 1 else ()
+    if OPT["core_w1"] == 2:
+        halves = [join(*one_parts[0:2]), join(*one_parts[2:4])]
+        one_others = join(*[swap(after(part, *deps), "core") for part in halves])
+    elif OPT["core_w1"] == 4:
+        one_others = join(*[swap(after(part, *deps), "core") for part in one_parts])
     else:
-        one_parts = spread_z([one_flat] * 4)
-    a01, b01 = jnp.concatenate([a0, a1]), jnp.concatenate([b0, b1])
-    if OPT["core_w1_after"] < 2:
-        deps = (a1, b1) if OPT["core_w1_after"] else ()
-        if OPT["core_w1"] == 4:
-            one_others = jnp.concatenate([swap(after(part[0:304], *deps), "core") for part in one_parts])
-        else:
-            one_others = swap(after(jnp.concatenate([part[0:304] for part in one_parts]), *deps), "core")
-        a01, b01 = pin("fwd_after_core_w1", a01, one_others), pin("fwd_after_core_w1", b01, one_others)
-        a23, b23 = swap(a01, "y"), swap(b01, "x")
-    else:
-        a23, b23 = swap(a01, "y"), swap(b01, "x")
-        deps = (a23, b23)
-        if OPT["core_w1"] == 4:
-            one_others = jnp.concatenate([swap(after(part[0:304], *deps), "core") for part in one_parts])
-        else:
-            one_others = swap(after(jnp.concatenate([part[0:304] for part in one_parts]), *deps), "core")
+        one_others = swap(after(join(*one_parts), *deps), "core")
+    a23, b23 = swap(a01, "y"), swap(b01, "x")
     inputs = (a0, a1, a23, b0, b1, b23)
-    if OPT["merge_w"]:
-        two_parts = [part[304:] for part in one_parts]
-        one_parts = [part[0:304] for part in one_parts]
-    else:
-        two_flat = jnp.concatenate([two_keep, got[144 : 144 + CHUNK]])
-        two_flat = {
-            0: lambda: two_flat,
-            1: lambda: after(two_flat, *one_parts[1:]),
-            2: lambda: after(two_flat, one_others),
-            3: lambda: after(two_flat, a1, b1),
-            4: lambda: after(two_flat, a1, b1, one_others),
-        }[OPT["w2_after"]]()
-        two_parts = spread_z([two_flat] * 4)
-    weight_one, gains = call(
+    two_flat = join(two_keep, got[144 : 144 + CHUNK])
+    two_flat = {
+        0: lambda: two_flat,
+        1: lambda: after(two_flat, *one_parts[1:]),
+        2: lambda: after(two_flat, one_others),
+        3: lambda: after(two_flat, a1, b1),
+        4: lambda: after(two_flat, a1, b1, one_others),
+    }[OPT["w2_after"]]()
+    two_parts = spread_z([two_flat] * 4)
+    weight_one, gains, facts = call(
         first_weight_kernel,
-        [shape_of((TAPS, MB, 32, C1)), shape_of((8, LANES), F32)],
-        [VM] * 5,
-        [VM] * 2,
-    )(*one_parts, one_others)
+        [shape_of((TAPS, MB, 32, C1)), shape_of((8, LANES), F32), shape_of((16, LANES), jnp.int32)],
+        [VM] * 6,
+        [VM] * 3,
+    )(*one_parts, one_others, facts)
     pre_one, masked, stat_one = call(
         first_conv_kernel,
         [shape_of((PIXELS, LANES), F32), shape_of((PIXELS, C1)), shape_of((8, LANES), F32)],
-        [VM] + [ANY] * 6 + [VM],
+        [VM] * 8,
         [VM] * 3,
-        [pltpu.SemaphoreType.DMA((8 * MB,))],
     )(
         after(facts, *two_parts[1:]) if OPT["w2_before"] == 2 else facts, *inputs, weight_one
     )
     stat_one_other = swap(stat_one, "core")
 
-    ha0, hb0 = call(
-        hidden_kernel, [shape_of((HALF, LANES))] * 2, [VM] * 5, [VM] * 2
+    ha_on, ha0, hb_on, hb0 = call(
+        hidden_kernel,
+        [shape_of((HALF + pad, LANES)) for pad in (OPT['pad_p'], OPT['pad_s'])] * 2,
+        [VM] * 5,
+        [VM] * 4,
     )(
         after(facts, *two_parts[1:]) if OPT["w2_before"] == 1 else facts, pre_one, stat_one, stat_one_other, gains
     )
-    hidden_parts = spread_plane(ha0, hb0)
-
-    two_all = jnp.concatenate(two_parts)
-    if OPT["core_w2_after"] == 1:
-        two_all = after(two_all, ha0)
-    if OPT["core_w2_after"] == 2:
-        two_all = after(two_all, hidden_parts[1], hidden_parts[5])
-    two_all_other = swap(two_all, "core")
-    two_all = pin("kw2_after", two_all, hidden_parts[1], hidden_parts[5])
-    weight_two = call(
-        second_weight_kernel, shape_of((TAPS, MB, 32, C2)), [VM, VM], VM
-    )(two_all, two_all_other)
+    ha1, hb1 = swap(ha_on, "x"), swap(hb_on, "y")
+    ha2, hb2 = swap(ha0, "y"), swap(hb0, "x")
+    ha3, hb3 = swap(ha1, "y"), swap(hb1, "x")
+    hidden_parts = (ha0, ha1, ha2, ha3, hb0, hb1, hb2, hb3)
+
+    deps = {0: (), 1: (ha0,), 2: (ha1, hb1)}[OPT["core_w2_after"]]
+    two_others = [swap(after(part, *deps), "core") for part in two_parts]
+    weight_two = call(second_weight_kernel, shape_of((TAPS, MB, 32, C2)), [VM] * 8, VM)(
+        *two_parts, *two_others
+    )
 
     if OPT["split_conv"]:
         ha = hidden_parts
@@ -1305,7 +1285,7 @@
             + [shape_of((2 * HALF, LANES))],
             [VM] * 10,
             [VM] * 7,
-            [pltpu.VMEM((ROWS, C2), F32)],
+            [pltpu.VMEM((TAPS * LANES, C2), BF)],
         )(
             facts, slope_two, pre_two, stat_two, stat_two_other, sum_two, sum_two_other, gains,
             weight_two, pooled_own,
@@ -1339,13 +1319,9 @@
         a_got = after(a_got, t1)
     else:
         a_got = pin("pass_after_g2", a_got, thirds[0])
-    a_next, b_next = call(pass_on_kernel, [shape_of((HALF, LANES))] * 2, [VM] * 4, [VM] * 2)(
-        a_mid,
-        pin("pass_after_near", a_got, a_near, b_near),
-        b_mid,
-        b_got,
-    )
-    a_next = jnp.concatenate([a_next, pooled_own, a_pool])
+    a_next, b_next = call(
+        pass_on_kernel, [shape_of((HALF + 32, LANES)), shape_of((HALF, LANES))], [VM] * 5, [VM] * 2
+    )(a_mid, a_got, b_mid, b_got, pooled_own)
     a_last, b_last = swap(a_next, "y"), swap(b_next, "x")
     if OPT["core_g2"] == 1:
         two_own, t1, t2, t3 = sum_cores(a_next)
@@ -1382,7 +1358,7 @@
 
     two_keep_sum, two_send_sum, square_two = call(
         second_sum_kernel,
-        [shape_of((CHUNK, LANES), F32)] * 2 + [shape_of((8, LANES), F32)],
+        [shape_of((CHUNK, LANES), F32), shape_of((CHUNK, LANES)), shape_of((8, LANES), F32)],
         [VM] * 4,
         [VM] * 3,
     )(*spread_z([two_own, t1, t2, t3]))
@@ -1405,6 +1381,7 @@
     f0, f1, f2, f3 = call(
         input_sum_kernel, [shape_of((CL_MB, 64, C1))] * MB, [VM] * 2, [VM] * 4
     )(facts, input_got)
+    two_got_sum = swap(pin("y2_after", two_send_sum, n1), "y")
     if not OPT["f_after_sum"]:
         f1, f2, f3 = spread_z([f0, f1, f2, f3])[1:]
     told, one_keep_sum, one_send_sum, norm_sum = call(
@@ -1412,16 +1389,17 @@
         [
             shape_of((32 * 8, LANES), F32),
             shape_of((144, LANES), F32),
-            shape_of((152 + CHUNK, LANES), F32),
+            shape_of((152, LANES), F32),
             shape_of((8, LANES), F32),
         ],
-        [VM] * 7,
+        [VM] * 6,
         [VM] * 4,
     )(
-        pin("sum_after_f", one_own, f0), n0, g1, g2, g3, square_two, two_send_sum
+        pin("sum_after_y2", pin("sum_after_f", one_own, f0), two_got_sum), n0, g1, g2, g3, square_two
     )
     if OPT["f_after_sum"]:
         f1, f2, f3 = spread_z([f0, after(f1, told), after(f2, told), after(f3, told)])[1:]
+    told_sent = told
     told = lax.all_to_all(told, AXES, 0, 0, tiled=True)
     one_got_sum = swap(one_send_sum, "y")
     one_shapes = [shape_of(one_view.shape, F32)] * 4 + [shape_of(one_view.shape)]
@@ -1450,7 +1428,7 @@
     updates = call(
         adam_kernel,
         [shape_of((1, 1), F32)] + one_shapes + two_shapes + norm_shapes,
-        [VM] * 14,
+        [VM] * 15,
         [VM] * 16,
         limit=OPT['adam_limit'] * 1024 * 1024,
     )(
@@ -1459,18 +1437,22 @@
         one_got_sum,
         norm_sum,
         two_keep_sum,
+        two_got_sum,
         *state,
     )
     grad_norm = updates[0].reshape(())
     first_update, norm_update = tuple(updates[1:6]), tuple(updates[11:16])
     second_update = tuple(jnp.swapaxes(part, 1, 2) for part in updates[6:11])
-    input_grad, pooled = call(
-        finish_kernel,
-        [shape_of((MB * CL_MB, 64, C1)), shape_of((MB * CL_MB, C2), F32)],
-        [VM] * 9,
-        [VM] * 2,
+    pooled = call(
+        pooled_kernel,
+        shape_of((MB * CL_MB, C2), F32),
+        [VM] * 5,
+        VM,
         [pltpu.VMEM((2, MB * CL_MB, C2), F32)],
-    )(facts, pin("finish_last", f0, updates[0]), f1, f2, f3, n0, g1, g2, g3)
+    )(facts, pin("pooled_after", n0, told_sent), g1, g2, g3)
+    input_grad = call(finish_kernel, shape_of((MB * CL_MB, 64, C1)), [VM] * 5, VM)(
+        facts, pin("finish_last", f0, updates[0]), f1, f2, f3
+    )
     input_grad = input_grad.reshape(clip_input.shape)
     return (pooled, input_grad, grad_norm) + first_update + second_update + norm_update
 

time: 143 us -> 141 us (0.986)
  Pallas kernels: 37.1 us -> 33.3 us
  local copies, waits for them, and re-layouts: 3.72 us -> 7.42 us
    unnamed x29 -> x28, local copies, waits for them, and re-layouts: 3.68 us -> 7.41 us
    pallas_call x1, Pallas kernels: 3.84 us -> 1.73 us  [fast_body(): call(first_conv_kernel, [shape_of((PIXELS, LANES), F32), shape_of((PIXELS...]
    ppermute x44 -> x51, waiting for transfers between devices: 41.7 us -> 39.9 us  [swap(): return lax.ppermute(value, axis, [(i, i ^ step) for i in range(size)])]
    pallas_call x6 -> x13, Pallas kernels: 4.23 us -> 3.4 us  [the longest x1 0.94 us: fast_body(): call(pooled_kernel, shape_of((MB * CL_MB, C2), F32), [VM] * 5, VM, [pltpu...]
    ppermute x44 -> x51, starting transfers between devices: 50.1 us -> 50.6 us  [swap(): return lax.ppermute(value, axis, [(i, i ^ step) for i in range(size)])]
  transfers between devices with their start and end apart: 46 -> 53, of which waited for: 21 -> 25; matrix products, arithmetic and copies ran while one was open for 1% -> 0% of each run, Pallas kernels for 19% -> 18%
where the time goes in v5:
time: 141 us; the launch traced here: 140 us
  starting transfers between devices  58.2 us (41%)
  waiting for transfers between devices  40.5 us (29%)
  Pallas kernels  33.3 us (24%)
  local copies, waits for them, and re-layouts  7.42 us (5%)
    ppermute x51, starting transfers between devices, swap(): return lax.ppermute(value, axis, [(i, i ^ step) for i in range(size)])  50.6 us
    ppermute x51, waiting for transfers between devices, swap(): return lax.ppermute(value, axis, [(i, i ^ step) for i in range(size)])  39.9 us
    unnamed x28, local copies, waits for them, and re-layouts  7.41 us
    pallas_call x1, Pallas kernels, fast_body(): call(second_weight_grad_kernel, [shape_of((MB, 2, 96, LANES), F32)] * 6,...  4.93 us
    all_to_all x1, starting transfers between devices, fast_body(): told = lax.all_to_all(told, AXES, 0, 0, tiled=True)  4.17 us
    all_to_all x1, starting transfers between devices, fast_body(): input_got = lax.all_to_all(input_part, ('x', 'y'), 0, 0, tiled=True)  3.51 us
    pallas_call x1, Pallas kernels, fast_body(): call(adam_kernel, [shape_of((1, 1), F32)] + one_shapes + two_shapes + nor...  3.51 us
    pallas_call x1, Pallas kernels, fast_body(): call(both_grad_kernel, [shape_of((PIXELS, TAPS * LANES))] + [shape_of((HA...  3.42 us
  transfers between devices with their start and end apart: 53, of which 25 were waited for; matrix products, arithmetic and copies ran while one was open for 0% of the time, Pallas kernels for 18%

profile of v5, /device:TPU:0, one launch (start us, length us, event | category | flops | bytes accessed | tf_op | source)
XLA Modules:
  0.0 140.5 jit_solution(5090556036759578325)
XLA Ops:
  2.4 3.1 %collective-permute-start.11 = (bf16[144,256]{1,0:T(8,128)(2,1)S(1)}, bf16[144,256]{1,0:T(8,128)(2,1)S(1)}, u32[]{:S(2)}, u32[]{:S(2)}) collective-permute-start(bf16[144,256]{1,0:T(8,128)(2,1)S(1)} %get-tuple-element.124), channel_id=1, source_target_pairs={{0,8},{8,0},{16,24},{24,16},{1,9},{9,1},{17,25},{25,17},{2,10},{10... | collective-permute-start | bytes 221192 | tf_op jit(solution)/shard_map/ppermute | solution.py:310
  5.5 2.6 %collective-permute-start.12 = (bf16[144,256]{1,0:T(8,128)(2,1)S(1)}, bf16[144,256]{1,0:T(8,128)(2,1)S(1)}, u32[]{:S(2)}, u32[]{:S(2)}) collective-permute-start(bf16[144,256]{1,0:T(8,128)(2,1)S(1)} %get-tuple-element.125), channel_id=1, source_target_pairs={{0,16},{8,24},{16,0},{24,8},{1,17},{9,25},{17,1},{25,9},{2,18},{10... | collective-permute-start | bytes 221192 | tf_op jit(solution)/shard_map/ppermute | solution.py:310
  8.1 2.8 %shard_map.269 = (bf16[144,128]{1,0:T(8,128)(2,1)}, bf16[288,128]{1,0:T(8,128)(2,1)}, bf16[448,128]{1,0:T(8,128)(2,1)}, bf16[16,128]{1,0:T(8,128)(2,1)}, f32[8,128]{1,0:T(8,128)}, /*index=5*/s32[16,128]{1,0:T(8,128)}) custom-call(s32[4,8]{1,0:T(4,128)} %order_ref.2, s32[1,32]{1,0:T(1,128)} %bitcast.21, f32[9,64,64]{2,1,0:T(8,128)} %refs_0_.1, ...), custom_call_target="tpu_custom_call" | custom-call | tf_op jit(solution)/shard_map/pallas_call | solution.py:1147
  10.9 1.8 %collective-permute-start = (bf16[448,128]{1,0:T(8,128)(2,1)}, bf16[448,128]{1,0:T(8,128)(2,1)S(1)}, u32[]{:S(2)}, u32[]{:S(2)}) collective-permute-start(bf16[448,128]{1,0:T(8,128)(2,1)} %get-tuple-element.117), channel_id=1, source_target_pairs={{0,2},{2,0},{1,3},{3,1},{4,6},{6,4},{5,7},{7,5},{8,10},{10,8},{9,1... | collective-permute-start | bytes 344072 | tf_op jit(solution)/shard_map/ppermute | solution.py:310
  14.4 1.6 %collective-permute-start.14 = (bf16[4,64,256]{2,1,0:T(8,128)(2,1)S(1)}, bf16[4,64,256]{2,1,0:T(8,128)(2,1)S(1)}, u32[]{:S(2)}, u32[]{:S(2)}) collective-permute-start(bf16[4,64,256]{2,1,0:T(8,128)(2,1)S(1)} %get-tuple-element.127.refs_0_.a0), channel_id=1, source_target_pairs={{0,4},{4,0},{1,5},{5,1},{2,6},{6,2},{3,7},{7,3},{8,12},{12,8},{9,1... | collective-permute-start | bytes 393224 | tf_op jit(solution)/shard_map/ppermute | solution.py:310
  18.9 3.2 %collective-permute-start.3 = (bf16[304,128]{1,0:T(8,128)(2,1)S(1)}, bf16[304,128]{1,0:T(8,128)(2,1)S(1)}, u32[]{:S(2)}, u32[]{:S(2)}) collective-permute-start(bf16[304,128]{1,0:T(8,128)(2,1)S(1)} %shard_map.270.o0), channel_id=1, source_target_pairs={{0,24},{8,16},{16,8},{24,0},{1,25},{9,17},{17,9},{25,1},{2,26},{10... | collective-permute-start | bytes 233480 | tf_op jit(solution)/shard_map/ppermute | solution.py:310
  29.0 2.5 %collective-permute-start.10 = (bf16[576,128]{1,0:T(8,128)(2,1)S(1)}, bf16[576,128]{1,0:T(8,128)(2,1)S(1)}, u32[]{:S(2)}, u32[]{:S(2)}) collective-permute-start(bf16[576,128]{1,0:T(8,128)(2,1)S(1)} %shard_map.273.o0), channel_id=1, source_target_pairs={{0,24},{8,16},{16,8},{24,0},{1,25},{9,17},{17,9},{25,1},{2,26},{10... | collective-permute-start | bytes 442376 | tf_op jit(solution)/shard_map/ppermute | solution.py:310
  31.5 2.0 %collective-permute-start.8 = (bf16[576,128]{1,0:T(8,128)(2,1)S(1)}, bf16[576,128]{1,0:T(8,128)(2,1)S(1)}, u32[]{:S(2)}, u32[]{:S(2)}) collective-permute-start(bf16[576,128]{1,0:T(8,128)(2,1)S(1)} %shard_map.273.o0), channel_id=1, source_target_pairs={{0,8},{8,0},{16,24},{24,16},{1,9},{9,1},{17,25},{25,17},{2,10},{10... | collective-permute-start | bytes 442376 | tf_op jit(solution)/shard_map/ppermute | solution.py:310
  34.7 1.7 %shard_map.277 = (f32[2048,128]{1,0:T(8,128)S(1)}, bf16[2048,256]{1,0:T(8,128)(2,1)S(1)}, f32[8,128]{1,0:T(8,128)S(1)}) custom-call(s32[16,128]{1,0:T(8,128)S(1)} %get-tuple-element.155.facts_ref, bf16[4,64,256]{2,1,0:T(8,128)(2,1)S(1)} %get-tuple-element.127.refs_0_.a0, bf16[4,64,256]{2,1,0:T(8,128)(2,1)S(1)} %collective-permute-done.14.refs_1_.a1, ...), custom_call_target="tpu_custom_call" | custom-call | tf_op jit(solution)/shard_map/pallas_call | solution.py:1202
  37.7 6.9 %collective-permute-done.9.o2 = bf16[576,128]{1,0:T(8,128)(2,1)S(1)} collective-permute-done((bf16[576,128]{1,0:T(8,128)(2,1)S(1)}, bf16[576,128]{1,0:T(8,128)(2,1)S(1)}, u32[]{:S(2)}, u32[]{:S(2)}) %collective-permute-start.9) | collective-permute-done | bytes 147488 | tf_op jit(solution)/shard_map/ppermute | solution.py:310
  50.4 2.8 %collective-permute-done.19.a1.rest_1_ = bf16[1056,128]{1,0:T(8,128)(2,1)S(1)} collective-permute-done((bf16[1056,128]{1,0:T(8,128)(2,1)S(1)}, bf16[1056,128]{1,0:T(8,128)(2,1)S(1)}, u32[]{:S(2)}, u32[]{:S(2)}) %collective-permute-start.19) | collective-permute-done | bytes 270368 | tf_op jit(solution)/shard_map/ppermute | solution.py:310
  53.2 2.1 %collective-permute-start.21 = (bf16[1056,128]{1,0:T(8,128)(2,1)S(1)}, bf16[1056,128]{1,0:T(8,128)(2,1)S(1)}, u32[]{:S(2)}, u32[]{:S(2)}) collective-permute-start(bf16[1056,128]{1,0:T(8,128)(2,1)S(1)} %collective-permute-done.19.a1.rest_1_), channel_id=1, source_target_pairs={{0,2},{2,0},{1,3},{3,1},{4,6},{6,4},{5,7},{7,5},{8,10},{10,8},{9,1... | collective-permute-start | bytes 811016 | tf_op jit(solution)/shard_map/ppermute | solution.py:310
  55.4 1.8 %collective-permute-start.24 = (bf16[1056,128]{1,0:T(8,128)(2,1)S(1)}, bf16[1056,128]{1,0:T(8,128)(2,1)S(1)}, u32[]{:S(2)}, u32[]{:S(2)}) collective-permute-start(bf16[1056,128]{1,0:T(8,128)(2,1)S(1)} %collective-permute-done.22.b1.rest_5_), channel_id=1, source_target_pairs={{0,4},{4,0},{1,5},{5,1},{2,6},{6,2},{3,7},{7,3},{8,12},{12,8},{9,1... | collective-permute-start | bytes 811016 | tf_op jit(solution)/shard_map/ppermute | solution.py:310
  59.4 1.6 %collective-permute-done.20.a2.rest_2_ = bf16[1072,128]{1,0:T(8,128)(2,1)S(1)} collective-permute-done((bf16[1072,128]{1,0:T(8,128)(2,1)S(1)}, bf16[1072,128]{1,0:T(8,128)(2,1)S(1)}, u32[]{:S(2)}, u32[]{:S(2)}) %collective-permute-start.20) | collective-permute-done | bytes 274464 | tf_op jit(solution)/shard_map/ppermute | solution.py:310
  61.0 2.9 %shard_map.280.near_ref = f32[2048,128]{1,0:T(8,128)S(1)} custom-call(bf16[1072,128]{1,0:T(8,128)(2,1)S(1)} %get-tuple-element.133.a0.rest_0_, bf16[1056,128]{1,0:T(8,128)(2,1)S(1)} %collective-permute-done.19.a1.rest_1_, bf16[1072,128]{1,0:T(8,128)(2,1)S(1)} %collective-permute-done.20.a2.rest_2_, bf16[1072,128]{1,0:T(8,128)(2,1)S(1)} %get-tuple-element.135.b0.rest_4_, ...), custom_call_target="tpu_custom_call" | custom-call | tf_op jit(solution)/shard_map/pallas_call | solution.py:1233
  63.8 1.5 %collective-permute-done.21.a3.rest_3_ = bf16[1056,128]{1,0:T(8,128)(2,1)S(1)} collective-permute-done((bf16[1056,128]{1,0:T(8,128)(2,1)S(1)}, bf16[1056,128]{1,0:T(8,128)(2,1)S(1)}, u32[]{:S(2)}, u32[]{:S(2)}) %collective-permute-start.21) | collective-permute-done | bytes 270368 | tf_op jit(solution)/shard_map/ppermute | solution.py:310
  70.5 3.4 %shard_map.283 = (bf16[2048,1152]{1,0:T(8,128)(2,1)S(1)}, f32[1024,128]{1,0:T(8,128)S(1)}, f32[1024,128]{1,0:T(8,128)S(1)}, bf16[2064,128]{1,0:T(8,128)(2,1)S(1)...) custom-call(s32[16,128]{1,0:T(8,128)S(1)} %get-tuple-element.155.facts_ref, ...), custom_call_target="tpu_custom_call" | custom-call | tf_op jit(solution)/shard_map/pallas_call | solution.py:1279
  76.0 4.9 %shard_map.284 = (f32[4,2,96,128]{3,2,1,0:T(8,128)S(1)}, f32[4,2,96,128]{3,2,1,0:T(8,128)S(1)}, f32[4,2,96,128]{3,2,1,0:T(8,128)S(1)}, f32[4,2,96,128]{3,2,1,0:T...) custom-call(bf16[1072,128]{1,0:T(8,128)(2,1)S(1)} %get-tuple-element.133.a0.rest_0_, ...), custom_call_target="tpu_custom_call" | custom-call | tf_op jit(solution)/shard_map/pallas_call | solution.py:1296
  84.7 3.3 %collective-permute-done.34.a_got.a_near = bf16[2064,128]{1,0:T(8,128)(2,1)S(1)} collective-permute-done((bf16[2064,128]{1,0:T(8,128)(2,1)S(1)}, bf16[2064,128]{1,0:T(8,128)(2,1)S(1)}, u32[]{:S(2)}, u32[]{:S(2)}) %collective-permute-start.34) | collective-permute-done | bytes 528416 | tf_op jit(solution)/shard_map/ppermute | solution.py:310
  91.2 2.6 %collective-permute-start.41 = (bf16[2,288,128]{2,1,0:T(8,128)(2,1)}, bf16[2,288,128]{2,1,0:T(8,128)(2,1)S(1)}, u32[]{:S(2)}, u32[]{:S(2)}) collective-permute-start(bf16[2,288,128]{2,1,0:T(8,128)(2,1)} %get-tuple-element.172), channel_id=1, source_target_pairs={{0,24},{8,16},{16,8},{24,0},{1,25},{9,17},{17,9},{25,1},{2,26},{10... | collective-permute-start | bytes 442376 | tf_op jit(solution)/shard_map/ppermute | solution.py:310
  94.7 2.1 %collective-permute-done.37.b_last = bf16[1024,128]{1,0:T(8,128)(2,1)S(1)} collective-permute-done((bf16[1024,128]{1,0:T(8,128)(2,1)S(1)}, bf16[1024,128]{1,0:T(8,128)(2,1)S(1)}, u32[]{:S(2)}, u32[]{:S(2)}) %collective-permute-start.37) | collective-permute-done | bytes 262176 | tf_op jit(solution)/shard_map/ppermute | solution.py:310
  98.9 2.4 %shard_map.288 = (bf16[2048,1152]{1,0:T(8,128)(2,1)S(1)}, f32[4,288,128]{2,1,0:T(8,128)S(1)}, f32[4,288,128]{2,1,0:T(8,128)S(1)}) custom-call(s32[16,128]{1,0:T(8,128)S(1)} %get-tuple-element.155.facts_ref, f32[2048,128]{1,0:T(8,128)S(1)} %get-tuple-element.165.slope_ref, f32[2048,128]{1,0:T(8,128)S(1)} %get-tuple-element.130.pre_ref, ...), custom_call_target="tpu_custom_call" | custom-call | tf_op jit(solution)/shard_map/pallas_call | solution.py:1337
  102.1 2.5 %shard_map.293 = bf16[4,512,256]{2,1,0:T(8,128)(2,1)} custom-call(bf16[2048,1152]{1,0:T(8,128)(2,1)S(1)} %get-tuple-element.182.columns, bf16[9,4,32,256]{3,2,1,0:T(8,128)(2,1)S(1)} %get-tuple-element.129.weight_ref), custom_call_target="tpu_custom_call" | custom-call | tf_op jit(solution)/shard_map/pallas_call | solution.py:1344
  104.6 3.5 %all-to-all-start = ((bf16[4,512,256]{2,1,0:T(8,128)(2,1)}), bf16[4,512,256]{2,1,0:T(8,128)(2,1)S(1)}, u32[]{:S(2)}, u32[]{:S(2)}) async-start(bf16[4,512,256]{2,1,0:T(8,128)(2,1)} %shard_map.293), calls=%async_computation | async-start | bytes 2097152 | tf_op jit(solution)/shard_map/all_to_all | solution.py:1380
  109.1 2.0 %collective-permute-done.42.got_ref = f32[4,288,128]{2,1,0:T(8,128)S(1)} collective-permute-done((f32[4,288,128]{2,1,0:T(8,128)}, f32[4,288,128]{2,1,0:T(8,128)S(1)}, u32[]{:S(2)}, u32[]{:S(2)}) %collective-permute-start.42) | collective-permute-done | bytes 589856 | tf_op jit(solution)/shard_map/ppermute | solution.py:310
  111.3 2.7 %collective-permute-start.45 = (bf16[320,128]{1,0:T(8,128)(2,1)S(1)}, bf16[320,128]{1,0:T(8,128)(2,1)S(1)}, u32[]{:S(2)}, u32[]{:S(2)}) collective-permute-start(bf16[320,128]{1,0:T(8,128)(2,1)S(1)} %get-tuple-element.179), channel_id=1, source_target_pairs={{0,24},{8,16},{16,8},{24,0},{1,25},{9,17},{17,9},{25,1},{2,26},{10... | collective-permute-start | bytes 245768 | tf_op jit(solution)/shard_map/ppermute | solution.py:310
  114.8 5.5 %collective-permute-done.44.g2.n2 = bf16[320,128]{1,0:T(8,128)(2,1)S(1)} collective-permute-done((bf16[320,128]{1,0:T(8,128)(2,1)S(1)}, bf16[320,128]{1,0:T(8,128)(2,1)S(1)}, u32[]{:S(2)}, u32[]{:S(2)}) %collective-permute-start.44) | collective-permute-done | bytes 81952 | tf_op jit(solution)/shard_map/ppermute | solution.py:310
  123.0 4.2 %all-to-all-start.1 = ((f32[32,8,128]{2,1,0:T(8,128)}), f32[32,8,128]{2,1,0:T(8,128)S(1)}, u32[]{:S(2)}, u32[]{:S(2)}) async-start(f32[32,8,128]{2,1,0:T(8,128)} %bitcast.3), calls=%async_computation.1 | async-start | bytes 262144 | tf_op jit(solution)/shard_map/all_to_all | solution.py:1403
  127.2 1.8 %collective-permute-start.46 = (f32[152,128]{1,0:T(8,128)S(1)}, f32[152,128]{1,0:T(8,128)S(1)}, u32[]{:S(2)}, u32[]{:S(2)}) collective-permute-start(f32[152,128]{1,0:T(8,128)S(1)} %get-tuple-element.185), channel_id=1, source_target_pairs={{0,2},{2,0},{1,3},{3,1},{4,6},{6,4},{5,7},{7,5},{8,10},{10,8},{9,1... | collective-permute-start | bytes 233480 | tf_op jit(solution)/shard_map/ppermute | solution.py:310
  129.4 1.8 %collective-permute-start.48 = (bf16[2,64,256]{2,1,0:T(8,128)(2,1)S(1)}, bf16[2,64,256]{2,1,0:T(8,128)(2,1)S(1)}, u32[]{:S(2)}, u32[]{:S(2)}) collective-permute-start(bf16[2,64,256]{2,1,0:T(8,128)(2,1)S(1)} %get-tuple-element.192), channel_id=1, source_target_pairs={{0,8},{8,0},{16,24},{24,16},{1,9},{9,1},{17,25},{25,17},{2,10},{10... | collective-permute-start | bytes 196616 | tf_op jit(solution)/shard_map/ppermute | solution.py:310
  131.3 2.4 %collective-permute-start.49 = (bf16[2,64,256]{2,1,0:T(8,128)(2,1)S(1)}, bf16[2,64,256]{2,1,0:T(8,128)(2,1)S(1)}, u32[]{:S(2)}, u32[]{:S(2)}) collective-permute-start(bf16[2,64,256]{2,1,0:T(8,128)(2,1)S(1)} %get-tuple-element.193), channel_id=1, source_target_pairs={{0,16},{8,24},{16,0},{24,8},{1,17},{9,25},{17,1},{25,9},{2,18},{10... | collective-permute-start | bytes 196616 | tf_op jit(solution)/shard_map/ppermute | solution.py:310
  136.0 3.5 %shard_map.295 = (f32[1,1]{1,0:T(1,128)}, f32[9,64,64]{2,1,0:T(8,128)}, f32[9,64,64]{2,1,0:T(8,128)}, f32[9,64,64]{2,1,0:T(8,128)}, f32[9,64,64]{2,1,0:T(8,128)}...) custom-call(f32[256,128]{1,0:T(8,128)} %bitcast.17, ...), custom_call_target="tpu_custom_call" | custom-call | tf_op jit(solution)/shard_map/pallas_call | solution.py:1428
  (134 shorter events, 50.0 us)
Async XLA Ops:
  2.4 10.3 %collective-permute-start.11 = (bf16[144,256]{1,0:T(8,128)(2,1)S(1)}, bf16[144,256]{1,0:T(8,128)(2,1)S(1)}, u32[]{:S(2)}, u32[]{:S(2)}) collective-permute-start(bf16[144,256]{1,0:T(8,128)(2,1)S(1)} %get-tuple-element.124), channel_id=1, source_target_pairs={{0,8},{8,0},{16,24},{24,16},{1,9},{9,1},{17,25},{25,17},{2,10},{10... | collective-permute-start | bytes 221192 | tf_op jit(solution)/shard_map/ppermute | solution.py:310
  5.5 7.8 %collective-permute-start.12 = (bf16[144,256]{1,0:T(8,128)(2,1)S(1)}, bf16[144,256]{1,0:T(8,128)(2,1)S(1)}, u32[]{:S(2)}, u32[]{:S(2)}) collective-permute-start(bf16[144,256]{1,0:T(8,128)(2,1)S(1)} %get-tuple-element.125), channel_id=1, source_target_pairs={{0,16},{8,24},{16,0},{24,8},{1,17},{9,25},{17,1},{25,9},{2,18},{10... | collective-permute-start | bytes 221192 | tf_op jit(solution)/shard_map/ppermute | solution.py:310
  14.4 8.9 %collective-permute-start.14 = (bf16[4,64,256]{2,1,0:T(8,128)(2,1)S(1)}, bf16[4,64,256]{2,1,0:T(8,128)(2,1)S(1)}, u32[]{:S(2)}, u32[]{:S(2)}) collective-permute-start(bf16[4,64,256]{2,1,0:T(8,128)(2,1)S(1)} %get-tuple-element.127.refs_0_.a0), channel_id=1, source_target_pairs={{0,4},{4,0},{1,5},{5,1},{2,6},{6,2},{3,7},{7,3},{8,12},{12,8},{9,1... | collective-permute-start | bytes 393224 | tf_op jit(solution)/shard_map/ppermute | solution.py:310
  16.0 7.4 %collective-permute-start.16 = (bf16[4,64,256]{2,1,0:T(8,128)(2,1)S(1)}, bf16[4,64,256]{2,1,0:T(8,128)(2,1)S(1)}, u32[]{:S(2)}, u32[]{:S(2)}) collective-permute-start(bf16[4,64,256]{2,1,0:T(8,128)(2,1)S(1)} %get-tuple-element.128.refs_0_.b0), channel_id=1, source_target_pairs={{0,2},{2,0},{1,3},{3,1},{4,6},{6,4},{5,7},{7,5},{8,10},{10,8},{9,1... | collective-permute-start | bytes 393224 | tf_op jit(solution)/shard_map/ppermute | solution.py:310
  23.4 11.3 %collective-permute-start.15 = (bf16[8,64,256]{2,1,0:T(8,128)(2,1)S(1)}, bf16[8,64,256]{2,1,0:T(8,128)(2,1)S(1)}, u32[]{:S(2)}, u32[]{:S(2)}) collective-permute-start(bf16[8,64,256]{2,1,0:T(8,128)(2,1)S(1)} %shard_map.275), channel_id=1, source_target_pairs={{0,2},{2,0},{1,3},{3,1},{4,6},{6,4},{5,7},{7,5},{8,10},{10,8},{9,1... | collective-permute-start | bytes 786440 | tf_op jit(solution)/shard_map/ppermute | solution.py:310
  25.2 9.5 %collective-permute-start.17 = (bf16[8,64,256]{2,1,0:T(8,128)(2,1)S(1)}, bf16[8,64,256]{2,1,0:T(8,128)(2,1)S(1)}, u32[]{:S(2)}, u32[]{:S(2)}) collective-permute-start(bf16[8,64,256]{2,1,0:T(8,128)(2,1)S(1)} %shard_map.276), channel_id=1, source_target_pairs={{0,4},{4,0},{1,5},{5,1},{2,6},{6,2},{3,7},{7,3},{8,12},{12,8},{9,1... | collective-permute-start | bytes 786440 | tf_op jit(solution)/shard_map/ppermute | solution.py:310
  29.0 8.7 %collective-permute-start.10 = (bf16[576,128]{1,0:T(8,128)(2,1)S(1)}, bf16[576,128]{1,0:T(8,128)(2,1)S(1)}, u32[]{:S(2)}, u32[]{:S(2)}) collective-permute-start(bf16[576,128]{1,0:T(8,128)(2,1)S(1)} %shard_map.273.o0), channel_id=1, source_target_pairs={{0,24},{8,16},{16,8},{24,0},{1,25},{9,17},{17,9},{25,1},{2,26},{10... | collective-permute-start | bytes 442376 | tf_op jit(solution)/shard_map/ppermute | solution.py:310
  31.5 13.0 %collective-permute-start.9 = (bf16[576,128]{1,0:T(8,128)(2,1)S(1)}, bf16[576,128]{1,0:T(8,128)(2,1)S(1)}, u32[]{:S(2)}, u32[]{:S(2)}) collective-permute-start(bf16[576,128]{1,0:T(8,128)(2,1)S(1)} %shard_map.273.o0), channel_id=1, source_target_pairs={{0,16},{8,24},{16,0},{24,8},{1,17},{9,25},{17,1},{25,9},{2,18},{10... | collective-permute-start | bytes 442376 | tf_op jit(solution)/shard_map/ppermute | solution.py:310
  31.5 13.0 %collective-permute-start.8 = (bf16[576,128]{1,0:T(8,128)(2,1)S(1)}, bf16[576,128]{1,0:T(8,128)(2,1)S(1)}, u32[]{:S(2)}, u32[]{:S(2)}) collective-permute-start(bf16[576,128]{1,0:T(8,128)(2,1)S(1)} %shard_map.273.o0), channel_id=1, source_target_pairs={{0,8},{8,0},{16,24},{24,16},{1,9},{9,1},{17,25},{25,17},{2,10},{10... | collective-permute-start | bytes 442376 | tf_op jit(solution)/shard_map/ppermute | solution.py:310
  36.4 8.1 %collective-permute-start.18 = (f32[8,128]{1,0:T(8,128)S(1)}, f32[8,128]{1,0:T(8,128)S(1)}, u32[]{:S(2)}, u32[]{:S(2)}) collective-permute-start(f32[8,128]{1,0:T(8,128)S(1)} %get-tuple-element.131.own_ref), channel_id=1, source_target_pairs={{0,1},{1,0},{2,3},{3,2},{4,5},{5,4},{6,7},{7,6},{8,9},{9,8},{10,11... | collective-permute-start | bytes 12296 | tf_op jit(solution)/shard_map/ppermute | solution.py:310
  44.9 8.3 %collective-permute-start.19 = (bf16[1056,128]{1,0:T(8,128)(2,1)S(1)}, bf16[1056,128]{1,0:T(8,128)(2,1)S(1)}, u32[]{:S(2)}, u32[]{:S(2)}) collective-permute-start(bf16[1056,128]{1,0:T(8,128)(2,1)S(1)} %get-tuple-element.134), channel_id=1, source_target_pairs={{0,4},{4,0},{1,5},{5,1},{2,6},{6,2},{3,7},{7,3},{8,12},{12,8},{9,1... | collective-permute-start | bytes 811016 | tf_op jit(solution)/shard_map/ppermute | solution.py:310
  46.4 9.0 %collective-permute-start.22 = (bf16[1056,128]{1,0:T(8,128)(2,1)S(1)}, bf16[1056,128]{1,0:T(8,128)(2,1)S(1)}, u32[]{:S(2)}, u32[]{:S(2)}) collective-permute-start(bf16[1056,128]{1,0:T(8,128)(2,1)S(1)} %get-tuple-element.136), channel_id=1, source_target_pairs={{0,2},{2,0},{1,3},{3,1},{4,6},{6,4},{5,7},{7,5},{8,10},{10,8},{9,1... | collective-permute-start | bytes 811016 | tf_op jit(solution)/shard_map/ppermute | solution.py:310
  48.2 8.9 %collective-permute-start.27 = (bf16[576,128]{1,0:T(8,128)(2,1)S(1)}, bf16[576,128]{1,0:T(8,128)(2,1)S(1)}, u32[]{:S(2)}, u32[]{:S(2)}) collective-permute-start(bf16[576,128]{1,0:T(8,128)(2,1)S(1)} %collective-permute-done.9.o2), channel_id=1, source_target_pairs={{0,1},{1,0},{2,3},{3,2},{4,5},{5,4},{6,7},{7,6},{8,9},{9,8},{10,11... | collective-permute-start | bytes 442376 | tf_op jit(solution)/shard_map/ppermute | solution.py:310
  49.1 10.3 %collective-permute-start.23 = (bf16[1072,128]{1,0:T(8,128)(2,1)S(1)}, bf16[1072,128]{1,0:T(8,128)(2,1)S(1)}, u32[]{:S(2)}, u32[]{:S(2)}) collective-permute-start(bf16[1072,128]{1,0:T(8,128)(2,1)S(1)} %get-tuple-element.135.b0.rest_4_), channel_id=1, source_target_pairs={{0,4},{4,0},{1,5},{5,1},{2,6},{6,2},{3,7},{7,3},{8,12},{12,8},{9,1... | collective-permute-start | bytes 823304 | tf_op jit(solution)/shard_map/ppermute | solution.py:310
  49.7 11.2 %collective-permute-start.20 = (bf16[1072,128]{1,0:T(8,128)(2,1)S(1)}, bf16[1072,128]{1,0:T(8,128)(2,1)S(1)}, u32[]{:S(2)}, u32[]{:S(2)}) collective-permute-start(bf16[1072,128]{1,0:T(8,128)(2,1)S(1)} %get-tuple-element.133.a0.rest_0_), channel_id=1, source_target_pairs={{0,2},{2,0},{1,3},{3,1},{4,6},{6,4},{5,7},{7,5},{8,10},{10,8},{9,1... | collective-permute-start | bytes 823304 | tf_op jit(solution)/shard_map/ppermute | solution.py:310
  53.2 12.1 %collective-permute-start.21 = (bf16[1056,128]{1,0:T(8,128)(2,1)S(1)}, bf16[1056,128]{1,0:T(8,128)(2,1)S(1)}, u32[]{:S(2)}, u32[]{:S(2)}) collective-permute-start(bf16[1056,128]{1,0:T(8,128)(2,1)S(1)} %collective-permute-done.19.a1.rest_1_), channel_id=1, source_target_pairs={{0,2},{2,0},{1,3},{3,1},{4,6},{6,4},{5,7},{7,5},{8,10},{10,8},{9,1... | collective-permute-start | bytes 811016 | tf_op jit(solution)/shard_map/ppermute | solution.py:310
  55.4 10.0 %collective-permute-start.24 = (bf16[1056,128]{1,0:T(8,128)(2,1)S(1)}, bf16[1056,128]{1,0:T(8,128)(2,1)S(1)}, u32[]{:S(2)}, u32[]{:S(2)}) collective-permute-start(bf16[1056,128]{1,0:T(8,128)(2,1)S(1)} %collective-permute-done.22.b1.rest_5_), channel_id=1, source_target_pairs={{0,4},{4,0},{1,5},{5,1},{2,6},{6,2},{3,7},{7,3},{8,12},{12,8},{9,1... | collective-permute-start | bytes 811016 | tf_op jit(solution)/shard_map/ppermute | solution.py:310
  73.9 14.1 %collective-permute-start.34 = (bf16[2064,128]{1,0:T(8,128)(2,1)S(1)}, bf16[2064,128]{1,0:T(8,128)(2,1)S(1)}, u32[]{:S(2)}, u32[]{:S(2)}) collective-permute-start(bf16[2064,128]{1,0:T(8,128)(2,1)S(1)} %get-tuple-element.157), channel_id=1, source_target_pairs={{0,4},{4,0},{1,5},{5,1},{2,6},{6,2},{3,7},{7,3},{8,12},{12,8},{9,1... | collective-permute-start | bytes 1585160 | tf_op jit(solution)/shard_map/ppermute | solution.py:310
  74.6 13.7 %collective-permute-start.35 = (bf16[2048,128]{1,0:T(8,128)(2,1)S(1)}, bf16[2048,128]{1,0:T(8,128)(2,1)S(1)}, u32[]{:S(2)}, u32[]{:S(2)}) collective-permute-start(bf16[2048,128]{1,0:T(8,128)(2,1)S(1)} %get-tuple-element.161), channel_id=1, source_target_pairs={{0,2},{2,0},{1,3},{3,1},{4,6},{6,4},{5,7},{7,5},{8,10},{10,8},{9,1... | collective-permute-start | bytes 1572872 | tf_op jit(solution)/shard_map/ppermute | solution.py:310
  88.4 8.4 %collective-permute-start.36 = (bf16[1056,128]{1,0:T(8,128)(2,1)S(1)}, bf16[1056,128]{1,0:T(8,128)(2,1)S(1)}, u32[]{:S(2)}, u32[]{:S(2)}) collective-permute-start(bf16[1056,128]{1,0:T(8,128)(2,1)S(1)} %get-tuple-element.162), channel_id=1, source_target_pairs={{0,2},{2,0},{1,3},{3,1},{4,6},{6,4},{5,7},{7,5},{8,10},{10,8},{9,1... | collective-permute-start | bytes 811016 | tf_op jit(solution)/shard_map/ppermute | solution.py:310
  89.9 6.9 %collective-permute-start.37 = (bf16[1024,128]{1,0:T(8,128)(2,1)S(1)}, bf16[1024,128]{1,0:T(8,128)(2,1)S(1)}, u32[]{:S(2)}, u32[]{:S(2)}) collective-permute-start(bf16[1024,128]{1,0:T(8,128)(2,1)S(1)} %get-tuple-element.164), channel_id=1, source_target_pairs={{0,4},{4,0},{1,5},{5,1},{2,6},{6,2},{3,7},{7,3},{8,12},{12,8},{9,1... | collective-permute-start | bytes 786440 | tf_op jit(solution)/shard_map/ppermute | solution.py:310
  91.2 16.9 %collective-permute-start.40 = (bf16[2,288,128]{2,1,0:T(8,128)(2,1)}, bf16[2,288,128]{2,1,0:T(8,128)(2,1)S(1)}, u32[]{:S(2)}, u32[]{:S(2)}) collective-permute-start(bf16[2,288,128]{2,1,0:T(8,128)(2,1)} %get-tuple-element.171), channel_id=1, source_target_pairs={{0,16},{8,24},{16,0},{24,8},{1,17},{9,25},{17,1},{25,9},{2,18},{10... | collective-permute-start | bytes 442376 | tf_op jit(solution)/shard_map/ppermute | solution.py:310
  91.2 16.9 %collective-permute-start.41 = (bf16[2,288,128]{2,1,0:T(8,128)(2,1)}, bf16[2,288,128]{2,1,0:T(8,128)(2,1)S(1)}, u32[]{:S(2)}, u32[]{:S(2)}) collective-permute-start(bf16[2,288,128]{2,1,0:T(8,128)(2,1)} %get-tuple-element.172), channel_id=1, source_target_pairs={{0,24},{8,16},{16,8},{24,0},{1,25},{9,17},{17,9},{25,1},{2,26},{10... | collective-permute-start | bytes 442376 | tf_op jit(solution)/shard_map/ppermute | solution.py:310
  93.8 14.3 %collective-permute-start.39 = (bf16[2,288,128]{2,1,0:T(8,128)(2,1)S(1)}, bf16[2,288,128]{2,1,0:T(8,128)(2,1)S(1)}, u32[]{:S(2)}, u32[]{:S(2)}) collective-permute-start(bf16[2,288,128]{2,1,0:T(8,128)(2,1)S(1)} %get-tuple-element.154), channel_id=1, source_target_pairs={{0,8},{8,0},{16,24},{24,16},{1,9},{9,1},{17,25},{25,17},{2,10},{10... | collective-permute-start | bytes 442376 | tf_op jit(solution)/shard_map/ppermute | solution.py:310
  104.6 18.4 %all-to-all-start = ((bf16[4,512,256]{2,1,0:T(8,128)(2,1)}), bf16[4,512,256]{2,1,0:T(8,128)(2,1)S(1)}, u32[]{:S(2)}, u32[]{:S(2)}) async-start(bf16[4,512,256]{2,1,0:T(8,128)(2,1)} %shard_map.293), calls=%async_computation | async-start | bytes 2097152 | tf_op jit(solution)/shard_map/all_to_all | solution.py:1380
  111.3 9.1 %collective-permute-start.44 = (bf16[320,128]{1,0:T(8,128)(2,1)S(1)}, bf16[320,128]{1,0:T(8,128)(2,1)S(1)}, u32[]{:S(2)}, u32[]{:S(2)}) collective-permute-start(bf16[320,128]{1,0:T(8,128)(2,1)S(1)} %get-tuple-element.178), channel_id=1, source_target_pairs={{0,16},{8,24},{16,0},{24,8},{1,17},{9,25},{17,1},{25,9},{2,18},{10... | collective-permute-start | bytes 245768 | tf_op jit(solution)/shard_map/ppermute | solution.py:310
  111.3 9.0 %collective-permute-start.45 = (bf16[320,128]{1,0:T(8,128)(2,1)S(1)}, bf16[320,128]{1,0:T(8,128)(2,1)S(1)}, u32[]{:S(2)}, u32[]{:S(2)}) collective-permute-start(bf16[320,128]{1,0:T(8,128)(2,1)S(1)} %get-tuple-element.179), channel_id=1, source_target_pairs={{0,24},{8,16},{16,8},{24,0},{1,25},{9,17},{17,9},{25,1},{2,26},{10... | collective-permute-start | bytes 245768 | tf_op jit(solution)/shard_map/ppermute | solution.py:310
  114.0 7.6 %collective-permute-start.43 = (bf16[320,128]{1,0:T(8,128)(2,1)S(1)}, bf16[320,128]{1,0:T(8,128)(2,1)S(1)}, u32[]{:S(2)}, u32[]{:S(2)}) collective-permute-start(bf16[320,128]{1,0:T(8,128)(2,1)S(1)} %get-tuple-element.177), channel_id=1, source_target_pairs={{0,8},{8,0},{16,24},{24,16},{1,9},{9,1},{17,25},{25,17},{2,10},{10... | collective-permute-start | bytes 245768 | tf_op jit(solution)/shard_map/ppermute | solution.py:310
  123.0 12.4 %all-to-all-start.1 = ((f32[32,8,128]{2,1,0:T(8,128)}), f32[32,8,128]{2,1,0:T(8,128)S(1)}, u32[]{:S(2)}, u32[]{:S(2)}) async-start(f32[32,8,128]{2,1,0:T(8,128)} %bitcast.3), calls=%async_computation.1 | async-start | bytes 262144 | tf_op jit(solution)/shard_map/all_to_all | solution.py:1403
  127.2 7.7 %collective-permute-start.46 = (f32[152,128]{1,0:T(8,128)S(1)}, f32[152,128]{1,0:T(8,128)S(1)}, u32[]{:S(2)}, u32[]{:S(2)}) collective-permute-start(f32[152,128]{1,0:T(8,128)S(1)} %get-tuple-element.185), channel_id=1, source_target_pairs={{0,2},{2,0},{1,3},{3,1},{4,6},{6,4},{5,7},{7,5},{8,10},{10,8},{9,1... | collective-permute-start | bytes 233480 | tf_op jit(solution)/shard_map/ppermute | solution.py:310
  129.4 10.1 %collective-permute-start.48 = (bf16[2,64,256]{2,1,0:T(8,128)(2,1)S(1)}, bf16[2,64,256]{2,1,0:T(8,128)(2,1)S(1)}, u32[]{:S(2)}, u32[]{:S(2)}) collective-permute-start(bf16[2,64,256]{2,1,0:T(8,128)(2,1)S(1)} %get-tuple-element.192), channel_id=1, source_target_pairs={{0,8},{8,0},{16,24},{24,16},{1,9},{9,1},{17,25},{25,17},{2,10},{10... | collective-permute-start | bytes 196616 | tf_op jit(solution)/shard_map/ppermute | solution.py:310
  131.3 8.3 %collective-permute-start.49 = (bf16[2,64,256]{2,1,0:T(8,128)(2,1)S(1)}, bf16[2,64,256]{2,1,0:T(8,128)(2,1)S(1)}, u32[]{:S(2)}, u32[]{:S(2)}) collective-permute-start(bf16[2,64,256]{2,1,0:T(8,128)(2,1)S(1)} %get-tuple-element.193), channel_id=1, source_target_pairs={{0,16},{8,24},{16,0},{24,8},{1,17},{9,25},{17,1},{25,9},{2,18},{10... | collective-permute-start | bytes 196616 | tf_op jit(solution)/shard_map/ppermute | solution.py:310
  (35 other events, 110.2 us)

commit v6 on v0

--- a/solution.py
+++ b/solution.py
@@ -1,7 +1,9 @@
 import jax
 import jax.numpy as jnp
 from jax import lax
-from jax.sharding import PartitionSpec as P
+from jax.experimental import pallas as pl
+from jax.experimental.pallas import tpu as pltpu
+from jax.sharding import Mesh, PartitionSpec as P
 
 C1 = 256
 C2 = 512
@@ -105,7 +107,7 @@
     )
 
 
-def body(
+def general_body(
     clip_input,
     frame_counts,
     clip_order,
@@ -254,40 +256,774 @@
     return (pooled, input_grad, grad_norm) + first_update + second_update + norm_update
 
 
+AXES = ('z', 'x', 'y', 'core')
+BF = jnp.bfloat16
+F32 = jnp.float32
+ROWS = 512
+CLIPS_CORE = 4
+PIXELS = ROWS * CLIPS_CORE
+HALF = PIXELS // 2
+LANES = 128
+TAPS = 9
+CHUNK = TAPS * 32
+ANY = pl.BlockSpec(memory_space=pl.ANY)
+VM = pl.BlockSpec(memory_space=pltpu.VMEM)
+HB = pl.BlockSpec(memory_space=pltpu.HBM)
+VMEM_LIMIT = 16 * 1024 * 1024
+
+
+def shape_of(shape, dtype=BF):
+    return jax.ShapeDtypeStruct(shape, dtype)
+
+
+def call(kernel, out, in_specs, out_specs, scratch=(), limit=VMEM_LIMIT):
+    return pl.pallas_call(kernel, out_shape=out, in_specs=in_specs, out_specs=out_specs, scratch_shapes=list(scratch), compiler_params=pltpu.CompilerParams(vmem_limit_bytes=limit), cost_estimate=pl.CostEstimate(flops=0, bytes_accessed=0, transcendentals=0))
+
+
+def join_kernel(*refs):
+    base = 0
+    for ref in refs[:-1]:
+        refs[-1][base:base + ref.shape[0]] = ref[...]
+        base += ref.shape[0]
+
+
+def join(*parts):
+    rows = sum((part.shape[0] for part in parts))
+    out = shape_of((rows,) + parts[0].shape[1:], parts[0].dtype)
+    return call(join_kernel, out, [VM] * len(parts), VM)(*parts)
+
+
+def swap(value, axis, step=1):
+    size = lax.axis_size(axis)
+    return lax.ppermute(value, axis, [(i, i ^ step) for i in range(size)])
+
+
+def start_copies(copies, sems, base=0):
+    started = []
+    for at, (source, target) in enumerate(copies):
+        copy = pltpu.make_async_copy(source, target, sems.at[base + at])
+        copy.start()
+        started.append(copy)
+    return started
+
+
+def wait_all(copies):
+    for copy in copies:
+        copy.wait()
+
+
+def place(*axes):
+    found = tuple((lax.axis_index(axis) for axis in axes))
+    return found if len(found) > 1 else found[0]
+
+
+def after(value, *others):
+    return lax.optimization_barrier((value,) + others)[0]
+
+
+def steps_of():
+    return [2, 3, 1]
+
+
+def order_entry(order, row, column):
+    row_of = lax.broadcasted_iota(jnp.int32, order.shape, 0)
+    column_of = lax.broadcasted_iota(jnp.int32, order.shape, 1)
+    chosen = jnp.where((row_of == row) & (column_of == column), order, 0).astype(F32)
+    return jnp.sum(jnp.sum(chosen, axis=1, keepdims=True), axis=0, keepdims=True)
+
+
+def write_facts(order_ref, counts_ref, facts_ref):
+    z, y, core = place('z', 'y', 'core')
+    order, counts = (order_ref[...], counts_ref[...])
+    column_of = lax.broadcasted_iota(jnp.int32, counts.shape, 1)
+    row_of = lax.broadcasted_iota(jnp.int32, (16, LANES), 0)
+    facts = jnp.zeros((16, LANES), F32)
+    total = jnp.zeros((1, 1), F32)
+    for row in range(4):
+        for j in range(CL_MB):
+            clip = order_entry(order, row, z * CL_MB + j).astype(jnp.int32) + row * 8
+            count = jnp.sum(jnp.where(column_of == clip, counts, 0).astype(F32), axis=1, keepdims=True)
+            total = total + count
+            target = jnp.where(row % 2 == core, row // 2 * CL_MB + j, -1)
+            facts = jnp.where(row_of == target, count, facts)
+    facts = jnp.where(row_of == 4, MEL * total, facts)
+    for slot in range(MB * CL_MB):
+        facts = jnp.where(row_of == 8 + slot, order_entry(order, y * 2 + core, slot), facts)
+    facts_ref[...] = facts.astype(jnp.int32)
+
+
+def count_row(facts_ref, clip):
+    return facts_ref[clip:clip + 1, :]
+
+
+def pixel_row(facts_ref):
+    return facts_ref[4:5, :].astype(F32)
+
+
+def time_shift(rows, step):
+    zero = jnp.zeros((MEL, rows.shape[1]), rows.dtype)
+    if step == 1:
+        return jnp.concatenate([rows[MEL:], zero], axis=0)
+    if step == -1:
+        return jnp.concatenate([zero, rows[:-MEL]], axis=0)
+    return rows
+
+
+def mel_shift(rows, step):
+    if step == 0:
+        return rows
+    cube = rows.reshape(rows.shape[0] // MEL, MEL, rows.shape[1])
+    turned = pltpu.roll(cube, -step % MEL, 1)
+    bin_at = lax.broadcasted_iota(jnp.int32, cube.shape, 1) + step
+    keep = (bin_at >= 0) & (bin_at < MEL)
+    return jnp.where(keep, turned, 0.0).reshape(rows.shape)
+
+
+def valid_rows(facts_ref, clip):
+    frame = lax.broadcasted_iota(jnp.int32, (ROWS, LANES), 0) // MEL
+    return (frame < count_row(facts_ref, clip)).astype(F32)
+
+
+def dot_nt(left, right):
+    return lax.dot_general(left, right, (((1,), (1,)), ((), ())), preferred_element_type=F32)
+
+
+def dot_nn(left, right):
+    return lax.dot_general(left, right, (((1,), (0,)), ((), ())), preferred_element_type=F32)
+
+
+def dot_tn(left, right):
+    return lax.dot_general(left, right, (((0,), (0,)), ((), ())), preferred_element_type=F32)
+
+
+def lanes_of(tap):
+    return slice(tap * LANES, (tap + 1) * LANES)
+
+
+def gather_taps(product):
+    total = None
+    for mel in range(3):
+        column = None
+        for time in range(3):
+            term = time_shift(product[:, lanes_of(3 * time + mel)], time - 1)
+            column = term if column is None else column + term
+        column = mel_shift(column, mel - 1)
+        total = column if total is None else total + column
+    return total
+
+
+def scatter_taps(grad, target, base):
+    for mel in range(3):
+        moved = mel_shift(grad, 1 - mel)
+        for time in range(3):
+            target[base:base + ROWS, lanes_of(3 * time + mel)] = time_shift(moved, 1 - time).astype(BF)
+
+
+def channel_sums(first, second):
+    return (jnp.sum(first, axis=0, keepdims=True), jnp.sum(second, axis=0, keepdims=True))
+
+
+def pair_sums(own_ref, other_ref):
+    return (own_ref[0:1, :] + other_ref[0:1, :], own_ref[1:2, :] + other_ref[1:2, :])
+
+
+def norm_rows(own_ref, other_ref, pixels):
+    total, squares = pair_sums(own_ref, other_ref)
+    mean = total / pixels
+    return (mean, lax.rsqrt(squares / pixels - mean * mean + NORM_EPS))
+
+
+def put_pair(ref, first, second):
+    ref[...] = jnp.zeros(ref.shape, F32)
+    ref[0:1, :] = first
+    ref[1:2, :] = second
+
+
+def exchange_matrix(rows, columns, source_of):
+    row = lax.broadcasted_iota(jnp.int32, (rows, columns), 0)
+    column = lax.broadcasted_iota(jnp.int32, (rows, columns), 1)
+    return (row == source_of(column)).astype(BF)
+
+
+def block_exchange(column):
+    return column // 32 % 4 * 128 + column // 128 * 32 + column % 32
+
+
+def lane_index(rows):
+    return lax.broadcasted_iota(jnp.int32, (rows, LANES), 1)
+
+
+def take_kernel(order_ref, clip_ref, p0, p1, p2, p3):
+    z, y, core = place('z', 'y', 'core')
+    order = order_ref[...]
+    for step, piece in enumerate((p0, p1, p2, p3)):
+        plane = jnp.bitwise_xor(z, step)
+        for j in range(CL_MB):
+            clip = order_entry(order, y * 2 + core, plane * CL_MB + j)[0, 0].astype(jnp.int32)
+            piece[j * 64:(j + 1) * 64, :] = clip_ref[clip]
+        piece[CL_MB * 64:, :] = jnp.zeros((piece.shape[0] - CL_MB * 64, C1), BF)
+
+
+def prepare_kernel(order_ref, counts_ref, one_in, two_in, norm_in, cot_in, one_keep, two_keep, send_ref, gain_ref, cot_own, facts_ref, one_ref, two_ref, norm_ref, cot_ref, sems):
+    z, x, y, core = place(*AXES)
+    group = y * 2 + core
+    loads = start_copies([(one_in, one_ref), (two_in, two_ref), (norm_in, norm_ref), (cot_in, cot_ref)], sems)
+    write_facts(order_ref, counts_ref, facts_ref)
+    wait_all(loads)
+    for tap in range(TAPS):
+        turned = jnp.swapaxes(one_ref[tap], 0, 1)
+        rows = [turned[at * 16:(at + 1) * 16] for at in range(4)]
+        low = jnp.concatenate([rows[0], rows[1]], axis=1).astype(BF)
+        high = jnp.concatenate([rows[2], rows[3]], axis=1).astype(BF)
+        span = slice(tap * 16, (tap + 1) * 16)
+        one_keep[span, :] = jnp.where(y == 0, low, high)
+        send_ref[span, :] = jnp.where(y == 0, high, low)
+        low, high = (two_ref[tap, 0:32, :].astype(BF), two_ref[tap, 32:64, :].astype(BF))
+        span = slice(tap * 32, (tap + 1) * 32)
+        two_keep[span, :] = jnp.where(y == 0, low, high)
+        span = slice(144 + tap * 32, 144 + (tap + 1) * 32)
+        send_ref[span, :] = jnp.where(y == 0, high, low)
+    wide = jnp.concatenate([norm_ref[...], norm_ref[...]], axis=1)
+    wide = jnp.concatenate([wide, jnp.zeros((4, LANES), F32)], axis=0)
+    turned = pltpu.roll(wide, (z * 32 - y * 32) % LANES, 1)
+    gain_rows = jnp.where(lane_index(8) // 32 == z, turned, 0.0)
+    gain_ref[...] = jnp.concatenate([gain_rows, jnp.zeros((8, LANES), F32)], axis=0).astype(BF)
+
+    def cot_rows(y_of):
+        rows = []
+        for j in range(CL_MB):
+            clip = order_entry(order_ref[...], group, z * CL_MB + j)[0, 0].astype(jnp.int32)
+            row = cot_ref[pl.ds(clip, 1), :]
+            picked = jnp.zeros((1, LANES), F32)
+            for block in range(MB):
+                moved = pltpu.roll(jnp.broadcast_to(row[:, lanes_of(block)], (8, LANES)), (block * 32 - x * 64 - y_of * 32) % LANES, 1)[0:1]
+                picked = jnp.where(lane_index(1) // 32 == block, moved, picked)
+            rows.append(picked)
+        return rows
+    own, send = (cot_rows(y), cot_rows(1 - y))
+    cot_own[...] = jnp.concatenate(own + [jnp.zeros((6, LANES), F32)], axis=0)
+    high = [row.astype(BF).astype(F32) for row in send]
+    rest = [row - top for row, top in zip(send, high)]
+    middle = [row.astype(BF).astype(F32) for row in rest]
+    low = [row - top for row, top in zip(rest, middle)]
+    packed = jnp.concatenate(high + middle + low + [jnp.zeros((10, LANES), F32)], axis=0)
+    send_ref[144 + CHUNK:160 + CHUNK, :] = packed.astype(BF)
+
+
+def first_weight_kernel(o0, o1, o2, o3, others, facts_in, weight_ref, gain_ref, facts_ref):
+    facts_ref[...] = facts_in[...]
+    z, y, core = place('z', 'y', 'core')
+    gains = jnp.zeros((8, LANES), F32)
+    for half in range(2):
+
+        def source_of(column, half=half):
+            from_core = jnp.bitwise_xor(column // 64 % 2, core)
+            from_y = jnp.bitwise_xor(column // 128, y)
+            return from_core * 256 + from_y * 128 + half * 64 + column % 64
+        spread = exchange_matrix(512, C1, source_of)
+        for step, own in enumerate((o0, o1, o2, o3)):
+            z_of = jnp.bitwise_xor(z, step)
+            other = others[step * 304:step * 304 + 288]
+            four = jnp.concatenate([own[0:144], own[144:288], other[0:144], other[144:288]], axis=1)
+            both = dot_nn(four, spread).astype(BF)
+            for tap in range(TAPS):
+                weight_ref[tap, z_of, half * 16:half * 16 + 16] = both[tap * 16:(tap + 1) * 16]
+            if half == 0:
+                gains = gains + own[CHUNK:CHUNK + 16].astype(F32)[0:8]
+    gain_ref[...] = gains
+
+
+def first_conv_kernel(facts_ref, a0, a1, a23, b0, b1, b23, weight_ref, pre_ref, x_ref, stat_ref):
+    z, x, y = place('z', 'x', 'y')
+    frame = lax.broadcasted_iota(jnp.int32, (64, LANES), 0) // MEL
+    for j, pieces in ((0, ((a0, 0, x, y), (a1, 0, 1 - x, y), (a23, 0, x, 1 - y), (a23, MB, 1 - x, 1 - y))), (1, ((b0, 0, x, y), (b1, 0, x, 1 - y), (b23, 0, 1 - x, y), (b23, MB, 1 - x, 1 - y)))):
+        for source, base, x_of, y_of in pieces:
+            count = facts_ref[pl.ds(y_of * CL_MB + j, 1), :]
+            for step in range(MB):
+                frames = (jnp.bitwise_xor(z, step) * 2 + x_of) * 8
+                mask = (frame + frames < count).astype(F32).astype(BF)
+                row = pl.multiple_of((y_of * CL_MB + j) * ROWS + frames * MEL, 64)
+                x_ref[pl.ds(row, 64), :] = source[base + step] * jnp.concatenate([mask, mask], axis=1)
+    weight = weight_ref[...].reshape(TAPS * LANES, C1)
+    first = jnp.zeros((1, LANES), F32)
+    second = jnp.zeros((1, LANES), F32)
+    for clip in range(CLIPS_CORE):
+        span = slice(clip * ROWS, (clip + 1) * ROWS)
+        pre = gather_taps(dot_nt(x_ref[span, :], weight))
+        pre_ref[span, :] = pre
+        kept = pre * valid_rows(facts_ref, clip)
+        plus = channel_sums(kept, kept * pre)
+        first, second = (first + plus[0], second + plus[1])
+    put_pair(stat_ref, first, second)
+
+
+def stack_kernel(p0, p1, p2, p3, a_ref, b_ref):
+    for step, piece in enumerate((p0, p1, p2, p3)):
+        a_ref[step] = piece[0:64]
+        b_ref[step] = piece[64:128]
+
+
+def hidden_kernel(facts_ref, pre_ref, own_ref, other_ref, gain_ref, *outs):
+    mean, scale = norm_rows(own_ref, other_ref, pixel_row(facts_ref))
+    for clip in range(CLIPS_CORE):
+        pre = pre_ref[clip * ROWS:(clip + 1) * ROWS, :]
+        shaped = gain_ref[0:1, :] * ((pre - mean) * scale) + gain_ref[1:2, :]
+        value = shaped * jax.nn.sigmoid(shaped) * valid_rows(facts_ref, clip)
+        for target in outs[clip // 2 * 2:clip // 2 * 2 + 2]:
+            target[clip % 2 * ROWS:(clip % 2 + 1) * ROWS, :] = value.astype(BF)
+    for target in outs:
+        target[HALF:, :] = jnp.zeros((target.shape[0] - HALF, LANES), BF)
+
+
+def second_weight_kernel(o0, o1, o2, o3, s0, s1, s2, s3, weight_ref):
+    z, y, core = place('z', 'y', 'core')
+    spread = exchange_matrix(C2, C2, block_exchange)
+    spans = [slice(0, CHUNK), slice(CHUNK, 2 * CHUNK)]
+    for step, (own_ref, other_ref) in enumerate(((o0, s0), (o1, s1), (o2, s2), (o3, s3))):
+        z_of = jnp.bitwise_xor(z, step)
+        parts = []
+        for y_of in range(2):
+            own = jnp.where(y == y_of, own_ref[spans[0]], own_ref[spans[1]])
+            other = jnp.where(y == y_of, other_ref[spans[0]], other_ref[spans[1]])
+            parts += [jnp.where(core == 0, own, other), jnp.where(core == 0, other, own)]
+        both = dot_nn(jnp.concatenate(parts, axis=1), spread).astype(BF)
+        for tap in range(TAPS):
+            weight_ref[tap, z_of] = both[tap * 32:(tap + 1) * 32]
+
+
+def hidden_copies(parts, target):
+    x, y = place('x', 'y')
+    chips = ((x, y), (1 - x, y), (x, 1 - y), (1 - x, 1 - y), (x, y), (x, 1 - y), (1 - x, y), (1 - x, 1 - y))
+    copies = []
+    for at, (source, (x_of, y_of)) in enumerate(zip(parts, chips)):
+        lane = pl.multiple_of((x_of * 2 + y_of) * LANES, LANES)
+        copies.append((source.at[pl.ds(0, HALF)], target.at[pl.ds(at // 4 * HALF, HALF), pl.ds(lane, LANES)]))
+    return copies
+
+
+def near_conv_kernel(a0, a1, a2, b0, b1, b2, weight_ref, pre_ref):
+    x, y = place('x', 'y')
+
+    def lane(x_of, y_of):
+        return pl.ds(pl.multiple_of((x_of * 2 + y_of) * LANES, LANES), LANES)
+    weight = jnp.concatenate([weight_ref[:, :, :, lane(*chip)].reshape(TAPS * LANES, LANES) for chip in ((x, y), (1 - x, y), (x, 1 - y))], axis=1)
+    for clip in range(CLIPS_CORE):
+        parts = (a0, a1, a2) if clip < 2 else (b0, b2, b1)
+        rows = slice(clip % 2 * ROWS, (clip % 2 + 1) * ROWS)
+        three = jnp.concatenate([part[rows, :] for part in parts], axis=1)
+        pre_ref[clip * ROWS:(clip + 1) * ROWS, :] = gather_taps(dot_nt(three, weight))
+
+
+def far_conv_kernel(facts_ref, a3, b3, weight_ref, near_ref, pre_ref, stat_ref):
+    x, y = place('x', 'y')
+    lane = pl.multiple_of(((1 - x) * 2 + 1 - y) * LANES, LANES)
+    weight = weight_ref[:, :, :, pl.ds(lane, LANES)].reshape(TAPS * LANES, LANES)
+    first = jnp.zeros((1, LANES), F32)
+    second = jnp.zeros((1, LANES), F32)
+    for clip in range(CLIPS_CORE):
+        span = slice(clip * ROWS, (clip + 1) * ROWS)
+        part = a3 if clip < 2 else b3
+        rows = slice(clip % 2 * ROWS, (clip % 2 + 1) * ROWS)
+        pre = near_ref[span, :] + gather_taps(dot_nt(part[rows, :], weight))
+        pre_ref[span, :] = pre
+        kept = pre * valid_rows(facts_ref, clip)
+        plus = channel_sums(kept, kept * pre)
+        first, second = (first + plus[0], second + plus[1])
+    put_pair(stat_ref, first, second)
+
+
+def pool_kernel(facts_ref, pre_ref, own_ref, other_ref, gain_ref, cot_own, cot_got, slope_ref, sum_ref, pooled_ref):
+    y = place('y')
+    mean, scale = norm_rows(own_ref, other_ref, pixel_row(facts_ref))
+    first = jnp.zeros((1, LANES), F32)
+    second = jnp.zeros((1, LANES), F32)
+    slots = ROWS // (2 * MEL)
+    got = cot_got[144 + CHUNK:160 + CHUNK, :].astype(F32)
+    pooled = []
+    for clip in range(CLIPS_CORE):
+        span = slice(clip * ROWS, (clip + 1) * ROWS)
+        count = count_row(facts_ref, clip)
+        j = clip % CL_MB
+        told = got[j:j + 1] + got[2 + j:3 + j] + got[4 + j:5 + j]
+        cot = jnp.where(y == clip // CL_MB, cot_own[j:j + 1, :], told)
+        mask = valid_rows(facts_ref, clip)
+        normed = (pre_ref[span, :] - mean) * scale
+        shaped = gain_ref[2:3, :] * normed + gain_ref[3:4, :]
+        gate = jax.nn.sigmoid(shaped)
+        active = (shaped * gate * mask).reshape(slots, 2 * MEL, LANES)
+        summary = jnp.sum(active, axis=1) / (2 * MEL)
+        slot = lax.broadcasted_iota(jnp.int32, (slots, LANES), 0)
+        keep = (2 * slot + 1 < count).astype(F32)
+        raised = jnp.exp(summary)
+        exp_total = jnp.sum(raised * keep, axis=0, keepdims=True)
+        halves = (count // 2).astype(F32)
+        pooled.append(jnp.sum(summary * keep, axis=0, keepdims=True) / halves + jnp.log(exp_total / halves))
+        summary_grad = keep * (cot / halves + cot * raised / exp_total) / (2 * MEL)
+        spread = jnp.broadcast_to(summary_grad[:, None, :], (slots, 2 * MEL, LANES))
+        slope = spread.reshape(ROWS, LANES) * mask * (gate * (1.0 + shaped * (1.0 - gate)))
+        slope_ref[span, :] = slope
+        plus = channel_sums(slope, slope * normed)
+        first, second = (first + plus[0], second + plus[1])
+    put_pair(sum_ref, first, second)
+    high = [row.astype(BF).astype(F32) for row in pooled]
+    low = [row - top for row, top in zip(pooled, high)]
+    rows = jnp.concatenate(high + low + [jnp.zeros((8, LANES), F32)], axis=0)
+    pooled_ref[...] = rows.astype(BF)
+
+
+def pre_grad(slope, pre, mask, mean, scale, gain, sums, pixels):
+    normed = (pre - mean) * scale
+    return mask * (scale * gain) * (slope - sums[0] / pixels - normed * (sums[1] / pixels))
+
+
+def both_grad_kernel(facts_ref, slope_ref, pre_ref, own_ref, other_ref, sum_own, sum_other, gain_ref, weight_ref, pooled_ref, columns, a_own, a_mid, a_send, b_own, b_mid, b_send, weight):
+    x, y = place('x', 'y')
+    pixels = pixel_row(facts_ref)
+    mean, scale = norm_rows(own_ref, other_ref, pixels)
+    sums = pair_sums(sum_own, sum_other)
+    a_send[2 * HALF:2 * HALF + 16, :] = pooled_ref[...]
+    for at, (x_of, y_of) in enumerate(((x, y), (x, 1 - y), (1 - x, y), (1 - x, 1 - y))):
+        lane = pl.multiple_of((x_of * 2 + y_of) * LANES, LANES)
+        weight[:, lanes_of(at)] = weight_ref[:, :, :, pl.ds(lane, LANES)].reshape(TAPS * LANES, LANES)
+    for clip in range(CLIPS_CORE):
+        span = slice(clip * ROWS, (clip + 1) * ROWS)
+        mask = valid_rows(facts_ref, clip)
+        grad = pre_grad(slope_ref[span, :], pre_ref[span, :], mask, mean, scale, gain_ref[2:3, :], sums, pixels)
+        scatter_taps(grad, columns, clip * ROWS)
+        partial = dot_nn(columns[span, :], weight[...])
+        rows = slice(clip % 2 * ROWS, (clip % 2 + 1) * ROWS)
+        near_rows = slice(HALF + clip % 2 * ROWS, HALF + (clip % 2 + 1) * ROWS)
+        far = partial[:, lanes_of(3)].astype(BF)
+        if clip < 2:
+            a_own[rows, :] = partial[:, lanes_of(0)]
+            a_mid[rows, :] = partial[:, lanes_of(1)]
+            a_send[rows, :] = far
+            a_send[near_rows, :] = partial[:, lanes_of(2)].astype(BF)
+        else:
+            b_own[rows, :] = partial[:, lanes_of(0)]
+            b_mid[rows, :] = partial[:, lanes_of(2)]
+            b_send[rows, :] = far
+            b_send[near_rows, :] = partial[:, lanes_of(1)].astype(BF)
+
+
+def pass_on_kernel(a_mid, a_got, b_mid, b_got, pooled_ref, a_next, b_next):
+    a_next[HALF:HALF + 16, :] = pooled_ref[...]
+    a_next[HALF + 16:HALF + 32, :] = a_got[2 * HALF:2 * HALF + 16]
+    a_next[0:HALF, :] = (a_mid[...] + a_got[0:HALF].astype(F32)).astype(BF)
+    b_next[...] = (b_mid[...] + b_got[0:HALF].astype(F32)).astype(BF)
+
+
+def second_weight_grad_kernel(*rest):
+    parts, columns, keeps, sends = (rest[:8], rest[8], rest[9:12], rest[12:15])
+    hidden, natural, sems = rest[15:]
+    core = place('core')
+    started = start_copies(hidden_copies(parts, hidden), sems)
+    spread = exchange_matrix(C2, C2, block_exchange)
+    wait_all(started)
+    for clip in range(CLIPS_CORE):
+        span = slice(clip * ROWS, (clip + 1) * ROWS)
+        hidden[span, :] = dot_nn(hidden[span, :], spread).astype(BF)
+    for tap in range(TAPS):
+        natural[...] = dot_tn(columns[:, lanes_of(tap)], hidden[...])
+        keep_ref, send_ref = (keeps[tap // 3], sends[tap // 3])
+        target = slice(tap % 3 * 32, (tap % 3 + 1) * 32)
+        for y_of in range(2):
+            keep = natural[:, pl.ds(pl.multiple_of((y_of * 2 + core) * LANES, LANES), LANES)]
+            send = natural[:, pl.ds(pl.multiple_of((y_of * 2 + 1 - core) * LANES, LANES), LANES)]
+            for z_of in range(MB):
+                rows = slice(z_of * 32, (z_of + 1) * 32)
+                keep_ref[z_of, y_of, target] = keep[rows]
+                send_ref[z_of, y_of, target] = send[rows]
+
+
+def second_core_kernel(k0, k1, k2, g0, g1, g2, own_ref, n1, n2, n3):
+    z = place('z')
+    for third, (keep_ref, got_ref) in enumerate(((k0, g0), (k1, g1), (k2, g2))):
+        rows = slice(third * 96, (third + 1) * 96)
+        own_ref[:, rows] = keep_ref[z] + got_ref[z]
+        for step, target in ((1, n1), (2, n2), (3, n3)):
+            at = jnp.bitwise_xor(z, step)
+            target[:, rows] = (keep_ref[at] + got_ref[at]).astype(BF)
+
+
+def second_sum_kernel(own_ref, g1, g2, g3, keep_ref, send_ref, square_ref):
+    y = place('y')
+    total = own_ref[...] + g1[...].astype(F32) + g2[...].astype(F32) + g3[...].astype(F32)
+    keep_ref[...] = jnp.where(y == 0, total[0], total[1])
+    send_ref[...] = jnp.where(y == 0, total[1], total[0]).astype(BF)
+    square_ref[...] = jnp.sum(total * total, axis=(0, 1), keepdims=False)[None, :] * jnp.ones((8, 1), F32)
+
+
+def first_slope_kernel(facts_ref, a_own, a_near, a_last, b_own, b_near, b_last, pre_ref, own_ref, other_ref, gain_ref, slope_ref, sum_ref):
+    mean, scale = norm_rows(own_ref, other_ref, pixel_row(facts_ref))
+    first = jnp.zeros((1, LANES), F32)
+    second = jnp.zeros((1, LANES), F32)
+    for clip in range(CLIPS_CORE):
+        span = slice(clip * ROWS, (clip + 1) * ROWS)
+        rows = slice(clip % 2 * ROWS, (clip % 2 + 1) * ROWS)
+        own, near, last = (a_own, a_near, a_last) if clip < 2 else (b_own, b_near, b_last)
+        base = near.shape[0] // HALF * HALF - HALF
+        near_rows = slice(base + clip % 2 * ROWS, base + (clip % 2 + 1) * ROWS)
+        outer = own[rows, :] + near[near_rows, :].astype(F32) + last[rows, :].astype(F32)
+        normed = (pre_ref[span, :] - mean) * scale
+        shaped = gain_ref[0:1, :] * normed + gain_ref[1:2, :]
+        gate = jax.nn.sigmoid(shaped)
+        slope = outer * valid_rows(facts_ref, clip) * (gate * (1.0 + shaped * (1.0 - gate)))
+        slope_ref[span, :] = slope
+        plus = channel_sums(slope, slope * normed)
+        first, second = (first + plus[0], second + plus[1])
+    put_pair(sum_ref, first, second)
+
+
+def first_weight_grad_kernel(facts_ref, slope_ref, pre_ref, own_ref, other_ref, sum_own, sum_other, gain_ref, x_ref, columns, keep_ref, send_ref, turned):
+    core = place('core')
+    pixels = pixel_row(facts_ref)
+    mean, scale = norm_rows(own_ref, other_ref, pixels)
+    sums = pair_sums(sum_own, sum_other)
+
+    def source_of(column):
+        core_of = jnp.where(column < 128, core, 1 - core)
+        return column // 64 % 2 * 128 + core_of * 64 + column % 64
+    spread = exchange_matrix(C1, C1, source_of)
+    for clip in range(CLIPS_CORE):
+        span = slice(clip * ROWS, (clip + 1) * ROWS)
+        mask = valid_rows(facts_ref, clip)
+        grad = pre_grad(slope_ref[span, :], pre_ref[span, :], mask, mean, scale, gain_ref[0:1, :], sums, pixels)
+        scatter_taps(grad, columns, clip * ROWS)
+        turned[span, :] = dot_nn(x_ref[span, :], spread).astype(BF)
+    for tap in range(TAPS):
+        both = dot_tn(columns[:, lanes_of(tap)], turned[...])
+        for z_of in range(MB):
+            rows = slice(z_of * 32, (z_of + 1) * 32)
+            target = slice(tap * 32, (tap + 1) * 32)
+            keep_ref[z_of, target] = both[rows, 0:LANES]
+            send_ref[z_of, target] = both[rows, LANES:2 * LANES]
+
+
+def input_grad_kernel(columns, weight_ref, part_ref):
+    weight = weight_ref[...].reshape(TAPS * LANES, C1)
+    for clip in range(CLIPS_CORE):
+        partial = dot_nn(columns[clip * ROWS:(clip + 1) * ROWS, :], weight).astype(BF)
+        for z_of in range(MB):
+            for x_of in range(2):
+                target = slice((clip % 2 * MB + z_of) * 64, (clip % 2 * MB + z_of + 1) * 64)
+                rows = slice((z_of * 2 + x_of) * 64, (z_of * 2 + x_of + 1) * 64)
+                part_ref[x_of * 2 + clip // 2, target, :] = partial[rows]
+
+
+def first_core_kernel(keep_ref, got_ref, one_own, one_other, two_own, two_other, pooled_own, pooled_near, pooled_last, own_ref, n0, n1, n2, n3, scratch):
+    z, x, y = place('z', 'x', 'y')
+    own_ref[...] = keep_ref[z] + got_ref[z]
+    one, two = (pair_sums(one_own, one_other), pair_sums(two_own, two_other))
+    sums = jnp.concatenate([one[1], one[0], two[1], two[0]], axis=0)
+    high = sums.astype(BF).astype(F32)
+    norm_tile = jnp.concatenate([high, sums - high, jnp.zeros((8, LANES), F32)], axis=0).astype(BF)
+    last = pooled_last[HALF:HALF + 32, :].astype(F32)
+    near = pooled_near[...].astype(F32)
+    own = pooled_own[...].astype(F32)
+    for rows, x_of, y_of in ((own, x, y), (near, 1 - x, y), (last[0:16], x, 1 - y), (last[16:32], 1 - x, 1 - y)):
+        for part in range(2):
+            for j in range(CL_MB):
+                row = jnp.where(y == 0, rows[part * 4 + j:part * 4 + j + 1], rows[part * 4 + 2 + j:part * 4 + 3 + j])
+                scratch[pl.ds((x_of * 2 + y_of) * 4 + part * 2 + j, 1), :] = row
+    pooled_tile = scratch[...].astype(BF)
+    for step, target in ((0, n0), (1, n1), (2, n2), (3, n3)):
+        at = jnp.bitwise_xor(z, step)
+        target[0:CHUNK, :] = (keep_ref[at] + got_ref[at]).astype(BF)
+        target[CHUNK:CHUNK + 16, :] = norm_tile
+        target[CHUNK + 16:CHUNK + 32, :] = pooled_tile
+
+
+def first_sum_kernel(own_ref, n0, g1, g2, g3, square_two, told_ref, keep_ref, send_ref, norm_ref):
+    z, y, core = place('z', 'y', 'core')
+    total = own_ref[...]
+    norm = n0[CHUNK:CHUNK + 16, :].astype(F32)
+    for got in (g1, g2, g3):
+        total = total + got[0:CHUNK, :].astype(F32)
+        norm = norm + got[CHUNK:CHUNK + 16, :].astype(F32)
+    norm = norm[0:4] + norm[4:8]
+    mine = (lane_index(4) // 32 == z) & (core == 0)
+    squares = jnp.sum(total * total, axis=0, keepdims=True) + jnp.sum(jnp.where(mine, norm * norm, 0.0), axis=0, keepdims=True)
+    first_rows = lax.broadcasted_iota(jnp.int32, told_ref.shape, 0) % 8 == 0
+    told_ref[...] = jnp.where(first_rows, squares + square_two[0:1, :], 0.0)
+    turned = pltpu.roll(total, 64, 1)
+    low = jnp.where(y == 0, total, turned)
+    high = jnp.where(y == 0, turned, total)
+    left = lane_index(144) < 64
+    keep_ref[...] = jnp.where(left, low[0:144], pltpu.roll(low[144:288], 64, 1))
+    send_ref[0:144, :] = jnp.where(left, high[0:144], pltpu.roll(high[144:288], 64, 1))
+    rows = jnp.concatenate([norm, jnp.zeros((4, LANES), F32)], axis=0)
+    send_ref[144:152, :] = rows
+    norm_ref[...] = rows
+
+
+def adam_write(refs, outs, gradient, factor, step_rate, decay_rate, at):
+    weight, moment, square = (ref[at] for ref in refs)
+    clipped = gradient * factor
+    moment_new = BETA_ONE * moment + (1.0 - BETA_ONE) * clipped
+    square_new = BETA_TWO * square + (1.0 - BETA_TWO) * clipped * clipped
+    corrected = moment_new * (1.0 / (1.0 - BETA_ONE ** STEP))
+    scaled = jnp.sqrt(square_new * (1.0 / (1.0 - BETA_TWO ** STEP))) + ADAM_EPS
+    weight_new = weight - step_rate * (corrected / scaled + decay_rate * weight)
+    for out, value in zip(outs, (clipped, moment_new, square_new, weight_new, weight_new.astype(BF))):
+        out[at] = value
+
+
+def adam_kernel(told_ref, keep_ref, got_ref, norm_ref, two_keep, two_got, *refs):
+    z, y = place('z', 'y')
+    one, two, norm, outs = (refs[0:3], refs[3:6], refs[6:9], refs[9:])
+    norm_out, one_out, two_out, small_out = (outs[0], outs[1:6], outs[6:11], outs[11:16])
+    told = jnp.sum(told_ref[...], axis=0, keepdims=True)
+    length = jnp.sqrt(jnp.sum(told, axis=1, keepdims=True))
+    norm_out[...] = length
+    factor = jnp.minimum(1.0, CLIP_NORM / (length + 1e-06))
+    keep, got = (keep_ref[...], got_ref[0:144, :])
+    first, second = (jnp.where(y == 0, keep, got), jnp.where(y == 0, got, keep))
+    spans = [jnp.concatenate([half[:, 0:64], half[:, 64:128]], axis=0) for half in (first, second)]
+    for tap in range(TAPS):
+        rows = slice(tap * 32, (tap + 1) * 32)
+        gradient = jnp.swapaxes(jnp.concatenate([span[rows] for span in spans], axis=0), 0, 1)
+        adam_write(one, one_out, gradient, factor, (9 * C1) ** (-0.5), WEIGHT_DECAY, tap)
+        keep, got = (two_keep[rows, :], two_got[rows, :].astype(F32))
+        gradient = jnp.concatenate([jnp.where(y == 0, keep, got), jnp.where(y == 0, got, keep)], axis=0)
+        adam_write(two, two_out, gradient, factor, (9 * C2) ** (-0.5), WEIGHT_DECAY, tap)
+    keep, got = (norm_ref[...], got_ref[144:152, :])
+    first, second = (jnp.where(y == 0, keep, got), jnp.where(y == 0, got, keep))
+    low = pltpu.roll(first, (0 - z * 32) % LANES, 1)
+    high = pltpu.roll(second, (32 - z * 32) % LANES, 1)
+    gradient = jnp.where(lane_index(8) < 32, low, high)[0:4, 0:64]
+    adam_write(norm, small_out, gradient, factor, GAIN_RATE, 0.0, slice(None))
+
+
+def input_sum_kernel(facts_ref, got_ref, f0, f1, f2, f3):
+    z, x, y = place('z', 'x', 'y')
+    for j in range(CL_MB):
+        count = jnp.where(y == 0, count_row(facts_ref, j), count_row(facts_ref, CL_MB + j))
+        count = jnp.concatenate([count, count], axis=1)
+        for step, target in enumerate((f0, f1, f2, f3)):
+            at = jnp.bitwise_xor(z, step)
+            rows = pl.ds(pl.multiple_of((j * MB + at) * 64, 64), 64)
+            total = got_ref[0, rows, :].astype(F32)
+            for chip in range(1, 4):
+                total = total + got_ref[chip, rows, :].astype(F32)
+            frame = (at * 2 + x) * 8 + lax.broadcasted_iota(jnp.int32, (64, C1), 0) // MEL
+            target[j] = jnp.where(frame < count, total, 0.0).astype(BF)
+
+
+def finish_kernel(facts_ref, f0, g1, g2, g3, grad_ref):
+    z = place('z')
+    for step, piece in enumerate((f0, g1, g2, g3)):
+        at = jnp.bitwise_xor(z, step)
+        for j in range(CL_MB):
+            clip = facts_ref[pl.ds(8 + at * CL_MB + j, 1), :][0, 0]
+            grad_ref[clip] = piece[j]
+
+
+def pooled_kernel(facts_ref, n0, n1, n2, n3, pooled_ref, scratch):
+    z = place('z')
+    for step, told in enumerate((n0, n1, n2, n3)):
+        at = jnp.bitwise_xor(z, step)
+        rows = told[CHUNK + 16:CHUNK + 32, :].astype(F32)
+        for j in range(CL_MB):
+            clip = facts_ref[pl.ds(8 + at * CL_MB + j, 1), :][0, 0]
+            for part in range(2):
+                chips = [rows[chip * 4 + part * 2 + j:chip * 4 + part * 2 + j + 1] for chip in range(4)]
+                scratch[part, pl.ds(clip, 1), :] = jnp.concatenate(chips, axis=1)
+    spread = exchange_matrix(C2, C2, block_exchange)
+    pooled_ref[...] = dot_nn(scratch[0].astype(BF), spread) + dot_nn(scratch[1].astype(BF), spread)
+
+
+def fast_body(clip_input, frame_counts, clip_order, cotangent, kernel_one, kernel_one_mean, kernel_one_square, kernel_two, kernel_two_mean, kernel_two_square, norm_params, norm_mean, norm_square):
+    one_view, two_view = (kernel_one, jnp.swapaxes(kernel_two, 1, 2))
+    p0, p1, p2, p3 = call(take_kernel, [shape_of((CL_MB * 64 + 16, C1))] * MB, [VM] * 2, [VM] * MB, limit=16 * 1024 * 1024)(clip_order, clip_input.reshape(MB * CL_MB, 64, C1))
+    one_keep, two_keep, send, gain_rows, cot_own, facts = call(prepare_kernel, [shape_of((144, LANES)), shape_of((CHUNK, LANES)), shape_of((160 + CHUNK, LANES))] + [shape_of((16, LANES)), shape_of((8, LANES), F32), shape_of((16, LANES), jnp.int32)], [VM, VM] + [HB] * 4, [VM] * 6, [pltpu.VMEM(one_view.shape, F32), pltpu.VMEM(two_view.shape, F32), pltpu.VMEM(norm_params.shape, F32), pltpu.VMEM(cotangent.shape, F32), pltpu.SemaphoreType.DMA((4,))], limit=16 * 1024 * 1024)(after(clip_order, p0), frame_counts.reshape(1, 32), one_view, two_view, norm_params, cotangent)
+
+    def spread_z(values):
+        got = {step: swap(values[step], 'z', step) for step in steps_of()}
+        return [values[0]] + [got[step] for step in (1, 2, 3)]
+    p1, p2, p3 = (part for part in (p1, p2, p3))
+    arrived = spread_z([p0, p1, p2, p3])
+    got = swap(send, 'y')
+    a0, b0 = call(stack_kernel, [shape_of((MB, 64, C1))] * 2, [VM] * 4, [VM] * 2)(*arrived)
+    one_flat = join(one_keep, got[0:144], gain_rows)
+    a1, b1 = (swap(a0, 'x'), swap(b0, 'y'))
+    one_parts = spread_z([one_flat] * 4)
+    a01, b01 = (join(a0, a1), join(b0, b1))
+    deps = ()
+    one_others = join(*[swap(after(part, *deps), 'core') for part in one_parts])
+    a23, b23 = (swap(a01, 'y'), swap(b01, 'x'))
+    inputs = (a0, a1, a23, b0, b1, b23)
+    two_flat = join(two_keep, got[144:144 + CHUNK])
+    two_flat = after(two_flat, *one_parts[1:])
+    two_parts = spread_z([two_flat] * 4)
+    weight_one, gains, facts = call(first_weight_kernel, [shape_of((TAPS, MB, 32, C1)), shape_of((8, LANES), F32), shape_of((16, LANES), jnp.int32)], [VM] * 6, [VM] * 3)(*one_parts, one_others, facts)
+    pre_one, masked, stat_one = call(first_conv_kernel, [shape_of((PIXELS, LANES), F32), shape_of((PIXELS, C1)), shape_of((8, LANES), F32)], [VM] * 8, [VM] * 3)(facts, *inputs, weight_one)
+    stat_one_other = swap(stat_one, 'core')
+    ha_on, ha0, hb_on, hb0 = call(hidden_kernel, [shape_of((HALF + pad, LANES)) for pad in (32, 48)] * 2, [VM] * 5, [VM] * 4)(after(facts, *two_parts[1:]), pre_one, stat_one, stat_one_other, gains)
+    ha1, hb1 = (swap(ha_on, 'x'), swap(hb_on, 'y'))
+    ha2, hb2 = (swap(ha0, 'y'), swap(hb0, 'x'))
+    ha3, hb3 = (swap(ha1, 'y'), swap(hb1, 'x'))
+    hidden_parts = (ha0, ha1, ha2, ha3, hb0, hb1, hb2, hb3)
+    deps = (ha0,)
+    two_others = [swap(after(part, *deps), 'core') for part in two_parts]
+    weight_two = call(second_weight_kernel, shape_of((TAPS, MB, 32, C2)), [VM] * 8, VM)(*two_parts, *two_others)
+    ha = hidden_parts
+    near_two = call(near_conv_kernel, shape_of((PIXELS, LANES), F32), [VM] * 7, VM)(ha[0], ha[1], ha[2], ha[4], ha[5], ha[6], weight_two)
+    pre_two, stat_two = call(far_conv_kernel, [shape_of((PIXELS, LANES), F32), shape_of((8, LANES), F32)], [VM] * 5, [VM] * 2)(facts, ha[3], ha[7], weight_two, near_two)
+    stat_two_other = swap(stat_two, 'core')
+    slope_two, sum_two, pooled_own = call(pool_kernel, [shape_of((PIXELS, LANES), F32), shape_of((8, LANES), F32), shape_of((16, LANES))], [VM] * 7, [VM] * 3)(facts, pre_two, stat_two, stat_two_other, gains, cot_own, got)
+    sum_two_other = swap(sum_two, 'core')
+    columns_two, a_own, a_mid, a_send, b_own, b_mid, b_send = call(both_grad_kernel, [shape_of((PIXELS, TAPS * LANES))] + [shape_of((HALF, LANES), F32)] * 2 + [shape_of((2 * HALF + 16, LANES))] + [shape_of((HALF, LANES), F32)] * 2 + [shape_of((2 * HALF, LANES))], [VM] * 10, [VM] * 7, [pltpu.VMEM((TAPS * LANES, C2), BF)])(facts, slope_two, pre_two, stat_two, stat_two_other, sum_two, sum_two_other, gains, weight_two, pooled_own)
+    a_got = a_near = swap(a_send, 'x')
+    b_got = b_near = swap(b_send, 'y')
+    a_pool = a_got[2 * HALF:]
+    thirds = call(second_weight_grad_kernel, [shape_of((MB, 2, 96, LANES), F32)] * 6, [ANY] * 8 + [VM], [VM] * 6, [pltpu.VMEM((PIXELS, C2), BF), pltpu.VMEM((LANES, C2), F32), pltpu.SemaphoreType.DMA((8,))])(*hidden_parts, columns_two)
+
+    def sum_cores(*deps):
+        sends = [after(part, *deps) if deps else part for part in thirds[3:6]]
+        return call(second_core_kernel, [shape_of((2, CHUNK, LANES), F32)] + [shape_of((2, CHUNK, LANES))] * 3, [VM] * 6, [VM] * 4)(*thirds[0:3], *[swap(part, 'core') for part in sends])
+    two_own, t1, t2, t3 = sum_cores()
+    a_got = after(a_got, t1)
+    a_next, b_next = call(pass_on_kernel, [shape_of((HALF + 32, LANES)), shape_of((HALF, LANES))], [VM] * 5, [VM] * 2)(a_mid, a_got, b_mid, b_got, pooled_own)
+    a_last, b_last = (swap(a_next, 'y'), swap(b_next, 'x'))
+    slope_one, sum_one = call(first_slope_kernel, [shape_of((PIXELS, LANES), F32), shape_of((8, LANES), F32)], [VM] * 11, [VM] * 2)(after(facts, t1), a_own, a_near, a_last, b_own, b_near, b_last, pre_one, stat_one, stat_one_other, gains)
+    sum_one_other = swap(sum_one, 'core')
+    columns_one, one_part, one_part_send = call(first_weight_grad_kernel, [shape_of((PIXELS, TAPS * LANES))] + [shape_of((MB, CHUNK, LANES), F32)] * 2, [VM] * 9, [VM] * 3, [pltpu.VMEM((PIXELS, C1), BF)])(facts, slope_one, pre_one, stat_one, stat_one_other, sum_one, sum_one_other, gains, masked)
+    input_part = call(input_grad_kernel, shape_of((4, ROWS, C1)), [VM] * 2, VM)(columns_one, weight_one)
+    two_keep_sum, two_send_sum, square_two = call(second_sum_kernel, [shape_of((CHUNK, LANES), F32), shape_of((CHUNK, LANES)), shape_of((8, LANES), F32)], [VM] * 4, [VM] * 3)(*spread_z([two_own, t1, t2, t3]))
+    one_own, n0, n1, n2, n3 = call(first_core_kernel, [shape_of((CHUNK, LANES), F32)] + [shape_of((CHUNK + 32, LANES))] * MB, [VM] * 9, [VM] * 5, [pltpu.VMEM((16, LANES), F32)])(one_part, swap(after(one_part_send, square_two), 'core'), sum_one, sum_one_other, sum_two, sum_two_other, pooled_own, a_pool, a_last)
+    g1, g2, g3 = spread_z([n0, n1, n2, n3])[1:]
+    input_got = lax.all_to_all(input_part, ('x', 'y'), 0, 0, tiled=True)
+    f0, f1, f2, f3 = call(input_sum_kernel, [shape_of((CL_MB, 64, C1))] * MB, [VM] * 2, [VM] * 4)(facts, input_got)
+    two_got_sum = swap(after(two_send_sum, n1), 'y')
+    f1, f2, f3 = spread_z([f0, f1, f2, f3])[1:]
+    told, one_keep_sum, one_send_sum, norm_sum = call(first_sum_kernel, [shape_of((32 * 8, LANES), F32), shape_of((144, LANES), F32), shape_of((152, LANES), F32), shape_of((8, LANES), F32)], [VM] * 6, [VM] * 4)(one_own, n0, g1, g2, g3, square_two)
+    told_sent = told
+    told = lax.all_to_all(told, AXES, 0, 0, tiled=True)
+    one_got_sum = swap(one_send_sum, 'y')
+    one_shapes = [shape_of(one_view.shape, F32)] * 4 + [shape_of(one_view.shape)]
+    two_shapes = [shape_of(two_view.shape, F32)] * 4 + [shape_of(two_view.shape)]
+    norm_shapes = [shape_of(norm_params.shape, F32)] * 4 + [shape_of(norm_params.shape)]
+    state = (kernel_one, kernel_one_mean, kernel_one_square, two_view, jnp.swapaxes(kernel_two_mean, 1, 2), jnp.swapaxes(kernel_two_square, 1, 2), norm_params, norm_mean, norm_square)
+    updates = call(adam_kernel, [shape_of((1, 1), F32)] + one_shapes + two_shapes + norm_shapes, [VM] * 15, [VM] * 16, limit=62 * 1024 * 1024)(told, one_keep_sum, one_got_sum, norm_sum, two_keep_sum, two_got_sum, *state)
+    grad_norm = updates[0].reshape(())
+    first_update, norm_update = (tuple(updates[1:6]), tuple(updates[11:16]))
+    second_update = tuple((jnp.swapaxes(part, 1, 2) for part in updates[6:11]))
+    pooled = call(pooled_kernel, shape_of((MB * CL_MB, C2), F32), [VM] * 5, VM, [pltpu.VMEM((2, MB * CL_MB, C2), F32)])(facts, n0, g1, g2, g3)
+    input_grad = call(finish_kernel, shape_of((MB * CL_MB, 64, C1)), [VM] * 5, VM)(facts, after(f0, updates[0]), f1, f2, f3)
+    input_grad = input_grad.reshape(clip_input.shape)
+    return (pooled, input_grad, grad_norm) + first_update + second_update + norm_update
+
+
 def solution(mesh):
-    in_specs = (
-        P("batch", "tm", None, None),
-        P(),
-        P(),
-        P("batch", None),
-        P(None, "batch", "tm"),
-        P(None, "batch", "tm"),
-        P(None, "batch", "tm"),
-        P(None, "batch", "tm"),
-        P(None, "batch", "tm"),
-        P(None, "batch", "tm"),
-        P(None, "tm"),
-        P(None, "tm"),
-        P(None, "tm"),
-    )
-    out_specs = (
-        P("batch", None),
-        P("batch", "tm", None, None),
-        P(),
-        P(None, "batch", "tm"),
-        P(None, "batch", "tm"),
-        P(None, "batch", "tm"),
-        P(None, "batch", "tm"),
-        P(None, "batch", "tm"),
-        P(None, "batch", "tm"),
-        P(None, "batch", "tm"),
-        P(None, "batch", "tm"),
-        P(None, "batch", "tm"),
-        P(None, "batch", "tm"),
-        P(None, "tm"),
-        P(None, "tm"),
-        P(None, "tm"),
-        P(None, "tm"),
-        P(None, "tm"),
-    )
-    return jax.shard_map(body, mesh=mesh, in_specs=in_specs, out_specs=out_specs, check_vma=False)
+    if mesh.shape['tm'] == 2 * MB and mesh.shape['batch'] == 4:
+        grid = Mesh(mesh.devices.reshape(MB, 2, 2, 2), AXES)
+        tm, batch, chosen = (('z', 'x'), ('y', 'core'), fast_body)
+    else:
+        grid, tm, batch, chosen = (mesh, 'tm', 'batch', general_body)
+    kernels = (P(None, batch, tm),) * 3
+    norms = (P(None, tm),) * 3
+    in_specs = (P(batch, tm, None, None), P(), P(), P(batch, None)) + 2 * kernels + norms
+    out_specs = (P(batch, None), P(batch, tm, None, None), P())
+    out_specs = out_specs + (P(None, batch, tm),) * 10 + (P(None, tm),) * 5
+    return jax.shard_map(chosen, mesh=grid, in_specs=in_specs, out_specs=out_specs, check_vma=False)

time: 803 us -> 140 us (0.17); the launches traced: 795 us -> 140 us
  blocking collectives: 325 us -> 0 us
  waiting for transfers between devices: 156 us -> 40.3 us
  local copies, waits for them, and re-layouts: 82.4 us -> 8.36 us
  matrix products: 55.3 us -> 0 us
  other arithmetic: 53.6 us -> 0 us
  starting transfers between devices: 99.5 us -> 59.4 us
  Pallas kernels: 0 us -> 31 us
  between operations: 22.6 us -> 0.98 us
    psum x7 -> x0, blocking collectives: 255 us -> none  [the longest x2 80.6 us: norm_forward(): lax.psum((jnp.sum(masked, axis=(0, 1, 2)), jnp.sum(masked * pre_norm, axi...]
    reduce_scatter x3 -> x0, waiting for transfers between devices: 100 us -> none  [the longest x1 70.6 us: body(): lax.psum_scatter(batch_parts[1], 'tm', scatter_dimension=2, tiled=True)]
    all_gather x2 -> x0, blocking collectives: 70.7 us -> none  [the longest x1 52.6 us: body(): lax.all_gather(low_one, 'tm', axis=2, tiled=True)]
    dot_general x24 -> x0, matrix products: 55.3 us -> none  [the longest x8 33.1 us: contract_rows(): lax.dot_general(columns, grads, (((0,), (0,)), ((), ())), preferred_eleme...]
    unnamed x8 -> x0, waiting for transfers between devices: 47.8 us -> none
    ppermute x32 -> x51, starting transfers between devices: 98.7 us -> 51.7 us  [swap(): return lax.ppermute(value, axis, [(i, i ^ step) for i in range(size)])]
    ppermute x32 -> x51, waiting for transfers between devices: 8.1 us -> 39.7 us  [swap(): return lax.ppermute(value, axis, [(i, i ^ step) for i in range(size)])]
    pallas_call x0 -> x29, Pallas kernels: none -> 31 us  [the longest x1 4.74 us: fast_body(): call(second_weight_grad_kernel, [shape_of((MB, 2, 96, LANES), F32)] * 6,...]
  transfers between devices with their start and end apart: 39 -> 53, of which waited for: 5 -> 24; matrix products, arithmetic and copies ran while one was open for 18% -> 0% of each run, Pallas kernels for 0% -> 17%
where the time goes in v6:
time: 140 us
  starting transfers between devices  59.4 us (42%)
  waiting for transfers between devices  40.3 us (29%)
  Pallas kernels  31 us (22%)
  local copies, waits for them, and re-layouts  8.36 us (6%)
    ppermute x51, starting transfers between devices, swap(): return lax.ppermute(value, axis, [(i, i ^ step) for i in range(size)])  51.7 us
    ppermute x51, waiting for transfers between devices, swap(): return lax.ppermute(value, axis, [(i, i ^ step) for i in range(size)])  39.7 us
    unnamed x28, local copies, waits for them, and re-layouts  8.35 us
    pallas_call x1, Pallas kernels, fast_body(): call(second_weight_grad_kernel, [shape_of((MB, 2, 96, LANES), F32)] * 6,...  4.74 us
    all_to_all x1, starting transfers between devices, fast_body(): told = lax.all_to_all(told, AXES, 0, 0, tiled=True)  4.23 us
    all_to_all x1, starting transfers between devices, fast_body(): input_got = lax.all_to_all(input_part, ('x', 'y'), 0, 0, tiled=True)  3.51 us
    pallas_call x1, Pallas kernels, fast_body(): call(adam_kernel, [shape_of((1, 1), F32)] + one_shapes + two_shapes + nor...  3.51 us
    pallas_call x1, Pallas kernels, fast_body(): call(both_grad_kernel, [shape_of((PIXELS, TAPS * LANES))] + [shape_of((HA...  3.33 us
  transfers between devices with their start and end apart: 53, of which 24 were waited for; matrix products, arithmetic and copies ran while one was open for 0% of the time, Pallas kernels for 17%

profile of v6, /device:TPU:0, one launch (start us, length us, event | category | flops | bytes accessed | tf_op | source)
XLA Modules:
  0.0 140.0 jit_solution(7793607496225029720)
XLA Ops:
  2.4 3.1 %collective-permute-start.11 = (bf16[144,256]{1,0:T(8,128)(2,1)S(1)}, bf16[144,256]{1,0:T(8,128)(2,1)S(1)}, u32[]{:S(2)}, u32[]{:S(2)}) collective-permute-start(bf16[144,256]{1,0:T(8,128)(2,1)S(1)} %get-tuple-element.123), channel_id=1, source_target_pairs={{0,8},{8,0},{16,24},{24,16},{1,9},{9,1},{17,25},{25,17},{2,10},{10... | collective-permute-start | bytes 221192 | tf_op jit(solution)/shard_map/ppermute | solution.py:298
  5.5 2.6 %collective-permute-start.12 = (bf16[144,256]{1,0:T(8,128)(2,1)S(1)}, bf16[144,256]{1,0:T(8,128)(2,1)S(1)}, u32[]{:S(2)}, u32[]{:S(2)}) collective-permute-start(bf16[144,256]{1,0:T(8,128)(2,1)S(1)} %get-tuple-element.124), channel_id=1, source_target_pairs={{0,16},{8,24},{16,0},{24,8},{1,17},{9,25},{17,1},{25,9},{2,18},{10... | collective-permute-start | bytes 221192 | tf_op jit(solution)/shard_map/ppermute | solution.py:298
  12.8 1.8 %collective-permute-start = (bf16[448,128]{1,0:T(8,128)(2,1)S(1)}, bf16[448,128]{1,0:T(8,128)(2,1)S(1)}, u32[]{:S(2)}, u32[]{:S(2)}) collective-permute-start(bf16[448,128]{1,0:T(8,128)(2,1)S(1)} %get-tuple-element.116), channel_id=1, source_target_pairs={{0,2},{2,0},{1,3},{3,1},{4,6},{6,4},{5,7},{7,5},{8,10},{10,8},{9,1... | collective-permute-start | bytes 344072 | tf_op jit(solution)/shard_map/ppermute | solution.py:298
  18.1 4.2 %collective-permute-start.3 = (bf16[304,128]{1,0:T(8,128)(2,1)S(1)}, bf16[304,128]{1,0:T(8,128)(2,1)S(1)}, u32[]{:S(2)}, u32[]{:S(2)}) collective-permute-start(bf16[304,128]{1,0:T(8,128)(2,1)S(1)} %shard_map.270.o0), channel_id=1, source_target_pairs={{0,24},{8,16},{16,8},{24,0},{1,25},{9,17},{17,9},{25,1},{2,26},{10... | collective-permute-start | bytes 233480 | tf_op jit(solution)/shard_map/ppermute | solution.py:298
  22.9 2.1 %collective-permute-start.15 = (bf16[8,64,256]{2,1,0:T(8,128)(2,1)S(1)}, bf16[8,64,256]{2,1,0:T(8,128)(2,1)S(1)}, u32[]{:S(2)}, u32[]{:S(2)}) collective-permute-start(bf16[8,64,256]{2,1,0:T(8,128)(2,1)S(1)} %shard_map.275), channel_id=1, source_target_pairs={{0,2},{2,0},{1,3},{3,1},{4,6},{6,4},{5,7},{7,5},{8,10},{10,8},{9,1... | collective-permute-start | bytes 786440 | tf_op jit(solution)/shard_map/ppermute | solution.py:298
  28.8 2.9 %collective-permute-start.10 = (bf16[576,128]{1,0:T(8,128)(2,1)S(1)}, bf16[576,128]{1,0:T(8,128)(2,1)S(1)}, u32[]{:S(2)}, u32[]{:S(2)}) collective-permute-start(bf16[576,128]{1,0:T(8,128)(2,1)S(1)} %shard_map.273.o0), channel_id=1, source_target_pairs={{0,24},{8,16},{16,8},{24,0},{1,25},{9,17},{17,9},{25,1},{2,26},{10... | collective-permute-start | bytes 442376 | tf_op jit(solution)/shard_map/ppermute | solution.py:298
  33.8 1.7 %shard_map.277 = (f32[2048,128]{1,0:T(8,128)S(1)}, bf16[2048,256]{1,0:T(8,128)(2,1)S(1)}, f32[8,128]{1,0:T(8,128)S(1)}) custom-call(s32[16,128]{1,0:T(8,128)S(1)} %get-tuple-element.154.facts_ref, bf16[4,64,256]{2,1,0:T(8,128)(2,1)S(1)} %get-tuple-element.126.refs_0_.a0, bf16[4,64,256]{2,1,0:T(8,128)(2,1)S(1)} %collective-permute-done.14.refs_1_.a1, ...), custom_call_target="tpu_custom_call" | custom-call | tf_op jit(solution)/shard_map/pallas_call | solution.py:960
  35.6 1.9 %collective-permute-done.10.o3 = bf16[576,128]{1,0:T(8,128)(2,1)S(1)} collective-permute-done((bf16[576,128]{1,0:T(8,128)(2,1)S(1)}, bf16[576,128]{1,0:T(8,128)(2,1)S(1)}, u32[]{:S(2)}, u32[]{:S(2)}) %collective-permute-start.10) | collective-permute-done | bytes 147488 | tf_op jit(solution)/shard_map/ppermute | solution.py:298
  37.4 6.3 %collective-permute-done.9.o2 = bf16[576,128]{1,0:T(8,128)(2,1)S(1)} collective-permute-done((bf16[576,128]{1,0:T(8,128)(2,1)S(1)}, bf16[576,128]{1,0:T(8,128)(2,1)S(1)}, u32[]{:S(2)}, u32[]{:S(2)}) %collective-permute-start.9) | collective-permute-done | bytes 147488 | tf_op jit(solution)/shard_map/ppermute | solution.py:298
  44.1 1.9 %collective-permute-start.19 = (bf16[1056,128]{1,0:T(8,128)(2,1)S(1)}, bf16[1056,128]{1,0:T(8,128)(2,1)S(1)}, u32[]{:S(2)}, u32[]{:S(2)}) collective-permute-start(bf16[1056,128]{1,0:T(8,128)(2,1)S(1)} %get-tuple-element.133), channel_id=1, source_target_pairs={{0,4},{4,0},{1,5},{5,1},{2,6},{6,2},{3,7},{7,3},{8,12},{12,8},{9,1... | collective-permute-start | bytes 811016 | tf_op jit(solution)/shard_map/ppermute | solution.py:298
  49.6 3.3 %collective-permute-done.19.a1.rest_1_ = bf16[1056,128]{1,0:T(8,128)(2,1)S(1)} collective-permute-done((bf16[1056,128]{1,0:T(8,128)(2,1)S(1)}, bf16[1056,128]{1,0:T(8,128)(2,1)S(1)}, u32[]{:S(2)}, u32[]{:S(2)}) %collective-permute-start.19) | collective-permute-done | bytes 270368 | tf_op jit(solution)/shard_map/ppermute | solution.py:298
  52.9 2.5 %collective-permute-start.21 = (bf16[1056,128]{1,0:T(8,128)(2,1)S(1)}, bf16[1056,128]{1,0:T(8,128)(2,1)S(1)}, u32[]{:S(2)}, u32[]{:S(2)}) collective-permute-start(bf16[1056,128]{1,0:T(8,128)(2,1)S(1)} %collective-permute-done.19.a1.rest_1_), channel_id=1, source_target_pairs={{0,2},{2,0},{1,3},{3,1},{4,6},{6,4},{5,7},{7,5},{8,10},{10,8},{9,1... | collective-permute-start | bytes 811016 | tf_op jit(solution)/shard_map/ppermute | solution.py:298
  58.8 2.2 %collective-permute-done.20.a2.rest_2_ = bf16[1072,128]{1,0:T(8,128)(2,1)S(1)} collective-permute-done((bf16[1072,128]{1,0:T(8,128)(2,1)S(1)}, bf16[1072,128]{1,0:T(8,128)(2,1)S(1)}, u32[]{:S(2)}, u32[]{:S(2)}) %collective-permute-start.20) | collective-permute-done | bytes 274464 | tf_op jit(solution)/shard_map/ppermute | solution.py:298
  61.1 2.9 %shard_map.280.near_ref = f32[2048,128]{1,0:T(8,128)S(1)} custom-call(bf16[1072,128]{1,0:T(8,128)(2,1)S(1)} %get-tuple-element.132.a0.rest_0_, bf16[1056,128]{1,0:T(8,128)(2,1)S(1)} %collective-permute-done.19.a1.rest_1_, bf16[1072,128]{1,0:T(8,128)(2,1)S(1)} %collective-permute-done.20.a2.rest_2_, bf16[1072,128]{1,0:T(8,128)(2,1)S(1)} %get-tuple-element.134.b0.rest_4_, ...), custom_call_target="tpu_custom_call" | custom-call | tf_op jit(solution)/shard_map/pallas_call | solution.py:971
  70.3 3.3 %shard_map.283 = (bf16[2048,1152]{1,0:T(8,128)(2,1)S(1)}, f32[1024,128]{1,0:T(8,128)S(1)}, f32[1024,128]{1,0:T(8,128)S(1)}, bf16[2064,128]{1,0:T(8,128)(2,1)S(1)...) custom-call(s32[16,128]{1,0:T(8,128)S(1)} %get-tuple-element.154.facts_ref, ...), custom_call_target="tpu_custom_call" | custom-call | tf_op jit(solution)/shard_map/pallas_call | solution.py:976
  74.0 1.6 %collective-permute-start.35 = (bf16[2048,128]{1,0:T(8,128)(2,1)S(1)}, bf16[2048,128]{1,0:T(8,128)(2,1)S(1)}, u32[]{:S(2)}, u32[]{:S(2)}) collective-permute-start(bf16[2048,128]{1,0:T(8,128)(2,1)S(1)} %get-tuple-element.160), channel_id=1, source_target_pairs={{0,2},{2,0},{1,3},{3,1},{4,6},{6,4},{5,7},{7,5},{8,10},{10,8},{9,1... | collective-permute-start | bytes 1572872 | tf_op jit(solution)/shard_map/ppermute | solution.py:298
  75.7 4.7 %shard_map.284 = (f32[4,2,96,128]{3,2,1,0:T(8,128)S(1)}, f32[4,2,96,128]{3,2,1,0:T(8,128)S(1)}, f32[4,2,96,128]{3,2,1,0:T(8,128)S(1)}, f32[4,2,96,128]{3,2,1,0:T...) custom-call(bf16[1072,128]{1,0:T(8,128)(2,1)S(1)} %get-tuple-element.132.a0.rest_0_, ...), custom_call_target="tpu_custom_call" | custom-call | tf_op jit(solution)/shard_map/pallas_call | solution.py:980
  84.2 3.6 %collective-permute-done.34.a_got.a_near = bf16[2064,128]{1,0:T(8,128)(2,1)S(1)} collective-permute-done((bf16[2064,128]{1,0:T(8,128)(2,1)S(1)}, bf16[2064,128]{1,0:T(8,128)(2,1)S(1)}, u32[]{:S(2)}, u32[]{:S(2)}) %collective-permute-start.34) | collective-permute-done | bytes 528416 | tf_op jit(solution)/shard_map/ppermute | solution.py:298
  87.9 1.7 %collective-permute-start.36 = (bf16[1056,128]{1,0:T(8,128)(2,1)S(1)}, bf16[1056,128]{1,0:T(8,128)(2,1)S(1)}, u32[]{:S(2)}, u32[]{:S(2)}) collective-permute-start(bf16[1056,128]{1,0:T(8,128)(2,1)S(1)} %get-tuple-element.161), channel_id=1, source_target_pairs={{0,2},{2,0},{1,3},{3,1},{4,6},{6,4},{5,7},{7,5},{8,10},{10,8},{9,1... | collective-permute-start | bytes 811016 | tf_op jit(solution)/shard_map/ppermute | solution.py:298
  90.8 2.4 %collective-permute-start.41 = (bf16[2,288,128]{2,1,0:T(8,128)(2,1)}, bf16[2,288,128]{2,1,0:T(8,128)(2,1)S(1)}, u32[]{:S(2)}, u32[]{:S(2)}) collective-permute-start(bf16[2,288,128]{2,1,0:T(8,128)(2,1)} %get-tuple-element.171), channel_id=1, source_target_pairs={{0,24},{8,16},{16,8},{24,0},{1,25},{9,17},{17,9},{25,1},{2,26},{10... | collective-permute-start | bytes 442376 | tf_op jit(solution)/shard_map/ppermute | solution.py:298
  94.3 2.2 %collective-permute-done.37.b_last = bf16[1024,128]{1,0:T(8,128)(2,1)S(1)} collective-permute-done((bf16[1024,128]{1,0:T(8,128)(2,1)S(1)}, bf16[1024,128]{1,0:T(8,128)(2,1)S(1)}, u32[]{:S(2)}, u32[]{:S(2)}) %collective-permute-start.37) | collective-permute-done | bytes 262176 | tf_op jit(solution)/shard_map/ppermute | solution.py:298
  98.5 2.4 %shard_map.288 = (bf16[2048,1152]{1,0:T(8,128)(2,1)S(1)}, f32[4,288,128]{2,1,0:T(8,128)S(1)}, f32[4,288,128]{2,1,0:T(8,128)S(1)}) custom-call(s32[16,128]{1,0:T(8,128)S(1)} %get-tuple-element.154.facts_ref, f32[2048,128]{1,0:T(8,128)S(1)} %get-tuple-element.164.slope_ref, f32[2048,128]{1,0:T(8,128)S(1)} %get-tuple-element.129.pre_ref, ...), custom_call_target="tpu_custom_call" | custom-call | tf_op jit(solution)/shard_map/pallas_call | solution.py:991
  101.8 2.5 %shard_map.292 = bf16[4,512,256]{2,1,0:T(8,128)(2,1)} custom-call(bf16[2048,1152]{1,0:T(8,128)(2,1)S(1)} %get-tuple-element.178.columns, bf16[9,4,32,256]{3,2,1,0:T(8,128)(2,1)S(1)} %get-tuple-element.128.weight_ref), custom_call_target="tpu_custom_call" | custom-call | tf_op jit(solution)/shard_map/pallas_call | solution.py:992
  104.3 3.5 %all-to-all-start = ((bf16[4,512,256]{2,1,0:T(8,128)(2,1)}), bf16[4,512,256]{2,1,0:T(8,128)(2,1)S(1)}, u32[]{:S(2)}, u32[]{:S(2)}) async-start(bf16[4,512,256]{2,1,0:T(8,128)(2,1)} %shard_map.292), calls=%async_computation | async-start | bytes 2097152 | tf_op jit(solution)/shard_map/all_to_all | solution.py:996
  108.8 2.0 %collective-permute-done.42.got_ref = f32[4,288,128]{2,1,0:T(8,128)S(1)} collective-permute-done((f32[4,288,128]{2,1,0:T(8,128)}, f32[4,288,128]{2,1,0:T(8,128)S(1)}, u32[]{:S(2)}, u32[]{:S(2)}) %collective-permute-start.42) | collective-permute-done | bytes 589856 | tf_op jit(solution)/shard_map/ppermute | solution.py:298
  111.0 2.4 %collective-permute-start.45 = (bf16[320,128]{1,0:T(8,128)(2,1)S(1)}, bf16[320,128]{1,0:T(8,128)(2,1)S(1)}, u32[]{:S(2)}, u32[]{:S(2)}) collective-permute-start(bf16[320,128]{1,0:T(8,128)(2,1)S(1)} %get-tuple-element.177), channel_id=1, source_target_pairs={{0,24},{8,16},{16,8},{24,0},{1,25},{9,17},{17,9},{25,1},{2,26},{10... | collective-permute-start | bytes 245768 | tf_op jit(solution)/shard_map/ppermute | solution.py:298
  114.5 5.3 %collective-permute-done.44.n2.g2 = bf16[320,128]{1,0:T(8,128)(2,1)S(1)} collective-permute-done((bf16[320,128]{1,0:T(8,128)(2,1)S(1)}, bf16[320,128]{1,0:T(8,128)(2,1)S(1)}, u32[]{:S(2)}, u32[]{:S(2)}) %collective-permute-start.44) | collective-permute-done | bytes 81952 | tf_op jit(solution)/shard_map/ppermute | solution.py:298
  122.4 4.2 %all-to-all-start.1 = ((f32[32,8,128]{2,1,0:T(8,128)}), f32[32,8,128]{2,1,0:T(8,128)S(1)}, u32[]{:S(2)}, u32[]{:S(2)}) async-start(f32[32,8,128]{2,1,0:T(8,128)} %bitcast.3), calls=%async_computation.1 | async-start | bytes 262144 | tf_op jit(solution)/shard_map/all_to_all | solution.py:1002
  126.7 1.8 %collective-permute-start.46 = (f32[152,128]{1,0:T(8,128)S(1)}, f32[152,128]{1,0:T(8,128)S(1)}, u32[]{:S(2)}, u32[]{:S(2)}) collective-permute-start(f32[152,128]{1,0:T(8,128)S(1)} %get-tuple-element.183), channel_id=1, source_target_pairs={{0,2},{2,0},{1,3},{3,1},{4,6},{6,4},{5,7},{7,5},{8,10},{10,8},{9,1... | collective-permute-start | bytes 233480 | tf_op jit(solution)/shard_map/ppermute | solution.py:298
  128.9 1.8 %collective-permute-start.48 = (bf16[2,64,256]{2,1,0:T(8,128)(2,1)S(1)}, bf16[2,64,256]{2,1,0:T(8,128)(2,1)S(1)}, u32[]{:S(2)}, u32[]{:S(2)}) collective-permute-start(bf16[2,64,256]{2,1,0:T(8,128)(2,1)S(1)} %get-tuple-element.190), channel_id=1, source_target_pairs={{0,8},{8,0},{16,24},{24,16},{1,9},{9,1},{17,25},{25,17},{2,10},{10... | collective-permute-start | bytes 196616 | tf_op jit(solution)/shard_map/ppermute | solution.py:298
  130.8 2.4 %collective-permute-start.49 = (bf16[2,64,256]{2,1,0:T(8,128)(2,1)S(1)}, bf16[2,64,256]{2,1,0:T(8,128)(2,1)S(1)}, u32[]{:S(2)}, u32[]{:S(2)}) collective-permute-start(bf16[2,64,256]{2,1,0:T(8,128)(2,1)S(1)} %get-tuple-element.191), channel_id=1, source_target_pairs={{0,16},{8,24},{16,0},{24,8},{1,17},{9,25},{17,1},{25,9},{2,18},{10... | collective-permute-start | bytes 196616 | tf_op jit(solution)/shard_map/ppermute | solution.py:298
  135.6 3.5 %shard_map.295 = (f32[1,1]{1,0:T(1,128)}, f32[9,64,64]{2,1,0:T(8,128)}, f32[9,64,64]{2,1,0:T(8,128)}, f32[9,64,64]{2,1,0:T(8,128)}, f32[9,64,64]{2,1,0:T(8,128)}...) custom-call(f32[256,128]{1,0:T(8,128)} %bitcast.18, ...), custom_call_target="tpu_custom_call" | custom-call | tf_op jit(solution)/shard_map/pallas_call | solution.py:1008
  (134 shorter events, 48.2 us)
Async XLA Ops:
  2.4 12.2 %collective-permute-start.11 = (bf16[144,256]{1,0:T(8,128)(2,1)S(1)}, bf16[144,256]{1,0:T(8,128)(2,1)S(1)}, u32[]{:S(2)}, u32[]{:S(2)}) collective-permute-start(bf16[144,256]{1,0:T(8,128)(2,1)S(1)} %get-tuple-element.123), channel_id=1, source_target_pairs={{0,8},{8,0},{16,24},{24,16},{1,9},{9,1},{17,25},{25,17},{2,10},{10... | collective-permute-start | bytes 221192 | tf_op jit(solution)/shard_map/ppermute | solution.py:298
  5.5 9.1 %collective-permute-start.12 = (bf16[144,256]{1,0:T(8,128)(2,1)S(1)}, bf16[144,256]{1,0:T(8,128)(2,1)S(1)}, u32[]{:S(2)}, u32[]{:S(2)}) collective-permute-start(bf16[144,256]{1,0:T(8,128)(2,1)S(1)} %get-tuple-element.124), channel_id=1, source_target_pairs={{0,16},{8,24},{16,0},{24,8},{1,17},{9,25},{17,1},{25,9},{2,18},{10... | collective-permute-start | bytes 221192 | tf_op jit(solution)/shard_map/ppermute | solution.py:298
  14.6 8.3 %collective-permute-start.14 = (bf16[4,64,256]{2,1,0:T(8,128)(2,1)S(1)}, bf16[4,64,256]{2,1,0:T(8,128)(2,1)S(1)}, u32[]{:S(2)}, u32[]{:S(2)}) collective-permute-start(bf16[4,64,256]{2,1,0:T(8,128)(2,1)S(1)} %get-tuple-element.126.refs_0_.a0), channel_id=1, source_target_pairs={{0,4},{4,0},{1,5},{5,1},{2,6},{6,2},{3,7},{7,3},{8,12},{12,8},{9,1... | collective-permute-start | bytes 393224 | tf_op jit(solution)/shard_map/ppermute | solution.py:298
  18.1 7.4 %collective-permute-start.3 = (bf16[304,128]{1,0:T(8,128)(2,1)S(1)}, bf16[304,128]{1,0:T(8,128)(2,1)S(1)}, u32[]{:S(2)}, u32[]{:S(2)}) collective-permute-start(bf16[304,128]{1,0:T(8,128)(2,1)S(1)} %shard_map.270.o0), channel_id=1, source_target_pairs={{0,24},{8,16},{16,8},{24,0},{1,25},{9,17},{17,9},{25,1},{2,26},{10... | collective-permute-start | bytes 233480 | tf_op jit(solution)/shard_map/ppermute | solution.py:298
  22.9 10.8 %collective-permute-start.15 = (bf16[8,64,256]{2,1,0:T(8,128)(2,1)S(1)}, bf16[8,64,256]{2,1,0:T(8,128)(2,1)S(1)}, u32[]{:S(2)}, u32[]{:S(2)}) collective-permute-start(bf16[8,64,256]{2,1,0:T(8,128)(2,1)S(1)} %shard_map.275), channel_id=1, source_target_pairs={{0,2},{2,0},{1,3},{3,1},{4,6},{6,4},{5,7},{7,5},{8,10},{10,8},{9,1... | collective-permute-start | bytes 786440 | tf_op jit(solution)/shard_map/ppermute | solution.py:298
  25.5 8.3 %collective-permute-start.17 = (bf16[8,64,256]{2,1,0:T(8,128)(2,1)S(1)}, bf16[8,64,256]{2,1,0:T(8,128)(2,1)S(1)}, u32[]{:S(2)}, u32[]{:S(2)}) collective-permute-start(bf16[8,64,256]{2,1,0:T(8,128)(2,1)S(1)} %shard_map.276), channel_id=1, source_target_pairs={{0,4},{4,0},{1,5},{5,1},{2,6},{6,2},{3,7},{7,3},{8,12},{12,8},{9,1... | collective-permute-start | bytes 786440 | tf_op jit(solution)/shard_map/ppermute | solution.py:298
  28.8 8.6 %collective-permute-start.10 = (bf16[576,128]{1,0:T(8,128)(2,1)S(1)}, bf16[576,128]{1,0:T(8,128)(2,1)S(1)}, u32[]{:S(2)}, u32[]{:S(2)}) collective-permute-start(bf16[576,128]{1,0:T(8,128)(2,1)S(1)} %shard_map.273.o0), channel_id=1, source_target_pairs={{0,24},{8,16},{16,8},{24,0},{1,25},{9,17},{17,9},{25,1},{2,26},{10... | collective-permute-start | bytes 442376 | tf_op jit(solution)/shard_map/ppermute | solution.py:298
  31.7 12.0 %collective-permute-start.9 = (bf16[576,128]{1,0:T(8,128)(2,1)S(1)}, bf16[576,128]{1,0:T(8,128)(2,1)S(1)}, u32[]{:S(2)}, u32[]{:S(2)}) collective-permute-start(bf16[576,128]{1,0:T(8,128)(2,1)S(1)} %shard_map.273.o0), channel_id=1, source_target_pairs={{0,16},{8,24},{16,0},{24,8},{1,17},{9,25},{17,1},{25,9},{2,18},{10... | collective-permute-start | bytes 442376 | tf_op jit(solution)/shard_map/ppermute | solution.py:298
  31.7 12.0 %collective-permute-start.8 = (bf16[576,128]{1,0:T(8,128)(2,1)S(1)}, bf16[576,128]{1,0:T(8,128)(2,1)S(1)}, u32[]{:S(2)}, u32[]{:S(2)}) collective-permute-start(bf16[576,128]{1,0:T(8,128)(2,1)S(1)} %shard_map.273.o0), channel_id=1, source_target_pairs={{0,8},{8,0},{16,24},{24,16},{1,9},{9,1},{17,25},{25,17},{2,10},{10... | collective-permute-start | bytes 442376 | tf_op jit(solution)/shard_map/ppermute | solution.py:298
  35.5 8.2 %collective-permute-start.18 = (f32[8,128]{1,0:T(8,128)S(1)}, f32[8,128]{1,0:T(8,128)S(1)}, u32[]{:S(2)}, u32[]{:S(2)}) collective-permute-start(f32[8,128]{1,0:T(8,128)S(1)} %get-tuple-element.130.own_ref), channel_id=1, source_target_pairs={{0,1},{1,0},{2,3},{3,2},{4,5},{5,4},{6,7},{7,6},{8,9},{9,8},{10,11... | collective-permute-start | bytes 12296 | tf_op jit(solution)/shard_map/ppermute | solution.py:298
  44.1 8.8 %collective-permute-start.19 = (bf16[1056,128]{1,0:T(8,128)(2,1)S(1)}, bf16[1056,128]{1,0:T(8,128)(2,1)S(1)}, u32[]{:S(2)}, u32[]{:S(2)}) collective-permute-start(bf16[1056,128]{1,0:T(8,128)(2,1)S(1)} %get-tuple-element.133), channel_id=1, source_target_pairs={{0,4},{4,0},{1,5},{5,1},{2,6},{6,2},{3,7},{7,3},{8,12},{12,8},{9,1... | collective-permute-start | bytes 811016 | tf_op jit(solution)/shard_map/ppermute | solution.py:298
  46.0 9.4 %collective-permute-start.22 = (bf16[1056,128]{1,0:T(8,128)(2,1)S(1)}, bf16[1056,128]{1,0:T(8,128)(2,1)S(1)}, u32[]{:S(2)}, u32[]{:S(2)}) collective-permute-start(bf16[1056,128]{1,0:T(8,128)(2,1)S(1)} %get-tuple-element.135), channel_id=1, source_target_pairs={{0,2},{2,0},{1,3},{3,1},{4,6},{6,4},{5,7},{7,5},{8,10},{10,8},{9,1... | collective-permute-start | bytes 811016 | tf_op jit(solution)/shard_map/ppermute | solution.py:298
  47.6 8.9 %collective-permute-start.27 = (bf16[576,128]{1,0:T(8,128)(2,1)S(1)}, bf16[576,128]{1,0:T(8,128)(2,1)S(1)}, u32[]{:S(2)}, u32[]{:S(2)}) collective-permute-start(bf16[576,128]{1,0:T(8,128)(2,1)S(1)} %collective-permute-done.9.o2), channel_id=1, source_target_pairs={{0,1},{1,0},{2,3},{3,2},{4,5},{5,4},{6,7},{7,6},{8,9},{9,8},{10,11... | collective-permute-start | bytes 442376 | tf_op jit(solution)/shard_map/ppermute | solution.py:298
  48.5 10.3 %collective-permute-start.23 = (bf16[1072,128]{1,0:T(8,128)(2,1)S(1)}, bf16[1072,128]{1,0:T(8,128)(2,1)S(1)}, u32[]{:S(2)}, u32[]{:S(2)}) collective-permute-start(bf16[1072,128]{1,0:T(8,128)(2,1)S(1)} %get-tuple-element.134.b0.rest_4_), channel_id=1, source_target_pairs={{0,4},{4,0},{1,5},{5,1},{2,6},{6,2},{3,7},{7,3},{8,12},{12,8},{9,1... | collective-permute-start | bytes 823304 | tf_op jit(solution)/shard_map/ppermute | solution.py:298
  49.4 11.7 %collective-permute-start.20 = (bf16[1072,128]{1,0:T(8,128)(2,1)S(1)}, bf16[1072,128]{1,0:T(8,128)(2,1)S(1)}, u32[]{:S(2)}, u32[]{:S(2)}) collective-permute-start(bf16[1072,128]{1,0:T(8,128)(2,1)S(1)} %get-tuple-element.132.a0.rest_0_), channel_id=1, source_target_pairs={{0,2},{2,0},{1,3},{3,1},{4,6},{6,4},{5,7},{7,5},{8,10},{10,8},{9,1... | collective-permute-start | bytes 823304 | tf_op jit(solution)/shard_map/ppermute | solution.py:298
  52.9 12.3 %collective-permute-start.21 = (bf16[1056,128]{1,0:T(8,128)(2,1)S(1)}, bf16[1056,128]{1,0:T(8,128)(2,1)S(1)}, u32[]{:S(2)}, u32[]{:S(2)}) collective-permute-start(bf16[1056,128]{1,0:T(8,128)(2,1)S(1)} %collective-permute-done.19.a1.rest_1_), channel_id=1, source_target_pairs={{0,2},{2,0},{1,3},{3,1},{4,6},{6,4},{5,7},{7,5},{8,10},{10,8},{9,1... | collective-permute-start | bytes 811016 | tf_op jit(solution)/shard_map/ppermute | solution.py:298
  55.4 9.8 %collective-permute-start.24 = (bf16[1056,128]{1,0:T(8,128)(2,1)S(1)}, bf16[1056,128]{1,0:T(8,128)(2,1)S(1)}, u32[]{:S(2)}, u32[]{:S(2)}) collective-permute-start(bf16[1056,128]{1,0:T(8,128)(2,1)S(1)} %collective-permute-done.22.b1.rest_5_), channel_id=1, source_target_pairs={{0,4},{4,0},{1,5},{5,1},{2,6},{6,2},{3,7},{7,3},{8,12},{12,8},{9,1... | collective-permute-start | bytes 811016 | tf_op jit(solution)/shard_map/ppermute | solution.py:298
  73.6 14.2 %collective-permute-start.34 = (bf16[2064,128]{1,0:T(8,128)(2,1)S(1)}, bf16[2064,128]{1,0:T(8,128)(2,1)S(1)}, u32[]{:S(2)}, u32[]{:S(2)}) collective-permute-start(bf16[2064,128]{1,0:T(8,128)(2,1)S(1)} %get-tuple-element.156), channel_id=1, source_target_pairs={{0,4},{4,0},{1,5},{5,1},{2,6},{6,2},{3,7},{7,3},{8,12},{12,8},{9,1... | collective-permute-start | bytes 1585160 | tf_op jit(solution)/shard_map/ppermute | solution.py:298
  74.0 13.8 %collective-permute-start.35 = (bf16[2048,128]{1,0:T(8,128)(2,1)S(1)}, bf16[2048,128]{1,0:T(8,128)(2,1)S(1)}, u32[]{:S(2)}, u32[]{:S(2)}) collective-permute-start(bf16[2048,128]{1,0:T(8,128)(2,1)S(1)} %get-tuple-element.160), channel_id=1, source_target_pairs={{0,2},{2,0},{1,3},{3,1},{4,6},{6,4},{5,7},{7,5},{8,10},{10,8},{9,1... | collective-permute-start | bytes 1572872 | tf_op jit(solution)/shard_map/ppermute | solution.py:298
  87.9 8.6 %collective-permute-start.36 = (bf16[1056,128]{1,0:T(8,128)(2,1)S(1)}, bf16[1056,128]{1,0:T(8,128)(2,1)S(1)}, u32[]{:S(2)}, u32[]{:S(2)}) collective-permute-start(bf16[1056,128]{1,0:T(8,128)(2,1)S(1)} %get-tuple-element.161), channel_id=1, source_target_pairs={{0,2},{2,0},{1,3},{3,1},{4,6},{6,4},{5,7},{7,5},{8,10},{10,8},{9,1... | collective-permute-start | bytes 811016 | tf_op jit(solution)/shard_map/ppermute | solution.py:298
  89.6 6.9 %collective-permute-start.37 = (bf16[1024,128]{1,0:T(8,128)(2,1)S(1)}, bf16[1024,128]{1,0:T(8,128)(2,1)S(1)}, u32[]{:S(2)}, u32[]{:S(2)}) collective-permute-start(bf16[1024,128]{1,0:T(8,128)(2,1)S(1)} %get-tuple-element.163), channel_id=1, source_target_pairs={{0,4},{4,0},{1,5},{5,1},{2,6},{6,2},{3,7},{7,3},{8,12},{12,8},{9,1... | collective-permute-start | bytes 786440 | tf_op jit(solution)/shard_map/ppermute | solution.py:298
  90.8 17.0 %collective-permute-start.40 = (bf16[2,288,128]{2,1,0:T(8,128)(2,1)}, bf16[2,288,128]{2,1,0:T(8,128)(2,1)S(1)}, u32[]{:S(2)}, u32[]{:S(2)}) collective-permute-start(bf16[2,288,128]{2,1,0:T(8,128)(2,1)} %get-tuple-element.170), channel_id=1, source_target_pairs={{0,16},{8,24},{16,0},{24,8},{1,17},{9,25},{17,1},{25,9},{2,18},{10... | collective-permute-start | bytes 442376 | tf_op jit(solution)/shard_map/ppermute | solution.py:298
  90.8 17.0 %collective-permute-start.41 = (bf16[2,288,128]{2,1,0:T(8,128)(2,1)}, bf16[2,288,128]{2,1,0:T(8,128)(2,1)S(1)}, u32[]{:S(2)}, u32[]{:S(2)}) collective-permute-start(bf16[2,288,128]{2,1,0:T(8,128)(2,1)} %get-tuple-element.171), channel_id=1, source_target_pairs={{0,24},{8,16},{16,8},{24,0},{1,25},{9,17},{17,9},{25,1},{2,26},{10... | collective-permute-start | bytes 442376 | tf_op jit(solution)/shard_map/ppermute | solution.py:298
  93.2 14.7 %collective-permute-start.39 = (bf16[2,288,128]{2,1,0:T(8,128)(2,1)S(1)}, bf16[2,288,128]{2,1,0:T(8,128)(2,1)S(1)}, u32[]{:S(2)}, u32[]{:S(2)}) collective-permute-start(bf16[2,288,128]{2,1,0:T(8,128)(2,1)S(1)} %get-tuple-element.153), channel_id=1, source_target_pairs={{0,8},{8,0},{16,24},{24,16},{1,9},{9,1},{17,25},{25,17},{2,10},{10... | collective-permute-start | bytes 442376 | tf_op jit(solution)/shard_map/ppermute | solution.py:298
  104.3 18.2 %all-to-all-start = ((bf16[4,512,256]{2,1,0:T(8,128)(2,1)}), bf16[4,512,256]{2,1,0:T(8,128)(2,1)S(1)}, u32[]{:S(2)}, u32[]{:S(2)}) async-start(bf16[4,512,256]{2,1,0:T(8,128)(2,1)} %shard_map.292), calls=%async_computation | async-start | bytes 2097152 | tf_op jit(solution)/shard_map/all_to_all | solution.py:996
  110.9 8.8 %collective-permute-start.44 = (bf16[320,128]{1,0:T(8,128)(2,1)S(1)}, bf16[320,128]{1,0:T(8,128)(2,1)S(1)}, u32[]{:S(2)}, u32[]{:S(2)}) collective-permute-start(bf16[320,128]{1,0:T(8,128)(2,1)S(1)} %get-tuple-element.176), channel_id=1, source_target_pairs={{0,16},{8,24},{16,0},{24,8},{1,17},{9,25},{17,1},{25,9},{2,18},{10... | collective-permute-start | bytes 245768 | tf_op jit(solution)/shard_map/ppermute | solution.py:298
  111.0 8.8 %collective-permute-start.45 = (bf16[320,128]{1,0:T(8,128)(2,1)S(1)}, bf16[320,128]{1,0:T(8,128)(2,1)S(1)}, u32[]{:S(2)}, u32[]{:S(2)}) collective-permute-start(bf16[320,128]{1,0:T(8,128)(2,1)S(1)} %get-tuple-element.177), channel_id=1, source_target_pairs={{0,24},{8,16},{16,8},{24,0},{1,25},{9,17},{17,9},{25,1},{2,26},{10... | collective-permute-start | bytes 245768 | tf_op jit(solution)/shard_map/ppermute | solution.py:298
  113.5 7.6 %collective-permute-start.43 = (bf16[320,128]{1,0:T(8,128)(2,1)S(1)}, bf16[320,128]{1,0:T(8,128)(2,1)S(1)}, u32[]{:S(2)}, u32[]{:S(2)}) collective-permute-start(bf16[320,128]{1,0:T(8,128)(2,1)S(1)} %get-tuple-element.175), channel_id=1, source_target_pairs={{0,8},{8,0},{16,24},{24,16},{1,9},{9,1},{17,25},{25,17},{2,10},{10... | collective-permute-start | bytes 245768 | tf_op jit(solution)/shard_map/ppermute | solution.py:298
  122.4 12.5 %all-to-all-start.1 = ((f32[32,8,128]{2,1,0:T(8,128)}), f32[32,8,128]{2,1,0:T(8,128)S(1)}, u32[]{:S(2)}, u32[]{:S(2)}) async-start(f32[32,8,128]{2,1,0:T(8,128)} %bitcast.3), calls=%async_computation.1 | async-start | bytes 262144 | tf_op jit(solution)/shard_map/all_to_all | solution.py:1002
  126.7 7.7 %collective-permute-start.46 = (f32[152,128]{1,0:T(8,128)S(1)}, f32[152,128]{1,0:T(8,128)S(1)}, u32[]{:S(2)}, u32[]{:S(2)}) collective-permute-start(f32[152,128]{1,0:T(8,128)S(1)} %get-tuple-element.183), channel_id=1, source_target_pairs={{0,2},{2,0},{1,3},{3,1},{4,6},{6,4},{5,7},{7,5},{8,10},{10,8},{9,1... | collective-permute-start | bytes 233480 | tf_op jit(solution)/shard_map/ppermute | solution.py:298
  128.9 10.1 %collective-permute-start.48 = (bf16[2,64,256]{2,1,0:T(8,128)(2,1)S(1)}, bf16[2,64,256]{2,1,0:T(8,128)(2,1)S(1)}, u32[]{:S(2)}, u32[]{:S(2)}) collective-permute-start(bf16[2,64,256]{2,1,0:T(8,128)(2,1)S(1)} %get-tuple-element.190), channel_id=1, source_target_pairs={{0,8},{8,0},{16,24},{24,16},{1,9},{9,1},{17,25},{25,17},{2,10},{10... | collective-permute-start | bytes 196616 | tf_op jit(solution)/shard_map/ppermute | solution.py:298
  130.8 8.3 %collective-permute-start.49 = (bf16[2,64,256]{2,1,0:T(8,128)(2,1)S(1)}, bf16[2,64,256]{2,1,0:T(8,128)(2,1)S(1)}, u32[]{:S(2)}, u32[]{:S(2)}) collective-permute-start(bf16[2,64,256]{2,1,0:T(8,128)(2,1)S(1)} %get-tuple-element.191), channel_id=1, source_target_pairs={{0,16},{8,24},{16,0},{24,8},{1,17},{9,25},{17,1},{25,9},{2,18},{10... | collective-permute-start | bytes 196616 | tf_op jit(solution)/shard_map/ppermute | solution.py:298
  (35 other events, 88.1 us)

commit v7 on v6

--- a/solution.py
+++ b/solution.py
@@ -775,11 +775,8 @@
     put_pair(sum_ref, first, second)
 
 
-def first_weight_grad_kernel(facts_ref, slope_ref, pre_ref, own_ref, other_ref, sum_own, sum_other, gain_ref, x_ref, columns, keep_ref, send_ref, turned):
+def turn_kernel(x_ref, turned):
     core = place('core')
-    pixels = pixel_row(facts_ref)
-    mean, scale = norm_rows(own_ref, other_ref, pixels)
-    sums = pair_sums(sum_own, sum_other)
 
     def source_of(column):
         core_of = jnp.where(column < 128, core, 1 - core)
@@ -787,10 +784,19 @@
     spread = exchange_matrix(C1, C1, source_of)
     for clip in range(CLIPS_CORE):
         span = slice(clip * ROWS, (clip + 1) * ROWS)
+        turned[span, :] = dot_nn(x_ref[span, :], spread).astype(BF)
+
+
+def first_weight_grad_kernel(facts_ref, slope_ref, pre_ref, own_ref, other_ref, sum_own, sum_other, gain_ref, turned, columns, keep_ref, send_ref):
+    pixels = pixel_row(facts_ref)
+    mean, scale = norm_rows(own_ref, other_ref, pixels)
+    sums = pair_sums(sum_own, sum_other)
+
+    for clip in range(CLIPS_CORE):
+        span = slice(clip * ROWS, (clip + 1) * ROWS)
         mask = valid_rows(facts_ref, clip)
         grad = pre_grad(slope_ref[span, :], pre_ref[span, :], mask, mean, scale, gain_ref[0:1, :], sums, pixels)
         scatter_taps(grad, columns, clip * ROWS)
-        turned[span, :] = dot_nn(x_ref[span, :], spread).astype(BF)
     for tap in range(TAPS):
         both = dot_tn(columns[:, lanes_of(tap)], turned[...])
         for z_of in range(MB):
@@ -968,7 +974,8 @@
     two_others = [swap(after(part, *deps), 'core') for part in two_parts]
     weight_two = call(second_weight_kernel, shape_of((TAPS, MB, 32, C2)), [VM] * 8, VM)(*two_parts, *two_others)
     ha = hidden_parts
-    near_two = call(near_conv_kernel, shape_of((PIXELS, LANES), F32), [VM] * 7, VM)(ha[0], ha[1], ha[2], ha[4], ha[5], ha[6], weight_two)
+    turned = call(turn_kernel, shape_of((PIXELS, C1)), [VM], VM)(masked)
+    near_two = call(near_conv_kernel, shape_of((PIXELS, LANES), F32), [VM] * 7, VM)(ha[0], ha[1], ha[2], ha[4], ha[5], ha[6], after(weight_two, turned))
     pre_two, stat_two = call(far_conv_kernel, [shape_of((PIXELS, LANES), F32), shape_of((8, LANES), F32)], [VM] * 5, [VM] * 2)(facts, ha[3], ha[7], weight_two, near_two)
     stat_two_other = swap(stat_two, 'core')
     slope_two, sum_two, pooled_own = call(pool_kernel, [shape_of((PIXELS, LANES), F32), shape_of((8, LANES), F32), shape_of((16, LANES))], [VM] * 7, [VM] * 3)(facts, pre_two, stat_two, stat_two_other, gains, cot_own, got)
@@ -988,7 +995,7 @@
     a_last, b_last = (swap(a_next, 'y'), swap(b_next, 'x'))
     slope_one, sum_one = call(first_slope_kernel, [shape_of((PIXELS, LANES), F32), shape_of((8, LANES), F32)], [VM] * 11, [VM] * 2)(after(facts, t1), a_own, a_near, a_last, b_own, b_near, b_last, pre_one, stat_one, stat_one_other, gains)
     sum_one_other = swap(sum_one, 'core')
-    columns_one, one_part, one_part_send = call(first_weight_grad_kernel, [shape_of((PIXELS, TAPS * LANES))] + [shape_of((MB, CHUNK, LANES), F32)] * 2, [VM] * 9, [VM] * 3, [pltpu.VMEM((PIXELS, C1), BF)])(facts, slope_one, pre_one, stat_one, stat_one_other, sum_one, sum_one_other, gains, masked)
+    columns_one, one_part, one_part_send = call(first_weight_grad_kernel, [shape_of((PIXELS, TAPS * LANES))] + [shape_of((MB, CHUNK, LANES), F32)] * 2, [VM] * 9, [VM] * 3)(facts, slope_one, pre_one, stat_one, stat_one_other, sum_one, sum_one_other, gains, turned)
     input_part = call(input_grad_kernel, shape_of((4, ROWS, C1)), [VM] * 2, VM)(columns_one, weight_one)
     two_keep_sum, two_send_sum, square_two = call(second_sum_kernel, [shape_of((CHUNK, LANES), F32), shape_of((CHUNK, LANES)), shape_of((8, LANES), F32)], [VM] * 4, [VM] * 3)(*spread_z([two_own, t1, t2, t3]))
     one_own, n0, n1, n2, n3 = call(first_core_kernel, [shape_of((CHUNK, LANES), F32)] + [shape_of((CHUNK + 32, LANES))] * MB, [VM] * 9, [VM] * 5, [pltpu.VMEM((16, LANES), F32)])(one_part, swap(after(one_part_send, square_two), 'core'), sum_one, sum_one_other, sum_two, sum_two_other, pooled_own, a_pool, a_last)

time: 140 us -> 140 us (level)
  no operation moved by 1% of the time
where the time goes in v7:
time: 140 us
  starting transfers between devices  59.4 us (42%)
  waiting for transfers between devices  39.9 us (28%)
  Pallas kernels  31.2 us (22%)
  local copies, waits for them, and re-layouts  8.36 us (6%)
    ppermute x51, starting transfers between devices, swap(): return lax.ppermute(value, axis, [(i, i ^ step) for i in range(size)])  51.7 us
    ppermute x51, waiting for transfers between devices, swap(): return lax.ppermute(value, axis, [(i, i ^ step) for i in range(size)])  39.3 us
    unnamed x28, local copies, waits for them, and re-layouts  8.35 us
    pallas_call x1, Pallas kernels, fast_body(): call(second_weight_grad_kernel, [shape_of((MB, 2, 96, LANES), F32)] * 6,...  4.74 us
    all_to_all x1, starting transfers between devices, fast_body(): told = lax.all_to_all(told, AXES, 0, 0, tiled=True)  4.24 us
    all_to_all x1, starting transfers between devices, fast_body(): input_got = lax.all_to_all(input_part, ('x', 'y'), 0, 0, tiled=True)  3.51 us
    pallas_call x1, Pallas kernels, fast_body(): call(adam_kernel, [shape_of((1, 1), F32)] + one_shapes + two_shapes + nor...  3.51 us
    pallas_call x1, Pallas kernels, fast_body(): call(both_grad_kernel, [shape_of((PIXELS, TAPS * LANES))] + [shape_of((HA...  3.39 us
  transfers between devices with their start and end apart: 53, of which 24 were waited for; matrix products, arithmetic and copies ran while one was open for 0% of the time, Pallas kernels for 17%

profile of v7, /device:TPU:0, one launch (start us, length us, event | category | flops | bytes accessed | tf_op | source)
XLA Modules:
  0.0 139.9 jit_solution(17572166246837105252)
XLA Ops:
  2.4 3.1 %collective-permute-start.11 = (bf16[144,256]{1,0:T(8,128)(2,1)S(1)}, bf16[144,256]{1,0:T(8,128)(2,1)S(1)}, u32[]{:S(2)}, u32[]{:S(2)}) collective-permute-start(bf16[144,256]{1,0:T(8,128)(2,1)S(1)} %get-tuple-element.124), channel_id=1, source_target_pairs={{0,8},{8,0},{16,24},{24,16},{1,9},{9,1},{17,25},{25,17},{2,10},{10... | collective-permute-start | bytes 221192 | tf_op jit(solution)/shard_map/ppermute | solution.py:298
  5.5 2.6 %collective-permute-start.12 = (bf16[144,256]{1,0:T(8,128)(2,1)S(1)}, bf16[144,256]{1,0:T(8,128)(2,1)S(1)}, u32[]{:S(2)}, u32[]{:S(2)}) collective-permute-start(bf16[144,256]{1,0:T(8,128)(2,1)S(1)} %get-tuple-element.125), channel_id=1, source_target_pairs={{0,16},{8,24},{16,0},{24,8},{1,17},{9,25},{17,1},{25,9},{2,18},{10... | collective-permute-start | bytes 221192 | tf_op jit(solution)/shard_map/ppermute | solution.py:298
  12.8 1.8 %collective-permute-start = (bf16[448,128]{1,0:T(8,128)(2,1)S(1)}, bf16[448,128]{1,0:T(8,128)(2,1)S(1)}, u32[]{:S(2)}, u32[]{:S(2)}) collective-permute-start(bf16[448,128]{1,0:T(8,128)(2,1)S(1)} %get-tuple-element.117), channel_id=1, source_target_pairs={{0,2},{2,0},{1,3},{3,1},{4,6},{6,4},{5,7},{7,5},{8,10},{10,8},{9,1... | collective-permute-start | bytes 344072 | tf_op jit(solution)/shard_map/ppermute | solution.py:298
  18.1 4.2 %collective-permute-start.3 = (bf16[304,128]{1,0:T(8,128)(2,1)S(1)}, bf16[304,128]{1,0:T(8,128)(2,1)S(1)}, u32[]{:S(2)}, u32[]{:S(2)}) collective-permute-start(bf16[304,128]{1,0:T(8,128)(2,1)S(1)} %shard_map.270.o0), channel_id=1, source_target_pairs={{0,24},{8,16},{16,8},{24,0},{1,25},{9,17},{17,9},{25,1},{2,26},{10... | collective-permute-start | bytes 233480 | tf_op jit(solution)/shard_map/ppermute | solution.py:298
  22.9 2.1 %collective-permute-start.15 = (bf16[8,64,256]{2,1,0:T(8,128)(2,1)S(1)}, bf16[8,64,256]{2,1,0:T(8,128)(2,1)S(1)}, u32[]{:S(2)}, u32[]{:S(2)}) collective-permute-start(bf16[8,64,256]{2,1,0:T(8,128)(2,1)S(1)} %shard_map.275), channel_id=1, source_target_pairs={{0,2},{2,0},{1,3},{3,1},{4,6},{6,4},{5,7},{7,5},{8,10},{10,8},{9,1... | collective-permute-start | bytes 786440 | tf_op jit(solution)/shard_map/ppermute | solution.py:298
  28.8 2.9 %collective-permute-start.10 = (bf16[576,128]{1,0:T(8,128)(2,1)S(1)}, bf16[576,128]{1,0:T(8,128)(2,1)S(1)}, u32[]{:S(2)}, u32[]{:S(2)}) collective-permute-start(bf16[576,128]{1,0:T(8,128)(2,1)S(1)} %shard_map.273.o0), channel_id=1, source_target_pairs={{0,24},{8,16},{16,8},{24,0},{1,25},{9,17},{17,9},{25,1},{2,26},{10... | collective-permute-start | bytes 442376 | tf_op jit(solution)/shard_map/ppermute | solution.py:298
  33.8 1.7 %shard_map.277 = (f32[2048,128]{1,0:T(8,128)S(1)}, bf16[2048,256]{1,0:T(8,128)(2,1)S(1)}, f32[8,128]{1,0:T(8,128)S(1)}) custom-call(s32[16,128]{1,0:T(8,128)S(1)} %get-tuple-element.157.facts_ref, bf16[4,64,256]{2,1,0:T(8,128)(2,1)S(1)} %get-tuple-element.127.refs_0_.a0, bf16[4,64,256]{2,1,0:T(8,128)(2,1)S(1)} %collective-permute-done.14.refs_1_.a1, ...), custom_call_target="tpu_custom_call" | custom-call | tf_op jit(solution)/shard_map/pallas_call | solution.py:966
  35.6 1.9 %collective-permute-done.10.o3 = bf16[576,128]{1,0:T(8,128)(2,1)S(1)} collective-permute-done((bf16[576,128]{1,0:T(8,128)(2,1)S(1)}, bf16[576,128]{1,0:T(8,128)(2,1)S(1)}, u32[]{:S(2)}, u32[]{:S(2)}) %collective-permute-start.10) | collective-permute-done | bytes 147488 | tf_op jit(solution)/shard_map/ppermute | solution.py:298
  37.4 6.3 %collective-permute-done.9.o2 = bf16[576,128]{1,0:T(8,128)(2,1)S(1)} collective-permute-done((bf16[576,128]{1,0:T(8,128)(2,1)S(1)}, bf16[576,128]{1,0:T(8,128)(2,1)S(1)}, u32[]{:S(2)}, u32[]{:S(2)}) %collective-permute-start.9) | collective-permute-done | bytes 147488 | tf_op jit(solution)/shard_map/ppermute | solution.py:298
  44.1 1.9 %collective-permute-start.19 = (bf16[1056,128]{1,0:T(8,128)(2,1)S(1)}, bf16[1056,128]{1,0:T(8,128)(2,1)S(1)}, u32[]{:S(2)}, u32[]{:S(2)}) collective-permute-start(bf16[1056,128]{1,0:T(8,128)(2,1)S(1)} %get-tuple-element.134), channel_id=1, source_target_pairs={{0,4},{4,0},{1,5},{5,1},{2,6},{6,2},{3,7},{7,3},{8,12},{12,8},{9,1... | collective-permute-start | bytes 811016 | tf_op jit(solution)/shard_map/ppermute | solution.py:298
  49.6 3.3 %collective-permute-done.19.a1.rest_1_ = bf16[1056,128]{1,0:T(8,128)(2,1)S(1)} collective-permute-done((bf16[1056,128]{1,0:T(8,128)(2,1)S(1)}, bf16[1056,128]{1,0:T(8,128)(2,1)S(1)}, u32[]{:S(2)}, u32[]{:S(2)}) %collective-permute-start.19) | collective-permute-done | bytes 270368 | tf_op jit(solution)/shard_map/ppermute | solution.py:298
  52.9 2.5 %collective-permute-start.21 = (bf16[1056,128]{1,0:T(8,128)(2,1)S(1)}, bf16[1056,128]{1,0:T(8,128)(2,1)S(1)}, u32[]{:S(2)}, u32[]{:S(2)}) collective-permute-start(bf16[1056,128]{1,0:T(8,128)(2,1)S(1)} %collective-permute-done.19.a1.rest_1_), channel_id=1, source_target_pairs={{0,2},{2,0},{1,3},{3,1},{4,6},{6,4},{5,7},{7,5},{8,10},{10,8},{9,1... | collective-permute-start | bytes 811016 | tf_op jit(solution)/shard_map/ppermute | solution.py:298
  58.8 2.2 %collective-permute-done.20.a2.rest_2_ = bf16[1072,128]{1,0:T(8,128)(2,1)S(1)} collective-permute-done((bf16[1072,128]{1,0:T(8,128)(2,1)S(1)}, bf16[1072,128]{1,0:T(8,128)(2,1)S(1)}, u32[]{:S(2)}, u32[]{:S(2)}) %collective-permute-start.20) | collective-permute-done | bytes 274464 | tf_op jit(solution)/shard_map/ppermute | solution.py:298
  61.1 2.8 %shard_map.281.near_ref = f32[2048,128]{1,0:T(8,128)S(1)} custom-call(bf16[1072,128]{1,0:T(8,128)(2,1)S(1)} %get-tuple-element.133.a0.rest_0_, bf16[1056,128]{1,0:T(8,128)(2,1)S(1)} %collective-permute-done.19.a1.rest_1_, bf16[1072,128]{1,0:T(8,128)(2,1)S(1)} %collective-permute-done.20.a2.rest_2_, bf16[1072,128]{1,0:T(8,128)(2,1)S(1)} %get-tuple-element.135.b0.rest_4_, ...), custom_call_target="tpu_custom_call" | custom-call | tf_op jit(solution)/shard_map/pallas_call | solution.py:978
  70.3 3.4 %shard_map.284 = (bf16[2048,1152]{1,0:T(8,128)(2,1)S(1)}, f32[1024,128]{1,0:T(8,128)S(1)}, f32[1024,128]{1,0:T(8,128)S(1)}, bf16[2064,128]{1,0:T(8,128)(2,1)S(1)...) custom-call(s32[16,128]{1,0:T(8,128)S(1)} %get-tuple-element.157.facts_ref, ...), custom_call_target="tpu_custom_call" | custom-call | tf_op jit(solution)/shard_map/pallas_call | solution.py:983
  74.1 1.6 %collective-permute-start.35 = (bf16[2048,128]{1,0:T(8,128)(2,1)S(1)}, bf16[2048,128]{1,0:T(8,128)(2,1)S(1)}, u32[]{:S(2)}, u32[]{:S(2)}) collective-permute-start(bf16[2048,128]{1,0:T(8,128)(2,1)S(1)} %get-tuple-element.163), channel_id=1, source_target_pairs={{0,2},{2,0},{1,3},{3,1},{4,6},{6,4},{5,7},{7,5},{8,10},{10,8},{9,1... | collective-permute-start | bytes 1572872 | tf_op jit(solution)/shard_map/ppermute | solution.py:298
  75.7 4.7 %shard_map.285 = (f32[4,2,96,128]{3,2,1,0:T(8,128)S(1)}, f32[4,2,96,128]{3,2,1,0:T(8,128)S(1)}, f32[4,2,96,128]{3,2,1,0:T(8,128)S(1)}, f32[4,2,96,128]{3,2,1,0:T...) custom-call(bf16[1072,128]{1,0:T(8,128)(2,1)S(1)} %get-tuple-element.133.a0.rest_0_, ...), custom_call_target="tpu_custom_call" | custom-call | tf_op jit(solution)/shard_map/pallas_call | solution.py:987
  84.2 3.7 %collective-permute-done.34.a_got.a_near = bf16[2064,128]{1,0:T(8,128)(2,1)S(1)} collective-permute-done((bf16[2064,128]{1,0:T(8,128)(2,1)S(1)}, bf16[2064,128]{1,0:T(8,128)(2,1)S(1)}, u32[]{:S(2)}, u32[]{:S(2)}) %collective-permute-start.34) | collective-permute-done | bytes 528416 | tf_op jit(solution)/shard_map/ppermute | solution.py:298
  88.0 1.6 %collective-permute-start.36 = (bf16[1056,128]{1,0:T(8,128)(2,1)S(1)}, bf16[1056,128]{1,0:T(8,128)(2,1)S(1)}, u32[]{:S(2)}, u32[]{:S(2)}) collective-permute-start(bf16[1056,128]{1,0:T(8,128)(2,1)S(1)} %get-tuple-element.164), channel_id=1, source_target_pairs={{0,2},{2,0},{1,3},{3,1},{4,6},{6,4},{5,7},{7,5},{8,10},{10,8},{9,1... | collective-permute-start | bytes 811016 | tf_op jit(solution)/shard_map/ppermute | solution.py:298
  90.8 2.4 %collective-permute-start.41 = (bf16[2,288,128]{2,1,0:T(8,128)(2,1)S(1)}, bf16[2,288,128]{2,1,0:T(8,128)(2,1)S(1)}, u32[]{:S(2)}, u32[]{:S(2)}) collective-permute-start(bf16[2,288,128]{2,1,0:T(8,128)(2,1)S(1)} %get-tuple-element.173), channel_id=1, source_target_pairs={{0,24},{8,16},{16,8},{24,0},{1,25},{9,17},{17,9},{25,1},{2,26},{10... | collective-permute-start | bytes 442376 | tf_op jit(solution)/shard_map/ppermute | solution.py:298
  94.3 2.2 %collective-permute-done.37.b_last = bf16[1024,128]{1,0:T(8,128)(2,1)S(1)} collective-permute-done((bf16[1024,128]{1,0:T(8,128)(2,1)S(1)}, bf16[1024,128]{1,0:T(8,128)(2,1)S(1)}, u32[]{:S(2)}, u32[]{:S(2)}) %collective-permute-start.37) | collective-permute-done | bytes 262176 | tf_op jit(solution)/shard_map/ppermute | solution.py:298
  98.6 2.2 %shard_map.289 = (bf16[2048,1152]{1,0:T(8,128)(2,1)S(1)}, f32[4,288,128]{2,1,0:T(8,128)S(1)}, f32[4,288,128]{2,1,0:T(8,128)S(1)}) custom-call(s32[16,128]{1,0:T(8,128)S(1)} %get-tuple-element.157.facts_ref, f32[2048,128]{1,0:T(8,128)S(1)} %get-tuple-element.167.slope_ref, f32[2048,128]{1,0:T(8,128)S(1)} %get-tuple-element.130.pre_ref, ...), custom_call_target="tpu_custom_call" | custom-call | tf_op jit(solution)/shard_map/pallas_call | solution.py:998
  101.6 2.5 %shard_map.293 = bf16[4,512,256]{2,1,0:T(8,128)(2,1)} custom-call(bf16[2048,1152]{1,0:T(8,128)(2,1)S(1)} %get-tuple-element.180.columns, bf16[9,4,32,256]{3,2,1,0:T(8,128)(2,1)S(1)} %get-tuple-element.129.weight_ref), custom_call_target="tpu_custom_call" | custom-call | tf_op jit(solution)/shard_map/pallas_call | solution.py:999
  104.1 3.5 %all-to-all-start = ((bf16[4,512,256]{2,1,0:T(8,128)(2,1)}), bf16[4,512,256]{2,1,0:T(8,128)(2,1)S(1)}, u32[]{:S(2)}, u32[]{:S(2)}) async-start(bf16[4,512,256]{2,1,0:T(8,128)(2,1)} %shard_map.293), calls=%async_computation | async-start | bytes 2097152 | tf_op jit(solution)/shard_map/all_to_all | solution.py:1003
  108.6 2.0 %collective-permute-done.42.got_ref = f32[4,288,128]{2,1,0:T(8,128)S(1)} collective-permute-done((f32[4,288,128]{2,1,0:T(8,128)}, f32[4,288,128]{2,1,0:T(8,128)S(1)}, u32[]{:S(2)}, u32[]{:S(2)}) %collective-permute-start.42) | collective-permute-done | bytes 589856 | tf_op jit(solution)/shard_map/ppermute | solution.py:298
  110.9 2.4 %collective-permute-start.45 = (bf16[320,128]{1,0:T(8,128)(2,1)S(1)}, bf16[320,128]{1,0:T(8,128)(2,1)S(1)}, u32[]{:S(2)}, u32[]{:S(2)}) collective-permute-start(bf16[320,128]{1,0:T(8,128)(2,1)S(1)} %get-tuple-element.179), channel_id=1, source_target_pairs={{0,24},{8,16},{16,8},{24,0},{1,25},{9,17},{17,9},{25,1},{2,26},{10... | collective-permute-start | bytes 245768 | tf_op jit(solution)/shard_map/ppermute | solution.py:298
  114.3 5.3 %collective-permute-done.44.n2.g2 = bf16[320,128]{1,0:T(8,128)(2,1)S(1)} collective-permute-done((bf16[320,128]{1,0:T(8,128)(2,1)S(1)}, bf16[320,128]{1,0:T(8,128)(2,1)S(1)}, u32[]{:S(2)}, u32[]{:S(2)}) %collective-permute-start.44) | collective-permute-done | bytes 81952 | tf_op jit(solution)/shard_map/ppermute | solution.py:298
  122.3 4.2 %all-to-all-start.1 = ((f32[32,8,128]{2,1,0:T(8,128)}), f32[32,8,128]{2,1,0:T(8,128)S(1)}, u32[]{:S(2)}, u32[]{:S(2)}) async-start(f32[32,8,128]{2,1,0:T(8,128)} %bitcast.3), calls=%async_computation.1 | async-start | bytes 262144 | tf_op jit(solution)/shard_map/all_to_all | solution.py:1009
  126.5 1.8 %collective-permute-start.46 = (f32[152,128]{1,0:T(8,128)S(1)}, f32[152,128]{1,0:T(8,128)S(1)}, u32[]{:S(2)}, u32[]{:S(2)}) collective-permute-start(f32[152,128]{1,0:T(8,128)S(1)} %get-tuple-element.185), channel_id=1, source_target_pairs={{0,2},{2,0},{1,3},{3,1},{4,6},{6,4},{5,7},{7,5},{8,10},{10,8},{9,1... | collective-permute-start | bytes 233480 | tf_op jit(solution)/shard_map/ppermute | solution.py:298
  128.8 1.8 %collective-permute-start.48 = (bf16[2,64,256]{2,1,0:T(8,128)(2,1)S(1)}, bf16[2,64,256]{2,1,0:T(8,128)(2,1)S(1)}, u32[]{:S(2)}, u32[]{:S(2)}) collective-permute-start(bf16[2,64,256]{2,1,0:T(8,128)(2,1)S(1)} %get-tuple-element.192), channel_id=1, source_target_pairs={{0,8},{8,0},{16,24},{24,16},{1,9},{9,1},{17,25},{25,17},{2,10},{10... | collective-permute-start | bytes 196616 | tf_op jit(solution)/shard_map/ppermute | solution.py:298
  130.6 2.4 %collective-permute-start.49 = (bf16[2,64,256]{2,1,0:T(8,128)(2,1)S(1)}, bf16[2,64,256]{2,1,0:T(8,128)(2,1)S(1)}, u32[]{:S(2)}, u32[]{:S(2)}) collective-permute-start(bf16[2,64,256]{2,1,0:T(8,128)(2,1)S(1)} %get-tuple-element.193), channel_id=1, source_target_pairs={{0,16},{8,24},{16,0},{24,8},{1,17},{9,25},{17,1},{25,9},{2,18},{10... | collective-permute-start | bytes 196616 | tf_op jit(solution)/shard_map/ppermute | solution.py:298
  135.4 3.5 %shard_map.296 = (f32[1,1]{1,0:T(1,128)}, f32[9,64,64]{2,1,0:T(8,128)}, f32[9,64,64]{2,1,0:T(8,128)}, f32[9,64,64]{2,1,0:T(8,128)}, f32[9,64,64]{2,1,0:T(8,128)}...) custom-call(f32[256,128]{1,0:T(8,128)} %bitcast.18, ...), custom_call_target="tpu_custom_call" | custom-call | tf_op jit(solution)/shard_map/pallas_call | solution.py:1015
  (135 shorter events, 48.2 us)
Async XLA Ops:
  2.4 12.2 %collective-permute-start.11 = (bf16[144,256]{1,0:T(8,128)(2,1)S(1)}, bf16[144,256]{1,0:T(8,128)(2,1)S(1)}, u32[]{:S(2)}, u32[]{:S(2)}) collective-permute-start(bf16[144,256]{1,0:T(8,128)(2,1)S(1)} %get-tuple-element.124), channel_id=1, source_target_pairs={{0,8},{8,0},{16,24},{24,16},{1,9},{9,1},{17,25},{25,17},{2,10},{10... | collective-permute-start | bytes 221192 | tf_op jit(solution)/shard_map/ppermute | solution.py:298
  5.5 9.1 %collective-permute-start.12 = (bf16[144,256]{1,0:T(8,128)(2,1)S(1)}, bf16[144,256]{1,0:T(8,128)(2,1)S(1)}, u32[]{:S(2)}, u32[]{:S(2)}) collective-permute-start(bf16[144,256]{1,0:T(8,128)(2,1)S(1)} %get-tuple-element.125), channel_id=1, source_target_pairs={{0,16},{8,24},{16,0},{24,8},{1,17},{9,25},{17,1},{25,9},{2,18},{10... | collective-permute-start | bytes 221192 | tf_op jit(solution)/shard_map/ppermute | solution.py:298
  14.6 8.3 %collective-permute-start.14 = (bf16[4,64,256]{2,1,0:T(8,128)(2,1)S(1)}, bf16[4,64,256]{2,1,0:T(8,128)(2,1)S(1)}, u32[]{:S(2)}, u32[]{:S(2)}) collective-permute-start(bf16[4,64,256]{2,1,0:T(8,128)(2,1)S(1)} %get-tuple-element.127.refs_0_.a0), channel_id=1, source_target_pairs={{0,4},{4,0},{1,5},{5,1},{2,6},{6,2},{3,7},{7,3},{8,12},{12,8},{9,1... | collective-permute-start | bytes 393224 | tf_op jit(solution)/shard_map/ppermute | solution.py:298
  18.1 7.4 %collective-permute-start.3 = (bf16[304,128]{1,0:T(8,128)(2,1)S(1)}, bf16[304,128]{1,0:T(8,128)(2,1)S(1)}, u32[]{:S(2)}, u32[]{:S(2)}) collective-permute-start(bf16[304,128]{1,0:T(8,128)(2,1)S(1)} %shard_map.270.o0), channel_id=1, source_target_pairs={{0,24},{8,16},{16,8},{24,0},{1,25},{9,17},{17,9},{25,1},{2,26},{10... | collective-permute-start | bytes 233480 | tf_op jit(solution)/shard_map/ppermute | solution.py:298
  22.9 10.8 %collective-permute-start.15 = (bf16[8,64,256]{2,1,0:T(8,128)(2,1)S(1)}, bf16[8,64,256]{2,1,0:T(8,128)(2,1)S(1)}, u32[]{:S(2)}, u32[]{:S(2)}) collective-permute-start(bf16[8,64,256]{2,1,0:T(8,128)(2,1)S(1)} %shard_map.275), channel_id=1, source_target_pairs={{0,2},{2,0},{1,3},{3,1},{4,6},{6,4},{5,7},{7,5},{8,10},{10,8},{9,1... | collective-permute-start | bytes 786440 | tf_op jit(solution)/shard_map/ppermute | solution.py:298
  25.5 8.3 %collective-permute-start.17 = (bf16[8,64,256]{2,1,0:T(8,128)(2,1)S(1)}, bf16[8,64,256]{2,1,0:T(8,128)(2,1)S(1)}, u32[]{:S(2)}, u32[]{:S(2)}) collective-permute-start(bf16[8,64,256]{2,1,0:T(8,128)(2,1)S(1)} %shard_map.276), channel_id=1, source_target_pairs={{0,4},{4,0},{1,5},{5,1},{2,6},{6,2},{3,7},{7,3},{8,12},{12,8},{9,1... | collective-permute-start | bytes 786440 | tf_op jit(solution)/shard_map/ppermute | solution.py:298
  28.8 8.6 %collective-permute-start.10 = (bf16[576,128]{1,0:T(8,128)(2,1)S(1)}, bf16[576,128]{1,0:T(8,128)(2,1)S(1)}, u32[]{:S(2)}, u32[]{:S(2)}) collective-permute-start(bf16[576,128]{1,0:T(8,128)(2,1)S(1)} %shard_map.273.o0), channel_id=1, source_target_pairs={{0,24},{8,16},{16,8},{24,0},{1,25},{9,17},{17,9},{25,1},{2,26},{10... | collective-permute-start | bytes 442376 | tf_op jit(solution)/shard_map/ppermute | solution.py:298
  31.7 12.0 %collective-permute-start.9 = (bf16[576,128]{1,0:T(8,128)(2,1)S(1)}, bf16[576,128]{1,0:T(8,128)(2,1)S(1)}, u32[]{:S(2)}, u32[]{:S(2)}) collective-permute-start(bf16[576,128]{1,0:T(8,128)(2,1)S(1)} %shard_map.273.o0), channel_id=1, source_target_pairs={{0,16},{8,24},{16,0},{24,8},{1,17},{9,25},{17,1},{25,9},{2,18},{10... | collective-permute-start | bytes 442376 | tf_op jit(solution)/shard_map/ppermute | solution.py:298
  31.7 12.0 %collective-permute-start.8 = (bf16[576,128]{1,0:T(8,128)(2,1)S(1)}, bf16[576,128]{1,0:T(8,128)(2,1)S(1)}, u32[]{:S(2)}, u32[]{:S(2)}) collective-permute-start(bf16[576,128]{1,0:T(8,128)(2,1)S(1)} %shard_map.273.o0), channel_id=1, source_target_pairs={{0,8},{8,0},{16,24},{24,16},{1,9},{9,1},{17,25},{25,17},{2,10},{10... | collective-permute-start | bytes 442376 | tf_op jit(solution)/shard_map/ppermute | solution.py:298
  35.5 8.2 %collective-permute-start.18 = (f32[8,128]{1,0:T(8,128)S(1)}, f32[8,128]{1,0:T(8,128)S(1)}, u32[]{:S(2)}, u32[]{:S(2)}) collective-permute-start(f32[8,128]{1,0:T(8,128)S(1)} %get-tuple-element.131.own_ref), channel_id=1, source_target_pairs={{0,1},{1,0},{2,3},{3,2},{4,5},{5,4},{6,7},{7,6},{8,9},{9,8},{10,11... | collective-permute-start | bytes 12296 | tf_op jit(solution)/shard_map/ppermute | solution.py:298
  44.1 8.8 %collective-permute-start.19 = (bf16[1056,128]{1,0:T(8,128)(2,1)S(1)}, bf16[1056,128]{1,0:T(8,128)(2,1)S(1)}, u32[]{:S(2)}, u32[]{:S(2)}) collective-permute-start(bf16[1056,128]{1,0:T(8,128)(2,1)S(1)} %get-tuple-element.134), channel_id=1, source_target_pairs={{0,4},{4,0},{1,5},{5,1},{2,6},{6,2},{3,7},{7,3},{8,12},{12,8},{9,1... | collective-permute-start | bytes 811016 | tf_op jit(solution)/shard_map/ppermute | solution.py:298
  46.0 9.4 %collective-permute-start.22 = (bf16[1056,128]{1,0:T(8,128)(2,1)S(1)}, bf16[1056,128]{1,0:T(8,128)(2,1)S(1)}, u32[]{:S(2)}, u32[]{:S(2)}) collective-permute-start(bf16[1056,128]{1,0:T(8,128)(2,1)S(1)} %get-tuple-element.136), channel_id=1, source_target_pairs={{0,2},{2,0},{1,3},{3,1},{4,6},{6,4},{5,7},{7,5},{8,10},{10,8},{9,1... | collective-permute-start | bytes 811016 | tf_op jit(solution)/shard_map/ppermute | solution.py:298
  47.6 8.9 %collective-permute-start.27 = (bf16[576,128]{1,0:T(8,128)(2,1)S(1)}, bf16[576,128]{1,0:T(8,128)(2,1)S(1)}, u32[]{:S(2)}, u32[]{:S(2)}) collective-permute-start(bf16[576,128]{1,0:T(8,128)(2,1)S(1)} %collective-permute-done.9.o2), channel_id=1, source_target_pairs={{0,1},{1,0},{2,3},{3,2},{4,5},{5,4},{6,7},{7,6},{8,9},{9,8},{10,11... | collective-permute-start | bytes 442376 | tf_op jit(solution)/shard_map/ppermute | solution.py:298
  48.5 10.3 %collective-permute-start.23 = (bf16[1072,128]{1,0:T(8,128)(2,1)S(1)}, bf16[1072,128]{1,0:T(8,128)(2,1)S(1)}, u32[]{:S(2)}, u32[]{:S(2)}) collective-permute-start(bf16[1072,128]{1,0:T(8,128)(2,1)S(1)} %get-tuple-element.135.b0.rest_4_), channel_id=1, source_target_pairs={{0,4},{4,0},{1,5},{5,1},{2,6},{6,2},{3,7},{7,3},{8,12},{12,8},{9,1... | collective-permute-start | bytes 823304 | tf_op jit(solution)/shard_map/ppermute | solution.py:298
  49.4 11.7 %collective-permute-start.20 = (bf16[1072,128]{1,0:T(8,128)(2,1)S(1)}, bf16[1072,128]{1,0:T(8,128)(2,1)S(1)}, u32[]{:S(2)}, u32[]{:S(2)}) collective-permute-start(bf16[1072,128]{1,0:T(8,128)(2,1)S(1)} %get-tuple-element.133.a0.rest_0_), channel_id=1, source_target_pairs={{0,2},{2,0},{1,3},{3,1},{4,6},{6,4},{5,7},{7,5},{8,10},{10,8},{9,1... | collective-permute-start | bytes 823304 | tf_op jit(solution)/shard_map/ppermute | solution.py:298
  52.9 12.3 %collective-permute-start.21 = (bf16[1056,128]{1,0:T(8,128)(2,1)S(1)}, bf16[1056,128]{1,0:T(8,128)(2,1)S(1)}, u32[]{:S(2)}, u32[]{:S(2)}) collective-permute-start(bf16[1056,128]{1,0:T(8,128)(2,1)S(1)} %collective-permute-done.19.a1.rest_1_), channel_id=1, source_target_pairs={{0,2},{2,0},{1,3},{3,1},{4,6},{6,4},{5,7},{7,5},{8,10},{10,8},{9,1... | collective-permute-start | bytes 811016 | tf_op jit(solution)/shard_map/ppermute | solution.py:298
  55.4 9.8 %collective-permute-start.24 = (bf16[1056,128]{1,0:T(8,128)(2,1)S(1)}, bf16[1056,128]{1,0:T(8,128)(2,1)S(1)}, u32[]{:S(2)}, u32[]{:S(2)}) collective-permute-start(bf16[1056,128]{1,0:T(8,128)(2,1)S(1)} %collective-permute-done.22.b1.rest_5_), channel_id=1, source_target_pairs={{0,4},{4,0},{1,5},{5,1},{2,6},{6,2},{3,7},{7,3},{8,12},{12,8},{9,1... | collective-permute-start | bytes 811016 | tf_op jit(solution)/shard_map/ppermute | solution.py:298
  73.7 14.1 %collective-permute-start.34 = (bf16[2064,128]{1,0:T(8,128)(2,1)S(1)}, bf16[2064,128]{1,0:T(8,128)(2,1)S(1)}, u32[]{:S(2)}, u32[]{:S(2)}) collective-permute-start(bf16[2064,128]{1,0:T(8,128)(2,1)S(1)} %get-tuple-element.159), channel_id=1, source_target_pairs={{0,4},{4,0},{1,5},{5,1},{2,6},{6,2},{3,7},{7,3},{8,12},{12,8},{9,1... | collective-permute-start | bytes 1585160 | tf_op jit(solution)/shard_map/ppermute | solution.py:298
  74.1 13.8 %collective-permute-start.35 = (bf16[2048,128]{1,0:T(8,128)(2,1)S(1)}, bf16[2048,128]{1,0:T(8,128)(2,1)S(1)}, u32[]{:S(2)}, u32[]{:S(2)}) collective-permute-start(bf16[2048,128]{1,0:T(8,128)(2,1)S(1)} %get-tuple-element.163), channel_id=1, source_target_pairs={{0,2},{2,0},{1,3},{3,1},{4,6},{6,4},{5,7},{7,5},{8,10},{10,8},{9,1... | collective-permute-start | bytes 1572872 | tf_op jit(solution)/shard_map/ppermute | solution.py:298
  88.0 8.6 %collective-permute-start.36 = (bf16[1056,128]{1,0:T(8,128)(2,1)S(1)}, bf16[1056,128]{1,0:T(8,128)(2,1)S(1)}, u32[]{:S(2)}, u32[]{:S(2)}) collective-permute-start(bf16[1056,128]{1,0:T(8,128)(2,1)S(1)} %get-tuple-element.164), channel_id=1, source_target_pairs={{0,2},{2,0},{1,3},{3,1},{4,6},{6,4},{5,7},{7,5},{8,10},{10,8},{9,1... | collective-permute-start | bytes 811016 | tf_op jit(solution)/shard_map/ppermute | solution.py:298
  89.6 7.0 %collective-permute-start.37 = (bf16[1024,128]{1,0:T(8,128)(2,1)S(1)}, bf16[1024,128]{1,0:T(8,128)(2,1)S(1)}, u32[]{:S(2)}, u32[]{:S(2)}) collective-permute-start(bf16[1024,128]{1,0:T(8,128)(2,1)S(1)} %get-tuple-element.166), channel_id=1, source_target_pairs={{0,4},{4,0},{1,5},{5,1},{2,6},{6,2},{3,7},{7,3},{8,12},{12,8},{9,1... | collective-permute-start | bytes 786440 | tf_op jit(solution)/shard_map/ppermute | solution.py:298
  90.8 16.8 %collective-permute-start.40 = (bf16[2,288,128]{2,1,0:T(8,128)(2,1)}, bf16[2,288,128]{2,1,0:T(8,128)(2,1)S(1)}, u32[]{:S(2)}, u32[]{:S(2)}) collective-permute-start(bf16[2,288,128]{2,1,0:T(8,128)(2,1)} %get-tuple-element.172), channel_id=1, source_target_pairs={{0,16},{8,24},{16,0},{24,8},{1,17},{9,25},{17,1},{25,9},{2,18},{10... | collective-permute-start | bytes 442376 | tf_op jit(solution)/shard_map/ppermute | solution.py:298
  90.8 16.8 %collective-permute-start.41 = (bf16[2,288,128]{2,1,0:T(8,128)(2,1)S(1)}, bf16[2,288,128]{2,1,0:T(8,128)(2,1)S(1)}, u32[]{:S(2)}, u32[]{:S(2)}) collective-permute-start(bf16[2,288,128]{2,1,0:T(8,128)(2,1)S(1)} %get-tuple-element.173), channel_id=1, source_target_pairs={{0,24},{8,16},{16,8},{24,0},{1,25},{9,17},{17,9},{25,1},{2,26},{10... | collective-permute-start | bytes 442376 | tf_op jit(solution)/shard_map/ppermute | solution.py:298
  93.2 14.5 %collective-permute-start.39 = (bf16[2,288,128]{2,1,0:T(8,128)(2,1)S(1)}, bf16[2,288,128]{2,1,0:T(8,128)(2,1)S(1)}, u32[]{:S(2)}, u32[]{:S(2)}) collective-permute-start(bf16[2,288,128]{2,1,0:T(8,128)(2,1)S(1)} %get-tuple-element.156), channel_id=1, source_target_pairs={{0,8},{8,0},{16,24},{24,16},{1,9},{9,1},{17,25},{25,17},{2,10},{10... | collective-permute-start | bytes 442376 | tf_op jit(solution)/shard_map/ppermute | solution.py:298
  104.1 18.2 %all-to-all-start = ((bf16[4,512,256]{2,1,0:T(8,128)(2,1)}), bf16[4,512,256]{2,1,0:T(8,128)(2,1)S(1)}, u32[]{:S(2)}, u32[]{:S(2)}) async-start(bf16[4,512,256]{2,1,0:T(8,128)(2,1)} %shard_map.293), calls=%async_computation | async-start | bytes 2097152 | tf_op jit(solution)/shard_map/all_to_all | solution.py:1003
  110.8 8.8 %collective-permute-start.44 = (bf16[320,128]{1,0:T(8,128)(2,1)S(1)}, bf16[320,128]{1,0:T(8,128)(2,1)S(1)}, u32[]{:S(2)}, u32[]{:S(2)}) collective-permute-start(bf16[320,128]{1,0:T(8,128)(2,1)S(1)} %get-tuple-element.178), channel_id=1, source_target_pairs={{0,16},{8,24},{16,0},{24,8},{1,17},{9,25},{17,1},{25,9},{2,18},{10... | collective-permute-start | bytes 245768 | tf_op jit(solution)/shard_map/ppermute | solution.py:298
  110.9 8.7 %collective-permute-start.45 = (bf16[320,128]{1,0:T(8,128)(2,1)S(1)}, bf16[320,128]{1,0:T(8,128)(2,1)S(1)}, u32[]{:S(2)}, u32[]{:S(2)}) collective-permute-start(bf16[320,128]{1,0:T(8,128)(2,1)S(1)} %get-tuple-element.179), channel_id=1, source_target_pairs={{0,24},{8,16},{16,8},{24,0},{1,25},{9,17},{17,9},{25,1},{2,26},{10... | collective-permute-start | bytes 245768 | tf_op jit(solution)/shard_map/ppermute | solution.py:298
  113.3 7.6 %collective-permute-start.43 = (bf16[320,128]{1,0:T(8,128)(2,1)S(1)}, bf16[320,128]{1,0:T(8,128)(2,1)S(1)}, u32[]{:S(2)}, u32[]{:S(2)}) collective-permute-start(bf16[320,128]{1,0:T(8,128)(2,1)S(1)} %get-tuple-element.177), channel_id=1, source_target_pairs={{0,8},{8,0},{16,24},{24,16},{1,9},{9,1},{17,25},{25,17},{2,10},{10... | collective-permute-start | bytes 245768 | tf_op jit(solution)/shard_map/ppermute | solution.py:298
  122.3 12.5 %all-to-all-start.1 = ((f32[32,8,128]{2,1,0:T(8,128)}), f32[32,8,128]{2,1,0:T(8,128)S(1)}, u32[]{:S(2)}, u32[]{:S(2)}) async-start(f32[32,8,128]{2,1,0:T(8,128)} %bitcast.3), calls=%async_computation.1 | async-start | bytes 262144 | tf_op jit(solution)/shard_map/all_to_all | solution.py:1009
  126.5 7.7 %collective-permute-start.46 = (f32[152,128]{1,0:T(8,128)S(1)}, f32[152,128]{1,0:T(8,128)S(1)}, u32[]{:S(2)}, u32[]{:S(2)}) collective-permute-start(f32[152,128]{1,0:T(8,128)S(1)} %get-tuple-element.185), channel_id=1, source_target_pairs={{0,2},{2,0},{1,3},{3,1},{4,6},{6,4},{5,7},{7,5},{8,10},{10,8},{9,1... | collective-permute-start | bytes 233480 | tf_op jit(solution)/shard_map/ppermute | solution.py:298
  128.8 10.1 %collective-permute-start.48 = (bf16[2,64,256]{2,1,0:T(8,128)(2,1)S(1)}, bf16[2,64,256]{2,1,0:T(8,128)(2,1)S(1)}, u32[]{:S(2)}, u32[]{:S(2)}) collective-permute-start(bf16[2,64,256]{2,1,0:T(8,128)(2,1)S(1)} %get-tuple-element.192), channel_id=1, source_target_pairs={{0,8},{8,0},{16,24},{24,16},{1,9},{9,1},{17,25},{25,17},{2,10},{10... | collective-permute-start | bytes 196616 | tf_op jit(solution)/shard_map/ppermute | solution.py:298
  130.6 8.3 %collective-permute-start.49 = (bf16[2,64,256]{2,1,0:T(8,128)(2,1)S(1)}, bf16[2,64,256]{2,1,0:T(8,128)(2,1)S(1)}, u32[]{:S(2)}, u32[]{:S(2)}) collective-permute-start(bf16[2,64,256]{2,1,0:T(8,128)(2,1)S(1)} %get-tuple-element.193), channel_id=1, source_target_pairs={{0,16},{8,24},{16,0},{24,8},{1,17},{9,25},{17,1},{25,9},{2,18},{10... | collective-permute-start | bytes 196616 | tf_op jit(solution)/shard_map/ppermute | solution.py:298
  (35 other events, 88.2 us)
